TPU v7x, 32 devices: a whole 2x2x4 slice. The times are simulated.
32 devices in a mesh: wide: 4 (over x, core), narrow: 8 (over z, y).
Axes of the slice: x: 2, y: 2, z: 4, core: 2. Of those that a mesh axis runs over, the one named last changes fastest.
Arguments:
- tokens: bfloat16 [8192, 1280], P(('wide', 'narrow')), may hold values from -6 to 6
- routes: int32 [8192, 7], P(('wide', 'narrow')), may hold values from 0 to 15, all different within a row; in each aligned block of 256 rows (0 to 255, 256 to 511, ...) at most 168 rows name the same one
- gates: float32 [8192, 7], P(('wide', 'narrow')), may hold values from 0.06 to 0.24
- attn_gain: bfloat16 [1280], replicated, may hold values from 0.5 to 1.5
- query_weight: bfloat16 [1280, 1280], replicated, may hold values from -0.15625 to 0.15625
- key_weight: bfloat16 [1280, 1280], replicated, may hold values from -0.15625 to 0.15625
- value_weight: bfloat16 [1280, 1280], replicated, may hold values from -0.15625 to 0.15625
- output_weight: bfloat16 [1280, 1280], replicated, may hold values from -1.25 to 1.25
- ffn_gain: bfloat16 [1280], replicated, may hold values from 0.5 to 1.5
- shared_gate: bfloat16 [1280, 896], replicated, may hold values from -0.15625 to 0.15625
- shared_up: bfloat16 [1280, 896], replicated, may hold values from -0.15625 to 0.15625
- shared_down: bfloat16 [896, 1280], replicated, may hold values from -0.1875 to 0.1875
- expert_gate: bfloat16 [16, 1280, 896], P('narrow'), may hold values from -0.15625 to 0.15625
- expert_up: bfloat16 [16, 1280, 896], P('narrow'), may hold values from -0.15625 to 0.15625
- expert_down: bfloat16 [16, 896, 1280], P('narrow'), may hold values from -0.1875 to 0.1875
- cotangent: bfloat16 [8192, 1280], P(('wide', 'narrow')), may hold values from -6 to 6
Outputs:
- mixed: bfloat16 [8192, 1280], P(('wide', 'narrow'))
- tokens_grad: float32 [8192, 1280], P(('wide', 'narrow'))
- attn_gain_grad: float32 [1280], P(('wide', 'narrow'))
- query_weight_grad: float32 [1280, 1280], P(('wide', 'narrow'))
- key_weight_grad: float32 [1280, 1280], P(('wide', 'narrow'))
- value_weight_grad: float32 [1280, 1280], P(('wide', 'narrow'))
- output_weight_grad: float32 [1280, 1280], P(('wide', 'narrow'))
- ffn_gain_grad: float32 [1280], P(('wide', 'narrow'))
- shared_gate_grad: float32 [1280, 896], P(('wide', 'narrow'))
- shared_up_grad: float32 [1280, 896], P(('wide', 'narrow'))
- shared_down_grad: float32 [896, 1280], P(('wide', 'narrow'))
- expert_gate_grad: float32 [16, 1280, 896], P('narrow', 'wide')
- expert_up_grad: float32 [16, 1280, 896], P('narrow', 'wide')
- expert_down_grad: float32 [16, 896, 1280], P('narrow', 'wide')
Inputs may be any that keep to these rules, and one draw needn't show every extreme that they name: `routes`: each row names 7 different experts. Within each aligned block of 256 rows no expert is named by more than 168 rows, and in some block one expert is named by exactly 168.
All inputs are finite; a program needn't handle non-finite values.
Results may differ from a plain program's by a relative error of at most 0.017.
Values may be sent and summed in bfloat16 or wider, within the bound.
No kernel may reach another device: no remote copies, remote signals or barrier semaphores. Data moves between devices by JAX's collectives and lax.ppermute only.
A program may use at most 320 MiB of HBM per device.

v0:
```python
import jax
import jax.numpy as jnp
from jax import lax
from jax.sharding import PartitionSpec as P

HEAD_DIM = 128


EPS = 1e-06
FLOAT = jnp.float32
HALF = jnp.bfloat16


def rope_tables(positions, width):
    half = width // 2
    freq = 10000.0 ** (-(jnp.arange(half, dtype=jnp.float32) * 2.0) / width)
    angles = positions.astype(jnp.float32)[:, None] * freq[None, :]
    return (jnp.cos(angles)[:, None, :], jnp.sin(angles)[:, None, :])


def rotate(values, cosine_table, sine_table):
    half = values.shape[-1] // 2
    first = values[..., :half]
    second = values[..., half:]
    return jnp.concatenate(
        [first * cosine_table - second * sine_table, second * cosine_table + first * sine_table],
        axis=-1,
    )


def silu_parts(pre_act):
    sigma = jax.nn.sigmoid(pre_act)
    return (pre_act * sigma, sigma * (1.0 + pre_act * (1.0 - sigma)))


def norm_back(grad_out, normed, inv_scale, gain):
    gain_grad = jnp.sum(grad_out * normed, axis=0)
    scaled = grad_out * gain
    return (
        inv_scale * (scaled - normed * jnp.mean(scaled * normed, axis=1, keepdims=True)),
        gain_grad,
    )


def slot_tables(routes, gates, experts, capacity):
    picked = routes[:, :, None] == jnp.arange(experts, dtype=jnp.int32)[None, None, :]
    member = jnp.sum(picked.astype(jnp.int32), axis=1)
    token_gate = jnp.sum(jnp.where(picked, gates[:, :, None], 0.0), axis=1)
    rank = jnp.cumsum(member, axis=0) - 1
    slot_ids = jnp.arange(capacity, dtype=jnp.int32)
    hit = (member.T[:, None, :] == 1) & (rank.T[:, None, :] == slot_ids[None, :, None])
    slot_gate = jnp.sum(jnp.where(hit, token_gate.T[:, None, :], 0.0), axis=2)
    return (hit.astype(HALF), slot_gate, token_gate)


def on_device(
    tokens,
    routes,
    gates,
    attn_gain,
    query_weight,
    key_weight,
    value_weight,
    output_weight,
    ffn_gain,
    shared_gate,
    shared_up,
    shared_down,
    expert_gate,
    expert_up,
    expert_down,
    cotangent,
):
    length, model_width = tokens.shape
    head_count = model_width // HEAD_DIM
    top_count = routes.shape[1]
    local_experts = expert_gate.shape[0]
    groups = lax.axis_size("narrow")
    experts = groups * local_experts
    seq_len = length * groups
    capacity = min(length, (length * top_count * 3 // (2 * experts) + 7) // 8 * 8)
    inputs = tokens.astype(FLOAT)
    inv_one = lax.rsqrt(jnp.mean(inputs * inputs, axis=1, keepdims=True) + EPS)
    normed_one = inputs * inv_one
    attn_in = (normed_one * attn_gain).astype(HALF)
    own_pos = lax.axis_index("narrow") * length + jnp.arange(length, dtype=jnp.int32)
    all_pos = jnp.arange(seq_len, dtype=jnp.int32)
    cosine_table, sine_table = rope_tables(own_pos, HEAD_DIM)
    cosine_all, sine_all = rope_tables(all_pos, HEAD_DIM)
    query_lin = jnp.dot(attn_in, query_weight, preferred_element_type=FLOAT).reshape(
        length, head_count, HEAD_DIM
    )
    key_lin = jnp.dot(attn_in, key_weight, preferred_element_type=FLOAT).reshape(
        length, head_count, HEAD_DIM
    )
    values = (
        jnp.dot(attn_in, value_weight, preferred_element_type=FLOAT)
        .astype(HALF)
        .reshape(length, head_count, HEAD_DIM)
    )
    queries = rotate(query_lin, cosine_table, sine_table).astype(HALF)
    key_rot = rotate(key_lin, cosine_table, sine_table).astype(HALF)
    all_keys, all_values = (
        lax.all_gather(key_rot, "narrow", axis=0, tiled=True),
        lax.all_gather(values, "narrow", axis=0, tiled=True),
    )
    causal = own_pos[:, None] >= all_pos[None, :]
    factor = HEAD_DIM ** (-0.5)

    def scores_of():
        raw_scores = (
            jnp.einsum("qhd,khd->hqk", queries, all_keys, preferred_element_type=FLOAT) * factor
        )
        return jnp.where(causal[None], raw_scores, -1e30)

    scores = scores_of()
    row_peak = jnp.max(scores, axis=2, keepdims=True)
    shifted = jnp.exp(scores - row_peak)
    row_total = jnp.sum(shifted, axis=2, keepdims=True)
    log_total = row_peak + jnp.log(row_total)
    prob_low = (shifted / row_total).astype(HALF)
    attended = (
        jnp.einsum("hqk,khd->qhd", prob_low, all_values, preferred_element_type=FLOAT)
        .astype(HALF)
        .reshape(length, model_width)
    )
    hidden = inputs + jnp.dot(attended, output_weight, preferred_element_type=FLOAT)
    inv_two = lax.rsqrt(jnp.mean(hidden * hidden, axis=1, keepdims=True) + EPS)
    normed_two = hidden * inv_two
    ffn_in = (normed_two * ffn_gain).astype(HALF)
    sgate_pre = jnp.dot(ffn_in, shared_gate, preferred_element_type=FLOAT)
    sup_pre = jnp.dot(ffn_in, shared_up, preferred_element_type=FLOAT)
    shared_act, shared_slope = silu_parts(sgate_pre)
    shared_inner = (shared_act * sup_pre).astype(HALF)
    shared_out = jnp.dot(shared_inner, shared_down, preferred_element_type=FLOAT)
    onehot, slot_gate, token_gate = slot_tables(routes, gates, experts, capacity)
    dispatched = (
        jnp.einsum("ect,td->ecd", onehot, ffn_in, preferred_element_type=FLOAT)
        .astype(HALF)
        .reshape(groups, local_experts, capacity, model_width)
    )
    arrived = lax.all_to_all(dispatched, "narrow", split_axis=0, concat_axis=0, tiled=True)
    gate_pre = jnp.einsum("secd,edf->secf", arrived, expert_gate, preferred_element_type=FLOAT)
    up_pre = jnp.einsum("secd,edf->secf", arrived, expert_up, preferred_element_type=FLOAT)
    active, silu_slope = silu_parts(gate_pre)
    inner_act = (active * up_pre).astype(HALF)
    result = jnp.einsum(
        "secf,efd->secd", inner_act, expert_down, preferred_element_type=FLOAT
    ).astype(HALF)
    returned = lax.all_to_all(result, "narrow", split_axis=0, concat_axis=0, tiled=True)
    returned, kept_rows = (returned, arrived)
    selected = jnp.einsum(
        "ect,ecd->etd",
        onehot,
        returned.reshape(experts, capacity, model_width),
        preferred_element_type=FLOAT,
    )
    routed = jnp.sum(token_gate.T[:, :, None] * selected, axis=0)
    mixed = (hidden + shared_out + routed).astype(HALF)
    upstream = cotangent.astype(FLOAT)
    slot_cot = jnp.einsum("ect,td->ecd", onehot, cotangent, preferred_element_type=FLOAT)
    grad_send = (
        (slot_cot * slot_gate[:, :, None])
        .astype(HALF)
        .reshape(groups, local_experts, capacity, model_width)
    )
    grad_recv = lax.all_to_all(grad_send, "narrow", split_axis=0, concat_axis=0, tiled=True)
    gate_pre = jnp.einsum("secd,edf->secf", kept_rows, expert_gate, preferred_element_type=FLOAT)
    up_pre = jnp.einsum("secd,edf->secf", kept_rows, expert_up, preferred_element_type=FLOAT)
    active, silu_slope = silu_parts(gate_pre)
    inner_act = (active * up_pre).astype(HALF)
    inner_grad = jnp.einsum("secd,efd->secf", grad_recv, expert_down, preferred_element_type=FLOAT)
    down_grad = jnp.einsum("secf,secd->efd", inner_act, grad_recv, preferred_element_type=FLOAT)
    rgate_grad = (inner_grad * up_pre * silu_slope).astype(HALF)
    rup_grad = (inner_grad * active).astype(HALF)
    gate_grad = jnp.einsum("secd,secf->edf", kept_rows, rgate_grad, preferred_element_type=FLOAT)
    up_grad = jnp.einsum("secd,secf->edf", kept_rows, rup_grad, preferred_element_type=FLOAT)
    row_grad = (
        jnp.einsum("secf,edf->secd", rgate_grad, expert_gate, preferred_element_type=FLOAT)
        + jnp.einsum("secf,edf->secd", rup_grad, expert_up, preferred_element_type=FLOAT)
    ).astype(HALF)
    grad_back = lax.all_to_all(row_grad, "narrow", split_axis=0, concat_axis=0, tiled=True)
    routed_grad = jnp.einsum(
        "ect,ecd->td",
        onehot,
        grad_back.reshape(experts, capacity, model_width),
        preferred_element_type=FLOAT,
    )
    expert_parts = (
        lax.psum_scatter(
            gate_grad.astype(jnp.bfloat16), "wide", scatter_dimension=1, tiled=True
        ).astype(jnp.float32),
        lax.psum_scatter(
            up_grad.astype(jnp.bfloat16), "wide", scatter_dimension=1, tiled=True
        ).astype(jnp.float32),
        lax.psum_scatter(
            down_grad.astype(jnp.bfloat16), "wide", scatter_dimension=1, tiled=True
        ).astype(jnp.float32),
    )
    sdown_grad = jnp.dot(shared_inner.T, cotangent, preferred_element_type=FLOAT)
    sinner_grad = jnp.dot(cotangent, shared_down.T, preferred_element_type=FLOAT)
    sgate_grad = (sinner_grad * sup_pre * shared_slope).astype(HALF)
    sup_grad = (sinner_grad * shared_act).astype(HALF)
    sgate_wgrad = jnp.dot(ffn_in.T, sgate_grad, preferred_element_type=FLOAT)
    sup_wgrad = jnp.dot(ffn_in.T, sup_grad, preferred_element_type=FLOAT)
    ffn_in_grad = (
        jnp.dot(sgate_grad, shared_gate.T, preferred_element_type=FLOAT)
        + jnp.dot(sup_grad, shared_up.T, preferred_element_type=FLOAT)
        + routed_grad
    )
    hidden_norm_grad, ffn_gain_grad = norm_back(ffn_in_grad, normed_two, inv_two, ffn_gain)
    hidden_grad = upstream + hidden_norm_grad
    branch_grad = hidden_grad.astype(HALF)
    output_wgrad = jnp.dot(attended.T, branch_grad, preferred_element_type=FLOAT)
    attended_grad = (
        jnp.dot(branch_grad, output_weight.T, preferred_element_type=FLOAT)
        .astype(HALF)
        .reshape(length, head_count, HEAD_DIM)
    )
    probs_full = jnp.exp(scores_of() - log_total)
    prob_grad = jnp.einsum("qhd,khd->hqk", attended_grad, all_values, preferred_element_type=FLOAT)
    score_grad = (
        probs_full * (prob_grad - jnp.sum(prob_grad * probs_full, axis=2, keepdims=True))
    ).astype(HALF)
    value_part = jnp.einsum(
        "hqk,qhd->khd", prob_low, attended_grad, preferred_element_type=FLOAT
    ).reshape(seq_len, model_width)
    query_rot_grad = (
        jnp.einsum("hqk,khd->qhd", score_grad, all_keys, preferred_element_type=FLOAT) * factor
    )
    key_rot_part = (
        jnp.einsum("hqk,qhd->khd", score_grad, queries, preferred_element_type=FLOAT) * factor
    )
    key_part = rotate(key_rot_part, cosine_all, -sine_all).reshape(seq_len, model_width)
    key_sum, value_sum = (
        lax.psum_scatter(
            key_part.astype(jnp.bfloat16), "narrow", scatter_dimension=0, tiled=True
        ).astype(jnp.float32),
        lax.psum_scatter(
            value_part.astype(jnp.bfloat16), "narrow", scatter_dimension=0, tiled=True
        ).astype(jnp.float32),
    )
    key_grad = key_sum.astype(HALF)
    value_grad = value_sum.astype(HALF)
    query_grad = (
        rotate(query_rot_grad, cosine_table, -sine_table).astype(HALF).reshape(length, model_width)
    )
    query_wgrad = jnp.dot(attn_in.T, query_grad, preferred_element_type=FLOAT)
    key_wgrad = jnp.dot(attn_in.T, key_grad, preferred_element_type=FLOAT)
    value_wgrad = jnp.dot(attn_in.T, value_grad, preferred_element_type=FLOAT)
    attn_in_grad = (
        jnp.dot(query_grad, query_weight.T, preferred_element_type=FLOAT)
        + jnp.dot(key_grad, key_weight.T, preferred_element_type=FLOAT)
        + jnp.dot(value_grad, value_weight.T, preferred_element_type=FLOAT)
    )
    input_norm_grad, attn_gain_grad = norm_back(attn_in_grad, normed_one, inv_one, attn_gain)
    tokens_grad = hidden_grad + input_norm_grad
    dense_parts = (
        lax.psum_scatter(attn_gain_grad, ("wide", "narrow"), scatter_dimension=0, tiled=True),
        lax.psum_scatter(query_wgrad, ("wide", "narrow"), scatter_dimension=0, tiled=True),
        lax.psum_scatter(key_wgrad, ("wide", "narrow"), scatter_dimension=0, tiled=True),
        lax.psum_scatter(value_wgrad, ("wide", "narrow"), scatter_dimension=0, tiled=True),
        lax.psum_scatter(output_wgrad, ("wide", "narrow"), scatter_dimension=0, tiled=True),
        lax.psum_scatter(ffn_gain_grad, ("wide", "narrow"), scatter_dimension=0, tiled=True),
        lax.psum_scatter(sgate_wgrad, ("wide", "narrow"), scatter_dimension=0, tiled=True),
        lax.psum_scatter(sup_wgrad, ("wide", "narrow"), scatter_dimension=0, tiled=True),
        lax.psum_scatter(sdown_grad, ("wide", "narrow"), scatter_dimension=0, tiled=True),
    )
    return (
        mixed,
        tokens_grad,
        dense_parts[0],
        dense_parts[1],
        dense_parts[2],
        dense_parts[3],
        dense_parts[4],
        dense_parts[5],
        dense_parts[6],
        dense_parts[7],
        dense_parts[8],
        expert_parts[0],
        expert_parts[1],
        expert_parts[2],
    )


def solution(mesh):
    in_specs = (
        P(("wide", "narrow"), None),
        P(("wide", "narrow"), None),
        P(("wide", "narrow"), None),
        P(),
        P(),
        P(),
        P(),
        P(),
        P(),
        P(),
        P(),
        P(),
        P("narrow", None, None),
        P("narrow", None, None),
        P("narrow", None, None),
        P(("wide", "narrow"), None),
    )
    out_specs = (
        P(("wide", "narrow"), None),
        P(("wide", "narrow"), None),
        P(("wide", "narrow")),
        P(("wide", "narrow"), None),
        P(("wide", "narrow"), None),
        P(("wide", "narrow"), None),
        P(("wide", "narrow"), None),
        P(("wide", "narrow")),
        P(("wide", "narrow"), None),
        P(("wide", "narrow"), None),
        P(("wide", "narrow"), None),
        P("narrow", "wide", None),
        P("narrow", "wide", None),
        P("narrow", "wide", None),
    )
    return jax.shard_map(
        on_device, mesh=mesh, in_specs=in_specs, out_specs=out_specs, check_vma=False
    )
```

profile of v0, /device:TPU:4, one launch (start us, length us, event | category | flops | bytes accessed | tf_op | source)
XLA Modules:
  0.0 2173.2 jit_solution(17403836865830437548)
XLA Ops:
  44.1 79.1 %all-gather.5.cloned.1.call-done = bf16[2048,10,128]{2,0,1:T(8,128)(2,1)} async-done(((bf16[256,10,128]{2,0,1:T(8,128)(2,1)}), bf16[2048,10,128]{2,0,1:T(8,128)(2,1)}) %all-gather.5.cloned.1.call-update) | async-done | bytes 5242896 | tf_op jit(solution)/shard_map/all_gather | solution.py:104
  123.2 15.0 fusion.2
  158.8 53.3 %all-gather.3.cloned.1.call-done = bf16[2048,10,128]{0,2,1:T(8,128)(2,1)} async-done(((bf16[256,10,128]{0,2,1:T(8,128)(2,1)}), bf16[2048,10,128]{0,2,1:T(8,128)(2,1)}) %all-gather.3.cloned.1.call-update) | async-done | bytes 5242896 | tf_op jit(solution)/shard_map/all_gather | solution.py:105
  241.6 143.6 %all-to-all-done = bf16[8,2,168,1280]{3,2,1,0:T(8,128)(2,1)} async-done(((bf16[8,2,168,1280]{3,2,1,0:T(8,128)(2,1)}), bf16[8,2,168,1280]{3,2,1,0:T(8,128)(2,1)}, u32[]{:S(2)}, u32[]{:S(2)}) %all-to-all-start) | async-done | bytes 6881312 | tf_op jit(solution)/shard_map/all_to_all | solution.py:142
  391.0 13.0 fusion.16
  417.0 123.2 %all-to-all-done.2 = bf16[8,2,168,1280]{3,2,1,0:T(8,128)(2,1)} async-done(((bf16[8,2,168,1280]{3,2,1,0:T(8,128)(2,1)}), bf16[8,2,168,1280]{3,2,1,0:T(8,128)(2,1)}, u32[]{:S(2)}, u32[]{:S(2)}) %all-to-all-start.2) | async-done | bytes 6881312 | tf_op jit(solution)/shard_map/all_to_all | solution.py:167
  540.3 19.7 fusion.5
  560.0 13.6 fusion.27
  573.6 13.8 fusion.22
  609.2 139.1 %all-to-all-done.3 = bf16[8,2,168,1280]{3,2,1,0:T(8,128)(2,1)} async-done(((bf16[8,2,168,1280]{3,2,1,0:T(8,128)(2,1)}), bf16[8,2,168,1280]{3,2,1,0:T(8,128)(2,1)}, u32[]{:S(2)}, u32[]{:S(2)}) %all-to-all-start.3) | async-done | bytes 6881312 | tf_op jit(solution)/shard_map/all_to_all | solution.py:182
  772.5 18.1 multiply_reduce_fusion
  790.6 15.7 multiply_convert_fusion
  818.5 13.9 bitcast_convert_fusion
  832.5 13.2 bitcast_convert_fusion.1
  845.9 13.7 bitcast_convert_fusion.2
  914.5 167.1 %reduce-scatter.20.cloned.1.call-done = bf16[256,1280]{0,1:T(8,128)(2,1)} async-done(((bf16[2048,1280]{0,1:T(8,128)(2,1)}), bf16[256,1280]{0,1:T(8,128)(2,1)}) %reduce-scatter.20.cloned.1.call-update) | async-done | bytes 655376 | tf_op jit(solution)/shard_map/reduce_scatter | solution.py:236
  1090.9 118.9 %fusion = f32[32,1280]{1,0:T(8,128)S(1)} fusion(f32[896,1280]{1,0:T(8,128)} %fusion.95), kind=kCustom, calls=%all-reduce-scatter | all-reduce-scatter fusion | flops 1310721 | bytes 4751360
  1278.0 43.8 %all-reduce.6 = (f32[1280]{0:T(1024)S(1)}, f32[1280]{0:T(1024)S(1)}) all-reduce(f32[1280]{0:T(1024)S(1)} %get-tuple-element.16, f32[1280]{0:T(1024)S(1)} %copy-done.43), channel_id=4, replica_groups=mesh['wide'=4,'narrow'=8] {'wide','narrow'}, use_global_device_ids=true, to_apply=%region_16.17.clone | all-reduce | flops 2560 | bytes 20480
  1326.4 76.7 %reduce-scatter.38.cloned.1.call-done = f32[40,896]{1,0:T(8,128)} async-done(((f32[1280,896]{1,0:T(8,128)}), f32[40,896]{1,0:T(8,128)}) %reduce-scatter.38.cloned.1.call-update) | async-done | bytes 143376
  1403.0 146.5 %reduce-scatter.40.cloned.1.call-done = f32[40,896]{1,0:T(8,128)} async-done(((f32[1280,896]{1,0:T(8,128)}), f32[40,896]{1,0:T(8,128)}) %reduce-scatter.40.cloned.1.call-update) | async-done | bytes 143376
  1549.5 154.1 %reduce-scatter.30.cloned.1.call-done = f32[40,1280]{1,0:T(8,128)} async-done(((f32[1280,1280]{1,0:T(8,128)}), f32[40,1280]{1,0:T(8,128)}) %reduce-scatter.30.cloned.1.call-update) | async-done | bytes 204816 | tf_op jit(solution)/shard_map/reduce_scatter | solution.py:263
  1703.7 153.8 %reduce-scatter.24.cloned.1.call-done = f32[40,1280]{1,0:T(8,128)} async-done(((f32[1280,1280]{1,0:T(8,128)}), f32[40,1280]{1,0:T(8,128)}) %reduce-scatter.24.cloned.1.call-update) | async-done | bytes 204816 | tf_op jit(solution)/shard_map/reduce_scatter | solution.py:260
  1857.5 153.2 %reduce-scatter.28.cloned.1.call-done = f32[40,1280]{1,0:T(8,128)} async-done(((f32[1280,1280]{1,0:T(8,128)}), f32[40,1280]{1,0:T(8,128)}) %reduce-scatter.28.cloned.1.call-update) | async-done | bytes 204816 | tf_op jit(solution)/shard_map/reduce_scatter | solution.py:262
  2010.7 155.7 %reduce-scatter.26.cloned.1.call-done = f32[40,1280]{1,0:T(8,128)} async-done(((f32[1280,1280]{1,0:T(8,128)}), f32[40,1280]{1,0:T(8,128)}) %reduce-scatter.26.cloned.1.call-update) | async-done | bytes 204816 | tf_op jit(solution)/shard_map/reduce_scatter | solution.py:261
  (233 shorter events, 300.2 us)
Async XLA Ops:
  7.2 29.5 %copy-start = (bf16[1280,1280]{1,0:T(8,128)(2,1)S(1)}, bf16[1280,1280]{1,0:T(8,128)(2,1)}, u32[]{:S(2)}) copy-start(bf16[1280,1280]{1,0:T(8,128)(2,1)} %param.22) | copy-start | bytes 9830404
  7.2 116.0 %all-gather.5.cloned.1.call-start = ((), (), s32[]{:S(2)}) async-start(), calls=%async_computation.16 | async-start | bytes 5898240 | tf_op jit(solution)/shard_map/all_gather | solution.py:104
  36.5 175.7 %all-gather.3.cloned.1.call-start = ((), (), s32[]{:S(2)}) async-start(), calls=%async_computation.15 | async-start | bytes 5898240 | tf_op jit(solution)/shard_map/all_gather | solution.py:105
  42.8 705.5 %copy-start.41 = (pred[16,256]{1,0:T(8,128)(4,1)}, pred[16,256]{1,0:T(8,128)(4,1)S(1)}, u32[]{:S(2)}) copy-start(pred[16,256]{1,0:T(8,128)(4,1)S(1)} %bitcast_compare_fusion) | copy-start | bytes 12292
  42.9 705.5 %copy-start.35 = (s32[16,256]{1,0:T(8,128)}, s32[16,256]{1,0:T(8,128)S(1)}, u32[]{:S(2)}) copy-start(s32[16,256]{1,0:T(8,128)S(1)} %copy_bitcast_fusion) | copy-start | bytes 49156
  229.7 155.5 %all-to-all-start = ((bf16[8,2,168,1280]{3,2,1,0:T(8,128)(2,1)}), bf16[8,2,168,1280]{3,2,1,0:T(8,128)(2,1)}, u32[]{:S(2)}, u32[]{:S(2)}) async-start(bf16[8,2,168,1280]{3,2,1,0:T(8,128)(2,1)} %bitcast.166), calls=%async_computation | async-start | bytes 13762560 | tf_op jit(solution)/shard_map/all_to_all | solution.py:142
  385.3 155.0 %all-to-all-start.2 = ((bf16[8,2,168,1280]{3,2,1,0:T(8,128)(2,1)}), bf16[8,2,168,1280]{3,2,1,0:T(8,128)(2,1)}, u32[]{:S(2)}, u32[]{:S(2)}) async-start(bf16[8,2,168,1280]{3,2,1,0:T(8,128)(2,1)} %bitcast.170), calls=%async_computation.2 | async-start | bytes 13762560 | tf_op jit(solution)/shard_map/all_to_all | solution.py:167
  593.6 154.7 %all-to-all-start.3 = ((bf16[8,2,168,1280]{3,2,1,0:T(8,128)(2,1)}), bf16[8,2,168,1280]{3,2,1,0:T(8,128)(2,1)}, u32[]{:S(2)}, u32[]{:S(2)}) async-start(bf16[8,2,168,1280]{3,2,1,0:T(8,128)(2,1)} %copy.106), calls=%async_computation.3 | async-start | bytes 13762560 | tf_op jit(solution)/shard_map/all_to_all | solution.py:182
  598.9 291.3 %reduce-scatter.22.cloned.1.call-start = ((), (), s32[]{:S(2)}) async-start(), calls=%async_computation.18 | async-start | bytes 5898240 | tf_op jit(solution)/shard_map/reduce_scatter | solution.py:239
  769.0 312.5 %reduce-scatter.20.cloned.1.call-start = ((), (), s32[]{:S(2)}) async-start(), calls=%async_computation.17 | async-start | bytes 5898240 | tf_op jit(solution)/shard_map/reduce_scatter | solution.py:236
  818.0 421.9 %reduce-scatter.36.cloned.1.call-start = ((), (), s32[]{:S(2)}) async-start(), calls=%async_computation.25 | async-start | bytes 5734400 | tf_op jit(solution)/shard_map/reduce_scatter | solution.py:196
  832.4 410.3 %reduce-scatter.34.cloned.1.call-start = ((), (), s32[]{:S(2)}) async-start(), calls=%async_computation.24 | async-start | bytes 5734400 | tf_op jit(solution)/shard_map/reduce_scatter | solution.py:193
  845.7 411.1 %reduce-scatter.32.cloned.1.call-start = ((), (), s32[]{:S(2)}) async-start(), calls=%async_computation.23 | async-start | bytes 5734400 | tf_op jit(solution)/shard_map/reduce_scatter | solution.py:190
  859.6 543.4 %reduce-scatter.38.cloned.1.call-start = ((), (), s32[]{:S(2)}) async-start(), calls=%async_computation.26 | async-start | bytes 4730880
  863.9 685.6 %reduce-scatter.40.cloned.1.call-start = ((), (), s32[]{:S(2)}) async-start(), calls=%async_computation.27 | async-start | bytes 4730880
  868.2 835.4 %reduce-scatter.30.cloned.1.call-start = ((), (), s32[]{:S(2)}) async-start(), calls=%async_computation.22 | async-start | bytes 6758400 | tf_op jit(solution)/shard_map/reduce_scatter | solution.py:263
  873.5 984.0 %reduce-scatter.24.cloned.1.call-start = ((), (), s32[]{:S(2)}) async-start(), calls=%async_computation.19 | async-start | bytes 6758400 | tf_op jit(solution)/shard_map/reduce_scatter | solution.py:260
  889.9 1120.8 %reduce-scatter.28.cloned.1.call-start = ((), (), s32[]{:S(2)}) async-start(), calls=%async_computation.21 | async-start | bytes 6758400 | tf_op jit(solution)/shard_map/reduce_scatter | solution.py:262
  909.3 354.6 %all-to-all-start.1 = ((bf16[8,2,168,1280]{3,2,1,0:T(8,128)(2,1)}), bf16[8,2,168,1280]{3,2,1,0:T(8,128)(2,1)}, u32[]{:S(2)}, u32[]{:S(2)}) async-start(bf16[8,2,168,1280]{3,2,1,0:T(8,128)(2,1)} %copy.104), calls=%async_computation.1 | async-start | bytes 13762560 | tf_op jit(solution)/shard_map/all_to_all | solution.py:150
  914.5 1252.0 %reduce-scatter.26.cloned.1.call-start = ((), (), s32[]{:S(2)}) async-start(), calls=%async_computation.20 | async-start | bytes 6758400 | tf_op jit(solution)/shard_map/reduce_scatter | solution.py:261
  1209.8 20.4 collective-permute-start.2
  1216.3 13.9 collective-permute-start.1
  1220.9 9.3 collective-permute-start
  1225.2 5.1 collective-permute-start.3
  (49 other events, 363.7 us)
Sparse Core Ops, SparseCore 0:
  36.6 86.5 all-gather.4
  125.8 86.3 all-gather.2
  769.1 102.1 reduce-scatter.21
  874.8 206.7 reduce-scatter.19
  1084.0 67.0 reduce-scatter.35
  1153.7 54.0 reduce-scatter.33
  1210.3 46.4 reduce-scatter.31
  1259.7 143.2 reduce-scatter.37
  1406.0 143.4 reduce-scatter.39
  1552.4 151.2 reduce-scatter.29
  1706.6 150.7 reduce-scatter.23
  1860.3 150.3 reduce-scatter.27
  2013.7 152.7 reduce-scatter.25
where the time goes:
time: 2180 us; the launch traced here: 2170 us
  waiting for transfers between devices  1560 us (72%)
  matrix products  274 us (13%)
  blocking collectives  163 us (7%)
  other arithmetic  71.4 us (3%)
  local copies, waits for them, and re-layouts  49.9 us (2%)
  starting transfers between devices  40.6 us (2%)
    unnamed x19, waiting for transfers between devices  226 us
    reduce_scatter x1, waiting for transfers between devices, on_device(): lax.psum_scatter(key_part.astype(jnp.bfloat16), 'narrow', scatter_dimensi...  167 us
    unnamed x2, blocking collectives  163 us
    reduce_scatter x1, waiting for transfers between devices, on_device(): lax.psum_scatter(key_wgrad, ('wide', 'narrow'), scatter_dimension=0, tile...  156 us
    reduce_scatter x1, waiting for transfers between devices, on_device(): lax.psum_scatter(output_wgrad, ('wide', 'narrow'), scatter_dimension=0, t...  154 us
    reduce_scatter x1, waiting for transfers between devices, on_device(): lax.psum_scatter(query_wgrad, ('wide', 'narrow'), scatter_dimension=0, ti...  154 us
    reduce_scatter x1, waiting for transfers between devices, on_device(): lax.psum_scatter(value_wgrad, ('wide', 'narrow'), scatter_dimension=0, ti...  153 us
    all_to_all x1, waiting for transfers between devices, on_device(): lax.all_to_all(dispatched, 'narrow', split_axis=0, concat_axis=0, tiled=T...  144 us
  transfers between devices with their start and end apart: 21, of which 14 were waited for; matrix products, arithmetic and copies ran while one was open for 18% of the time, Pallas kernels for 0%

commit v1 on v0

v1 whole, which is shorter than its diff:
```python
import jax
import jax.numpy as jnp
from jax import lax
from jax.sharding import PartitionSpec as P

HEAD_DIM = 128
EPS = 1e-06
FLOAT = jnp.float32
HALF = jnp.bfloat16


def matmul(a, b, contract):
    return lax.dot_general(a, b, ((contract[:1], contract[1:]), ((), ())), preferred_element_type=FLOAT)


def rotate(values, cosine, sine):
    half = values.shape[-1] // 2
    first = values[..., :half]
    second = values[..., half:]
    return jnp.concatenate(
        [first * cosine - second * sine, second * cosine + first * sine], axis=-1
    )


def ring_order(count):
    return list(range(0, count, 2)) + list(range(count - 1, 0, -2))


def ring_steps(count):
    order = ring_order(count)
    ahead = [(order[i], order[(i + 1) % count]) for i in range(count)]
    back = [(b, a) for a, b in ahead]
    return ahead, back


def ring_gather(block):
    count = lax.axis_size("narrow")
    ahead, back = ring_steps(count)
    slots = [None] * count
    slots[0] = block
    forward = backward = block
    for step in range(1, count // 2 + 1):
        forward = lax.ppermute(forward, "narrow", ahead)
        slots[count - step] = forward
        if step < count // 2:
            backward = lax.ppermute(backward, "narrow", back)
            slots[step] = backward
    return slots


def ring_scatter(parts):
    count = lax.axis_size("narrow")
    ahead, back = ring_steps(count)
    half = count // 2
    forward = parts[half].astype(HALF)
    backward = parts[half + 1].astype(HALF)
    for step in range(1, half + 1):
        forward = lax.ppermute(forward, "narrow", ahead).astype(FLOAT)
        if step < half:
            forward = (forward + parts[half - step].astype(FLOAT)).astype(HALF)
            backward = lax.ppermute(backward, "narrow", back).astype(FLOAT)
            if step < half - 1:
                backward = (backward + parts[half + 1 + step].astype(FLOAT)).astype(HALF)
    return parts[0].astype(FLOAT) + forward + backward


def wide_scatter(chunks):
    count = lax.axis_size("wide")
    place = lax.axis_index("wide")
    bit = 1
    while bit < count:
        pairs = chunks.reshape((chunks.shape[0] // 2, 2) + chunks.shape[1:])
        mine = (place // bit) % 2
        kept = lax.dynamic_index_in_dim(pairs, mine, axis=1, keepdims=False)
        sent = lax.dynamic_index_in_dim(pairs, 1 - mine, axis=1, keepdims=False)
        got = lax.ppermute(sent, "wide", [(i, i ^ bit) for i in range(count)])
        chunks = (kept.astype(FLOAT) + got.astype(FLOAT)).astype(HALF)
        bit *= 2
    return chunks[0]


def norm_back(grad_out, normed, inv_scale, gain):
    scaled = grad_out * gain
    return inv_scale * (scaled - normed * jnp.mean(scaled * normed, axis=1, keepdims=True))


def causal_attention(queries, keys, values, query_pos, key_pos):
    scores = jnp.einsum("qd,kd->qk", queries, keys, preferred_element_type=FLOAT)
    scores = jnp.where(
        query_pos[:, None] >= key_pos[None, :], scores * HEAD_DIM**-0.5, -1e30
    )
    peak = jnp.max(scores, axis=1, keepdims=True)
    shifted = jnp.exp(scores - peak)
    total = jnp.sum(shifted, axis=1, keepdims=True)
    low = (shifted / total).astype(HALF)
    out = matmul(low, values, (1, 0)).astype(HALF)
    return out, peak + jnp.log(total)


def causal_back(queries, keys, values, query_pos, key_pos, log_total, out_grad):
    scores = jnp.einsum("qd,kd->qk", queries, keys, preferred_element_type=FLOAT)
    scores = jnp.where(
        query_pos[:, None] >= key_pos[None, :], scores * HEAD_DIM**-0.5, -1e30
    )
    probs = jnp.exp(scores - log_total)
    prob_grad = matmul(out_grad, values, (1, 1))
    score_grad = (
        probs * (prob_grad - jnp.sum(prob_grad * probs, axis=1, keepdims=True))
    ).astype(HALF)
    value_grad = matmul(probs.astype(HALF), out_grad, (0, 0))
    query_grad = matmul(score_grad, keys, (1, 0)) * HEAD_DIM**-0.5
    key_grad = matmul(score_grad, queries, (0, 0)) * HEAD_DIM**-0.5
    return query_grad, key_grad, value_grad


def on_device(
    tokens,
    routes,
    gates,
    attn_gain,
    query_weight,
    key_weight,
    value_weight,
    output_weight,
    ffn_gain,
    shared_gate,
    shared_up,
    shared_down,
    expert_gate,
    expert_up,
    expert_down,
    cotangent,
):
    length, width = tokens.shape
    hidden_units = expert_gate.shape[2]
    local_experts = expert_gate.shape[0]
    group = lax.axis_size("narrow")
    copies = lax.axis_size("wide")
    place = lax.axis_index("narrow")
    experts = group * local_experts
    seq_len = length * group
    own_heads = group * HEAD_DIM
    spare_heads = width // HEAD_DIM - group

    order = jnp.asarray(ring_order(group), dtype=jnp.int32)
    ring_place = jnp.where(place % 2 == 0, place // 2, group - 1 - place // 2)
    slot_block = order[(ring_place + jnp.arange(group, dtype=jnp.int32)) % group]
    blocks = jnp.arange(group, dtype=jnp.int32)
    block_ring = jnp.where(blocks % 2 == 0, blocks // 2, group - 1 - blocks // 2)
    block_slot = (block_ring - ring_place) % group

    def by_slot(array):
        return jnp.take(array, slot_block, axis=0)

    def by_block(array):
        return jnp.take(array, block_slot, axis=0)

    inputs = tokens.astype(FLOAT)
    inv_one = lax.rsqrt(jnp.mean(inputs * inputs, axis=1, keepdims=True) + EPS)
    normed_one = inputs * inv_one
    attn_in = (normed_one * attn_gain).astype(HALF)
    attn_slots = ring_gather(attn_in)
    cot_slots = ring_gather(cotangent)

    expert_ids = jnp.arange(experts, dtype=jnp.int32)
    picked = routes[:, :, None] == expert_ids[None, None, :]
    token_gate = jnp.sum(jnp.where(picked, gates[:, :, None], 0.0), axis=1)
    all_gates = lax.all_gather(token_gate.T, "narrow", axis=0)
    own_gates = lax.dynamic_slice_in_dim(all_gates, place * local_experts, local_experts, axis=1)
    own_gates = by_slot(own_gates)

    def head_columns(weight):
        return lax.dynamic_slice_in_dim(weight, place * HEAD_DIM, HEAD_DIM, axis=1)

    own_weights = jnp.concatenate(
        [head_columns(query_weight), head_columns(key_weight), head_columns(value_weight)], axis=1
    )
    spare_weights = jnp.concatenate([key_weight[:, own_heads:], value_weight[:, own_heads:]], axis=1)
    spare_query_weight = query_weight[:, own_heads:]
    attn_all = jnp.concatenate(attn_slots, axis=0)
    positions = (
        slot_block[:, None] * length + jnp.arange(length, dtype=jnp.int32)[None, :]
    ).reshape(seq_len)
    half = HEAD_DIM // 2
    freq = 10000.0 ** (-(jnp.arange(half, dtype=FLOAT) * 2.0) / HEAD_DIM)
    angles = positions.astype(FLOAT)[:, None] * freq[None, :]
    cosine, sine = jnp.cos(angles), jnp.sin(angles)
    own_lin = matmul(attn_all, own_weights, (1, 0))
    spare_lin = matmul(attn_all, spare_weights, (1, 0))
    spare_query_lin = matmul(attn_in, spare_query_weight, (1, 0))

    heads = []
    own_q = rotate(own_lin[:, :HEAD_DIM], cosine, sine).astype(HALF)
    own_k = rotate(own_lin[:, HEAD_DIM : 2 * HEAD_DIM], cosine, sine).astype(HALF)
    own_v = own_lin[:, 2 * HEAD_DIM :].astype(HALF)
    heads.append((own_q, own_k, own_v, positions))
    for head in range(spare_heads):
        columns = slice(head * HEAD_DIM, (head + 1) * HEAD_DIM)
        value_columns = slice(
            (spare_heads + head) * HEAD_DIM, (spare_heads + head + 1) * HEAD_DIM
        )
        q = rotate(spare_query_lin[:, columns], cosine[:length], sine[:length]).astype(HALF)
        k = rotate(spare_lin[:, columns], cosine, sine).astype(HALF)
        v = spare_lin[:, value_columns].astype(HALF)
        heads.append((q, k, v, positions[:length]))
    outs = [causal_attention(q, k, v, pos, positions) for q, k, v, pos in heads]

    own_out = by_block(outs[0][0].reshape(group, length, HEAD_DIM))
    returned = lax.all_to_all(own_out, "narrow", split_axis=0, concat_axis=0, tiled=True)
    attended = jnp.concatenate(
        [returned.transpose(1, 0, 2).reshape(length, own_heads)] + [out for out, _ in outs[1:]],
        axis=1,
    )
    hidden = inputs + matmul(attended, output_weight, (1, 0))
    inv_two = lax.rsqrt(jnp.mean(hidden * hidden, axis=1, keepdims=True) + EPS)
    normed_two = hidden * inv_two
    ffn_in = (normed_two * ffn_gain).astype(HALF)

    share = hidden_units // (copies * group)
    taken = copies * share
    padded = -(-taken // 128) * 128
    column = jnp.arange(padded, dtype=jnp.int32)
    unit = jnp.where(
        column < taken, ((column // share) * group + place) * share + column % share, -1
    )
    choice = (jnp.arange(hidden_units, dtype=jnp.int32)[:, None] == unit[None, :]).astype(HALF)
    share_gate = matmul(shared_gate, choice, (1, 0)).astype(HALF)
    share_up = matmul(shared_up, choice, (1, 0)).astype(HALF)
    share_down = matmul(choice, shared_down, (0, 0)).astype(HALF)
    gate_weight = jnp.concatenate([expert_gate[e] for e in range(local_experts)] + [share_gate], axis=1)
    up_weight = jnp.concatenate([expert_up[e] for e in range(local_experts)] + [share_up], axis=1)
    down_weight = jnp.concatenate([expert_down[e] for e in range(local_experts)] + [share_down], axis=0)

    ffn_slots = ring_gather(ffn_in)
    rows = jnp.concatenate(ffn_slots, axis=0)
    cots = jnp.concatenate(cot_slots, axis=0)
    gate_columns = own_gates.transpose(0, 2, 1).reshape(seq_len, local_experts)
    scale = jnp.concatenate(
        [
            jnp.broadcast_to(gate_columns[:, e : e + 1], (seq_len, hidden_units))
            for e in range(local_experts)
        ]
        + [jnp.ones((seq_len, padded), FLOAT)],
        axis=1,
    )
    gate_pre = matmul(rows, gate_weight, (1, 0))
    up_pre = matmul(rows, up_weight, (1, 0))
    sigma = jax.nn.sigmoid(gate_pre)
    active = gate_pre * sigma
    slope = sigma * (1.0 + gate_pre * (1.0 - sigma))
    gated_inner = (scale * active * up_pre).astype(HALF)
    out_part = matmul(gated_inner, down_weight, (1, 0)).astype(HALF)
    inner_grad = matmul(cots, down_weight, (1, 1)) * scale
    gate_grad = (inner_grad * up_pre * slope).astype(HALF)
    up_grad = (inner_grad * active).astype(HALF)
    row_part = (
        matmul(gate_grad, gate_weight, (1, 1)) + matmul(up_grad, up_weight, (1, 1))
    ).astype(HALF)
    row_part = row_part.reshape(group, length, width)
    ffn_in_grad = ring_scatter([row_part[j] for j in range(group)])
    out_part = out_part.reshape(group, length, width)

    down_wgrad = matmul(gated_inner, cots, (0, 0)).astype(HALF)
    gate_wgrad = matmul(rows, gate_grad, (0, 0)).astype(HALF)
    up_wgrad = matmul(rows, up_grad, (0, 0)).astype(HALF)
    routed = local_experts * hidden_units

    def expert_sum(grad):
        return wide_scatter(
            grad.reshape(copies, width // copies, grad.shape[1])[:, :, :routed]
        ).reshape(width // copies, local_experts, hidden_units)

    expert_gate_grad = expert_sum(gate_wgrad).transpose(1, 0, 2).astype(FLOAT)
    expert_up_grad = expert_sum(up_wgrad).transpose(1, 0, 2).astype(FLOAT)
    expert_down_grad = wide_scatter(
        down_wgrad[:routed]
        .reshape(local_experts, copies, hidden_units // copies, width)
        .transpose(1, 0, 2, 3)
    ).astype(FLOAT)
    shared_down_grad = wide_scatter(
        down_wgrad[routed : routed + taken].reshape(copies, share, width)
    ).astype(FLOAT)

    hidden_grad = cotangent.astype(FLOAT) + norm_back(ffn_in_grad, normed_two, inv_two, ffn_gain)
    branch_grad = hidden_grad.astype(HALF)
    attended_grad = matmul(branch_grad, output_weight, (1, 1)).astype(HALF)
    own_out_grad = lax.all_to_all(
        attended_grad[:, :own_heads].reshape(length, group, HEAD_DIM).transpose(1, 0, 2),
        "narrow",
        split_axis=0,
        concat_axis=0,
        tiled=True,
    )
    own_out_grad = by_slot(own_out_grad).reshape(seq_len, HEAD_DIM)
    out_grads = [own_out_grad] + [
        attended_grad[:, own_heads + h * HEAD_DIM : own_heads + (h + 1) * HEAD_DIM]
        for h in range(spare_heads)
    ]
    mixed = (hidden + ring_scatter([out_part[j] for j in range(group)])).astype(HALF)
    grads = [
        causal_back(q, k, v, pos, positions, log_total, out_grad)
        for (q, k, v, pos), (_, log_total), out_grad in zip(heads, outs, out_grads)
    ]
    own_grad = jnp.concatenate(
        [
            rotate(grads[0][0], cosine, -sine).astype(HALF),
            rotate(grads[0][1], cosine, -sine).astype(HALF),
            grads[0][2].astype(HALF),
        ],
        axis=1,
    )
    spare_grad = jnp.concatenate(
        [rotate(g[1], cosine, -sine).astype(HALF) for g in grads[1:]]
        + [g[2].astype(HALF) for g in grads[1:]],
        axis=1,
    )
    spare_query_grad = jnp.concatenate(
        [rotate(g[0], cosine[:length], -sine[:length]).astype(HALF) for g in grads[1:]], axis=1
    )
    attn_part = (
        matmul(own_grad, own_weights, (1, 1)) + matmul(spare_grad, spare_weights, (1, 1))
    ).astype(HALF)
    attn_part = attn_part.reshape(group, length, width)
    attn_in_grad = ring_scatter([attn_part[j] for j in range(group)]) + matmul(
        spare_query_grad, spare_query_weight, (1, 1)
    )
    tokens_grad = hidden_grad + norm_back(attn_in_grad, normed_one, inv_one, attn_gain)

    def spread(grad):
        return wide_scatter(grad.astype(HALF).reshape(copies, width // copies, grad.shape[1]))

    def exchange(part):
        return lax.all_to_all(
            part.reshape(group, part.shape[0] // group, part.shape[1]),
            "narrow",
            split_axis=0,
            concat_axis=0,
            tiled=True,
        ).astype(FLOAT)

    gain_terms = (ffn_in_grad * normed_two).astype(HALF)
    gain_column = matmul(gain_terms, jnp.ones((length, 128), HALF), (0, 0))
    out_wgrad = matmul(attended, branch_grad, (0, 0))
    first = exchange(
        jnp.concatenate(
            [
                spread(jnp.concatenate([out_wgrad, gain_column], axis=1)),
                spread(
                    jnp.concatenate(
                        [
                            gate_wgrad[:, routed : routed + taken],
                            up_wgrad[:, routed : routed + taken],
                        ],
                        axis=1,
                    )
                ),
            ],
            axis=1,
        )
    )
    summed = jnp.sum(first[:, :, : width + 128], axis=0)
    output_weight_grad = summed[:, :width]
    ffn_gain_grad = summed[:, width]

    def shared_columns(part):
        own = part.shape[1]
        return part.reshape(group, own, copies, share).transpose(1, 2, 0, 3).reshape(own, hidden_units)

    shared_gate_grad = shared_columns(first[:, :, width + 128 : width + 128 + taken])
    shared_up_grad = shared_columns(first[:, :, width + 128 + taken :])

    own_wgrad = matmul(attn_all, own_grad, (0, 0))
    spare_wgrad = jnp.concatenate(
        [matmul(attn_in, spare_query_grad, (0, 0)), matmul(attn_all, spare_grad, (0, 0))], axis=1
    )
    second = exchange(spread(jnp.concatenate([own_wgrad, spare_wgrad], axis=1)))
    spare_sum = jnp.sum(second[:, :, 3 * HEAD_DIM :], axis=0)
    spare_width = spare_heads * HEAD_DIM

    def head_grad(index):
        own = second[:, :, index * HEAD_DIM : (index + 1) * HEAD_DIM]
        own = own.transpose(1, 0, 2).reshape(own.shape[1], own_heads)
        return jnp.concatenate(
            [own, spare_sum[:, index * spare_width : (index + 1) * spare_width]], axis=1
        )

    query_weight_grad = head_grad(0)
    key_weight_grad = head_grad(1)
    value_weight_grad = head_grad(2)
    own_rows = width // (copies * group)
    first_row = (lax.axis_index("wide") * group + place) * own_rows

    def own_part(array):
        return lax.dynamic_slice_in_dim(array, first_row, own_rows, axis=0).astype(FLOAT)

    attn_gain_grad = (
        jnp.sum(
            query_weight_grad * own_part(query_weight)
            + key_weight_grad * own_part(key_weight)
            + value_weight_grad * own_part(value_weight),
            axis=1,
        )
        / own_part(attn_gain)
    )
    return (
        mixed,
        tokens_grad,
        attn_gain_grad,
        query_weight_grad,
        key_weight_grad,
        value_weight_grad,
        output_weight_grad,
        ffn_gain_grad,
        shared_gate_grad,
        shared_up_grad,
        shared_down_grad,
        expert_gate_grad,
        expert_up_grad,
        expert_down_grad,
    )


def solution(mesh):
    rows = P(("wide", "narrow"), None)
    vector = P(("wide", "narrow"))
    held = P("narrow", None, None)
    in_specs = (rows, rows, rows) + (P(),) * 9 + (held, held, held, rows)
    out_specs = (rows, rows, vector) + (rows,) * 4 + (vector,) + (rows,) * 3 + (P("narrow", "wide", None),) * 3
    return jax.shard_map(
        on_device, mesh=mesh, in_specs=in_specs, out_specs=out_specs, check_vma=False
    )
```

time: 2180 us -> 843 us (0.39)
  waiting for transfers between devices: 1560 us -> 198 us
  blocking collectives: 163 us -> 46.2 us
  local copies, waits for them, and re-layouts: 49.9 us -> 143 us
  starting transfers between devices: 40.6 us -> 82.2 us
  other arithmetic: 71.4 us -> 101 us
    reduce_scatter x9 -> x0, waiting for transfers between devices: 795 us -> none  [the longest x1 167 us: on_device(): lax.psum_scatter(key_part.astype(jnp.bfloat16), 'narrow', scatter_dimensi...]
    all_to_all x4, waiting for transfers between devices: 406 us -> 15.3 us  [the longest x2 10.9 us: exchange(): lax.all_to_all(part.reshape(group, part.shape[0] // group, part.shape[1])...]
    unnamed x19 -> x0, waiting for transfers between devices: 226 us -> none
    ppermute x0 -> x56, waiting for transfers between devices: none -> 183 us  [the longest x12 97.9 us: ring_scatter(): forward = lax.ppermute(forward, 'narrow', ahead).astype(FLOAT)]
    unnamed x2 -> x0, blocking collectives: 163 us -> none
    all_gather x2 -> x0, waiting for transfers between devices: 132 us -> none  [the longest x1 79.1 us: on_device(): lax.all_gather(key_rot, 'narrow', axis=0, tiled=True)]
    ppermute x0 -> x56, starting transfers between devices: none -> 57.4 us  [the longest x12 16.9 us: ring_gather(): forward = lax.ppermute(forward, 'narrow', ahead)]
    all_gather x0 -> x1, blocking collectives: none -> 46.2 us  [on_device(): all_gates = lax.all_gather(token_gate.T, 'narrow', axis=0)]
  transfers between devices with their start and end apart: 21 -> 60, of which waited for: 14 -> 28; matrix products, arithmetic and copies ran while one was open for 18% -> 40% of each run, Pallas kernels for 0% -> 0%
where the time goes in v1:
time: 843 us; the launch traced here: 829 us
  matrix products  255 us (30%)
  waiting for transfers between devices  198 us (23%)
  local copies, waits for them, and re-layouts  143 us (17%)
  other arithmetic  101 us (12%)
  starting transfers between devices  82.2 us (10%)
  blocking collectives  46.2 us (5%)
    dot_general x40, matrix products, matmul(): lax.dot_general(a, b, ((contract[:1], contract[1:]), ((), ())), preferred...  246 us
    ppermute x12, waiting for transfers between devices, ring_scatter(): forward = lax.ppermute(forward, 'narrow', ahead).astype(FLOAT)  97.9 us
    ppermute x12, waiting for transfers between devices, ring_gather(): forward = lax.ppermute(forward, 'narrow', ahead)  62.8 us
    unnamed x289, local copies, waits for them, and re-layouts  48.4 us
    all_gather x1, blocking collectives, on_device(): all_gates = lax.all_gather(token_gate.T, 'narrow', axis=0)  46.2 us
  transfers between devices with their start and end apart: 60, of which 28 were waited for; matrix products, arithmetic and copies ran while one was open for 40% of the time, Pallas kernels for 0%

profile of v1, /device:TPU:4, one launch (start us, length us, event | category | flops | bytes accessed | tf_op | source)
XLA Modules:
  0.0 828.8 jit_solution(18134707193998101021)
XLA Ops:
  11.7 46.2 %all-gather = f32[128,256]{1,0:T(8,128)} all-gather(f32[16,256]{1,0:T(8,128)S(1)} %bitcast.218), channel_id=2, replica_groups=mesh['wide'=4,'narrow'=8] {'narrow'}, dimensions={0}, use_global_device_ids=true | all-gather | bytes 147456 | tf_op jit(solution)/shard_map/all_gather | solution.py:168
  146.4 10.0 %collective-permute-done.6 = bf16[256,1280]{1,0:T(8,128)(2,1)S(1)} collective-permute-done((bf16[256,1280]{1,0:T(8,128)(2,1)}, bf16[256,1280]{1,0:T(8,128)(2,1)S(1)}, u32[]{:S(2)}, u32[]{:S(2)}) %collective-permute-start.6) | collective-permute-done | bytes 655392 | tf_op jit(solution)/shard_map/ppermute | solution.py:43
  192.4 9.5 %fusion.26 = bf16[2048,128]{1,0:T(8,128)(2,1)} fusion(f32[2048,2048]{0,1:T(8,128)} %get-tuple-element.176, f32[2048]{0:T(1024)S(1)} %fusion.5, f32[2048]{0:T(1024)S(1)} %get-tuple-element.175, f32[2048,384]{0,1:T(8,128)S(1)} %fusion.138), kind=kOutput, calls=%fused_computation.71 | convolution fusion | flops 1086586880 | bytes 17842176 | tf_op jit(solution)/shard_map/dot_general | solution.py:13
  285.1 13.9 %fusion.30 = f32[2048,1920]{1,0:T(8,128)} fusion(bf16[2048,1280]{1,0:T(8,128)(2,1)S(1)} %constant_dynamic-update-slice_fusion.8, bf16[1280,128]{1,0:T(8,128)(2,1)S(1)} %copy-done.64, bf16[1280,896]{1,0:T(8,128)(2,1)S(1)} %copy-done.33, bf16[1280,896]{1,0:T(8,128)(2,1)S(1)} %copy-done.32), kind=kOutput, calls=%fused_computation.97 | convolution fusion | flops 10081075200 | bytes 25886720 | tf_op jit(solution)/shard_map/dot_general | solution.py:13
  299.0 13.7 %fusion.32 = f32[2048,1920]{1,0:T(8,128)} fusion(bf16[2048,1280]{1,0:T(8,128)(2,1)S(1)} %constant_dynamic-update-slice_fusion.8, bf16[1280,128]{1,0:T(8,128)(2,1)S(1)} %copy-done.66, bf16[1280,896]{1,0:T(8,128)(2,1)S(1)} %copy-done.36, bf16[1280,896]{1,0:T(8,128)(2,1)S(1)} %copy-done.34), kind=kOutput, calls=%fused_computation.99 | convolution fusion | flops 10081075200 | bytes 25886720 | tf_op jit(solution)/shard_map/dot_general | solution.py:13
  319.8 32.6 %multiply_convert_fusion.1 = (bf16[2048,1920]{1,0:T(8,128)(2,1)}, bf16[2048,1920]{1,0:T(8,128)(2,1)}, bf16[2048,1920]{1,0:T(8,128)(2,1)}) fusion(f32[2048,896]{1,0:T(8,128)} %broadcast_in_dim.105, f32[2048,896]{1,0:T(8,128)} %broadcast_in_dim.64, f32[1920]{0:T(1024)S(1)} %copy-done.116, f32[2048,1920]{1,0:T(8,128)} %fusion.32, f32[2048,1920]{1,0:T(8,128)} %fusion.30, ...), kind=kOutput, calls=%fused_computation.15 | convolution fusion | flops 10155786240 | bytes 79896064 | tf_op jit(solution)/shard_map/dot_general | solution.py:13
  352.4 14.2 %convolution_convert_fusion.3 = bf16[1920,1280]{1,0:T(8,128)(2,1)S(1)} fusion(bf16[2048,1920]{1,0:T(8,128)(2,1)} %get-tuple-element.95, bf16[2048,1280]{1,0:T(8,128)(2,1)} %constant_dynamic-update-slice_fusion.16), kind=kOutput, calls=%fused_computation.29 | convolution fusion | flops 10068787200 | bytes 18022400 | tf_op jit(solution)/shard_map/dot_general | solution.py:13
  370.8 15.5 %convolution_convert_fusion.4 = bf16[2048,1280]{1,0:T(8,128)(2,1)} fusion(bf16[2048,1920]{1,0:T(8,128)(2,1)} %get-tuple-element.95, bf16[128,1280]{1,0:T(8,128)(2,1)S(1)} %copy-done.68, bf16[896,1280]{1,0:T(8,128)(2,1)S(1)} %copy-done.39, bf16[896,1280]{1,0:T(8,128)(2,1)S(1)} %copy-done.38), kind=kOutput, calls=%fused_computation.30 | convolution fusion | flops 10083696640 | bytes 18022400 | tf_op jit(solution)/shard_map/dot_general | solution.py:13
  386.4 15.6 %convolution_convert_fusion.1 = bf16[1280,1920]{1,0:T(8,128)(2,1)} fusion(bf16[2048,1280]{1,0:T(8,128)(2,1)S(1)} %bitcast.217, bf16[2048,1920]{1,0:T(8,128)(2,1)} %get-tuple-element.94), kind=kOutput, calls=%fused_computation.27 | convolution fusion | flops 10068787200 | bytes 18022400 | tf_op jit(solution)/shard_map/dot_general | solution.py:13
  402.0 15.3 %fusion.31 = f32[2048,1280]{1,0:T(8,128)} fusion(bf16[2048,1920]{1,0:T(8,128)(2,1)} %get-tuple-element.94, bf16[1280,128]{1,0:T(8,128)(2,1)S(1)} %copy-done.67, bf16[1280,896]{1,0:T(8,128)(2,1)S(1)} %copy-done.37, bf16[1280,896]{1,0:T(8,128)(2,1)S(1)} %copy-done.35), kind=kOutput, calls=%fused_computation.98 | convolution fusion | flops 10081075200 | bytes 23265280 | tf_op jit(solution)/shard_map/dot_general | solution.py:13
  430.8 16.6 %convolution_convert_fusion = bf16[1280,1920]{1,0:T(8,128)(2,1)} fusion(bf16[2048,1280]{1,0:T(8,128)(2,1)} %copy-done.94, bf16[2048,1920]{1,0:T(8,128)(2,1)} %get-tuple-element.93), kind=kOutput, calls=%fused_computation.26 | convolution fusion | flops 10068787200 | bytes 18022400 | tf_op jit(solution)/shard_map/dot_general | solution.py:13
  447.4 16.3 %add_convert_fusion.1 = bf16[2048,1280]{1,0:T(8,128)(2,1)S(1)} fusion(f32[2048,1280]{1,0:T(8,128)} %fusion.31, bf16[2048,1920]{1,0:T(8,128)(2,1)} %get-tuple-element.93, bf16[1280,128]{1,0:T(8,128)(2,1)S(1)} %copy-done.65, bf16[1280,896]{1,0:T(8,128)(2,1)} %get-tuple-element.121, bf16[1280,896]{1,0:T(8,128)(2,1)} %get-tuple-element.120), kind=kOutput, calls=%fused_computation.22 | convolution fusion | flops 10086318080 | bytes 28508160 | tf_op jit(solution)/shard_map/dot_general | solution.py:13
  480.0 13.2 %collective-permute-done.28 = bf16[256,1280]{1,0:T(8,128)(2,1)S(1)} collective-permute-done((bf16[256,1280]{1,0:T(8,128)(2,1)S(1)}, bf16[256,1280]{1,0:T(8,128)(2,1)S(1)}, u32[]{:S(2)}, u32[]{:S(2)}) %collective-permute-start.28) | collective-permute-done | bytes 655392 | tf_op jit(solution)/shard_map/ppermute | solution.py:58
  493.8 13.5 %collective-permute-done.15 = bf16[256,1280]{1,0:T(8,128)(2,1)S(1)} collective-permute-done((bf16[256,1280]{1,0:T(8,128)(2,1)S(1)}, bf16[256,1280]{1,0:T(8,128)(2,1)S(1)}, u32[]{:S(2)}, u32[]{:S(2)}) %collective-permute-start.15) | collective-permute-done | bytes 655392 | tf_op jit(solution)/shard_map/ppermute | solution.py:58
  510.7 10.7 %collective-permute-done.29 = bf16[256,1280]{1,0:T(8,128)(2,1)S(1)} collective-permute-done((bf16[256,1280]{1,0:T(8,128)(2,1)S(1)}, bf16[256,1280]{1,0:T(8,128)(2,1)S(1)}, u32[]{:S(2)}, u32[]{:S(2)}) %collective-permute-start.29) | collective-permute-done | bytes 655392 | tf_op jit(solution)/shard_map/ppermute | solution.py:58
  523.8 11.6 %collective-permute-done.16 = bf16[256,1280]{1,0:T(8,128)(2,1)S(1)} collective-permute-done((bf16[256,1280]{1,0:T(8,128)(2,1)S(1)}, bf16[256,1280]{1,0:T(8,128)(2,1)S(1)}, u32[]{:S(2)}, u32[]{:S(2)}) %collective-permute-start.16) | collective-permute-done | bytes 655392 | tf_op jit(solution)/shard_map/ppermute | solution.py:58
  538.6 9.3 %collective-permute-done.30 = bf16[256,1280]{1,0:T(8,128)(2,1)S(1)} collective-permute-done((bf16[256,1280]{1,0:T(8,128)(2,1)S(1)}, bf16[256,1280]{1,0:T(8,128)(2,1)S(1)}, u32[]{:S(2)}, u32[]{:S(2)}) %collective-permute-start.30) | collective-permute-done | bytes 655392 | tf_op jit(solution)/shard_map/ppermute | solution.py:58
  624.3 10.2 %collective-permute-done.51 = bf16[1,320,1792]{2,1,0:T(8,128)(2,1)} collective-permute-done((bf16[1,320,1792]{2,1,0:T(8,128)(2,1)}, bf16[1,320,1792]{2,1,0:T(8,128)(2,1)}, u32[]{:S(2)}, u32[]{:S(2)}) %collective-permute-start.51) | collective-permute-done | bytes 1146912 | tf_op jit(solution)/shard_map/ppermute | solution.py:76
  647.9 11.0 %multiply_reduce_fusion = (f32[2048]{0:T(1024)S(1)}, f32[2048,2048]{0,1:T(8,128)}) fusion(f32[2048,2048]{0,1:T(8,128)} %get-tuple-element.176, f32[2048]{0:T(1024)S(1)} %copy-done.63, bf16[2048,128]{1,0:T(8,128)(2,1)S(1)} %bitcast.186, f32[2048,384]{0,1:T(8,128)} %copy-done.27), kind=kOutput, calls=%fused_computation.5 | convolution fusion | flops 1086322688 | bytes 34619392 | tf_op jit(solution)/shard_map/dot_general | solution.py:13
  659.0 12.7 %multiply_convert_fusion = bf16[2048,2048]{0,1:T(8,128)(2,1)S(1)} fusion(f32[2048,2048]{0,1:T(8,128)} %get-tuple-element.184, f32[2048,2048]{0,1:T(8,128)} %get-tuple-element.176, f32[2048]{0:T(1024)S(1)} %get-tuple-element.183, f32[2048]{0:T(1024)S(1)} %copy-done.63), kind=kLoop, calls=%fused_computation.4 | loop fusion | flops 16777216 | bytes 41959424 | tf_op jit(solution)/shard_map/convert_element_type | solution.py:109
  694.3 8.7 %fusion.21 = bf16[2048,384]{0,1:T(8,128)(2,1)S(1)} fusion(bf16[2048,384]{0,1:T(8,128)(2,1)S(1)} %get-tuple-element.151, bf16[2048,128]{1,0:T(8,128)(2,1)S(1)} %bitcast.187, f32[2048,2048]{0,1:T(8,128)} %get-tuple-element.176, f32[2048]{0:T(1024)S(1)} %copy-done.63), kind=kOutput, calls=%fused_computation.63 | convolution fusion | flops 1082392576 | bytes 17833984 | tf_op jit(solution)/shard_map/dot_general | solution.py:13
  751.8 11.7 %collective-permute-done.37 = bf16[256,1280]{1,0:T(8,128)(2,1)} collective-permute-done((bf16[256,1280]{1,0:T(8,128)(2,1)}, bf16[256,1280]{1,0:T(8,128)(2,1)}, u32[]{:S(2)}, u32[]{:S(2)}) %collective-permute-start.37) | collective-permute-done | bytes 655392 | tf_op jit(solution)/shard_map/ppermute | solution.py:58
  784.1 8.4 %all-to-all-start.3 = ((bf16[8,40,1632]{2,1,0:T(8,128)(2,1)}), bf16[8,40,1632]{2,1,0:T(8,128)(2,1)}, u32[]{:S(2)}, u32[]{:S(2)}) async-start(bf16[8,40,1632]{2,1,0:T(8,128)(2,1)} %pad_maximum_fusion.11), calls=%async_computation.3 | async-start | bytes 2129920 | tf_op jit(solution)/shard_map/all_to_all | solution.py:333
  801.2 10.9 %all-to-all-done.3 = bf16[8,40,1632]{2,1,0:T(8,128)(2,1)} async-done(((bf16[8,40,1632]{2,1,0:T(8,128)(2,1)}), bf16[8,40,1632]{2,1,0:T(8,128)(2,1)}, u32[]{:S(2)}, u32[]{:S(2)}) %all-to-all-start.3) | async-done | bytes 1044512 | tf_op jit(solution)/shard_map/all_to_all | solution.py:333
  (579 shorter events, 474.7 us)
Async XLA Ops:
  0.7 103.3 %collective-permute-start.21 = (bf16[256,1280]{1,0:T(8,128)(2,1)}, bf16[256,1280]{1,0:T(8,128)(2,1)}, u32[]{:S(2)}, u32[]{:S(2)}) collective-permute-start(bf16[256,1280]{1,0:T(8,128)(2,1)} %param.34), channel_id=1, source_target_pairs={{2,0},{4,2},{6,4},{7,6},{5,7},{3,5},{1,3},{0,1},{10,8},{12,10},{14... | collective-permute-start | bytes 1966088 | tf_op jit(solution)/shard_map/ppermute | solution.py:46
  2.3 86.8 %collective-permute-start.24 = (bf16[256,1280]{1,0:T(8,128)(2,1)}, bf16[256,1280]{1,0:T(8,128)(2,1)}, u32[]{:S(2)}, u32[]{:S(2)}) collective-permute-start(bf16[256,1280]{1,0:T(8,128)(2,1)} %param.34), channel_id=1, source_target_pairs={{0,2},{2,4},{4,6},{6,7},{7,5},{5,3},{3,1},{1,0},{8,10},{10,12},{12... | collective-permute-start | bytes 1966088 | tf_op jit(solution)/shard_map/ppermute | solution.py:43
  7.7 73.6 %collective-permute-start.3 = (bf16[256,1280]{1,0:T(8,128)(2,1)}, bf16[256,1280]{1,0:T(8,128)(2,1)}, u32[]{:S(2)}, u32[]{:S(2)}) collective-permute-start(bf16[256,1280]{1,0:T(8,128)(2,1)} %get-tuple-element.92), channel_id=1, source_target_pairs={{0,2},{2,4},{4,6},{6,7},{7,5},{5,3},{3,1},{1,0},{8,10},{10,12},{12... | collective-permute-start | bytes 1966088 | tf_op jit(solution)/shard_map/ppermute | solution.py:43
  7.9 81.2 %collective-permute-start = (bf16[256,1280]{1,0:T(8,128)(2,1)}, bf16[256,1280]{1,0:T(8,128)(2,1)}, u32[]{:S(2)}, u32[]{:S(2)}) collective-permute-start(bf16[256,1280]{1,0:T(8,128)(2,1)} %get-tuple-element.92), channel_id=1, source_target_pairs={{2,0},{4,2},{6,4},{7,6},{5,7},{3,5},{1,3},{0,1},{10,8},{12,10},{14... | collective-permute-start | bytes 1966088 | tf_op jit(solution)/shard_map/ppermute | solution.py:46
  89.1 29.6 %collective-permute-start.1 = (bf16[256,1280]{1,0:T(8,128)(2,1)}, bf16[256,1280]{1,0:T(8,128)(2,1)}, u32[]{:S(2)}, u32[]{:S(2)}) collective-permute-start(bf16[256,1280]{1,0:T(8,128)(2,1)} %collective-permute-done), channel_id=1, source_target_pairs={{2,0},{4,2},{6,4},{7,6},{5,7},{3,5},{1,3},{0,1},{10,8},{12,10},{14... | collective-permute-start | bytes 1966088 | tf_op jit(solution)/shard_map/ppermute | solution.py:46
  100.9 28.1 %collective-permute-start.5 = (bf16[256,1280]{1,0:T(8,128)(2,1)}, bf16[256,1280]{1,0:T(8,128)(2,1)}, u32[]{:S(2)}, u32[]{:S(2)}) collective-permute-start(bf16[256,1280]{1,0:T(8,128)(2,1)} %collective-permute-done.4), channel_id=1, source_target_pairs={{0,2},{2,4},{4,6},{6,7},{7,5},{5,3},{3,1},{1,0},{8,10},{10,12},{12... | collective-permute-start | bytes 1966088 | tf_op jit(solution)/shard_map/ppermute | solution.py:43
  104.0 29.4 %collective-permute-start.22 = (bf16[256,1280]{1,0:T(8,128)(2,1)}, bf16[256,1280]{1,0:T(8,128)(2,1)}, u32[]{:S(2)}, u32[]{:S(2)}) collective-permute-start(bf16[256,1280]{1,0:T(8,128)(2,1)} %collective-permute-done.21), channel_id=1, source_target_pairs={{2,0},{4,2},{6,4},{7,6},{5,7},{3,5},{1,3},{0,1},{10,8},{12,10},{14... | collective-permute-start | bytes 1966088 | tf_op jit(solution)/shard_map/ppermute | solution.py:46
  133.4 99.9 %collective-permute-start.23 = (bf16[256,1280]{1,0:T(8,128)(2,1)}, bf16[256,1280]{1,0:T(8,128)(2,1)}, u32[]{:S(2)}, u32[]{:S(2)}) collective-permute-start(bf16[256,1280]{1,0:T(8,128)(2,1)} %collective-permute-done.22), channel_id=1, source_target_pairs={{2,0},{4,2},{6,4},{7,6},{5,7},{3,5},{1,3},{0,1},{10,8},{12,10},{14... | collective-permute-start | bytes 1966088 | tf_op jit(solution)/shard_map/ppermute | solution.py:46
  143.0 92.6 %collective-permute-start.27 = (bf16[256,1280]{1,0:T(8,128)(2,1)}, bf16[256,1280]{1,0:T(8,128)(2,1)}, u32[]{:S(2)}, u32[]{:S(2)}) collective-permute-start(bf16[256,1280]{1,0:T(8,128)(2,1)} %collective-permute-done.26), channel_id=1, source_target_pairs={{0,2},{2,4},{4,6},{6,7},{7,5},{5,3},{3,1},{1,0},{8,10},{10,12},{12... | collective-permute-start | bytes 1966088 | tf_op jit(solution)/shard_map/ppermute | solution.py:43
  423.0 46.8 %collective-permute-start.48 = (bf16[2,28,1280]{2,1,0:T(8,128)(2,1)}, bf16[2,28,1280]{2,1,0:T(8,128)(2,1)}, u32[]{:S(2)}, u32[]{:S(2)}) collective-permute-start(bf16[2,28,1280]{2,1,0:T(8,128)(2,1)} %dynamic-slice_bitcast_fusion.5), channel_id=1, source_target_pairs={{0,8},{8,0},{16,24},{24,16},{1,9},{9,1},{17,25},{25,17},{2,10},{10... | collective-permute-start | bytes 430088 | tf_op jit(solution)/shard_map/ppermute | solution.py:76
  425.2 51.4 %collective-permute-start.14 = (bf16[256,1280]{1,0:T(8,128)(2,1)}, bf16[256,1280]{1,0:T(8,128)(2,1)}, u32[]{:S(2)}, u32[]{:S(2)}) collective-permute-start(bf16[256,1280]{1,0:T(8,128)(2,1)} %get-tuple-element.114), channel_id=1, source_target_pairs={{0,2},{2,4},{4,6},{6,7},{7,5},{5,3},{3,1},{1,0},{8,10},{10,12},{12... | collective-permute-start | bytes 1966088 | tf_op jit(solution)/shard_map/ppermute | solution.py:58
  425.5 67.9 %collective-permute-start.18 = (bf16[256,1280]{1,0:T(8,128)(2,1)S(1)}, bf16[256,1280]{1,0:T(8,128)(2,1)}, u32[]{:S(2)}, u32[]{:S(2)}) collective-permute-start(bf16[256,1280]{1,0:T(8,128)(2,1)S(1)} %get-tuple-element.115), channel_id=1, source_target_pairs={{2,0},{4,2},{6,4},{7,6},{5,7},{3,5},{1,3},{0,1},{10,8},{12,10},{14... | collective-permute-start | bytes 1966088 | tf_op jit(solution)/shard_map/ppermute | solution.py:61
  430.8 121.4 %collective-permute-start.54 = (bf16[2,2,224,1280]{3,2,1,0:T(8,128)(2,1)}, bf16[2,2,224,1280]{3,2,1,0:T(8,128)(2,1)}, u32[]{:S(2)}, u32[]{:S(2)}) collective-permute-start(bf16[2,2,224,1280]{3,2,1,0:T(8,128)(2,1)} %dynamic-slice_bitcast_fusion), channel_id=1, source_target_pairs={{0,8},{8,0},{16,24},{24,16},{1,9},{9,1},{17,25},{25,17},{2,10},{10... | collective-permute-start | bytes 6881288 | tf_op jit(solution)/shard_map/ppermute | solution.py:76
  476.6 32.5 %collective-permute-start.32 = (bf16[256,1280]{1,0:T(8,128)(2,1)S(1)}, bf16[256,1280]{1,0:T(8,128)(2,1)S(1)}, u32[]{:S(2)}, u32[]{:S(2)}) collective-permute-start(bf16[256,1280]{1,0:T(8,128)(2,1)S(1)} %get-tuple-element.109), channel_id=1, source_target_pairs={{2,0},{4,2},{6,4},{7,6},{5,7},{3,5},{1,3},{0,1},{10,8},{12,10},{14... | collective-permute-start | bytes 1966088 | tf_op jit(solution)/shard_map/ppermute | solution.py:61
  479.6 27.7 %collective-permute-start.15 = (bf16[256,1280]{1,0:T(8,128)(2,1)S(1)}, bf16[256,1280]{1,0:T(8,128)(2,1)S(1)}, u32[]{:S(2)}, u32[]{:S(2)}) collective-permute-start(bf16[256,1280]{1,0:T(8,128)(2,1)S(1)} %add_convert_fusion.22), channel_id=1, source_target_pairs={{0,2},{2,4},{4,6},{6,7},{7,5},{5,3},{3,1},{1,0},{8,10},{10,12},{12... | collective-permute-start | bytes 1966088 | tf_op jit(solution)/shard_map/ppermute | solution.py:58
  493.3 62.8 %collective-permute-start.52 = (bf16[2,320,1792]{2,1,0:T(8,128)(2,1)S(1)}, bf16[2,320,1792]{2,1,0:T(8,128)(2,1)S(1)}, u32[]{:S(2)}, u32[]{:S(2)}) collective-permute-start(bf16[2,320,1792]{2,1,0:T(8,128)(2,1)S(1)} %dynamic-slice_bitcast_fusion.1), channel_id=1, source_target_pairs={{0,8},{8,0},{16,24},{24,16},{1,9},{9,1},{17,25},{25,17},{2,10},{10... | collective-permute-start | bytes 6881288 | tf_op jit(solution)/shard_map/ppermute | solution.py:76
  493.5 27.9 %collective-permute-start.29 = (bf16[256,1280]{1,0:T(8,128)(2,1)S(1)}, bf16[256,1280]{1,0:T(8,128)(2,1)S(1)}, u32[]{:S(2)}, u32[]{:S(2)}) collective-permute-start(bf16[256,1280]{1,0:T(8,128)(2,1)S(1)} %add_convert_fusion.16), channel_id=1, source_target_pairs={{0,2},{2,4},{4,6},{6,7},{7,5},{5,3},{3,1},{1,0},{8,10},{10,12},{12... | collective-permute-start | bytes 1966088 | tf_op jit(solution)/shard_map/ppermute | solution.py:58
  561.3 152.8 %collective-permute-start.55 = (bf16[1,2,224,1280]{3,2,1,0:T(8,128)(2,1)}, bf16[1,2,224,1280]{3,2,1,0:T(8,128)(2,1)}, u32[]{:S(2)}, u32[]{:S(2)}) collective-permute-start(bf16[1,2,224,1280]{3,2,1,0:T(8,128)(2,1)} %constant_dynamic-slice_fusion.5), channel_id=1, source_target_pairs={{0,16},{8,24},{16,0},{24,8},{1,17},{9,25},{17,1},{25,9},{2,18},{10... | collective-permute-start | bytes 3440648 | tf_op jit(solution)/shard_map/ppermute | solution.py:76
  567.3 47.1 %collective-permute-start.53 = (bf16[1,320,1792]{2,1,0:T(8,128)(2,1)}, bf16[1,320,1792]{2,1,0:T(8,128)(2,1)}, u32[]{:S(2)}, u32[]{:S(2)}) collective-permute-start(bf16[1,320,1792]{2,1,0:T(8,128)(2,1)} %constant_dynamic-slice_fusion), channel_id=1, source_target_pairs={{0,16},{8,24},{16,0},{24,8},{1,17},{9,25},{17,1},{25,9},{2,18},{10... | collective-permute-start | bytes 3440648 | tf_op jit(solution)/shard_map/ppermute | solution.py:76
  568.1 66.4 %collective-permute-start.51 = (bf16[1,320,1792]{2,1,0:T(8,128)(2,1)}, bf16[1,320,1792]{2,1,0:T(8,128)(2,1)}, u32[]{:S(2)}, u32[]{:S(2)}) collective-permute-start(bf16[1,320,1792]{2,1,0:T(8,128)(2,1)} %constant_dynamic-slice_fusion.1), channel_id=1, source_target_pairs={{0,16},{8,24},{16,0},{24,8},{1,17},{9,25},{17,1},{25,9},{2,18},{10... | collective-permute-start | bytes 3440648 | tf_op jit(solution)/shard_map/ppermute | solution.py:76
  590.7 53.5 %all-to-all-start.1 = ((bf16[8,256,128]{2,1,0:T(8,128)(2,1)}), bf16[8,256,128]{2,1,0:T(8,128)(2,1)}, u32[]{:S(2)}, u32[]{:S(2)}) async-start(bf16[8,256,128]{2,1,0:T(8,128)(2,1)} %bitcast_bitcast_fusion), calls=%async_computation.1 | async-start | bytes 1048576 | tf_op jit(solution)/shard_map/all_to_all | solution.py:287
  606.2 120.8 %collective-permute-start.44 = (bf16[2,320,1408]{2,1,0:T(8,128)(2,1)}, bf16[2,320,1408]{2,1,0:T(8,128)(2,1)}, u32[]{:S(2)}, u32[]{:S(2)}) collective-permute-start(bf16[2,320,1408]{2,1,0:T(8,128)(2,1)} %fusion.39), channel_id=1, source_target_pairs={{0,8},{8,0},{16,24},{24,16},{1,9},{9,1},{17,25},{25,17},{2,10},{10... | collective-permute-start | bytes 5406728 | tf_op jit(solution)/shard_map/ppermute | solution.py:76
  747.3 36.8 %all-to-all-start.2 = ((bf16[8,40,1152]{2,1,0:T(8,128)(2,1)}), bf16[8,40,1152]{2,1,0:T(8,128)(2,1)}, u32[]{:S(2)}, u32[]{:S(2)}) async-start(bf16[8,40,1152]{2,1,0:T(8,128)(2,1)} %bitcast.197), calls=%async_computation.2 | async-start | bytes 1474560 | tf_op jit(solution)/shard_map/all_to_all | solution.py:333
  784.1 28.0 %all-to-all-start.3 = ((bf16[8,40,1632]{2,1,0:T(8,128)(2,1)}), bf16[8,40,1632]{2,1,0:T(8,128)(2,1)}, u32[]{:S(2)}, u32[]{:S(2)}) async-start(bf16[8,40,1632]{2,1,0:T(8,128)(2,1)} %pad_maximum_fusion.11), calls=%async_computation.3 | async-start | bytes 2129920 | tf_op jit(solution)/shard_map/all_to_all | solution.py:333
  (171 other events, 2080.8 us)

commit v2 on v1

--- a/solution.py
+++ b/solution.py
@@ -1,6 +1,10 @@
+import functools
+
 import jax
 import jax.numpy as jnp
 from jax import lax
+from jax.experimental import pallas as pl
+from jax.experimental.pallas import tpu as pltpu
 from jax.sharding import PartitionSpec as P
 
 HEAD_DIM = 128
@@ -79,6 +83,28 @@
     return chunks[0]
 
 
+def wide_finish(kept, sent):
+    count = lax.axis_size("wide")
+    place = lax.axis_index("wide")
+    got = lax.ppermute(sent, "wide", [(i, i ^ 1) for i in range(count)])
+    bit = 2
+    while bit < count:
+        mine = (place // bit) % 2
+
+        def half(array, index):
+            pairs = array.reshape((array.shape[0] // 2, 2) + array.shape[1:])
+            return lax.dynamic_index_in_dim(pairs, index, axis=1, keepdims=False)
+
+        def added(index):
+            return (half(kept, index).astype(FLOAT) + half(got, index).astype(FLOAT)).astype(HALF)
+
+        kept, got = added(mine), lax.ppermute(
+            added(1 - mine), "wide", [(i, i ^ bit) for i in range(count)]
+        )
+        bit *= 2
+    return kept[0].astype(FLOAT) + got[0].astype(FLOAT)
+
+
 def norm_back(grad_out, normed, inv_scale, gain):
     scaled = grad_out * gain
     return inv_scale * (scaled - normed * jnp.mean(scaled * normed, axis=1, keepdims=True))
@@ -111,6 +137,223 @@
     query_grad = matmul(score_grad, keys, (1, 0)) * HEAD_DIM**-0.5
     key_grad = matmul(score_grad, queries, (0, 0)) * HEAD_DIM**-0.5
     return query_grad, key_grad, value_grad
+
+
+VMEM_LIMIT = 60 * 2**20
+CHUNK = 512
+
+
+def whole_block(shape):
+    return pl.BlockSpec(shape, lambda *_: (0,) * len(shape))
+
+
+def rows_kernel(count, units, chained, *refs):
+    xs, cs, gates = refs[:count], refs[count : 2 * count], refs[2 * count : 3 * count]
+    gate_w, up_w, down_w = refs[3 * count : 3 * count + 3]
+    outs = refs[3 * count + 3 + (3 if chained else 0) :]
+    inner, gate_g, up_g = outs[:3]
+    ys, ds = outs[3 : 3 + count], outs[3 + count : 3 + 2 * count]
+    y_sum, d_sum, x_rows, c_rows = outs[3 + 2 * count :]
+    step = pl.program_id(0)
+    length = xs[0].shape[0]
+    chunk = gate_w.shape[1]
+    per_expert = pl.num_programs(0) // gates[0].shape[1]
+
+    @pl.when(step == 0)
+    def _():
+        for i in range(count):
+            x_rows[i * length : (i + 1) * length] = xs[i][...]
+            c_rows[i * length : (i + 1) * length] = cs[i][...]
+        y_sum[...] = jnp.zeros_like(y_sum)
+        d_sum[...] = jnp.zeros_like(d_sum)
+
+    x, c = x_rows[...], c_rows[...]
+    expert = step // per_expert
+    column = (step % per_expert) * chunk + lax.broadcasted_iota(
+        jnp.int32, (count * length, chunk), 1
+    )
+    picked = []
+    for gate in gates:
+        own = gate[:, 0:1]
+        for e in range(1, gate.shape[1]):
+            own = jnp.where(expert == e, gate[:, e : e + 1], own)
+        picked.append(own)
+    scale = jnp.where(column < units, jnp.concatenate(picked, axis=0), 1.0)
+    gate_pre = matmul(x, gate_w[...], (1, 0))
+    up_pre = matmul(x, up_w[...], (1, 0))
+    inner_grad = matmul(c, down_w[...], (1, 1)) * scale
+    sigma = 0.5 * jnp.tanh(0.5 * gate_pre) + 0.5
+    active = gate_pre * sigma
+    inner[...] = (active * up_pre * scale).astype(HALF)
+    gate_g[...] = (inner_grad * up_pre * (sigma + active * (1.0 - sigma))).astype(HALF)
+    up_g[...] = (inner_grad * active).astype(HALF)
+    y_sum[...] += matmul(inner[...], down_w[...], (1, 0))
+    d_sum[...] += matmul(gate_g[...], gate_w[...], (1, 1)) + matmul(up_g[...], up_w[...], (1, 1))
+
+    @pl.when(step == pl.num_programs(0) - 1)
+    def _():
+        for i in range(count):
+            ys[i][...] = y_sum[i * length : (i + 1) * length].astype(HALF)
+            ds[i][...] = d_sum[i * length : (i + 1) * length].astype(HALF)
+
+
+def expert_rows(units, place, total, kept, xs, cs, gates, gate_w, up_w, down_w):
+    count = len(xs)
+    length, width = xs[0].shape
+    padded = gate_w.shape[1]
+    rows = count * length
+    column_block = pl.BlockSpec((width, CHUNK), lambda f: (0, f))
+    row_block = pl.BlockSpec((CHUNK, width), lambda f: (f, 0))
+    kept_block = pl.BlockSpec((rows, CHUNK), lambda f: (place // rows, f))
+    chained = kept is not None
+    first_kept = 3 * count + 3
+    return pl.pallas_call(
+        functools.partial(rows_kernel, count, units, chained),
+        grid=(padded // CHUNK,),
+        in_specs=[whole_block(xs[0].shape)] * (2 * count)
+        + [whole_block(gates[0].shape)] * count
+        + [column_block, column_block, row_block]
+        + [pl.BlockSpec(memory_space=pl.ANY)] * (3 if chained else 0),
+        out_specs=[kept_block] * 3 + [whole_block(xs[0].shape)] * (2 * count),
+        out_shape=[jax.ShapeDtypeStruct((total, padded), HALF)] * 3
+        + [jax.ShapeDtypeStruct(xs[0].shape, HALF)] * (2 * count),
+        input_output_aliases={first_kept + i: i for i in range(3)} if chained else {},
+        scratch_shapes=[pltpu.VMEM((rows, width), FLOAT)] * 2 + [pltpu.VMEM((rows, width), HALF)] * 2,
+        compiler_params=pltpu.CompilerParams(vmem_limit_bytes=VMEM_LIMIT),
+        cost_estimate=pl.CostEstimate(
+            flops=12 * rows * width * padded,
+            bytes_accessed=6 * width * padded + 6 * rows * padded + 8 * rows * width,
+            transcendentals=rows * padded,
+        ),
+        name="expert_rows",
+    )(*xs, *cs, *gates, gate_w, up_w, down_w, *(kept if chained else ()))
+
+
+def fetch_rows(slots, rows, sems):
+    length = slots[0].shape[0]
+    copies = [
+        pltpu.make_async_copy(slot, rows.at[pl.ds(i * length, length)], sems.at[i])
+        for i, slot in enumerate(slots)
+    ]
+    for copy in copies:
+        copy.start()
+    for copy in copies:
+        copy.wait()
+
+
+def split_rows(source, core, kept, sent, first, size, columns):
+    for j in range(kept.shape[0]):
+        for target, parity in ((kept, core), (sent, 1 - core)):
+            start = pl.multiple_of(first + (2 * j + parity) * size, 8)
+            target[j, 0, :, columns] = source[pl.ds(start, size), : columns.stop - columns.start].astype(HALF)
+
+
+def in_grad_kernel(count, units, core_ref, *refs):
+    slots, grad = refs[:count], refs[count]
+    kept, sent, share, rows, total, sems = refs[count + 1 :]
+    step = pl.program_id(0)
+    chunk = grad.shape[1]
+    per_expert = pl.num_programs(0) // 2
+
+    @pl.when(step == 0)
+    def _():
+        fetch_rows(slots, rows, sems)
+
+    total[...] = matmul(rows[...], grad[...], (0, 0))
+    core = core_ref[0]
+    for part in range(per_expert):
+        columns = slice(part * chunk, min((part + 1) * chunk, units))
+
+        @pl.when(step % per_expert == part)
+        def _():
+            split_rows(total, core, kept, sent, 0, kept.shape[2], columns)
+
+    @pl.when(step == per_expert - 1)
+    def _():
+        share[...] = total[:, units - (per_expert - 1) * chunk :].astype(HALF)
+
+
+def in_grad(units, experts, copies, core, slots, grad):
+    length, width = slots[0].shape
+    total, padded = grad.shape
+    per_expert = padded // experts // CHUNK
+    part = (copies // 2, experts, width // copies, units)
+    part_block = pl.BlockSpec((part[0], 1) + part[2:], lambda f, c: (0, f // per_expert, 0, 0))
+    share = padded // experts - units
+    return pl.pallas_call(
+        functools.partial(in_grad_kernel, len(slots), units),
+        grid_spec=pltpu.PrefetchScalarGridSpec(
+            num_scalar_prefetch=1,
+            grid=(padded // CHUNK,),
+            in_specs=[pl.BlockSpec(memory_space=pl.ANY)] * len(slots)
+            + [pl.BlockSpec((total, CHUNK), lambda f, c: (0, f))],
+            out_specs=[part_block, part_block, whole_block((width, share))],
+            scratch_shapes=[
+                pltpu.VMEM((total, width), HALF),
+                pltpu.VMEM((width, CHUNK), FLOAT),
+                pltpu.SemaphoreType.DMA((len(slots),)),
+            ],
+        ),
+        out_shape=[jax.ShapeDtypeStruct(part, HALF)] * 2 + [jax.ShapeDtypeStruct((width, share), HALF)],
+        compiler_params=pltpu.CompilerParams(vmem_limit_bytes=VMEM_LIMIT),
+        cost_estimate=pl.CostEstimate(
+            flops=2 * total * width * padded, bytes_accessed=2 * (total + width) * (padded + width), transcendentals=0
+        ),
+        name="expert_in_grad",
+    )(core, *slots, grad)
+
+
+def out_grad_kernel(count, units, core_ref, *refs):
+    slots, inner = refs[:count], refs[count]
+    kept, sent, share, rows, total, sems = refs[count + 1 :]
+    step = pl.program_id(0)
+    chunk = inner.shape[1]
+    per_expert = pl.num_programs(0) // 2
+
+    @pl.when(step == 0)
+    def _():
+        fetch_rows(slots, rows, sems)
+
+    part = step % per_expert
+    total[pl.ds(pl.multiple_of(part * chunk, chunk), chunk)] = matmul(inner[...], rows[...], (0, 0))
+
+    @pl.when(part == per_expert - 1)
+    def _():
+        split_rows(total, core_ref[0], kept, sent, 0, kept.shape[2], slice(0, kept.shape[3]))
+
+    @pl.when(step == per_expert - 1)
+    def _():
+        share[...] = total[units:, :].astype(HALF)
+
+
+def out_grad(units, experts, copies, core, slots, inner):
+    length, width = slots[0].shape
+    total, padded = inner.shape
+    per_expert = padded // experts // CHUNK
+    part = (copies // 2, experts, units // copies, width)
+    part_block = pl.BlockSpec((part[0], 1) + part[2:], lambda f, c: (0, f // per_expert, 0, 0))
+    share = padded // experts - units
+    return pl.pallas_call(
+        functools.partial(out_grad_kernel, len(slots), units),
+        grid_spec=pltpu.PrefetchScalarGridSpec(
+            num_scalar_prefetch=1,
+            grid=(padded // CHUNK,),
+            in_specs=[pl.BlockSpec(memory_space=pl.ANY)] * len(slots)
+            + [pl.BlockSpec((total, CHUNK), lambda f, c: (0, f))],
+            out_specs=[part_block, part_block, whole_block((share, width))],
+            scratch_shapes=[
+                pltpu.VMEM((total, width), HALF),
+                pltpu.VMEM((padded // experts, width), FLOAT),
+                pltpu.SemaphoreType.DMA((len(slots),)),
+            ],
+        ),
+        out_shape=[jax.ShapeDtypeStruct(part, HALF)] * 2 + [jax.ShapeDtypeStruct((share, width), HALF)],
+        compiler_params=pltpu.CompilerParams(vmem_limit_bytes=VMEM_LIMIT),
+        cost_estimate=pl.CostEstimate(
+            flops=2 * total * width * padded, bytes_accessed=2 * (total + width) * (padded + width), transcendentals=0
+        ),
+        name="expert_out_grad",
+    )(core, *slots, inner)
 
 
 def on_device(
@@ -165,9 +408,14 @@
     expert_ids = jnp.arange(experts, dtype=jnp.int32)
     picked = routes[:, :, None] == expert_ids[None, None, :]
     token_gate = jnp.sum(jnp.where(picked, gates[:, :, None], 0.0), axis=1)
-    all_gates = lax.all_gather(token_gate.T, "narrow", axis=0)
-    own_gates = lax.dynamic_slice_in_dim(all_gates, place * local_experts, local_experts, axis=1)
-    own_gates = by_slot(own_gates)
+    own_gates = lax.all_to_all(
+        token_gate.T.reshape(group, local_experts, length),
+        "narrow",
+        split_axis=0,
+        concat_axis=0,
+        tiled=True,
+    )
+    own_gates = by_slot(own_gates.transpose(0, 2, 1))
 
     def head_columns(weight):
         return lax.dynamic_slice_in_dim(weight, place * HEAD_DIM, HEAD_DIM, axis=1)
@@ -227,59 +475,68 @@
     share_gate = matmul(shared_gate, choice, (1, 0)).astype(HALF)
     share_up = matmul(shared_up, choice, (1, 0)).astype(HALF)
     share_down = matmul(choice, shared_down, (0, 0)).astype(HALF)
-    gate_weight = jnp.concatenate([expert_gate[e] for e in range(local_experts)] + [share_gate], axis=1)
-    up_weight = jnp.concatenate([expert_up[e] for e in range(local_experts)] + [share_up], axis=1)
-    down_weight = jnp.concatenate([expert_down[e] for e in range(local_experts)] + [share_down], axis=0)
+    per_expert = -(-(hidden_units + padded) // CHUNK) * CHUNK
+    spare_units = per_expert - hidden_units
+
+    def packed(weight, share_part, axis):
+        pieces = []
+        for e in range(local_experts):
+            pieces.append(weight[e])
+            filler = share_part if e == 0 else jnp.zeros_like(share_part)
+            pieces.append(filler)
+        return jnp.concatenate(pieces, axis=axis)
+
+    if padded < spare_units:
+        share_gate = jnp.pad(share_gate, ((0, 0), (0, spare_units - padded)))
+        share_up = jnp.pad(share_up, ((0, 0), (0, spare_units - padded)))
+        share_down = jnp.pad(share_down, ((0, spare_units - padded), (0, 0)))
+    gate_weight = packed(expert_gate, share_gate, 1)
+    up_weight = packed(expert_up, share_up, 1)
+    down_weight = packed(expert_down, share_down, 0)
 
     ffn_slots = ring_gather(ffn_in)
-    rows = jnp.concatenate(ffn_slots, axis=0)
-    cots = jnp.concatenate(cot_slots, axis=0)
-    gate_columns = own_gates.transpose(0, 2, 1).reshape(seq_len, local_experts)
-    scale = jnp.concatenate(
-        [
-            jnp.broadcast_to(gate_columns[:, e : e + 1], (seq_len, hidden_units))
-            for e in range(local_experts)
-        ]
-        + [jnp.ones((seq_len, padded), FLOAT)],
-        axis=1,
-    )
-    gate_pre = matmul(rows, gate_weight, (1, 0))
-    up_pre = matmul(rows, up_weight, (1, 0))
-    sigma = jax.nn.sigmoid(gate_pre)
-    active = gate_pre * sigma
-    slope = sigma * (1.0 + gate_pre * (1.0 - sigma))
-    gated_inner = (scale * active * up_pre).astype(HALF)
-    out_part = matmul(gated_inner, down_weight, (1, 0)).astype(HALF)
-    inner_grad = matmul(cots, down_weight, (1, 1)) * scale
-    gate_grad = (inner_grad * up_pre * slope).astype(HALF)
-    up_grad = (inner_grad * active).astype(HALF)
-    row_part = (
-        matmul(gate_grad, gate_weight, (1, 1)) + matmul(up_grad, up_weight, (1, 1))
-    ).astype(HALF)
-    row_part = row_part.reshape(group, length, width)
-    ffn_in_grad = ring_scatter([row_part[j] for j in range(group)])
-    out_part = out_part.reshape(group, length, width)
-
-    down_wgrad = matmul(gated_inner, cots, (0, 0)).astype(HALF)
-    gate_wgrad = matmul(rows, gate_grad, (0, 0)).astype(HALF)
-    up_wgrad = matmul(rows, up_grad, (0, 0)).astype(HALF)
-    routed = local_experts * hidden_units
-
-    def expert_sum(grad):
-        return wide_scatter(
-            grad.reshape(copies, width // copies, grad.shape[1])[:, :, :routed]
-        ).reshape(width // copies, local_experts, hidden_units)
-
-    expert_gate_grad = expert_sum(gate_wgrad).transpose(1, 0, 2).astype(FLOAT)
-    expert_up_grad = expert_sum(up_wgrad).transpose(1, 0, 2).astype(FLOAT)
-    expert_down_grad = wide_scatter(
-        down_wgrad[:routed]
-        .reshape(local_experts, copies, hidden_units // copies, width)
-        .transpose(1, 0, 2, 3)
-    ).astype(FLOAT)
-    shared_down_grad = wide_scatter(
-        down_wgrad[routed : routed + taken].reshape(copies, share, width)
-    ).astype(FLOAT)
+    half_ring = group // 2
+    batches = [(0,), (1, group - 1), (2,), (half_ring, half_ring + 1), (half_ring - 1, half_ring + 2)]
+    row_order = [slot for batch in batches if len(batch) == 2 for slot in batch]
+    row_order += [slot for batch in batches if len(batch) == 1 for slot in batch]
+    kept = None
+    out_parts, row_parts = [None] * group, [None] * group
+    for batch in batches:
+        result = expert_rows(
+            hidden_units,
+            row_order.index(batch[0]) * length,
+            seq_len,
+            kept,
+            [ffn_slots[j] for j in batch],
+            [cot_slots[j] for j in batch],
+            [own_gates[j] for j in batch],
+            gate_weight,
+            up_weight,
+            down_weight,
+        )
+        kept = result[:3]
+        for i, j in enumerate(batch):
+            out_parts[j] = result[3 + i]
+            row_parts[j] = result[3 + len(batch) + i]
+    gated_inner, gate_grad, up_grad = kept
+    ffn_in_grad = ring_scatter(row_parts)
+
+    core = (lax.axis_index("wide") % 2).astype(jnp.int32).reshape(1)
+    ordered_cots = [cot_slots[j] for j in row_order]
+    ordered_rows = [ffn_slots[j] for j in row_order]
+    down_kept, down_sent, down_share = out_grad(
+        hidden_units, local_experts, copies, core, ordered_cots, gated_inner
+    )
+    gate_kept, gate_sent, gate_share = in_grad(
+        hidden_units, local_experts, copies, core, ordered_rows, gate_grad
+    )
+    up_kept, up_sent, up_share = in_grad(
+        hidden_units, local_experts, copies, core, ordered_rows, up_grad
+    )
+    expert_down_grad = wide_finish(down_kept, down_sent)
+    expert_gate_grad = wide_finish(gate_kept, gate_sent)
+    expert_up_grad = wide_finish(up_kept, up_sent)
+    shared_down_grad = wide_scatter(down_share[:taken].reshape(copies, share, width)).astype(FLOAT)
 
     hidden_grad = cotangent.astype(FLOAT) + norm_back(ffn_in_grad, normed_two, inv_two, ffn_gain)
     branch_grad = hidden_grad.astype(HALF)
@@ -296,7 +553,7 @@
         attended_grad[:, own_heads + h * HEAD_DIM : own_heads + (h + 1) * HEAD_DIM]
         for h in range(spare_heads)
     ]
-    mixed = (hidden + ring_scatter([out_part[j] for j in range(group)])).astype(HALF)
+    mixed = (hidden + ring_scatter(out_parts)).astype(HALF)
     grads = [
         causal_back(q, k, v, pos, positions, log_total, out_grad)
         for (q, k, v, pos), (_, log_total), out_grad in zip(heads, outs, out_grads)
@@ -348,8 +605,8 @@
                 spread(
                     jnp.concatenate(
                         [
-                            gate_wgrad[:, routed : routed + taken],
-                            up_wgrad[:, routed : routed + taken],
+                            gate_share[:, :taken],
+                            up_share[:, :taken],
                         ],
                         axis=1,
                     )

time: 843 us -> 740 us (0.88)
  Pallas kernels: 0 us -> 154 us
  matrix products: 255 us -> 104 us
  local copies, waits for them, and re-layouts: 143 us -> 75.4 us
  blocking collectives: 46.2 us -> 0 us
  other arithmetic: 101 us -> 110 us
    pallas_call x0 -> x8, Pallas kernels: none -> 154 us  [the longest x5 99 us: expert_rows(): pl.pallas_call(functools.partial(rows_kernel, count, units, chained), gri...]
    dot_general x40 -> x31, matrix products: 246 us -> 94.4 us  [matmul(): lax.dot_general(a, b, ((contract[:1], contract[1:]), ((), ())), preferred...]
    all_gather x1 -> x0, blocking collectives: 46.2 us -> none  [on_device(): all_gates = lax.all_gather(token_gate.T, 'narrow', axis=0)]
    ppermute x9, waiting for transfers between devices: 5.19 us -> 38.1 us  [ring_scatter(): backward = lax.ppermute(backward, 'narrow', back).astype(FLOAT)]
    unnamed x289 -> x270, local copies, waits for them, and re-layouts: 48.4 us -> 21.5 us
    ppermute x12, waiting for transfers between devices: 97.9 us -> 73.5 us  [ring_scatter(): forward = lax.ppermute(forward, 'narrow', ahead).astype(FLOAT)]
    concatenate x1 -> x3, other arithmetic: 0.3 us -> 16.9 us  [the longest x2 15.5 us: packed(): return jnp.concatenate(pieces, axis=axis)]
    ppermute x12, starting transfers between devices: 16.9 us -> 5.09 us  [ring_gather(): forward = lax.ppermute(forward, 'narrow', ahead)]
  transfers between devices with their start and end apart: 60 -> 61, of which waited for: 28 -> 24; matrix products, arithmetic and copies ran while one was open for 40% -> 36% of each run, Pallas kernels for 0% -> 21%
where the time goes in v2:
time: 740 us; the launch traced here: 728 us
  waiting for transfers between devices  198 us (27%)
  Pallas kernels  154 us (21%)
  other arithmetic  110 us (15%)
  matrix products  104 us (14%)
  starting transfers between devices  83.2 us (11%)
  local copies, waits for them, and re-layouts  75.4 us (10%)
    pallas_call x5, Pallas kernels, expert_rows(): pl.pallas_call(functools.partial(rows_kernel, count, units, chained), gri...  99 us
    dot_general x31, matrix products, matmul(): lax.dot_general(a, b, ((contract[:1], contract[1:]), ((), ())), preferred...  94.4 us
    ppermute x12, waiting for transfers between devices, ring_scatter(): forward = lax.ppermute(forward, 'narrow', ahead).astype(FLOAT)  73.5 us
    ppermute x12, waiting for transfers between devices, ring_gather(): forward = lax.ppermute(forward, 'narrow', ahead)  64.7 us
    ppermute x9, waiting for transfers between devices, ring_scatter(): backward = lax.ppermute(backward, 'narrow', back).astype(FLOAT)  38.1 us
    pallas_call x2, Pallas kernels, in_grad(): pl.pallas_call(functools.partial(in_grad_kernel, len(slots), units), grid...  36.9 us
    unnamed x270, local copies, waits for them, and re-layouts  21.5 us
    pallas_call x1, Pallas kernels, out_grad(): pl.pallas_call(functools.partial(out_grad_kernel, len(slots), units), gri...  18.1 us
  transfers between devices with their start and end apart: 61, of which 24 were waited for; matrix products, arithmetic and copies ran while one was open for 36% of the time, Pallas kernels for 21%

profile of v2, /device:TPU:4, one launch (start us, length us, event | category | flops | bytes accessed | tf_op | source)
XLA Modules:
  0.0 727.7 jit_solution(12514631219375820864)
XLA Ops:
  36.5 10.1 %maximum_maximum_fusion.2.refs_5_.refs_8_ = bf16[2048,1280]{1,0:T(8,128)(2,1)} fusion(bf16[896,1280]{1,0:T(8,128)(2,1)S(1)} %copy-done.17, bf16[128,1280]{1,0:T(8,128)(2,1)S(1)} %copy-done.47, bf16[896,1280]{1,0:T(8,128)(2,1)S(1)} %copy-done.16, bf16[2048]{0:T(1024)(128)(2,1)S(1)} %pad.30.clone), kind=kLoop, calls=%fused_computation.19 | loop fusion | flops 20971520 | bytes 10162176 | tf_op jit(solution)/shard_map/concatenate | solution.py:487
  57.7 14.7 %collective-permute-done.4 = bf16[256,1280]{1,0:T(8,128)(2,1)} collective-permute-done((bf16[256,1280]{1,0:T(8,128)(2,1)}, bf16[256,1280]{1,0:T(8,128)(2,1)}, u32[]{:S(2)}, u32[]{:S(2)}) %collective-permute-start.4) | collective-permute-done | bytes 655392 | tf_op jit(solution)/shard_map/ppermute | solution.py:47
  89.5 11.0 %collective-permute-done.5 = bf16[256,1280]{1,0:T(8,128)(2,1)} collective-permute-done((bf16[256,1280]{1,0:T(8,128)(2,1)}, bf16[256,1280]{1,0:T(8,128)(2,1)}, u32[]{:S(2)}, u32[]{:S(2)}) %collective-permute-start.5) | collective-permute-done | bytes 655392 | tf_op jit(solution)/shard_map/ppermute | solution.py:47
  115.7 12.8 %collective-permute-done.6 = bf16[256,1280]{1,0:T(8,128)(2,1)S(1)} collective-permute-done((bf16[256,1280]{1,0:T(8,128)(2,1)}, bf16[256,1280]{1,0:T(8,128)(2,1)S(1)}, u32[]{:S(2)}, u32[]{:S(2)}) %collective-permute-start.6) | collective-permute-done | bytes 655392 | tf_op jit(solution)/shard_map/ppermute | solution.py:47
  164.3 9.5 %fusion.18 = bf16[2048,128]{1,0:T(8,128)(2,1)} fusion(f32[2048,2048]{0,1:T(8,128)} %get-tuple-element.177, f32[2048]{0:T(1024)S(1)} %fusion, f32[2048]{0:T(1024)S(1)} %get-tuple-element.176, f32[2048,384]{0,1:T(8,128)S(1)} %fusion.121), kind=kOutput, calls=%fused_computation.51 | convolution fusion | flops 1086586880 | bytes 17842176 | tf_op jit(solution)/shard_map/dot_general | solution.py:17
  202.5 13.8 %collective-permute-done.7.refs_1_ = bf16[256,1280]{1,0:T(8,128)(2,1)} collective-permute-done((bf16[256,1280]{1,0:T(8,128)(2,1)S(1)}, bf16[256,1280]{1,0:T(8,128)(2,1)}, u32[]{:S(2)}, u32[]{:S(2)}) %collective-permute-start.7) | collective-permute-done | bytes 655392 | tf_op jit(solution)/shard_map/ppermute | solution.py:47
  216.9 13.9 %expert_rows.5 = (bf16[2048,2048]{1,0:T(8,128)(2,1)}, bf16[2048,2048]{1,0:T(8,128)(2,1)}, bf16[2048,2048]{1,0:T(8,128)(2,1)}, bf16[256,1280]{1,0:T(8,128)(2,1)}, bf16[256,1280]{1,0:T(8,128)(2,1)}) custom-call(bf16[256,1280]{1,0:T(8,128)(2,1)} %copy-done.58, bf16[256,1280]{1,0:T(8,128)(2,1)} %refs_6_.1, f32[256,2]{1,0:T(8,128)} %get-tuple-element.146.refs_2_, ...), custom_call_target="tpu_custom_call" | custom-call | flops 8053063680 | bytes 21495808 | tf_op jit(solution)/shard_map/expert_rows/pallas_call | solution.py:210
  233.8 23.6 %expert_rows.6 = (bf16[2048,2048]{1,0:T(8,128)(2,1)}, bf16[2048,2048]{1,0:T(8,128)(2,1)}, bf16[2048,2048]{1,0:T(8,128)(2,1)}, bf16[256,1280]{1,0:T(8,128)(2,1)},...) custom-call(bf16[256,1280]{1,0:T(8,128)(2,1)} %collective-permute-do, ...), custom_call_target="tpu_custom_call", output_to_operand_aliasing={{0}: (9, {}), {1}: (10, {}), {2}: (11, {})} | custom-call | flops 16106127360 | bytes 27262976 | tf_op jit(solution)/shard_map/expert_rows/pallas_call | solution.py:210
  259.5 14.1 %expert_rows.7 = (bf16[2048,2048]{1,0:T(8,128)(2,1)}, bf16[2048,2048]{1,0:T(8,128)(2,1)}, bf16[2048,2048]{1,0:T(8,128)(2,1)}, bf16[256,1280]{1,0:T(8,128)(2,1)}, bf16[256,1280]{1,0:T(8,128)(2,1)}) custom-call(bf16[256,1280]{1,0:T(8,128)(2,1)} %copy-done.75, ...), custom_call_target="tpu_custom_call", output_to_operand_aliasing={{0}: (6, {}), {1}: (7, {}), {2}: (8, {})} | custom-call | flops 8053063680 | bytes 21495808 | tf_op jit(solution)/shard_map/expert_rows/pallas_call | solution.py:210
  273.6 23.6 %expert_rows.8 = (bf16[2048,2048]{1,0:T(8,128)(2,1)}, bf16[2048,2048]{1,0:T(8,128)(2,1)}, bf16[2048,2048]{1,0:T(8,128)(2,1)}, bf16[256,1280]{1,0:T(8,128)(2,1)},...) custom-call(bf16[256,1280]{1,0:T(8,128)(2,1)} %collective-permute-do, ...), custom_call_target="tpu_custom_call", output_to_operand_aliasing={{0}: (9, {}), {1}: (10, {}), {2}: (11, {})} | custom-call | flops 16106127360 | bytes 27262976 | tf_op jit(solution)/shard_map/expert_rows/pallas_call | solution.py:210
  301.3 23.8 %expert_rows.9 = (bf16[2048,2048]{1,0:T(8,128)(2,1)}, bf16[2048,2048]{1,0:T(8,128)(2,1)}, bf16[2048,2048]{1,0:T(8,128)(2,1)}, bf16[256,1280]{1,0:T(8,128)(2,1)},...) custom-call(bf16[256,1280]{1,0:T(8,128)(2,1)} %collective-permute-do, ...), custom_call_target="tpu_custom_call", output_to_operand_aliasing={{0}: (9, {}), {1}: (10, {}), {2}: (11, {})} | custom-call | flops 16106127360 | bytes 27262976 | tf_op jit(solution)/shard_map/expert_rows/pallas_call | solution.py:210
  325.2 18.1 %expert_out_grad.1 = (bf16[2,2,224,1280]{3,2,1,0:T(8,128)(2,1)}, bf16[2,2,224,1280]{3,2,1,0:T(8,128)(2,1)}, bf16[128,1280]{1,0:T(8,128)(2,1)}) custom-call(s32[1]{0:T(128)} %bitcast.43.core_ref, bf16[256,1280]{1,0:T(8,128)(2,1)} %collective-permute-done.17.refs_2_.refs_0_, bf16[256,1280]{1,0:T(8,128)(2,1)} %collective-permute-done.11.refs_3_.refs_1_, ...), custom_call_target="tpu_custom_call" | custom-call | flops 10737418240 | bytes 22151168 | tf_op jit(solution)/shard_map/expert_out_grad/pallas_call | solution.py:336
  348.3 18.2 %expert_in_grad.3 = (bf16[2,2,320,896]{3,2,1,0:T(8,128)(2,1)}, bf16[2,2,320,896]{3,2,1,0:T(8,128)(2,1)}, bf16[1280,128]{1,0:T(8,128)(2,1)}) custom-call(s32[1]{0:T(128)} %bitcast.43.core_ref, bf16[256,1280]{1,0:T(8,128)(2,1)} %collective-permute-done.15.refs_0_, bf16[256,1280]{1,0:T(8,128)(2,1)} %collective-permute-done.7.refs_1_, ...), custom_call_target="tpu_custom_call" | custom-call | flops 10737418240 | bytes 22151168 | tf_op jit(solution)/shard_map/expert_in_grad/pallas_call | solution.py:283
  366.6 18.7 %expert_in_grad.2 = (bf16[2,2,320,896]{3,2,1,0:T(8,128)(2,1)}, bf16[2,2,320,896]{3,2,1,0:T(8,128)(2,1)}, bf16[1280,128]{1,0:T(8,128)(2,1)}) custom-call(s32[1]{0:T(128)} %bitcast.43.core_ref, bf16[256,1280]{1,0:T(8,128)(2,1)} %collective-permute-done.15.refs_0_, bf16[256,1280]{1,0:T(8,128)(2,1)} %collective-permute-done.7.refs_1_, ...), custom_call_target="tpu_custom_call" | custom-call | flops 10737418240 | bytes 22151168 | tf_op jit(solution)/shard_map/expert_in_grad/pallas_call | solution.py:283
  402.4 12.4 %collective-permute-done.26 = bf16[256,1280]{1,0:T(8,128)(2,1)S(1)} collective-permute-done((bf16[256,1280]{1,0:T(8,128)(2,1)S(1)}, bf16[256,1280]{1,0:T(8,128)(2,1)S(1)}, u32[]{:S(2)}, u32[]{:S(2)}) %collective-permute-start.26) | collective-permute-done | bytes 655392 | tf_op jit(solution)/shard_map/ppermute | solution.py:65
  417.9 13.5 %collective-permute-done.29 = bf16[256,1280]{1,0:T(8,128)(2,1)S(1)} collective-permute-done((bf16[256,1280]{1,0:T(8,128)(2,1)S(1)}, bf16[256,1280]{1,0:T(8,128)(2,1)S(1)}, u32[]{:S(2)}, u32[]{:S(2)}) %collective-permute-start.29) | collective-permute-done | bytes 655392 | tf_op jit(solution)/shard_map/ppermute | solution.py:62
  433.9 15.1 %collective-permute-done.23 = bf16[256,1280]{1,0:T(8,128)(2,1)S(1)} collective-permute-done((bf16[256,1280]{1,0:T(8,128)(2,1)S(1)}, bf16[256,1280]{1,0:T(8,128)(2,1)S(1)}, u32[]{:S(2)}, u32[]{:S(2)}) %collective-permute-start.23) | collective-permute-done | bytes 655392 | tf_op jit(solution)/shard_map/ppermute | solution.py:62
  450.7 10.4 %collective-permute-done.30 = bf16[256,1280]{1,0:T(8,128)(2,1)S(1)} collective-permute-done((bf16[256,1280]{1,0:T(8,128)(2,1)S(1)}, bf16[256,1280]{1,0:T(8,128)(2,1)S(1)}, u32[]{:S(2)}, u32[]{:S(2)}) %collective-permute-start.30) | collective-permute-done | bytes 655392 | tf_op jit(solution)/shard_map/ppermute | solution.py:62
  480.2 9.7 %collective-permute-done.34 = bf16[256,1280]{1,0:T(8,128)(2,1)S(1)} collective-permute-done((bf16[256,1280]{1,0:T(8,128)(2,1)S(1)}, bf16[256,1280]{1,0:T(8,128)(2,1)S(1)}, u32[]{:S(2)}, u32[]{:S(2)}) %collective-permute-start.34) | collective-permute-done | bytes 655392 | tf_op jit(solution)/shard_map/ppermute | solution.py:65
  533.3 11.0 %multiply_reduce_fusion = (f32[2048]{0:T(1024)S(1)}, f32[2048,2048]{0,1:T(8,128)}) fusion(f32[2048,2048]{0,1:T(8,128)} %get-tuple-element.177, f32[2048]{0:T(1024)S(1)} %log_add_fusion, bf16[2048,128]{1,0:T(8,128)(2,1)S(1)} %bitcast.154, f32[2048,384]{0,1:T(8,128)} %copy-done.22), kind=kOutput, calls=%fused_computation.5 | convolution fusion | flops 1086322688 | bytes 34619392 | tf_op jit(solution)/shard_map/dot_general | solution.py:17
  544.3 12.3 %multiply_convert_fusion = bf16[2048,2048]{0,1:T(8,128)(2,1)S(1)} fusion(f32[2048,2048]{0,1:T(8,128)} %get-tuple-element.185, f32[2048,2048]{0,1:T(8,128)} %get-tuple-element.177, f32[2048]{0:T(1024)S(1)} %get-tuple-element.184, f32[2048]{0:T(1024)S(1)} %log_add_fusion), kind=kLoop, calls=%fused_computation.4 | loop fusion | flops 16777216 | bytes 41959424 | tf_op jit(solution)/shard_map/convert_element_type | solution.py:135
  579.4 8.7 %fusion.13 = bf16[2048,384]{0,1:T(8,128)(2,1)S(1)} fusion(bf16[2048,384]{0,1:T(8,128)(2,1)S(1)} %get-tuple-element.150, bf16[2048,128]{1,0:T(8,128)(2,1)S(1)} %bitcast.155, f32[2048,2048]{0,1:T(8,128)} %get-tuple-element.177, f32[2048]{0:T(1024)S(1)} %log_add_fusion), kind=kOutput, calls=%fused_computation.43 | convolution fusion | flops 1082392576 | bytes 17833984 | tf_op jit(solution)/shard_map/dot_general | solution.py:17
  661.0 13.0 %collective-permute-done.38 = bf16[256,1280]{1,0:T(8,128)(2,1)S(1)} collective-permute-done((bf16[256,1280]{1,0:T(8,128)(2,1)S(1)}, bf16[256,1280]{1,0:T(8,128)(2,1)S(1)}, u32[]{:S(2)}, u32[]{:S(2)}) %collective-permute-start.38) | collective-permute-done | bytes 655392 | tf_op jit(solution)/shard_map/ppermute | solution.py:62
  696.1 14.7 %all-to-all-done.4 = bf16[8,40,1632]{2,1,0:T(8,128)(2,1)} async-done(((bf16[8,40,1632]{2,1,0:T(8,128)(2,1)}), bf16[8,40,1632]{2,1,0:T(8,128)(2,1)}, u32[]{:S(2)}, u32[]{:S(2)}) %all-to-all-start.4) | async-done | bytes 1044512 | tf_op jit(solution)/shard_map/all_to_all | solution.py:590
  (537 shorter events, 377.8 us)
Async XLA Ops:
  0.7 79.0 %collective-permute-start.17 = (bf16[256,1280]{1,0:T(8,128)(2,1)}, bf16[256,1280]{1,0:T(8,128)(2,1)}, u32[]{:S(2)}, u32[]{:S(2)}) collective-permute-start(bf16[256,1280]{1,0:T(8,128)(2,1)} %refs_6_.1), channel_id=1, source_target_pairs={{2,0},{4,2},{6,4},{7,6},{5,7},{3,5},{1,3},{0,1},{10,8},{12,10},{14... | collective-permute-start | bytes 1966088 | tf_op jit(solution)/shard_map/ppermute | solution.py:50
  2.3 52.7 %collective-permute-start.11 = (bf16[256,1280]{1,0:T(8,128)(2,1)}, bf16[256,1280]{1,0:T(8,128)(2,1)}, u32[]{:S(2)}, u32[]{:S(2)}) collective-permute-start(bf16[256,1280]{1,0:T(8,128)(2,1)} %refs_6_.1), channel_id=1, source_target_pairs={{0,2},{2,4},{4,6},{6,7},{7,5},{5,3},{3,1},{1,0},{8,10},{10,12},{12... | collective-permute-start | bytes 1966088 | tf_op jit(solution)/shard_map/ppermute | solution.py:47
  7.8 46.7 %collective-permute-start.3 = (bf16[256,1280]{1,0:T(8,128)(2,1)}, bf16[256,1280]{1,0:T(8,128)(2,1)}, u32[]{:S(2)}, u32[]{:S(2)}) collective-permute-start(bf16[256,1280]{1,0:T(8,128)(2,1)} %get-tuple-element.100), channel_id=1, source_target_pairs={{0,2},{2,4},{4,6},{6,7},{7,5},{5,3},{3,1},{1,0},{8,10},{10,12},{12... | collective-permute-start | bytes 1966088 | tf_op jit(solution)/shard_map/ppermute | solution.py:47
  7.9 49.2 %collective-permute-start = (bf16[256,1280]{1,0:T(8,128)(2,1)}, bf16[256,1280]{1,0:T(8,128)(2,1)}, u32[]{:S(2)}, u32[]{:S(2)}) collective-permute-start(bf16[256,1280]{1,0:T(8,128)(2,1)} %get-tuple-element.100), channel_id=1, source_target_pairs={{2,0},{4,2},{6,4},{7,6},{5,7},{3,5},{1,3},{0,1},{10,8},{12,10},{14... | collective-permute-start | bytes 1966088 | tf_op jit(solution)/shard_map/ppermute | solution.py:50
  10.4 67.3 %all-to-all-start.1 = ((f32[8,2,256]{2,1,0:T(2,128)}), f32[8,2,256]{2,1,0:T(2,128)S(1)}, u32[]{:S(2)}, u32[]{:S(2)}) async-start(f32[8,2,256]{2,1,0:T(2,128)} %reshape.428), calls=%async_computation.1 | async-start | bytes 32768 | tf_op jit(solution)/shard_map/all_to_all | solution.py:411
  55.0 31.5 %collective-permute-start.12 = (bf16[256,1280]{1,0:T(8,128)(2,1)}, bf16[256,1280]{1,0:T(8,128)(2,1)}, u32[]{:S(2)}, u32[]{:S(2)}) collective-permute-start(bf16[256,1280]{1,0:T(8,128)(2,1)} %collective-permute-done.11.refs_3_.refs_1_), channel_id=1, source_target_pairs={{0,2},{2,4},{4,6},{6,7},{7,5},{5,3},{3,1},{1,0},{8,10},{10,12},{12... | collective-permute-start | bytes 1966088 | tf_op jit(solution)/shard_map/ppermute | solution.py:47
  102.5 196.9 %collective-permute-start.21 = (bf16[256,1280]{1,0:T(8,128)(2,1)}, bf16[256,1280]{1,0:T(8,128)(2,1)}, u32[]{:S(2)}, u32[]{:S(2)}) collective-permute-start(bf16[256,1280]{1,0:T(8,128)(2,1)} %collective-permute-done.18.refs_1_.refs_7_), channel_id=1, source_target_pairs={{2,0},{4,2},{6,4},{7,6},{5,7},{3,5},{1,3},{0,1},{10,8},{12,10},{14... | collective-permute-start | bytes 1966088 | tf_op jit(solution)/shard_map/ppermute | solution.py:50
  114.6 159.1 %collective-permute-start.14 = (bf16[256,1280]{1,0:T(8,128)(2,1)}, bf16[256,1280]{1,0:T(8,128)(2,1)}, u32[]{:S(2)}, u32[]{:S(2)}) collective-permute-start(bf16[256,1280]{1,0:T(8,128)(2,1)} %collective-permute-done.13.refs_3_), channel_id=1, source_target_pairs={{0,2},{2,4},{4,6},{6,7},{7,5},{5,3},{3,1},{1,0},{8,10},{10,12},{12... | collective-permute-start | bytes 1966088 | tf_op jit(solution)/shard_map/ppermute | solution.py:47
  201.0 29.8 %collective-permute-start.15 = (bf16[256,1280]{1,0:T(8,128)(2,1)S(1)}, bf16[256,1280]{1,0:T(8,128)(2,1)}, u32[]{:S(2)}, u32[]{:S(2)}) collective-permute-start(bf16[256,1280]{1,0:T(8,128)(2,1)S(1)} %multiply_convert_fusion.4.refs_0_.refs_6_), channel_id=1, source_target_pairs={{2,0},{4,2},{6,4},{7,6},{5,7},{3,5},{1,3},{0,1},{10,8},{12,10},{14... | collective-permute-start | bytes 1966088 | tf_op jit(solution)/shard_map/ppermute | solution.py:50
  257.4 43.9 %collective-permute-start.20 = (bf16[256,1280]{1,0:T(8,128)(2,1)S(1)}, bf16[256,1280]{1,0:T(8,128)(2,1)}, u32[]{:S(2)}, u32[]{:S(2)}) collective-permute-start(bf16[256,1280]{1,0:T(8,128)(2,1)S(1)} %collective-permute-done.16.refs_0_.refs_7_), channel_id=1, source_target_pairs={{2,0},{4,2},{6,4},{7,6},{5,7},{3,5},{1,3},{0,1},{10,8},{12,10},{14... | collective-permute-start | bytes 1966088 | tf_op jit(solution)/shard_map/ppermute | solution.py:50
  297.2 100.5 %collective-permute-start.19 = (bf16[256,1280]{1,0:T(8,128)(2,1)}, bf16[256,1280]{1,0:T(8,128)(2,1)}, u32[]{:S(2)}, u32[]{:S(2)}) collective-permute-start(bf16[256,1280]{1,0:T(8,128)(2,1)} %get-tuple-element.65), channel_id=1, source_target_pairs={{0,2},{2,4},{4,6},{6,7},{7,5},{5,3},{3,1},{1,0},{8,10},{10,12},{12... | collective-permute-start | bytes 1966088 | tf_op jit(solution)/shard_map/ppermute | solution.py:62
  297.3 99.0 %collective-permute-start.25 = (bf16[256,1280]{1,0:T(8,128)(2,1)}, bf16[256,1280]{1,0:T(8,128)(2,1)}, u32[]{:S(2)}, u32[]{:S(2)}) collective-permute-start(bf16[256,1280]{1,0:T(8,128)(2,1)} %get-tuple-element.72), channel_id=1, source_target_pairs={{2,0},{4,2},{6,4},{7,6},{5,7},{3,5},{1,3},{0,1},{10,8},{12,10},{14... | collective-permute-start | bytes 1966088 | tf_op jit(solution)/shard_map/ppermute | solution.py:65
  299.3 101.3 %collective-permute-start.28 = (bf16[256,1280]{1,0:T(8,128)(2,1)}, bf16[256,1280]{1,0:T(8,128)(2,1)}, u32[]{:S(2)}, u32[]{:S(2)}) collective-permute-start(bf16[256,1280]{1,0:T(8,128)(2,1)} %get-tuple-element.76), channel_id=1, source_target_pairs={{0,2},{2,4},{4,6},{6,7},{7,5},{5,3},{3,1},{1,0},{8,10},{10,12},{12... | collective-permute-start | bytes 1966088 | tf_op jit(solution)/shard_map/ppermute | solution.py:62
  299.4 95.2 %collective-permute-start.32 = (bf16[256,1280]{1,0:T(8,128)(2,1)}, bf16[256,1280]{1,0:T(8,128)(2,1)}, u32[]{:S(2)}, u32[]{:S(2)}) collective-permute-start(bf16[256,1280]{1,0:T(8,128)(2,1)} %get-tuple-element.80), channel_id=1, source_target_pairs={{2,0},{4,2},{6,4},{7,6},{5,7},{3,5},{1,3},{0,1},{10,8},{12,10},{14... | collective-permute-start | bytes 1966088 | tf_op jit(solution)/shard_map/ppermute | solution.py:65
  348.3 38.4 %collective-permute-start.48 = (bf16[2,28,1280]{2,1,0:T(8,128)(2,1)}, bf16[2,28,1280]{2,1,0:T(8,128)(2,1)}, u32[]{:S(2)}, u32[]{:S(2)}) collective-permute-start(bf16[2,28,1280]{2,1,0:T(8,128)(2,1)} %dynamic-slice_bitcast_fusion.2), channel_id=1, source_target_pairs={{0,8},{8,0},{16,24},{24,16},{1,9},{9,1},{17,25},{25,17},{2,10},{10... | collective-permute-start | bytes 430088 | tf_op jit(solution)/shard_map/ppermute | solution.py:80
  394.3 68.6 %collective-permute-start.54 = (bf16[2,2,224,1280]{3,2,1,0:T(8,128)(2,1)S(1)}, bf16[2,2,224,1280]{3,2,1,0:T(8,128)(2,1)S(1)}, u32[]{:S(2)}, u32[]{:S(2)}) collective-permute-start(bf16[2,2,224,1280]{3,2,1,0:T(8,128)(2,1)S(1)} %copy-done.127), channel_id=1, source_target_pairs={{0,8},{8,0},{16,24},{24,16},{1,9},{9,1},{17,25},{25,17},{2,10},{10... | collective-permute-start | bytes 6881288 | tf_op jit(solution)/shard_map/ppermute | solution.py:89
  394.6 69.5 %collective-permute-start.52 = (bf16[2,2,320,896]{3,2,1,0:T(8,128)(2,1)}, bf16[2,2,320,896]{3,2,1,0:T(8,128)(2,1)S(1)}, u32[]{:S(2)}, u32[]{:S(2)}) collective-permute-start(bf16[2,2,320,896]{3,2,1,0:T(8,128)(2,1)} %get-tuple-element.92), channel_id=1, source_target_pairs={{0,8},{8,0},{16,24},{24,16},{1,9},{9,1},{17,25},{25,17},{2,10},{10... | collective-permute-start | bytes 6881288 | tf_op jit(solution)/shard_map/ppermute | solution.py:89
  396.3 71.8 %collective-permute-start.50 = (bf16[2,2,320,896]{3,2,1,0:T(8,128)(2,1)S(1)}, bf16[2,2,320,896]{3,2,1,0:T(8,128)(2,1)S(1)}, u32[]{:S(2)}, u32[]{:S(2)}) collective-permute-start(bf16[2,2,320,896]{3,2,1,0:T(8,128)(2,1)S(1)} %copy-done.128), channel_id=1, source_target_pairs={{0,8},{8,0},{16,24},{24,16},{1,9},{9,1},{17,25},{25,17},{2,10},{10... | collective-permute-start | bytes 6881288 | tf_op jit(solution)/shard_map/ppermute | solution.py:89
  468.1 58.3 %collective-permute-start.55 = (bf16[1,2,224,1280]{3,2,1,0:T(8,128)(2,1)}, bf16[1,2,224,1280]{3,2,1,0:T(8,128)(2,1)}, u32[]{:S(2)}, u32[]{:S(2)}) collective-permute-start(bf16[1,2,224,1280]{3,2,1,0:T(8,128)(2,1)} %add_convert_fusion.1), channel_id=1, source_target_pairs={{0,16},{8,24},{16,0},{24,8},{1,17},{9,25},{17,1},{25,9},{2,18},{10... | collective-permute-start | bytes 3440648 | tf_op jit(solution)/shard_map/ppermute | solution.py:101
  478.8 121.0 %collective-permute-start.53 = (bf16[1,2,320,896]{3,2,1,0:T(8,128)(2,1)}, bf16[1,2,320,896]{3,2,1,0:T(8,128)(2,1)}, u32[]{:S(2)}, u32[]{:S(2)}) collective-permute-start(bf16[1,2,320,896]{3,2,1,0:T(8,128)(2,1)} %add_convert_fusion.3), channel_id=1, source_target_pairs={{0,16},{8,24},{16,0},{24,8},{1,17},{9,25},{17,1},{25,9},{2,18},{10... | collective-permute-start | bytes 3440648 | tf_op jit(solution)/shard_map/ppermute | solution.py:101
  489.9 115.0 %collective-permute-start.51 = (bf16[1,2,320,896]{3,2,1,0:T(8,128)(2,1)}, bf16[1,2,320,896]{3,2,1,0:T(8,128)(2,1)}, u32[]{:S(2)}, u32[]{:S(2)}) collective-permute-start(bf16[1,2,320,896]{3,2,1,0:T(8,128)(2,1)} %add_convert_fusion.5), channel_id=1, source_target_pairs={{0,16},{8,24},{16,0},{24,8},{1,17},{9,25},{17,1},{25,9},{2,18},{10... | collective-permute-start | bytes 3440648 | tf_op jit(solution)/shard_map/ppermute | solution.py:101
  520.3 94.7 %collective-permute-start.44 = (bf16[2,320,1408]{2,1,0:T(8,128)(2,1)}, bf16[2,320,1408]{2,1,0:T(8,128)(2,1)}, u32[]{:S(2)}, u32[]{:S(2)}) collective-permute-start(bf16[2,320,1408]{2,1,0:T(8,128)(2,1)} %fusion.27), channel_id=1, source_target_pairs={{0,8},{8,0},{16,24},{24,16},{1,9},{9,1},{17,25},{25,17},{2,10},{10... | collective-permute-start | bytes 5406728 | tf_op jit(solution)/shard_map/ppermute | solution.py:80
  637.2 41.6 %all-to-all-start.3 = ((bf16[8,40,1152]{2,1,0:T(8,128)(2,1)}), bf16[8,40,1152]{2,1,0:T(8,128)(2,1)}, u32[]{:S(2)}, u32[]{:S(2)}) async-start(bf16[8,40,1152]{2,1,0:T(8,128)(2,1)} %bitcast.157), calls=%async_computation.3 | async-start | bytes 1474560 | tf_op jit(solution)/shard_map/all_to_all | solution.py:590
  678.9 31.9 %all-to-all-start.4 = ((bf16[8,40,1632]{2,1,0:T(8,128)(2,1)}), bf16[8,40,1632]{2,1,0:T(8,128)(2,1)}, u32[]{:S(2)}, u32[]{:S(2)}) async-start(bf16[8,40,1632]{2,1,0:T(8,128)(2,1)} %pad_maximum_fusion.2), calls=%async_computation.4 | async-start | bytes 2129920 | tf_op jit(solution)/shard_map/all_to_all | solution.py:590
  (168 other events, 2826.8 us)

commit v3 on v2

--- a/solution.py
+++ b/solution.py
@@ -17,15 +17,6 @@
     return lax.dot_general(a, b, ((contract[:1], contract[1:]), ((), ())), preferred_element_type=FLOAT)
 
 
-def rotate(values, cosine, sine):
-    half = values.shape[-1] // 2
-    first = values[..., :half]
-    second = values[..., half:]
-    return jnp.concatenate(
-        [first * cosine - second * sine, second * cosine + first * sine], axis=-1
-    )
-
-
 def ring_order(count):
     return list(range(0, count, 2)) + list(range(count - 1, 0, -2))
 
@@ -37,35 +28,49 @@
     return ahead, back
 
 
-def ring_gather(block):
+def after(value, *others):
+    return lax.optimization_barrier((value, others))[0]
+
+
+def ring_gather(block, work=None):
     count = lax.axis_size("narrow")
     ahead, back = ring_steps(count)
     slots = [None] * count
     slots[0] = block
     forward = backward = block
+    done = ()
     for step in range(1, count // 2 + 1):
-        forward = lax.ppermute(forward, "narrow", ahead)
+        sent_ahead, sent_back = after((forward, backward), *done)
+        forward = lax.ppermute(sent_ahead, "narrow", ahead)
+        if step < count // 2:
+            backward = lax.ppermute(sent_back, "narrow", back)
+        done = work(step - 1, slots) if work else ()
         slots[count - step] = forward
         if step < count // 2:
-            backward = lax.ppermute(backward, "narrow", back)
             slots[step] = backward
     return slots
 
 
-def ring_scatter(parts):
+def ring_scatter(parts, work=None):
     count = lax.axis_size("narrow")
     ahead, back = ring_steps(count)
     half = count // 2
-    forward = parts[half].astype(HALF)
-    backward = parts[half + 1].astype(HALF)
+    forward, backward = parts[half], parts[half + 1]
+    before = done = ()
     for step in range(1, half + 1):
-        forward = lax.ppermute(forward, "narrow", ahead).astype(FLOAT)
+        forward, backward = after((forward, backward), *before)
+        before = done
+        forward = lax.ppermute(forward, "narrow", ahead)
         if step < half:
-            forward = (forward + parts[half - step].astype(FLOAT)).astype(HALF)
-            backward = lax.ppermute(backward, "narrow", back).astype(FLOAT)
+            backward = lax.ppermute(backward, "narrow", back)
+        done = work(step, (forward, backward)) if work else ()
+        if step < half:
+            forward = (forward.astype(FLOAT) + parts[half - step].astype(FLOAT)).astype(HALF)
             if step < half - 1:
-                backward = (backward + parts[half + 1 + step].astype(FLOAT)).astype(HALF)
-    return parts[0].astype(FLOAT) + forward + backward
+                backward = (
+                    backward.astype(FLOAT) + parts[half + 1 + step].astype(FLOAT)
+                ).astype(HALF)
+    return parts[0].astype(FLOAT) + forward.astype(FLOAT) + backward.astype(FLOAT)
 
 
 def wide_scatter(chunks):
@@ -108,35 +113,6 @@
 def norm_back(grad_out, normed, inv_scale, gain):
     scaled = grad_out * gain
     return inv_scale * (scaled - normed * jnp.mean(scaled * normed, axis=1, keepdims=True))
-
-
-def causal_attention(queries, keys, values, query_pos, key_pos):
-    scores = jnp.einsum("qd,kd->qk", queries, keys, preferred_element_type=FLOAT)
-    scores = jnp.where(
-        query_pos[:, None] >= key_pos[None, :], scores * HEAD_DIM**-0.5, -1e30
-    )
-    peak = jnp.max(scores, axis=1, keepdims=True)
-    shifted = jnp.exp(scores - peak)
-    total = jnp.sum(shifted, axis=1, keepdims=True)
-    low = (shifted / total).astype(HALF)
-    out = matmul(low, values, (1, 0)).astype(HALF)
-    return out, peak + jnp.log(total)
-
-
-def causal_back(queries, keys, values, query_pos, key_pos, log_total, out_grad):
-    scores = jnp.einsum("qd,kd->qk", queries, keys, preferred_element_type=FLOAT)
-    scores = jnp.where(
-        query_pos[:, None] >= key_pos[None, :], scores * HEAD_DIM**-0.5, -1e30
-    )
-    probs = jnp.exp(scores - log_total)
-    prob_grad = matmul(out_grad, values, (1, 1))
-    score_grad = (
-        probs * (prob_grad - jnp.sum(prob_grad * probs, axis=1, keepdims=True))
-    ).astype(HALF)
-    value_grad = matmul(probs.astype(HALF), out_grad, (0, 0))
-    query_grad = matmul(score_grad, keys, (1, 0)) * HEAD_DIM**-0.5
-    key_grad = matmul(score_grad, queries, (0, 0)) * HEAD_DIM**-0.5
-    return query_grad, key_grad, value_grad
 
 
 VMEM_LIMIT = 60 * 2**20
@@ -229,6 +205,50 @@
     )(*xs, *cs, *gates, gate_w, up_w, down_w, *(kept if chained else ()))
 
 
+def pack_experts_kernel(units, choice, shared_gate, shared_up, shared_down, gate, up, down, *rest):
+    gate_out, up_out, down_out, sems = rest
+    experts = gate.shape[0]
+    per_expert = gate_out.shape[1] // experts
+    copies = []
+    for e in range(experts):
+        own = pl.ds(e * per_expert, units)
+        for source, target in (
+            (gate.at[e], gate_out.at[:, own]),
+            (up.at[e], up_out.at[:, own]),
+            (down.at[e], down_out.at[own]),
+        ):
+            copies.append(pltpu.make_async_copy(source, target, sems.at[len(copies)]))
+    start_all(copies)
+    for e in range(experts):
+        gap = slice(e * per_expert + units, (e + 1) * per_expert)
+        if e == 0:
+            gate_out[:, gap] = matmul(shared_gate[...], choice[...], (1, 0)).astype(HALF)
+            up_out[:, gap] = matmul(shared_up[...], choice[...], (1, 0)).astype(HALF)
+            down_out[gap] = matmul(choice[...], shared_down[...], (0, 0)).astype(HALF)
+        else:
+            gate_out[:, gap] = jnp.zeros((gate_out.shape[0], per_expert - units), HALF)
+            up_out[:, gap] = jnp.zeros((up_out.shape[0], per_expert - units), HALF)
+            down_out[gap] = jnp.zeros((per_expert - units, down_out.shape[1]), HALF)
+    wait_all(copies)
+
+
+def pack_experts(per_expert, choice, shared_gate, shared_up, shared_down, gate, up, down):
+    experts, width, units = gate.shape
+    padded = experts * per_expert
+    anywhere = pl.BlockSpec(memory_space=pl.ANY)
+    shapes = [(width, padded), (width, padded), (padded, width)]
+    return pl.pallas_call(
+        functools.partial(pack_experts_kernel, units),
+        in_specs=[pl.BlockSpec(memory_space=pltpu.VMEM)] * 4 + [anywhere] * 3,
+        out_specs=[pl.BlockSpec(memory_space=pltpu.VMEM)] * 3,
+        out_shape=[jax.ShapeDtypeStruct(shape, HALF) for shape in shapes],
+        scratch_shapes=[pltpu.SemaphoreType.DMA((3 * experts,))],
+        compiler_params=pltpu.CompilerParams(vmem_limit_bytes=VMEM_LIMIT),
+        cost_estimate=pl.CostEstimate(flops=0, bytes_accessed=12 * width * padded, transcendentals=0),
+        name="pack_experts",
+    )(choice, shared_gate, shared_up, shared_down, gate, up, down)
+
+
 def fetch_rows(slots, rows, sems):
     length = slots[0].shape[0]
     copies = [
@@ -354,6 +374,352 @@
         ),
         name="expert_out_grad",
     )(core, *slots, inner)
+
+
+def turn(values, cosine, sine):
+    return values * cosine + pltpu.roll(values, HEAD_DIM // 2, 1) * sine
+
+
+def head_slice(index):
+    return slice(index * HEAD_DIM, (index + 1) * HEAD_DIM)
+
+
+def start_all(copies):
+    for copy in copies:
+        copy.start()
+
+
+def wait_all(copies):
+    for copy in copies:
+        copy.wait()
+
+
+def pack_heads_kernel(spare, place_ref, query, key, value, out, sems):
+    width = query.shape[1]
+    own = pl.ds(pl.multiple_of(place_ref[0] * HEAD_DIM, HEAD_DIM), HEAD_DIM)
+    rest = pl.ds(width - spare * HEAD_DIM, spare * HEAD_DIM)
+    pieces = [
+        (query, own, 1),
+        (key, own, 1),
+        (key, rest, spare),
+        (value, own, 1),
+        (value, rest, spare),
+        (query, rest, spare),
+    ]
+    copies, tile = [], 0
+    for i, (source, columns, tiles) in enumerate(pieces):
+        target = out.at[:, pl.ds(tile * HEAD_DIM, tiles * HEAD_DIM)]
+        copies.append(pltpu.make_async_copy(source.at[:, columns], target, sems.at[i]))
+        tile += tiles
+    start_all(copies)
+    wait_all(copies)
+
+
+def pack_heads(place, spare, query, key, value):
+    width = query.shape[0]
+    columns = (3 + 3 * spare) * HEAD_DIM
+    anywhere = pl.BlockSpec(memory_space=pl.ANY)
+    return pl.pallas_call(
+        functools.partial(pack_heads_kernel, spare),
+        grid_spec=pltpu.PrefetchScalarGridSpec(
+            num_scalar_prefetch=1,
+            grid=(1,),
+            in_specs=[anywhere] * 3,
+            out_specs=whole_block((width, columns)),
+            scratch_shapes=[pltpu.SemaphoreType.DMA((6,))],
+        ),
+        out_shape=jax.ShapeDtypeStruct((width, columns), HALF),
+        compiler_params=pltpu.CompilerParams(vmem_limit_bytes=VMEM_LIMIT),
+        cost_estimate=pl.CostEstimate(flops=0, bytes_accessed=4 * width * columns, transcendentals=0),
+        name="pack_heads",
+    )(place, query, key, value)
+
+
+def project_kernel(turned, tiles, chained, block_ref, *refs):
+    x, weight, cosine, sine = refs[:4]
+    outs = refs[5 if chained else 4 :]
+    lin = matmul(x[...], weight[...], (1, 0))
+    for tile in range(weight.shape[1] // HEAD_DIM):
+        part = lin[:, head_slice(tile)]
+        if tile < turned or tile >= tiles:
+            part = turn(part, cosine[0], sine[0])
+        if tile < tiles:
+            outs[0][0, :, head_slice(tile)] = part.astype(HALF)
+        else:
+            outs[1][:, head_slice(tile - tiles)] = part.astype(HALF)
+
+
+def project(blocks, slot, x, weight, cosine, sine, turned, tiles, packed):
+    length, width = x.shape
+    count = cosine.shape[0]
+    extra = weight.shape[1] - tiles * HEAD_DIM if packed is None else 0
+    columns = tiles * HEAD_DIM + extra
+    chained = packed is not None
+    table = pl.BlockSpec((1, length, HEAD_DIM), lambda i, b: (b[slot], 0, 0))
+    packed_shape = (count, length, tiles * HEAD_DIM)
+    out_specs = [pl.BlockSpec((1,) + packed_shape[1:], lambda i, b: (b[slot], 0, 0))]
+    out_shape = [jax.ShapeDtypeStruct(packed_shape, HALF)]
+    if extra:
+        out_specs.append(whole_block((length, extra)))
+        out_shape.append(jax.ShapeDtypeStruct((length, extra), HALF))
+    return pl.pallas_call(
+        functools.partial(project_kernel, turned, tiles, chained),
+        grid_spec=pltpu.PrefetchScalarGridSpec(
+            num_scalar_prefetch=1,
+            grid=(1,),
+            in_specs=[whole_block(x.shape), whole_block((width, columns)), table, table]
+            + ([pl.BlockSpec(memory_space=pl.ANY)] if chained else []),
+            out_specs=out_specs,
+        ),
+        out_shape=out_shape,
+        input_output_aliases={5: 0} if chained else {},
+        compiler_params=pltpu.CompilerParams(vmem_limit_bytes=VMEM_LIMIT),
+        cost_estimate=pl.CostEstimate(
+            flops=2 * length * width * columns,
+            bytes_accessed=2 * (length * width + (length + width) * columns),
+            transcendentals=0,
+        ),
+        name="project",
+    )(blocks, x, weight, cosine, sine, *([packed] if chained else []))
+
+
+EXP_SCALE = HEAD_DIM**-0.5 * 1.4426950408889634
+
+
+def masked_scores(query, keys, first):
+    scores = matmul(query, keys, (1, 1)) * EXP_SCALE
+    row = lax.broadcasted_iota(jnp.int32, scores.shape, 0)
+    column = lax.broadcasted_iota(jnp.int32, scores.shape, 1)
+    return jnp.where(column <= row + first, scores, -1e30)
+
+
+def attend(query, keys, values, first):
+    scores = masked_scores(query, keys, first)
+    peak = jnp.max(scores, axis=1, keepdims=True)
+    shifted = jnp.exp2(scores - peak)
+    total = jnp.sum(shifted, axis=1, keepdims=True)
+    out = matmul(shifted.astype(HALF), values, (1, 0)) / total
+    level = jnp.broadcast_to(peak + jnp.log2(total), (query.shape[0], HEAD_DIM))
+    return out.astype(HALF), level
+
+
+def attention_kernel(spare, place_ref, packed, spare_q, out, spare_out, level, spare_level):
+    count, length = packed.shape[:2]
+    keys_at, values_at = head_slice(1), head_slice(2 + spare)
+
+    def rows(columns, blocks):
+        return packed[:blocks, :, columns].reshape(blocks * length, HEAD_DIM)
+
+    for block in range(count):
+        out[block], level[block] = attend(
+            packed[block, :, head_slice(0)],
+            rows(keys_at, block + 1),
+            rows(values_at, block + 1),
+            block * length,
+        )
+    for head in range(spare):
+        spare_out[:, head_slice(head)], spare_level[head] = attend(
+            spare_q[:, head_slice(head)],
+            rows(head_slice(2 + head), count),
+            rows(head_slice(3 + spare + head), count),
+            place_ref[0] * length,
+        )
+
+
+def attention(place, packed, spare_q):
+    count, length, columns = packed.shape
+    spare = spare_q.shape[1] // HEAD_DIM
+    area = (count * (count + 1) // 2 + spare * count) * length * length
+    shapes = [
+        ((count, length, HEAD_DIM), HALF),
+        (spare_q.shape, HALF),
+        ((count, length, HEAD_DIM), FLOAT),
+        ((spare, length, HEAD_DIM), FLOAT),
+    ]
+    return pl.pallas_call(
+        functools.partial(attention_kernel, spare),
+        grid_spec=pltpu.PrefetchScalarGridSpec(
+            num_scalar_prefetch=1,
+            grid=(1,),
+            in_specs=[whole_block(packed.shape), whole_block(spare_q.shape)],
+            out_specs=[whole_block(shape) for shape, _ in shapes],
+        ),
+        out_shape=[jax.ShapeDtypeStruct(shape, kind) for shape, kind in shapes],
+        compiler_params=pltpu.CompilerParams(vmem_limit_bytes=VMEM_LIMIT),
+        cost_estimate=pl.CostEstimate(
+            flops=8 * area * HEAD_DIM, bytes_accessed=4 * count * length * columns, transcendentals=area
+        ),
+        name="attention",
+    )(place, packed, spare_q)
+
+
+def attend_back(query, keys, values, first, level, out, out_grad):
+    scores = masked_scores(query, keys, first)
+    probs = jnp.exp2(scores - level[:, :1])
+    prob_grad = matmul(out_grad, values, (1, 1))
+    shared = jnp.sum(out_grad.astype(FLOAT) * out.astype(FLOAT), axis=1, keepdims=True)
+    score_grad = (probs * (prob_grad - shared)).astype(HALF)
+    value_grad = matmul(probs.astype(HALF), out_grad, (0, 0))
+    query_grad = matmul(score_grad, keys, (1, 0)) * HEAD_DIM**-0.5
+    key_grad = matmul(score_grad, query, (0, 0)) * HEAD_DIM**-0.5
+    return query_grad, key_grad, value_grad
+
+
+def attention_back_kernel(
+    spare, place_ref, packed, spare_q, out, spare_out, level, spare_level, out_grad, spare_out_grad,
+    cosine, sine, grad, spare_grad, key_sum, value_sum
+):
+    count, length = packed.shape[:2]
+    keys_at, values_at = head_slice(1), head_slice(2 + spare)
+
+    def rows(columns, blocks):
+        return packed[:blocks, :, columns].reshape(blocks * length, HEAD_DIM)
+
+    key_sum[...] = jnp.zeros_like(key_sum)
+    value_sum[...] = jnp.zeros_like(value_sum)
+    for block in range(count):
+        query_grad, key_grad, value_grad = attend_back(
+            packed[block, :, head_slice(0)],
+            rows(keys_at, block + 1),
+            rows(values_at, block + 1),
+            block * length,
+            level[block],
+            out[block],
+            out_grad[block],
+        )
+        grad[block, :, head_slice(0)] = turn(query_grad, cosine[block], -sine[block]).astype(HALF)
+        seen = (block + 1) * length
+        key_sum[:seen] += key_grad
+        value_sum[:seen] += value_grad
+
+    def put(index, values, turned):
+        for block in range(count):
+            part = values[block * length : (block + 1) * length]
+            if turned:
+                part = turn(part, cosine[block], -sine[block])
+            grad[block, :, head_slice(index)] = part.astype(HALF)
+
+    put(1, key_sum[...], True)
+    put(2 + spare, value_sum[...], False)
+    place = place_ref[0]
+    for head in range(spare):
+        query_grad, key_grad, value_grad = attend_back(
+            spare_q[:, head_slice(head)],
+            rows(head_slice(2 + head), count),
+            rows(head_slice(3 + spare + head), count),
+            place * length,
+            spare_level[head],
+            spare_out[:, head_slice(head)],
+            spare_out_grad[:, head_slice(head)],
+        )
+        spare_grad[:, head_slice(head)] = turn(query_grad, cosine[place], -sine[place]).astype(HALF)
+        put(2 + head, key_grad, True)
+        put(3 + spare + head, value_grad, False)
+
+
+def attention_back(place, packed, spare_q, out, spare_out, level, spare_level, out_grad, spare_out_grad, cosine, sine):
+    count, length, columns = packed.shape
+    spare = spare_q.shape[1] // HEAD_DIM
+    area = (count * (count + 1) // 2 + spare * count) * length * length
+    operands = (packed, spare_q, out, spare_out, level, spare_level, out_grad, spare_out_grad, cosine, sine)
+    return pl.pallas_call(
+        functools.partial(attention_back_kernel, spare),
+        grid_spec=pltpu.PrefetchScalarGridSpec(
+            num_scalar_prefetch=1,
+            grid=(1,),
+            in_specs=[whole_block(array.shape) for array in operands],
+            out_specs=[whole_block(packed.shape), whole_block(spare_q.shape)],
+            scratch_shapes=[pltpu.VMEM((count * length, HEAD_DIM), FLOAT)] * 2,
+        ),
+        out_shape=[jax.ShapeDtypeStruct(packed.shape, HALF), jax.ShapeDtypeStruct(spare_q.shape, HALF)],
+        compiler_params=pltpu.CompilerParams(vmem_limit_bytes=VMEM_LIMIT),
+        cost_estimate=pl.CostEstimate(
+            flops=20 * area * HEAD_DIM, bytes_accessed=8 * count * length * columns, transcendentals=area
+        ),
+        name="attention_back",
+    )(place, *operands)
+
+
+def part_kernel(slots, blocks_ref, grad, weight, *outs):
+    for slot, out in zip(slots, outs):
+        out[...] = matmul(grad[blocks_ref[slot]], weight[...], (1, 1)).astype(HALF)
+
+
+def attn_parts(blocks, slots, grad, weight):
+    length, columns = grad.shape[1:]
+    width = weight.shape[0]
+    count = len(slots)
+    return pl.pallas_call(
+        functools.partial(part_kernel, slots),
+        grid_spec=pltpu.PrefetchScalarGridSpec(
+            num_scalar_prefetch=1,
+            grid=(1,),
+            in_specs=[whole_block(grad.shape), whole_block((width, columns))],
+            out_specs=[whole_block((length, width))] * count,
+        ),
+        out_shape=[jax.ShapeDtypeStruct((length, width), HALF)] * count,
+        compiler_params=pltpu.CompilerParams(vmem_limit_bytes=VMEM_LIMIT),
+        cost_estimate=pl.CostEstimate(
+            flops=2 * count * length * width * columns,
+            bytes_accessed=2 * (count * length + columns) * width,
+            transcendentals=0,
+        ),
+        name="attn_parts",
+    )(blocks, grad, weight)
+
+
+def attn_wgrad_kernel(count, blocks_ref, core_ref, *refs):
+    slots, own, grad, spare_grad = refs[:count], refs[count], refs[count + 1], refs[count + 2]
+    kept, sent, rows, total, sems = refs[count + 3 :]
+    length = own.shape[0]
+    copies = [
+        pltpu.make_async_copy(
+            slot, rows.at[pl.ds(pl.multiple_of(blocks_ref[i] * length, length), length)], sems.at[i]
+        )
+        for i, slot in enumerate(slots)
+    ]
+    for copy in copies:
+        copy.start()
+    columns = grad.shape[2]
+    total[:, columns:] = matmul(own[...], spare_grad[...], (0, 0))
+    for copy in copies:
+        copy.wait()
+    total[:, :columns] = matmul(rows[...], grad[...].reshape(count * length, columns), (0, 0))
+    size = kept.shape[1]
+    for j in range(kept.shape[0]):
+        for target, parity in ((kept, core_ref[0]), (sent, 1 - core_ref[0])):
+            start = pl.multiple_of((2 * j + parity) * size, 8)
+            target[j] = total[pl.ds(start, size)].astype(HALF)
+
+
+def attn_wgrad(blocks, core, copies, slots, grad, spare_grad):
+    length, width = slots[0].shape
+    count, _, columns = grad.shape
+    wide = columns + spare_grad.shape[1]
+    part = (copies // 2, width // copies, wide)
+    return pl.pallas_call(
+        functools.partial(attn_wgrad_kernel, count),
+        grid_spec=pltpu.PrefetchScalarGridSpec(
+            num_scalar_prefetch=2,
+            grid=(1,),
+            in_specs=[pl.BlockSpec(memory_space=pl.ANY)] * count
+            + [whole_block(slots[0].shape), whole_block(grad.shape), whole_block(spare_grad.shape)],
+            out_specs=[whole_block(part)] * 2,
+            scratch_shapes=[
+                pltpu.VMEM((count * length, width), HALF),
+                pltpu.VMEM((width, wide), FLOAT),
+                pltpu.SemaphoreType.DMA((count,)),
+            ],
+        ),
+        out_shape=[jax.ShapeDtypeStruct(part, HALF)] * 2,
+        compiler_params=pltpu.CompilerParams(vmem_limit_bytes=VMEM_LIMIT),
+        cost_estimate=pl.CostEstimate(
+            flops=2 * count * length * width * wide,
+            bytes_accessed=2 * (count * length + wide) * width,
+            transcendentals=0,
+        ),
+        name="attn_wgrad",
+    )(blocks, core, *slots, slots[0], grad, spare_grad)
 
 
 def on_device(
@@ -402,11 +768,8 @@
     inv_one = lax.rsqrt(jnp.mean(inputs * inputs, axis=1, keepdims=True) + EPS)
     normed_one = inputs * inv_one
     attn_in = (normed_one * attn_gain).astype(HALF)
-    attn_slots = ring_gather(attn_in)
-    cot_slots = ring_gather(cotangent)
-
     expert_ids = jnp.arange(experts, dtype=jnp.int32)
-    picked = routes[:, :, None] == expert_ids[None, None, :]
+    picked = after(routes, attn_in)[:, :, None] == expert_ids[None, None, :]
     token_gate = jnp.sum(jnp.where(picked, gates[:, :, None], 0.0), axis=1)
     own_gates = lax.all_to_all(
         token_gate.T.reshape(group, local_experts, length),
@@ -417,122 +780,137 @@
     )
     own_gates = by_slot(own_gates.transpose(0, 2, 1))
 
-    def head_columns(weight):
-        return lax.dynamic_slice_in_dim(weight, place * HEAD_DIM, HEAD_DIM, axis=1)
-
-    own_weights = jnp.concatenate(
-        [head_columns(query_weight), head_columns(key_weight), head_columns(value_weight)], axis=1
-    )
-    spare_weights = jnp.concatenate([key_weight[:, own_heads:], value_weight[:, own_heads:]], axis=1)
+    own_place = place.astype(jnp.int32).reshape(1)
+    packed_weight = pack_heads(own_place, spare_heads, query_weight, key_weight, value_weight)
     spare_query_weight = query_weight[:, own_heads:]
-    attn_all = jnp.concatenate(attn_slots, axis=0)
-    positions = (
-        slot_block[:, None] * length + jnp.arange(length, dtype=jnp.int32)[None, :]
-    ).reshape(seq_len)
+    turned, tiles = 2 + spare_heads, 3 + 2 * spare_heads
     half = HEAD_DIM // 2
     freq = 10000.0 ** (-(jnp.arange(half, dtype=FLOAT) * 2.0) / HEAD_DIM)
-    angles = positions.astype(FLOAT)[:, None] * freq[None, :]
+    angles = jnp.arange(seq_len, dtype=FLOAT)[:, None] * freq[None, :]
     cosine, sine = jnp.cos(angles), jnp.sin(angles)
-    own_lin = matmul(attn_all, own_weights, (1, 0))
-    spare_lin = matmul(attn_all, spare_weights, (1, 0))
-    spare_query_lin = matmul(attn_in, spare_query_weight, (1, 0))
-
-    heads = []
-    own_q = rotate(own_lin[:, :HEAD_DIM], cosine, sine).astype(HALF)
-    own_k = rotate(own_lin[:, HEAD_DIM : 2 * HEAD_DIM], cosine, sine).astype(HALF)
-    own_v = own_lin[:, 2 * HEAD_DIM :].astype(HALF)
-    heads.append((own_q, own_k, own_v, positions))
-    for head in range(spare_heads):
-        columns = slice(head * HEAD_DIM, (head + 1) * HEAD_DIM)
-        value_columns = slice(
-            (spare_heads + head) * HEAD_DIM, (spare_heads + head + 1) * HEAD_DIM
-        )
-        q = rotate(spare_query_lin[:, columns], cosine[:length], sine[:length]).astype(HALF)
-        k = rotate(spare_lin[:, columns], cosine, sine).astype(HALF)
-        v = spare_lin[:, value_columns].astype(HALF)
-        heads.append((q, k, v, positions[:length]))
-    outs = [causal_attention(q, k, v, pos, positions) for q, k, v, pos in heads]
-
-    own_out = by_block(outs[0][0].reshape(group, length, HEAD_DIM))
+    cosine = jnp.concatenate([cosine, cosine], axis=1).reshape(group, length, HEAD_DIM)
+    sine = jnp.concatenate([-sine, sine], axis=1).reshape(group, length, HEAD_DIM)
+
+    share = hidden_units // (copies * group)
+    taken = copies * share
+    padded = -(-taken // 128) * 128
+    per_expert = -(-(hidden_units + padded) // CHUNK) * CHUNK
+    gap = per_expert - hidden_units
+    column = jnp.arange(gap, dtype=jnp.int32)
+    unit = jnp.where(
+        column < taken, ((column // share) * group + place) * share + column % share, -1
+    )
+    choice = (jnp.arange(hidden_units, dtype=jnp.int32)[:, None] == unit[None, :]).astype(HALF)
+
+    heads = {}
+
+    def project_slots(step, slots):
+        for slot in (step, group - step) if step else (0,):
+            result = project(
+                slot_block,
+                slot,
+                slots[slot],
+                packed_weight,
+                cosine,
+                sine,
+                turned,
+                tiles,
+                heads.get("packed"),
+            )
+            heads["packed"] = result[0]
+            if slot == 0:
+                heads["spare"] = result[1]
+        if step == 0:
+            heads["gates"] = own_gates
+        if step == 1:
+            heads["experts"] = pack_experts(
+                per_expert,
+                *after((choice, shared_gate, shared_up, shared_down, expert_gate, expert_up, expert_down), slots[1]),
+            )
+        return tuple(heads.values())
+
+    half_ring = group // 2
+    attn_slots = ring_gather(attn_in, project_slots)
+    gate_weight, up_weight, down_weight = heads["experts"]
+    (packed_heads,) = project(
+        slot_block,
+        half_ring,
+        attn_slots[half_ring],
+        packed_weight,
+        cosine,
+        sine,
+        turned,
+        tiles,
+        heads["packed"],
+    )
+    spare_q = heads["spare"]
+    cot_slots = ring_gather(after(cotangent, attn_slots[half_ring]))
+    own_out, spare_out, level, spare_level = attention(own_place, packed_heads, spare_q)
     returned = lax.all_to_all(own_out, "narrow", split_axis=0, concat_axis=0, tiled=True)
     attended = jnp.concatenate(
-        [returned.transpose(1, 0, 2).reshape(length, own_heads)] + [out for out, _ in outs[1:]],
-        axis=1,
+        [returned.transpose(1, 0, 2).reshape(length, own_heads), spare_out], axis=1
     )
     hidden = inputs + matmul(attended, output_weight, (1, 0))
     inv_two = lax.rsqrt(jnp.mean(hidden * hidden, axis=1, keepdims=True) + EPS)
     normed_two = hidden * inv_two
     ffn_in = (normed_two * ffn_gain).astype(HALF)
 
-    share = hidden_units // (copies * group)
-    taken = copies * share
-    padded = -(-taken // 128) * 128
-    column = jnp.arange(padded, dtype=jnp.int32)
-    unit = jnp.where(
-        column < taken, ((column // share) * group + place) * share + column % share, -1
-    )
-    choice = (jnp.arange(hidden_units, dtype=jnp.int32)[:, None] == unit[None, :]).astype(HALF)
-    share_gate = matmul(shared_gate, choice, (1, 0)).astype(HALF)
-    share_up = matmul(shared_up, choice, (1, 0)).astype(HALF)
-    share_down = matmul(choice, shared_down, (0, 0)).astype(HALF)
-    per_expert = -(-(hidden_units + padded) // CHUNK) * CHUNK
-    spare_units = per_expert - hidden_units
-
-    def packed(weight, share_part, axis):
-        pieces = []
-        for e in range(local_experts):
-            pieces.append(weight[e])
-            filler = share_part if e == 0 else jnp.zeros_like(share_part)
-            pieces.append(filler)
-        return jnp.concatenate(pieces, axis=axis)
-
-    if padded < spare_units:
-        share_gate = jnp.pad(share_gate, ((0, 0), (0, spare_units - padded)))
-        share_up = jnp.pad(share_up, ((0, 0), (0, spare_units - padded)))
-        share_down = jnp.pad(share_down, ((0, spare_units - padded), (0, 0)))
-    gate_weight = packed(expert_gate, share_gate, 1)
-    up_weight = packed(expert_up, share_up, 1)
-    down_weight = packed(expert_down, share_down, 0)
-
-    ffn_slots = ring_gather(ffn_in)
-    half_ring = group // 2
-    batches = [(0,), (1, group - 1), (2,), (half_ring, half_ring + 1), (half_ring - 1, half_ring + 2)]
-    row_order = [slot for batch in batches if len(batch) == 2 for slot in batch]
-    row_order += [slot for batch in batches if len(batch) == 1 for slot in batch]
-    kept = None
+    batches = [(0,)] + [(k, group - k) for k in range(1, half_ring)] + [(half_ring,)]
+    row_order = [slot for batch in batches if len(batch) == 2 for slot in batch] + [0, half_ring]
+    experts_state = {"kept": None}
     out_parts, row_parts = [None] * group, [None] * group
-    for batch in batches:
+
+    def expert_batch(step, slots):
+        batch = batches[step]
         result = expert_rows(
             hidden_units,
             row_order.index(batch[0]) * length,
             seq_len,
-            kept,
-            [ffn_slots[j] for j in batch],
+            experts_state["kept"],
+            [slots[j] for j in batch],
             [cot_slots[j] for j in batch],
             [own_gates[j] for j in batch],
             gate_weight,
             up_weight,
             down_weight,
         )
-        kept = result[:3]
+        experts_state["kept"] = result[:3]
         for i, j in enumerate(batch):
             out_parts[j] = result[3 + i]
             row_parts[j] = result[3 + len(batch) + i]
-    gated_inner, gate_grad, up_grad = kept
-    ffn_in_grad = ring_scatter(row_parts)
+        return tuple(result[3:])
+
+    ffn_slots = ring_gather(ffn_in, expert_batch)
+    expert_batch(half_ring, ffn_slots)
+    gated_inner, gate_grad, up_grad = experts_state["kept"]
 
     core = (lax.axis_index("wide") % 2).astype(jnp.int32).reshape(1)
     ordered_cots = [cot_slots[j] for j in row_order]
     ordered_rows = [ffn_slots[j] for j in row_order]
-    down_kept, down_sent, down_share = out_grad(
-        hidden_units, local_experts, copies, core, ordered_cots, gated_inner
-    )
-    gate_kept, gate_sent, gate_share = in_grad(
-        hidden_units, local_experts, copies, core, ordered_rows, gate_grad
-    )
-    up_kept, up_sent, up_share = in_grad(
-        hidden_units, local_experts, copies, core, ordered_rows, up_grad
-    )
+    weight_grads = {}
+
+    def expert_weights(step, arrived):
+        if step == 2:
+            weight_grads["down"] = out_grad(
+                hidden_units, local_experts, copies, core, ordered_cots, after(gated_inner, *arrived)
+            )
+            return tuple(weight_grads["down"])
+        if step == 1:
+            weight_grads["gate"] = in_grad(
+                hidden_units, local_experts, copies, core, ordered_rows, after(gate_grad, *arrived)
+            )
+            return tuple(weight_grads["gate"])
+        if step == 3:
+            weight_grads["up"] = in_grad(
+                hidden_units, local_experts, copies, core, ordered_rows, after(up_grad, *arrived)
+            )
+            return tuple(weight_grads["up"])
+        return ()
+
+    ffn_in_grad = ring_scatter(row_parts, expert_weights)
+    down_kept, down_sent, down_share = weight_grads["down"]
+    gate_kept, gate_sent, gate_share = weight_grads["gate"]
+    up_kept, up_sent, up_share = weight_grads["up"]
     expert_down_grad = wide_finish(down_kept, down_sent)
     expert_gate_grad = wide_finish(gate_kept, gate_sent)
     expert_up_grad = wide_finish(up_kept, up_sent)
@@ -548,39 +926,30 @@
         concat_axis=0,
         tiled=True,
     )
-    own_out_grad = by_slot(own_out_grad).reshape(seq_len, HEAD_DIM)
-    out_grads = [own_out_grad] + [
-        attended_grad[:, own_heads + h * HEAD_DIM : own_heads + (h + 1) * HEAD_DIM]
-        for h in range(spare_heads)
-    ]
-    mixed = (hidden + ring_scatter(out_parts)).astype(HALF)
-    grads = [
-        causal_back(q, k, v, pos, positions, log_total, out_grad)
-        for (q, k, v, pos), (_, log_total), out_grad in zip(heads, outs, out_grads)
-    ]
-    own_grad = jnp.concatenate(
-        [
-            rotate(grads[0][0], cosine, -sine).astype(HALF),
-            rotate(grads[0][1], cosine, -sine).astype(HALF),
-            grads[0][2].astype(HALF),
-        ],
-        axis=1,
-    )
-    spare_grad = jnp.concatenate(
-        [rotate(g[1], cosine, -sine).astype(HALF) for g in grads[1:]]
-        + [g[2].astype(HALF) for g in grads[1:]],
-        axis=1,
-    )
-    spare_query_grad = jnp.concatenate(
-        [rotate(g[0], cosine[:length], -sine[:length]).astype(HALF) for g in grads[1:]], axis=1
-    )
-    attn_part = (
-        matmul(own_grad, own_weights, (1, 1)) + matmul(spare_grad, spare_weights, (1, 1))
-    ).astype(HALF)
-    attn_part = attn_part.reshape(group, length, width)
-    attn_in_grad = ring_scatter([attn_part[j] for j in range(group)]) + matmul(
-        spare_query_grad, spare_query_weight, (1, 1)
-    )
+    late_parts = list(out_parts)
+    late_parts[half_ring], late_parts[half_ring + 1] = after(
+        (out_parts[half_ring], out_parts[half_ring + 1]), ffn_in_grad
+    )
+    mixed = (hidden + ring_scatter(late_parts)).astype(HALF)
+    head_grad, spare_query_grad = attention_back(
+        own_place,
+        packed_heads,
+        spare_q,
+        own_out,
+        spare_out,
+        level,
+        spare_level,
+        own_out_grad,
+        attended_grad[:, own_heads:],
+        cosine,
+        sine,
+    )
+    far = (half_ring, half_ring + 1)
+    near = tuple(j for j in range(group) if j not in far)
+    attn_part = dict(zip(far, attn_parts(slot_block, far, head_grad, packed_weight)))
+    attn_part.update(zip(near, attn_parts(slot_block, near, head_grad, packed_weight)))
+    attn_in_grad = ring_scatter([attn_part[j] for j in range(group)])
+    attn_in_grad = attn_in_grad + matmul(spare_query_grad, spare_query_weight, (1, 1))
     tokens_grad = hidden_grad + norm_back(attn_in_grad, normed_one, inv_one, attn_gain)
 
     def spread(grad):
@@ -605,8 +974,8 @@
                 spread(
                     jnp.concatenate(
                         [
-                            gate_share[:, :taken],
-                            up_share[:, :taken],
+                            gate_share[:, :padded],
+                            up_share[:, :padded],
                         ],
                         axis=1,
                     )
@@ -619,31 +988,38 @@
     output_weight_grad = summed[:, :width]
     ffn_gain_grad = summed[:, width]
 
+    spot = jnp.arange(group * padded, dtype=jnp.int32)
+    spot_column = spot % padded
+    spot_unit = jnp.where(
+        spot_column < taken,
+        ((spot_column // share) * group + spot // padded) * share + spot_column % share,
+        -1,
+    )
+    to_units = (spot_unit[:, None] == jnp.arange(hidden_units, dtype=jnp.int32)[None, :]).astype(HALF)
+    to_units = to_units.reshape(group, padded, hidden_units)
+
     def shared_columns(part):
-        own = part.shape[1]
-        return part.reshape(group, own, copies, share).transpose(1, 2, 0, 3).reshape(own, hidden_units)
-
-    shared_gate_grad = shared_columns(first[:, :, width + 128 : width + 128 + taken])
-    shared_up_grad = shared_columns(first[:, :, width + 128 + taken :])
-
-    own_wgrad = matmul(attn_all, own_grad, (0, 0))
-    spare_wgrad = jnp.concatenate(
-        [matmul(attn_in, spare_query_grad, (0, 0)), matmul(attn_all, spare_grad, (0, 0))], axis=1
-    )
-    second = exchange(spread(jnp.concatenate([own_wgrad, spare_wgrad], axis=1)))
-    spare_sum = jnp.sum(second[:, :, 3 * HEAD_DIM :], axis=0)
+        return jnp.einsum("grc,gcu->ru", part.astype(HALF), to_units, preferred_element_type=FLOAT)
+
+    shared_gate_grad = shared_columns(first[:, :, width + 128 : width + 128 + padded])
+    shared_up_grad = shared_columns(first[:, :, width + 128 + padded :])
+
+    attn_kept, attn_sent = attn_wgrad(
+        slot_block, core, copies, attn_slots, head_grad, spare_query_grad
+    )
+    second = exchange(wide_finish(attn_kept, attn_sent).astype(HALF))
+    packed_sum = jnp.sum(second, axis=0)
     spare_width = spare_heads * HEAD_DIM
 
-    def head_grad(index):
-        own = second[:, :, index * HEAD_DIM : (index + 1) * HEAD_DIM]
+    def head_grads(own_tile, spare_tile):
+        own = second[:, :, head_slice(own_tile)]
         own = own.transpose(1, 0, 2).reshape(own.shape[1], own_heads)
-        return jnp.concatenate(
-            [own, spare_sum[:, index * spare_width : (index + 1) * spare_width]], axis=1
-        )
-
-    query_weight_grad = head_grad(0)
-    key_weight_grad = head_grad(1)
-    value_weight_grad = head_grad(2)
+        first = spare_tile * HEAD_DIM
+        return jnp.concatenate([own, packed_sum[:, first : first + spare_width]], axis=1)
+
+    query_weight_grad = head_grads(0, tiles)
+    key_weight_grad = head_grads(1, 2)
+    value_weight_grad = head_grads(turned, turned + 1)
     own_rows = width // (copies * group)
     first_row = (lax.axis_index("wide") * group + place) * own_rows
 

time: 740 us -> 621 us (0.84)
  Pallas kernels: 154 us -> 257 us
  matrix products: 104 us -> 13 us
  local copies, waits for them, and re-layouts: 75.4 us -> 26 us
  waiting for transfers between devices: 198 us -> 162 us
  other arithmetic: 110 us -> 75.4 us
    pallas_call x0 -> x15, Pallas kernels: none -> 104 us  [the longest x8 33.3 us: project(): pl.pallas_call(functools.partial(project_kernel, turned, tiles, chained),...]
    dot_general x31 -> x5, matrix products: 94.4 us -> 8.22 us  [matmul(): lax.dot_general(a, b, ((contract[:1], contract[1:]), ((), ())), preferred...]
    ppermute x42, waiting for transfers between devices: 176 us -> 105 us  [the longest x9 46 us: ring_scatter(): backward = lax.ppermute(backward, 'narrow', back)]
    ppermute x3 -> x4, waiting for transfers between devices: 0.01 us -> 27.4 us  [wide_finish(): lax.ppermute(added(1 - mine), 'wide', [(i, i ^ bit) for i in range(count)])]
    unnamed x270 -> x113, local copies, waits for them, and re-layouts: 21.5 us -> 5.36 us
    concatenate x4 -> x2, other arithmetic: 17.2 us -> 3.21 us  [the longest x1 1.92 us: on_device(): jnp.concatenate([cosine, cosine], axis=1).reshape(group, length, HEAD_DIM)]
    unnamed x6 -> x0, other arithmetic: 11.9 us -> none
    reduce_sum x4 -> x2, other arithmetic: 8.99 us -> 1.55 us  [the longest x1 1.23 us: on_device(): packed_sum = jnp.sum(second, axis=0)]
  transfers between devices with their start and end apart: 61 -> 61, of which waited for: 24 -> 25; matrix products, arithmetic and copies ran while one was open for 36% -> 15% of each run, Pallas kernels for 21% -> 37%
where the time goes in v3:
time: 621 us; the launch traced here: 612 us
  Pallas kernels  257 us (41%)
  waiting for transfers between devices  162 us (26%)
  starting transfers between devices  76.5 us (12%)
  other arithmetic  75.4 us (12%)
  local copies, waits for them, and re-layouts  26 us (4%)
  matrix products  13 us (2%)
    pallas_call x5, Pallas kernels, expert_rows(): pl.pallas_call(functools.partial(rows_kernel, count, units, chained), gri...  98.7 us
    ppermute x9, waiting for transfers between devices, ring_scatter(): backward = lax.ppermute(backward, 'narrow', back)  46 us
    pallas_call x2, Pallas kernels, in_grad(): pl.pallas_call(functools.partial(in_grad_kernel, len(slots), units), grid...  36.5 us
    pallas_call x8, Pallas kernels, project(): pl.pallas_call(functools.partial(project_kernel, turned, tiles, chained),...  33.3 us
    ppermute x4, waiting for transfers between devices, wide_finish(): lax.ppermute(added(1 - mine), 'wide', [(i, i ^ bit) for i in range(count)])  27.4 us
    ppermute x12, waiting for transfers between devices, ring_scatter(): forward = lax.ppermute(forward, 'narrow', ahead)  23.8 us
    ppermute x12, waiting for transfers between devices, ring_gather(): forward = lax.ppermute(sent_ahead, 'narrow', ahead)  21.9 us
    all_to_all x2, waiting for transfers between devices, exchange(): lax.all_to_all(part.reshape(group, part.shape[0] // group, part.shape[1])...  19.4 us
  transfers between devices with their start and end apart: 61, of which 25 were waited for; matrix products, arithmetic and copies ran while one was open for 15% of the time, Pallas kernels for 37%

profile of v3, /device:TPU:4, one launch (start us, length us, event | category | flops | bytes accessed | tf_op | source)
XLA Modules:
  0.0 611.7 jit_solution(3126059332742760127)
XLA Ops:
  36.0 13.6 %pack_experts.1 = (bf16[1280,2048]{1,0:T(8,128)(2,1)}, bf16[1280,2048]{1,0:T(8,128)(2,1)}, bf16[2048,1280]{1,0:T(8,128)(2,1)}) custom-call(bf16[896,128]{1,0:T(8,128)(2,1)} %fusion.26.choice, bf16[1280,896]{1,0:T(8,128)(2,1)} %shared_gate, bf16[1280,896]{1,0:T(8,128)(2,1)} %shared_up, bf16[896,1280]{1,0:T(8,128)(2,1)} %shared_down, ...), custom_call_target="tpu_custom_call" | custom-call | bytes 31457280 | tf_op jit(solution)/shard_map/pack_experts/pallas_call | solution.py:240
  92.7 9.9 %attention.1 = (bf16[8,256,128]{2,1,0:T(8,128)(2,1)}, bf16[256,256]{1,0:T(8,128)(2,1)}, f32[8,256,128]{2,1,0:T(8,128)}, f32[2,256,128]{2,1,0:T(8,128)}) custom-call(s32[1]{0:T(128)} %bitcast.place_ref, bf16[8,256,896]{2,1,0:T(8,128)(2,1)} %project.15.packed, bf16[256,256]{1,0:T(8,128)(2,1)} %get-tuple-element.135.spare_q), custom_call_target="tpu_custom_call" | custom-call | flops 3489660928 | bytes 7340032 | tf_op jit(solution)/shard_map/attention/pallas_call | solution.py:539
  113.7 13.3 %collective-permute-done.11.refs_2_.refs_0_ = bf16[256,1280]{1,0:T(8,128)(2,1)} collective-permute-done((bf16[256,1280]{1,0:T(8,128)(2,1)}, bf16[256,1280]{1,0:T(8,128)(2,1)}, u32[]{:S(2)}, u32[]{:S(2)}) %collective-permute-start.11) | collective-permute-done | bytes 655392 | tf_op jit(solution)/shard_map/ppermute | solution.py:46
  141.4 13.9 %expert_rows.5 = (bf16[2048,2048]{1,0:T(8,128)(2,1)}, bf16[2048,2048]{1,0:T(8,128)(2,1)}, bf16[2048,2048]{1,0:T(8,128)(2,1)}, bf16[256,1280]{1,0:T(8,128)(2,1)}, bf16[256,1280]{1,0:T(8,128)(2,1)}) custom-call(bf16[256,1280]{1,0:T(8,128)(2,1)} %copy-done.28, bf16[256,1280]{1,0:T(8,128)(2,1)} %refs_6_, f32[256,2]{1,0:T(8,128)} %get-tuple-element.268.refs_2_, ...), custom_call_target="tpu_custom_call" | custom-call | flops 8053063680 | bytes 21495808 | tf_op jit(solution)/shard_map/expert_rows/pallas_call | solution.py:186
  157.4 7.9 %collective-permute-done.7.refs_1_ = bf16[256,1280]{1,0:T(8,128)(2,1)} collective-permute-done((bf16[256,1280]{1,0:T(8,128)(2,1)S(1)}, bf16[256,1280]{1,0:T(8,128)(2,1)}, u32[]{:S(2)}, u32[]{:S(2)}) %collective-permute-start.7) | collective-permute-done | bytes 655392 | tf_op jit(solution)/shard_map/ppermute | solution.py:44
  167.3 23.5 %expert_rows.6 = (bf16[2048,2048]{1,0:T(8,128)(2,1)}, bf16[2048,2048]{1,0:T(8,128)(2,1)}, bf16[2048,2048]{1,0:T(8,128)(2,1)}, bf16[256,1280]{1,0:T(8,128)(2,1)},...) custom-call(bf16[256,1280]{1,0:T(8,128)(2,1)} %collective-permute-do, ...), custom_call_target="tpu_custom_call", output_to_operand_aliasing={{0}: (9, {}), {1}: (10, {}), {2}: (11, {})} | custom-call | flops 16106127360 | bytes 27262976 | tf_op jit(solution)/shard_map/expert_rows/pallas_call | solution.py:186
  195.3 23.5 %expert_rows.7 = (bf16[2048,2048]{1,0:T(8,128)(2,1)}, bf16[2048,2048]{1,0:T(8,128)(2,1)}, bf16[2048,2048]{1,0:T(8,128)(2,1)}, bf16[256,1280]{1,0:T(8,128)(2,1)},...) custom-call(bf16[256,1280]{1,0:T(8,128)(2,1)} %copy-done.53, ...), custom_call_target="tpu_custom_call", output_to_operand_aliasing={{0}: (9, {}), {1}: (10, {}), {2}: (11, {})} | custom-call | flops 16106127360 | bytes 27262976 | tf_op jit(solution)/shard_map/expert_rows/pallas_call | solution.py:186
  219.9 23.6 %expert_rows.8 = (bf16[2048,2048]{1,0:T(8,128)(2,1)}, bf16[2048,2048]{1,0:T(8,128)(2,1)}, bf16[2048,2048]{1,0:T(8,128)(2,1)}, bf16[256,1280]{1,0:T(8,128)(2,1)},...) custom-call(bf16[256,1280]{1,0:T(8,128)(2,1)} %collective-permute-do, ...), custom_call_target="tpu_custom_call", output_to_operand_aliasing={{0}: (9, {}), {1}: (10, {}), {2}: (11, {})} | custom-call | flops 16106127360 | bytes 27262976 | tf_op jit(solution)/shard_map/expert_rows/pallas_call | solution.py:186
  244.5 14.0 %expert_rows.9 = (bf16[2048,2048]{1,0:T(8,128)(2,1)}, bf16[2048,2048]{1,0:T(8,128)(2,1)}, bf16[2048,2048]{1,0:T(8,128)(2,1)}, bf16[256,1280]{1,0:T(8,128)(2,1)}, bf16[256,1280]{1,0:T(8,128)(2,1)}) custom-call(bf16[256,1280]{1,0:T(8,128)(2,1)} %copy-done.41, ...), custom_call_target="tpu_custom_call", output_to_operand_aliasing={{0}: (6, {}), {1}: (7, {}), {2}: (8, {})} | custom-call | flops 8053063680 | bytes 21495808 | tf_op jit(solution)/shard_map/expert_rows/pallas_call | solution.py:186
  260.6 9.1 %collective-permute-done.22 = bf16[256,1280]{1,0:T(8,128)(2,1)} collective-permute-done((bf16[256,1280]{1,0:T(8,128)(2,1)}, bf16[256,1280]{1,0:T(8,128)(2,1)}, u32[]{:S(2)}, u32[]{:S(2)}) %collective-permute-start.22) | collective-permute-done | bytes 655392 | tf_op jit(solution)/shard_map/ppermute | solution.py:65
  278.1 18.3 %expert_in_grad.2 = (bf16[2,2,320,896]{3,2,1,0:T(8,128)(2,1)}, bf16[2,2,320,896]{3,2,1,0:T(8,128)(2,1)}, bf16[1280,128]{1,0:T(8,128)(2,1)}) custom-call(s32[1]{0:T(128)} %bitcast.16.core_ref, bf16[256,1280]{1,0:T(8,128)(2,1)} %collective-permute-done.8.refs_0_, bf16[256,1280]{1,0:T(8,128)(2,1)} %collective-permute-done.7.refs_1_, ...), custom_call_target="tpu_custom_call" | custom-call | flops 10737418240 | bytes 22151168 | tf_op jit(solution)/shard_map/expert_in_grad/pallas_call | solution.py:303
  303.1 18.2 %expert_out_grad.1 = (bf16[2,2,224,1280]{3,2,1,0:T(8,128)(2,1)}, bf16[2,2,224,1280]{3,2,1,0:T(8,128)(2,1)}, bf16[128,1280]{1,0:T(8,128)(2,1)}) custom-call(s32[1]{0:T(128)} %bitcast.16.core_ref, bf16[256,1280]{1,0:T(8,128)(2,1)} %collective-permute-done.11.refs_2_.refs_0_, bf16[256,1280]{1,0:T(8,128)(2,1)} %collective-permute-done.12.refs_3_.refs_1_, ...), custom_call_target="tpu_custom_call" | custom-call | flops 10737418240 | bytes 22151168 | tf_op jit(solution)/shard_map/expert_out_grad/pallas_call | solution.py:356
  328.5 18.2 %expert_in_grad.3 = (bf16[2,2,320,896]{3,2,1,0:T(8,128)(2,1)}, bf16[2,2,320,896]{3,2,1,0:T(8,128)(2,1)}, bf16[1280,128]{1,0:T(8,128)(2,1)}) custom-call(s32[1]{0:T(128)} %bitcast.16.core_ref, bf16[256,1280]{1,0:T(8,128)(2,1)} %collective-permute-done.8.refs_0_, bf16[256,1280]{1,0:T(8,128)(2,1)} %collective-permute-done.7.refs_1_, ...), custom_call_target="tpu_custom_call" | custom-call | flops 10737418240 | bytes 22151168 | tf_op jit(solution)/shard_map/expert_in_grad/pallas_call | solution.py:303
  355.3 13.0 %collective-permute-done.29 = bf16[256,1280]{1,0:T(8,128)(2,1)S(1)} collective-permute-done((bf16[256,1280]{1,0:T(8,128)(2,1)S(1)}, bf16[256,1280]{1,0:T(8,128)(2,1)S(1)}, u32[]{:S(2)}, u32[]{:S(2)}) %collective-permute-start.29) | collective-permute-done | bytes 655392 | tf_op jit(solution)/shard_map/ppermute | solution.py:65
  377.3 10.6 %collective-permute-done.31 = bf16[256,1280]{1,0:T(8,128)(2,1)} collective-permute-done((bf16[256,1280]{1,0:T(8,128)(2,1)}, bf16[256,1280]{1,0:T(8,128)(2,1)}, u32[]{:S(2)}, u32[]{:S(2)}) %collective-permute-start.31) | collective-permute-done | bytes 655392 | tf_op jit(solution)/shard_map/ppermute | solution.py:65
  399.0 10.6 %collective-permute-done.32 = bf16[256,1280]{1,0:T(8,128)(2,1)S(1)} collective-permute-done((bf16[256,1280]{1,0:T(8,128)(2,1)S(1)}, bf16[256,1280]{1,0:T(8,128)(2,1)S(1)}, u32[]{:S(2)}, u32[]{:S(2)}) %collective-permute-start.32) | collective-permute-done | bytes 655392 | tf_op jit(solution)/shard_map/ppermute | solution.py:63
  440.3 9.2 %collective-permute-done.55 = bf16[1,2,224,1280]{3,2,1,0:T(8,128)(2,1)} collective-permute-done((bf16[1,2,224,1280]{3,2,1,0:T(8,128)(2,1)}, bf16[1,2,224,1280]{3,2,1,0:T(8,128)(2,1)}, u32[]{:S(2)}, u32[]{:S(2)}) %collective-permute-start.55) | collective-permute-done | bytes 1146912 | tf_op jit(solution)/shard_map/ppermute | solution.py:106
  458.2 16.2 %attention_back.1 = (bf16[8,256,896]{2,1,0:T(8,128)(2,1)}, bf16[256,256]{1,0:T(8,128)(2,1)}) custom-call(s32[1]{0:T(128)} %bitcast.place_ref, bf16[8,256,896]{2,1,0:T(8,128)(2,1)} %project.15.packed, bf16[256,256]{1,0:T(8,128)(2,1)} %get-tuple-element.135.spare_q, bf16[8,256,128]{2,1,0:T(8,128)(2,1)} %get-tuple-element.152.out, ...), custom_call_target="tpu_custom_call" | custom-call | flops 8724152320 | bytes 14680064 | tf_op jit(solution)/shard_map/attention_back/pallas_call | solution.py:625
  482.3 12.7 %attn_wgrad.1 = (bf16[2,320,1152]{2,1,0:T(8,128)(2,1)}, bf16[2,320,1152]{2,1,0:T(8,128)(2,1)}) custom-call(s32[8]{0:T(128)} %copy-done.47, s32[1]{0:T(128)} %bitcast.16.core_ref, bf16[256,1280]{1,0:T(8,128)(2,1)} %fusion.12.refs_0_.refs_8_, bf16[256,1280]{1,0:T(8,128)(2,1)} %collective-permute-done.1.refs_0_.refs_1_, ...), custom_call_target="tpu_custom_call" | custom-call | flops 6039797760 | bytes 8192000 | tf_op jit(solution)/shard_map/attn_wgrad/pallas_call | solution.py:700
  495.0 8.6 %attn_parts.2 = (bf16[256,1280]{1,0:T(8,128)(2,1)}, bf16[256,1280]{1,0:T(8,128)(2,1)}, bf16[256,1280]{1,0:T(8,128)(2,1)}, bf16[256,1280]{1,0:T(8,128)(2,1)}, bf1...) custom-call(s32[8]{0:T(128)} %copy-done.47, bf16[8,256,896]{2,1,0:T(8,128)(2,1)} %get-tuple-element.227.grad.refs_9_, ...), custom_call_target="tpu_custom_call" | custom-call | flops 3523215360 | bytes 6225920 | tf_op jit(solution)/shard_map/attn_parts/pallas_call | solution.py:652
  514.1 9.6 %collective-permute-done.38 = bf16[256,1280]{1,0:T(8,128)(2,1)S(1)} collective-permute-done((bf16[256,1280]{1,0:T(8,128)(2,1)S(1)}, bf16[256,1280]{1,0:T(8,128)(2,1)S(1)}, u32[]{:S(2)}, u32[]{:S(2)}) %collective-permute-start.38) | collective-permute-done | bytes 655392 | tf_op jit(solution)/shard_map/ppermute | solution.py:65
  533.1 11.2 %collective-permute-done.43 = bf16[1,320,1152]{2,1,0:T(8,128)(2,1)S(1)} collective-permute-done((bf16[1,320,1152]{2,1,0:T(8,128)(2,1)S(1)}, bf16[1,320,1152]{2,1,0:T(8,128)(2,1)S(1)}, u32[]{:S(2)}, u32[]{:S(2)}) %collective-permute-start.43) | collective-permute-done | bytes 737312 | tf_op jit(solution)/shard_map/ppermute | solution.py:106
  552.8 9.7 %collective-permute-done.45 = bf16[1,320,1408]{2,1,0:T(8,128)(2,1)} collective-permute-done((bf16[1,320,1408]{2,1,0:T(8,128)(2,1)}, bf16[1,320,1408]{2,1,0:T(8,128)(2,1)}, u32[]{:S(2)}, u32[]{:S(2)}) %collective-permute-start.45) | collective-permute-done | bytes 901152 | tf_op jit(solution)/shard_map/ppermute | solution.py:85
  588.5 15.3 %all-to-all-done.4 = bf16[8,40,1664]{2,1,0:T(8,128)(2,1)} async-done(((bf16[8,40,1664]{2,1,0:T(8,128)(2,1)}), bf16[8,40,1664]{2,1,0:T(8,128)(2,1)}, u32[]{:S(2)}, u32[]{:S(2)}) %all-to-all-start.4) | async-done | bytes 1064992 | tf_op jit(solution)/shard_map/all_to_all | solution.py:959
  (328 shorter events, 275.7 us)
Async XLA Ops:
  102.5 30.8 %all-to-all-start.1 = ((bf16[8,256,128]{2,1,0:T(8,128)(2,1)}), bf16[8,256,128]{2,1,0:T(8,128)(2,1)}, u32[]{:S(2)}, u32[]{:S(2)}) async-start(bf16[8,256,128]{2,1,0:T(8,128)(2,1)} %get-tuple-element.152.out), calls=%async_computation.1 | async-start | bytes 1048576 | tf_op jit(solution)/shard_map/all_to_all | solution.py:849
  129.1 26.2 %collective-permute-start.15 = (bf16[256,1280]{1,0:T(8,128)(2,1)}, bf16[256,1280]{1,0:T(8,128)(2,1)}, u32[]{:S(2)}, u32[]{:S(2)}) collective-permute-start(bf16[256,1280]{1,0:T(8,128)(2,1)} %collective-permute-done.11.refs_2_.refs_0_), channel_id=1, source_target_pairs={{2,0},{4,2},{6,4},{7,6},{5,7},{3,5},{1,3},{0,1},{10,8},{12,10},{14... | collective-permute-start | bytes 1966088 | tf_op jit(solution)/shard_map/ppermute | solution.py:46
  139.0 26.3 %collective-permute-start.7 = (bf16[256,1280]{1,0:T(8,128)(2,1)S(1)}, bf16[256,1280]{1,0:T(8,128)(2,1)}, u32[]{:S(2)}, u32[]{:S(2)}) collective-permute-start(bf16[256,1280]{1,0:T(8,128)(2,1)S(1)} %multiply_convert_fusion.1.refs_0_.refs_6_), channel_id=1, source_target_pairs={{0,2},{2,4},{4,6},{6,7},{7,5},{5,3},{3,1},{1,0},{8,10},{10,12},{12... | collective-permute-start | bytes 1966088 | tf_op jit(solution)/shard_map/ppermute | solution.py:44
  139.7 25.6 %collective-permute-start.8 = (bf16[256,1280]{1,0:T(8,128)(2,1)S(1)}, bf16[256,1280]{1,0:T(8,128)(2,1)}, u32[]{:S(2)}, u32[]{:S(2)}) collective-permute-start(bf16[256,1280]{1,0:T(8,128)(2,1)S(1)} %multiply_convert_fusion.1.refs_0_.refs_6_), channel_id=1, source_target_pairs={{2,0},{4,2},{6,4},{7,6},{5,7},{3,5},{1,3},{0,1},{10,8},{12,10},{14... | collective-permute-start | bytes 1966088 | tf_op jit(solution)/shard_map/ppermute | solution.py:46
  155.3 35.6 %collective-permute-start.18 = (bf16[256,1280]{1,0:T(8,128)(2,1)}, bf16[256,1280]{1,0:T(8,128)(2,1)}, u32[]{:S(2)}, u32[]{:S(2)}) collective-permute-start(bf16[256,1280]{1,0:T(8,128)(2,1)} %collective-permute-done.16.refs_3_), channel_id=1, source_target_pairs={{0,2},{2,4},{4,6},{6,7},{7,5},{5,3},{3,1},{1,0},{8,10},{10,12},{12... | collective-permute-start | bytes 1966088 | tf_op jit(solution)/shard_map/ppermute | solution.py:44
  155.9 35.0 %collective-permute-start.19 = (bf16[256,1280]{1,0:T(8,128)(2,1)}, bf16[256,1280]{1,0:T(8,128)(2,1)}, u32[]{:S(2)}, u32[]{:S(2)}) collective-permute-start(bf16[256,1280]{1,0:T(8,128)(2,1)} %collective-permute-done.15.refs_2_), channel_id=1, source_target_pairs={{2,0},{4,2},{6,4},{7,6},{5,7},{3,5},{1,3},{0,1},{10,8},{12,10},{14... | collective-permute-start | bytes 1966088 | tf_op jit(solution)/shard_map/ppermute | solution.py:46
  165.3 25.7 %collective-permute-start.10 = (bf16[256,1280]{1,0:T(8,128)(2,1)}, bf16[256,1280]{1,0:T(8,128)(2,1)S(1)}, u32[]{:S(2)}, u32[]{:S(2)}) collective-permute-start(bf16[256,1280]{1,0:T(8,128)(2,1)} %collective-permute-done.8.refs_0_), channel_id=1, source_target_pairs={{2,0},{4,2},{6,4},{7,6},{5,7},{3,5},{1,3},{0,1},{10,8},{12,10},{14... | collective-permute-start | bytes 1966088 | tf_op jit(solution)/shard_map/ppermute | solution.py:46
  165.9 27.4 %collective-permute-start.9 = (bf16[256,1280]{1,0:T(8,128)(2,1)}, bf16[256,1280]{1,0:T(8,128)(2,1)}, u32[]{:S(2)}, u32[]{:S(2)}) collective-permute-start(bf16[256,1280]{1,0:T(8,128)(2,1)} %collective-permute-done.7.refs_1_), channel_id=1, source_target_pairs={{0,2},{2,4},{4,6},{6,7},{7,5},{5,3},{3,1},{1,0},{8,10},{10,12},{12... | collective-permute-start | bytes 1966088 | tf_op jit(solution)/shard_map/ppermute | solution.py:44
  190.9 52.7 %collective-permute-start.20 = (bf16[256,1280]{1,0:T(8,128)(2,1)}, bf16[256,1280]{1,0:T(8,128)(2,1)}, u32[]{:S(2)}, u32[]{:S(2)}) collective-permute-start(bf16[256,1280]{1,0:T(8,128)(2,1)} %collective-permute-done.18.refs_3_.refs_5_), channel_id=1, source_target_pairs={{0,2},{2,4},{4,6},{6,7},{7,5},{5,3},{3,1},{1,0},{8,10},{10,12},{12... | collective-permute-start | bytes 1966088 | tf_op jit(solution)/shard_map/ppermute | solution.py:44
  193.3 26.4 %collective-permute-start.13 = (bf16[256,1280]{1,0:T(8,128)(2,1)}, bf16[256,1280]{1,0:T(8,128)(2,1)}, u32[]{:S(2)}, u32[]{:S(2)}) collective-permute-start(bf16[256,1280]{1,0:T(8,128)(2,1)} %collective-permute-done.9.refs_1_.refs_3_), channel_id=1, source_target_pairs={{0,2},{2,4},{4,6},{6,7},{7,5},{5,3},{3,1},{1,0},{8,10},{10,12},{12... | collective-permute-start | bytes 1966088 | tf_op jit(solution)/shard_map/ppermute | solution.py:44
  193.3 26.4 %collective-permute-start.14 = (bf16[256,1280]{1,0:T(8,128)(2,1)S(1)}, bf16[256,1280]{1,0:T(8,128)(2,1)}, u32[]{:S(2)}, u32[]{:S(2)}) collective-permute-start(bf16[256,1280]{1,0:T(8,128)(2,1)S(1)} %collective-permute-done.10.refs_0_.refs_2_), channel_id=1, source_target_pairs={{2,0},{4,2},{6,4},{7,6},{5,7},{3,5},{1,3},{0,1},{10,8},{12,10},{14... | collective-permute-start | bytes 1966088 | tf_op jit(solution)/shard_map/ppermute | solution.py:46
  296.3 98.6 %collective-permute-start.50 = (bf16[2,2,320,896]{3,2,1,0:T(8,128)(2,1)}, bf16[2,2,320,896]{3,2,1,0:T(8,128)(2,1)}, u32[]{:S(2)}, u32[]{:S(2)}) collective-permute-start(bf16[2,2,320,896]{3,2,1,0:T(8,128)(2,1)} %get-tuple-element.203), channel_id=1, source_target_pairs={{0,8},{8,0},{16,24},{24,16},{1,9},{9,1},{17,25},{25,17},{2,10},{10... | collective-permute-start | bytes 6881288 | tf_op jit(solution)/shard_map/ppermute | solution.py:94
  300.7 26.3 %collective-permute-start.25 = (bf16[256,1280]{1,0:T(8,128)(2,1)}, bf16[256,1280]{1,0:T(8,128)(2,1)}, u32[]{:S(2)}, u32[]{:S(2)}) collective-permute-start(bf16[256,1280]{1,0:T(8,128)(2,1)} %add_convert_fusion.23), channel_id=1, source_target_pairs={{0,2},{2,4},{4,6},{6,7},{7,5},{5,3},{3,1},{1,0},{8,10},{10,12},{12... | collective-permute-start | bytes 1966088 | tf_op jit(solution)/shard_map/ppermute | solution.py:63
  300.7 26.3 %collective-permute-start.26 = (bf16[256,1280]{1,0:T(8,128)(2,1)}, bf16[256,1280]{1,0:T(8,128)(2,1)}, u32[]{:S(2)}, u32[]{:S(2)}) collective-permute-start(bf16[256,1280]{1,0:T(8,128)(2,1)} %add_convert_fusion.22), channel_id=1, source_target_pairs={{2,0},{4,2},{6,4},{7,6},{5,7},{3,5},{1,3},{0,1},{10,8},{12,10},{14... | collective-permute-start | bytes 1966088 | tf_op jit(solution)/shard_map/ppermute | solution.py:65
  321.3 92.5 %collective-permute-start.54 = (bf16[2,2,224,1280]{3,2,1,0:T(8,128)(2,1)}, bf16[2,2,224,1280]{3,2,1,0:T(8,128)(2,1)}, u32[]{:S(2)}, u32[]{:S(2)}) collective-permute-start(bf16[2,2,224,1280]{3,2,1,0:T(8,128)(2,1)} %get-tuple-element.210), channel_id=1, source_target_pairs={{0,8},{8,0},{16,24},{24,16},{1,9},{9,1},{17,25},{25,17},{2,10},{10... | collective-permute-start | bytes 6881288 | tf_op jit(solution)/shard_map/ppermute | solution.py:94
  326.5 27.0 %collective-permute-start.48 = (bf16[2,28,1280]{2,1,0:T(8,128)(2,1)}, bf16[2,28,1280]{2,1,0:T(8,128)(2,1)S(1)}, u32[]{:S(2)}, u32[]{:S(2)}) collective-permute-start(bf16[2,28,1280]{2,1,0:T(8,128)(2,1)} %dynamic-slice_bitcast_fusion.1), channel_id=1, source_target_pairs={{0,8},{8,0},{16,24},{24,16},{1,9},{9,1},{17,25},{25,17},{2,10},{10... | collective-permute-start | bytes 430088 | tf_op jit(solution)/shard_map/ppermute | solution.py:85
  374.4 53.5 %collective-permute-start.52 = (bf16[2,2,320,896]{3,2,1,0:T(8,128)(2,1)}, bf16[2,2,320,896]{3,2,1,0:T(8,128)(2,1)}, u32[]{:S(2)}, u32[]{:S(2)}) collective-permute-start(bf16[2,2,320,896]{3,2,1,0:T(8,128)(2,1)} %get-tuple-element.249), channel_id=1, source_target_pairs={{0,8},{8,0},{16,24},{24,16},{1,9},{9,1},{17,25},{25,17},{2,10},{10... | collective-permute-start | bytes 6881288 | tf_op jit(solution)/shard_map/ppermute | solution.py:94
  396.6 28.3 %collective-permute-start.51 = (bf16[1,2,320,896]{3,2,1,0:T(8,128)(2,1)S(1)}, bf16[1,2,320,896]{3,2,1,0:T(8,128)(2,1)S(1)}, u32[]{:S(2)}, u32[]{:S(2)}) collective-permute-start(bf16[1,2,320,896]{3,2,1,0:T(8,128)(2,1)S(1)} %add_convert_fusion.4), channel_id=1, source_target_pairs={{0,16},{8,24},{16,0},{24,8},{1,17},{9,25},{17,1},{25,9},{2,18},{10... | collective-permute-start | bytes 3440648 | tf_op jit(solution)/shard_map/ppermute | solution.py:106
  416.4 33.2 %collective-permute-start.55 = (bf16[1,2,224,1280]{3,2,1,0:T(8,128)(2,1)}, bf16[1,2,224,1280]{3,2,1,0:T(8,128)(2,1)}, u32[]{:S(2)}, u32[]{:S(2)}) collective-permute-start(bf16[1,2,224,1280]{3,2,1,0:T(8,128)(2,1)} %add_convert_fusion), channel_id=1, source_target_pairs={{0,16},{8,24},{16,0},{24,8},{1,17},{9,25},{17,1},{25,9},{2,18},{10... | collective-permute-start | bytes 3440648 | tf_op jit(solution)/shard_map/ppermute | solution.py:106
  430.6 77.4 %collective-permute-start.53 = (bf16[1,2,320,896]{3,2,1,0:T(8,128)(2,1)}, bf16[1,2,320,896]{3,2,1,0:T(8,128)(2,1)}, u32[]{:S(2)}, u32[]{:S(2)}) collective-permute-start(bf16[1,2,320,896]{3,2,1,0:T(8,128)(2,1)} %add_convert_fusion.2), channel_id=1, source_target_pairs={{0,16},{8,24},{16,0},{24,8},{1,17},{9,25},{17,1},{25,9},{2,18},{10... | collective-permute-start | bytes 3440648 | tf_op jit(solution)/shard_map/ppermute | solution.py:106
  458.2 53.9 %collective-permute-start.44 = (bf16[2,320,1408]{2,1,0:T(8,128)(2,1)}, bf16[2,320,1408]{2,1,0:T(8,128)(2,1)}, u32[]{:S(2)}, u32[]{:S(2)}) collective-permute-start(bf16[2,320,1408]{2,1,0:T(8,128)(2,1)} %fusion.9), channel_id=1, source_target_pairs={{0,8},{8,0},{16,24},{24,16},{1,9},{9,1},{17,25},{25,17},{2,10},{10... | collective-permute-start | bytes 5406728 | tf_op jit(solution)/shard_map/ppermute | solution.py:85
  531.0 31.5 %collective-permute-start.45 = (bf16[1,320,1408]{2,1,0:T(8,128)(2,1)}, bf16[1,320,1408]{2,1,0:T(8,128)(2,1)}, u32[]{:S(2)}, u32[]{:S(2)}) collective-permute-start(bf16[1,320,1408]{2,1,0:T(8,128)(2,1)} %constant_dynamic-slice_fusion.2), channel_id=1, source_target_pairs={{0,16},{8,24},{16,0},{24,8},{1,17},{9,25},{17,1},{25,9},{2,18},{10... | collective-permute-start | bytes 2703368 | tf_op jit(solution)/shard_map/ppermute | solution.py:85
  552.7 25.9 %collective-permute-start.41 = (bf16[256,1280]{1,0:T(8,128)(2,1)}, bf16[256,1280]{1,0:T(8,128)(2,1)}, u32[]{:S(2)}, u32[]{:S(2)}) collective-permute-start(bf16[256,1280]{1,0:T(8,128)(2,1)} %add_convert_fusion.10), channel_id=1, source_target_pairs={{0,2},{2,4},{4,6},{6,7},{7,5},{5,3},{3,1},{1,0},{8,10},{10,12},{12... | collective-permute-start | bytes 1966088 | tf_op jit(solution)/shard_map/ppermute | solution.py:63
  569.1 34.8 %all-to-all-start.4 = ((bf16[8,40,1664]{2,1,0:T(8,128)(2,1)}), bf16[8,40,1664]{2,1,0:T(8,128)(2,1)}, u32[]{:S(2)}, u32[]{:S(2)}) async-start(bf16[8,40,1664]{2,1,0:T(8,128)(2,1)} %pad_maximum_fusion), calls=%async_computation.4 | async-start | bytes 2129920 | tf_op jit(solution)/shard_map/all_to_all | solution.py:959
  (93 other events, 1243.6 us)

commit v4 on v3

--- a/solution.py
+++ b/solution.py
@@ -51,47 +51,65 @@
     return slots
 
 
-def ring_scatter(parts, work=None):
-    count = lax.axis_size("narrow")
-    ahead, back = ring_steps(count)
-    half = count // 2
-    forward, backward = parts[half], parts[half + 1]
-    before = done = ()
-    for step in range(1, half + 1):
-        forward, backward = after((forward, backward), *before)
-        before = done
-        forward = lax.ppermute(forward, "narrow", ahead)
-        if step < half:
-            backward = lax.ppermute(backward, "narrow", back)
-        done = work(step, (forward, backward)) if work else ()
-        if step < half:
-            forward = (forward.astype(FLOAT) + parts[half - step].astype(FLOAT)).astype(HALF)
-            if step < half - 1:
-                backward = (
-                    backward.astype(FLOAT) + parts[half + 1 + step].astype(FLOAT)
-                ).astype(HALF)
-    return parts[0].astype(FLOAT) + forward.astype(FLOAT) + backward.astype(FLOAT)
-
-
-def wide_scatter(chunks):
+class RingSum:
+    def __init__(self, parts):
+        self.parts = parts
+        self.half = len(parts) // 2
+        self.step = 0
+        self.forward, self.backward = parts[self.half], parts[self.half + 1]
+
+    def hop(self, *others):
+        ahead, back = ring_steps(len(self.parts))
+        self.step += 1
+        forward, backward = after((self.forward, self.backward), *others)
+        self.forward = lax.ppermute(forward, "narrow", ahead)
+        if self.step < self.half:
+            self.backward = lax.ppermute(backward, "narrow", back)
+        return self.forward, self.backward
+
+    def add(self):
+        own_forward = self.parts[self.half - self.step]
+        if self.step < self.half - 1:
+            own_backward = self.parts[self.half + 1 + self.step]
+            self.forward, self.backward = add_pairs(
+                (self.forward, self.backward), (own_forward, own_backward)
+            )
+        else:
+            (self.forward,) = add_pairs((self.forward,), (own_forward,))
+
+    def last(self):
+        return self.parts[0], self.forward, self.backward
+
+
+def add_kernel(count, *refs):
+    for i in range(count):
+        total = refs[i][...].astype(FLOAT) + refs[count + i][...].astype(FLOAT)
+        refs[2 * count + i][...] = total.astype(HALF)
+
+
+def add_pairs(left, right):
+    count = len(left)
+    shape = left[0].shape
+    return pl.pallas_call(
+        functools.partial(add_kernel, count),
+        out_shape=[jax.ShapeDtypeStruct(shape, HALF)] * count,
+        compiler_params=pltpu.CompilerParams(vmem_limit_bytes=VMEM_LIMIT),
+        cost_estimate=pl.CostEstimate(
+            flops=count * left[0].size, bytes_accessed=6 * count * left[0].size, transcendentals=0
+        ),
+        name="add_pairs",
+    )(*left, *right)
+
+
+def wide_first(sent):
+    count = lax.axis_size("wide")
+    return lax.ppermute(sent, "wide", [(i, i ^ 1) for i in range(count)])
+
+
+def wide_rest(kept, got):
     count = lax.axis_size("wide")
     place = lax.axis_index("wide")
-    bit = 1
-    while bit < count:
-        pairs = chunks.reshape((chunks.shape[0] // 2, 2) + chunks.shape[1:])
-        mine = (place // bit) % 2
-        kept = lax.dynamic_index_in_dim(pairs, mine, axis=1, keepdims=False)
-        sent = lax.dynamic_index_in_dim(pairs, 1 - mine, axis=1, keepdims=False)
-        got = lax.ppermute(sent, "wide", [(i, i ^ bit) for i in range(count)])
-        chunks = (kept.astype(FLOAT) + got.astype(FLOAT)).astype(HALF)
-        bit *= 2
-    return chunks[0]
-
-
-def wide_finish(kept, sent):
-    count = lax.axis_size("wide")
-    place = lax.axis_index("wide")
-    got = lax.ppermute(sent, "wide", [(i, i ^ 1) for i in range(count)])
+    terms = [kept, got]
     bit = 2
     while bit < count:
         mine = (place // bit) % 2
@@ -100,19 +118,15 @@
             pairs = array.reshape((array.shape[0] // 2, 2) + array.shape[1:])
             return lax.dynamic_index_in_dim(pairs, index, axis=1, keepdims=False)
 
-        def added(index):
-            return (half(kept, index).astype(FLOAT) + half(got, index).astype(FLOAT)).astype(HALF)
-
-        kept, got = added(mine), lax.ppermute(
-            added(1 - mine), "wide", [(i, i ^ bit) for i in range(count)]
-        )
+        sent = sum(half(term, 1 - mine).astype(FLOAT) for term in terms).astype(HALF)
+        swap = [(i, i ^ bit) for i in range(count)]
+        terms = [half(term, mine) for term in terms] + [lax.ppermute(sent, "wide", swap)]
         bit *= 2
-    return kept[0].astype(FLOAT) + got[0].astype(FLOAT)
-
-
-def norm_back(grad_out, normed, inv_scale, gain):
-    scaled = grad_out * gain
-    return inv_scale * (scaled - normed * jnp.mean(scaled * normed, axis=1, keepdims=True))
+    return terms
+
+
+def wide_total(terms):
+    return sum(term[0].astype(FLOAT) for term in terms)
 
 
 VMEM_LIMIT = 60 * 2**20
@@ -123,17 +137,18 @@
     return pl.BlockSpec(shape, lambda *_: (0,) * len(shape))
 
 
-def rows_kernel(count, units, chained, *refs):
-    xs, cs, gates = refs[:count], refs[count : 2 * count], refs[2 * count : 3 * count]
-    gate_w, up_w, down_w = refs[3 * count : 3 * count + 3]
-    outs = refs[3 * count + 3 + (3 if chained else 0) :]
+def rows_kernel(slots, units, chained, blocks_ref, *refs):
+    count = len(slots)
+    xs, cs, gates = refs[:count], refs[count : 2 * count], refs[2 * count]
+    gate_w, up_w, down_w = refs[2 * count + 1 : 2 * count + 4]
+    outs = refs[2 * count + 4 + (3 if chained else 0) :]
     inner, gate_g, up_g = outs[:3]
     ys, ds = outs[3 : 3 + count], outs[3 + count : 3 + 2 * count]
     y_sum, d_sum, x_rows, c_rows = outs[3 + 2 * count :]
     step = pl.program_id(0)
     length = xs[0].shape[0]
     chunk = gate_w.shape[1]
-    per_expert = pl.num_programs(0) // gates[0].shape[1]
+    per_expert = pl.num_programs(0) // gates.shape[2]
 
     @pl.when(step == 0)
     def _():
@@ -149,7 +164,8 @@
         jnp.int32, (count * length, chunk), 1
     )
     picked = []
-    for gate in gates:
+    for slot in slots:
+        gate = gates[blocks_ref[slot]]
         own = gate[:, 0:1]
         for e in range(1, gate.shape[1]):
             own = jnp.where(expert == e, gate[:, e : e + 1], own)
@@ -173,28 +189,31 @@
             ds[i][...] = d_sum[i * length : (i + 1) * length].astype(HALF)
 
 
-def expert_rows(units, place, total, kept, xs, cs, gates, gate_w, up_w, down_w):
+def expert_rows(units, slots, place, total, kept, blocks, xs, cs, gates, gate_w, up_w, down_w):
     count = len(xs)
     length, width = xs[0].shape
     padded = gate_w.shape[1]
     rows = count * length
-    column_block = pl.BlockSpec((width, CHUNK), lambda f: (0, f))
-    row_block = pl.BlockSpec((CHUNK, width), lambda f: (f, 0))
-    kept_block = pl.BlockSpec((rows, CHUNK), lambda f: (place // rows, f))
+    column_block = pl.BlockSpec((width, CHUNK), lambda f, b: (0, f))
+    row_block = pl.BlockSpec((CHUNK, width), lambda f, b: (f, 0))
+    kept_block = pl.BlockSpec((rows, CHUNK), lambda f, b: (place // rows, f))
     chained = kept is not None
-    first_kept = 3 * count + 3
-    return pl.pallas_call(
-        functools.partial(rows_kernel, count, units, chained),
-        grid=(padded // CHUNK,),
-        in_specs=[whole_block(xs[0].shape)] * (2 * count)
-        + [whole_block(gates[0].shape)] * count
-        + [column_block, column_block, row_block]
-        + [pl.BlockSpec(memory_space=pl.ANY)] * (3 if chained else 0),
-        out_specs=[kept_block] * 3 + [whole_block(xs[0].shape)] * (2 * count),
+    first_kept = 1 + 2 * count + 4
+    return pl.pallas_call(
+        functools.partial(rows_kernel, slots, units, chained),
+        grid_spec=pltpu.PrefetchScalarGridSpec(
+            num_scalar_prefetch=1,
+            grid=(padded // CHUNK,),
+            in_specs=[whole_block(xs[0].shape)] * (2 * count)
+            + [whole_block(gates.shape), column_block, column_block, row_block]
+            + [pl.BlockSpec(memory_space=pl.ANY)] * (3 if chained else 0),
+            out_specs=[kept_block] * 3 + [whole_block(xs[0].shape)] * (2 * count),
+            scratch_shapes=[pltpu.VMEM((rows, width), FLOAT)] * 2
+            + [pltpu.VMEM((rows, width), HALF)] * 2,
+        ),
         out_shape=[jax.ShapeDtypeStruct((total, padded), HALF)] * 3
         + [jax.ShapeDtypeStruct(xs[0].shape, HALF)] * (2 * count),
         input_output_aliases={first_kept + i: i for i in range(3)} if chained else {},
-        scratch_shapes=[pltpu.VMEM((rows, width), FLOAT)] * 2 + [pltpu.VMEM((rows, width), HALF)] * 2,
         compiler_params=pltpu.CompilerParams(vmem_limit_bytes=VMEM_LIMIT),
         cost_estimate=pl.CostEstimate(
             flops=12 * rows * width * padded,
@@ -202,7 +221,7 @@
             transcendentals=rows * padded,
         ),
         name="expert_rows",
-    )(*xs, *cs, *gates, gate_w, up_w, down_w, *(kept if chained else ()))
+    )(blocks, *xs, *cs, gates, gate_w, up_w, down_w, *(kept if chained else ()))
 
 
 def pack_experts_kernel(units, choice, shared_gate, shared_up, shared_down, gate, up, down, *rest):
@@ -290,7 +309,7 @@
 
     @pl.when(step == per_expert - 1)
     def _():
-        share[...] = total[:, units - (per_expert - 1) * chunk :].astype(HALF)
+        share[...] = total[:, units - (per_expert - 1) * chunk :]
 
 
 def in_grad(units, experts, copies, core, slots, grad):
@@ -314,7 +333,7 @@
                 pltpu.SemaphoreType.DMA((len(slots),)),
             ],
         ),
-        out_shape=[jax.ShapeDtypeStruct(part, HALF)] * 2 + [jax.ShapeDtypeStruct((width, share), HALF)],
+        out_shape=[jax.ShapeDtypeStruct(part, HALF)] * 2 + [jax.ShapeDtypeStruct((width, share), FLOAT)],
         compiler_params=pltpu.CompilerParams(vmem_limit_bytes=VMEM_LIMIT),
         cost_estimate=pl.CostEstimate(
             flops=2 * total * width * padded, bytes_accessed=2 * (total + width) * (padded + width), transcendentals=0
@@ -325,10 +344,12 @@
 
 def out_grad_kernel(count, units, core_ref, *refs):
     slots, inner = refs[:count], refs[count]
-    kept, sent, share, rows, total, sems = refs[count + 1 :]
+    kept, sent, rows, total, sems = refs[count + 1 :]
     step = pl.program_id(0)
     chunk = inner.shape[1]
-    per_expert = pl.num_programs(0) // 2
+    per_expert = total.shape[0] // chunk
+    experts = pl.num_programs(0) // per_expert
+    copies = 2 * kept.shape[0]
 
     @pl.when(step == 0)
     def _():
@@ -337,22 +358,26 @@
     part = step % per_expert
     total[pl.ds(pl.multiple_of(part * chunk, chunk), chunk)] = matmul(inner[...], rows[...], (0, 0))
 
-    @pl.when(part == per_expert - 1)
-    def _():
-        split_rows(total, core_ref[0], kept, sent, 0, kept.shape[2], slice(0, kept.shape[3]))
-
-    @pl.when(step == per_expert - 1)
-    def _():
-        share[...] = total[units:, :].astype(HALF)
+    def split(first, size, row):
+        for j in range(kept.shape[0]):
+            for target, parity in ((kept, core_ref[0]), (sent, 1 - core_ref[0])):
+                start = pl.multiple_of(first + (2 * j + parity) * size, 8)
+                target[j, row : row + size] = total[pl.ds(start, size)].astype(HALF)
+
+    for e in range(experts):
+
+        @pl.when(step == (e + 1) * per_expert - 1)
+        def _():
+            split(0, units // copies, e * (units // copies))
+            if e == 0:
+                split(units, (total.shape[0] - units) // copies, experts * (units // copies))
 
 
 def out_grad(units, experts, copies, core, slots, inner):
     length, width = slots[0].shape
     total, padded = inner.shape
-    per_expert = padded // experts // CHUNK
-    part = (copies // 2, experts, units // copies, width)
-    part_block = pl.BlockSpec((part[0], 1) + part[2:], lambda f, c: (0, f // per_expert, 0, 0))
     share = padded // experts - units
+    part = (copies // 2, (experts * units + share) // copies, width)
     return pl.pallas_call(
         functools.partial(out_grad_kernel, len(slots), units),
         grid_spec=pltpu.PrefetchScalarGridSpec(
@@ -360,20 +385,153 @@
             grid=(padded // CHUNK,),
             in_specs=[pl.BlockSpec(memory_space=pl.ANY)] * len(slots)
             + [pl.BlockSpec((total, CHUNK), lambda f, c: (0, f))],
-            out_specs=[part_block, part_block, whole_block((share, width))],
+            out_specs=[whole_block(part)] * 2,
             scratch_shapes=[
                 pltpu.VMEM((total, width), HALF),
                 pltpu.VMEM((padded // experts, width), FLOAT),
                 pltpu.SemaphoreType.DMA((len(slots),)),
             ],
         ),
-        out_shape=[jax.ShapeDtypeStruct(part, HALF)] * 2 + [jax.ShapeDtypeStruct((share, width), HALF)],
+        out_shape=[jax.ShapeDtypeStruct(part, HALF)] * 2,
         compiler_params=pltpu.CompilerParams(vmem_limit_bytes=VMEM_LIMIT),
         cost_estimate=pl.CostEstimate(
             flops=2 * total * width * padded, bytes_accessed=2 * (total + width) * (padded + width), transcendentals=0
         ),
         name="expert_out_grad",
     )(core, *slots, inner)
+
+
+def scaled_rows(values):
+    scale = lax.rsqrt(jnp.mean(values * values, axis=1, keepdims=True) + EPS)
+    return values * scale, scale
+
+
+def mix_kernel(returned, spare_out, weight, tokens, gain, hidden, attended, ffn_in):
+    for head in range(returned.shape[0]):
+        attended[:, head_slice(head)] = returned[head]
+    attended[:, returned.shape[0] * HEAD_DIM :] = spare_out[...]
+    hidden[...] = tokens[...].astype(FLOAT) + matmul(attended[...], weight[...], (1, 0))
+    ffn_in[...] = (scaled_rows(hidden[...])[0] * gain[...]).astype(HALF)
+
+
+def mix(returned, spare_out, weight, tokens, gain):
+    shape = tokens.shape
+    return pl.pallas_call(
+        mix_kernel,
+        out_shape=[
+            jax.ShapeDtypeStruct(shape, FLOAT),
+            jax.ShapeDtypeStruct(shape, HALF),
+            jax.ShapeDtypeStruct(shape, HALF),
+        ],
+        compiler_params=pltpu.CompilerParams(vmem_limit_bytes=VMEM_LIMIT),
+        cost_estimate=pl.CostEstimate(
+            flops=2 * shape[0] * shape[1] ** 2, bytes_accessed=2 * shape[1] ** 2 + 12 * shape[0] * shape[1], transcendentals=0
+        ),
+        name="mix",
+    )(returned, spare_out, weight, tokens, gain)
+
+
+def norm_grad(grad_out, normed, scale, gain):
+    scaled = grad_out * gain
+    return scale * (scaled - normed * jnp.mean(scaled * normed, axis=1, keepdims=True))
+
+
+def back_kernel(
+    own, forward, backward, hidden, cotangent, gain, weight, hidden_grad, branch, out_grad, spare_grad, terms
+):
+    ffn_in_grad = own[...].astype(FLOAT) + forward[...].astype(FLOAT) + backward[...].astype(FLOAT)
+    normed, scale = scaled_rows(hidden[...])
+    terms[...] = (ffn_in_grad * normed).astype(HALF)
+    hidden_grad[...] = cotangent[...].astype(FLOAT) + norm_grad(ffn_in_grad, normed, scale, gain[...])
+    branch[...] = hidden_grad[...].astype(HALF)
+    attended_grad = matmul(branch[...], weight[...], (1, 1)).astype(HALF)
+    for head in range(out_grad.shape[0]):
+        out_grad[head] = attended_grad[:, head_slice(head)]
+    spare_grad[...] = attended_grad[:, out_grad.shape[0] * HEAD_DIM :]
+
+
+def back(arrived, hidden, cotangent, gain, weight, heads):
+    length, width = hidden.shape
+    shapes = [
+        ((length, width), FLOAT),
+        ((length, width), HALF),
+        ((heads, length, HEAD_DIM), HALF),
+        ((length, width - heads * HEAD_DIM), HALF),
+        ((length, width), HALF),
+    ]
+    return pl.pallas_call(
+        back_kernel,
+        out_shape=[jax.ShapeDtypeStruct(shape, kind) for shape, kind in shapes],
+        compiler_params=pltpu.CompilerParams(vmem_limit_bytes=VMEM_LIMIT),
+        cost_estimate=pl.CostEstimate(
+            flops=2 * length * width**2, bytes_accessed=2 * width**2 + 24 * length * width, transcendentals=0
+        ),
+        name="back",
+    )(*arrived, hidden, cotangent, gain, weight)
+
+
+def dense_wgrad_kernel(core_ref, attended, branch, terms, gate_share, up_share, kept, sent, total):
+    width = attended.shape[1]
+    total[:, :width] = matmul(attended[...], branch[...], (0, 0))
+    ones = jnp.ones((terms.shape[0], HEAD_DIM), HALF)
+    total[:, width : width + HEAD_DIM] = matmul(terms[...], ones, (0, 0))
+    size = kept.shape[1]
+    for j in range(kept.shape[0]):
+        for target, parity in ((kept, core_ref[0]), (sent, 1 - core_ref[0])):
+            start = pl.multiple_of((2 * j + parity) * size, 8)
+            rows = pl.ds(start, size)
+            column = width + HEAD_DIM
+            target[j, :, :column] = total[rows].astype(HALF)
+            for share in (gate_share, up_share):
+                target[j, :, column : column + share.shape[1]] = share[rows, :].astype(HALF)
+                column += share.shape[1]
+
+
+def dense_wgrad(core, copies, attended, branch, terms, gate_share, up_share):
+    length, width = attended.shape
+    columns = width + HEAD_DIM + gate_share.shape[1] + up_share.shape[1]
+    part = (copies // 2, width // copies, columns)
+    operands = (attended, branch, terms, gate_share, up_share)
+    return pl.pallas_call(
+        dense_wgrad_kernel,
+        grid_spec=pltpu.PrefetchScalarGridSpec(
+            num_scalar_prefetch=1,
+            grid=(1,),
+            in_specs=[whole_block(array.shape) for array in operands],
+            out_specs=[whole_block(part)] * 2,
+            scratch_shapes=[pltpu.VMEM((width, width + HEAD_DIM), FLOAT)],
+        ),
+        out_shape=[jax.ShapeDtypeStruct(part, HALF)] * 2,
+        compiler_params=pltpu.CompilerParams(vmem_limit_bytes=VMEM_LIMIT),
+        cost_estimate=pl.CostEstimate(
+            flops=2 * length * width**2, bytes_accessed=2 * width * columns + 8 * length * width, transcendentals=0
+        ),
+        name="dense_wgrad",
+    )(core, *operands)
+
+
+def tokens_grad_kernel(own, forward, backward, spare_grad, weight, tokens, gain, hidden_grad, out):
+    attn_in_grad = (
+        own[...].astype(FLOAT)
+        + forward[...].astype(FLOAT)
+        + backward[...].astype(FLOAT)
+        + matmul(spare_grad[...], weight[...], (1, 1))
+    )
+    normed, scale = scaled_rows(tokens[...].astype(FLOAT))
+    out[...] = hidden_grad[...] + norm_grad(attn_in_grad, normed, scale, gain[...])
+
+
+def input_grad(arrived, spare_grad, weight, tokens, gain, hidden_grad):
+    length, width = tokens.shape
+    return pl.pallas_call(
+        tokens_grad_kernel,
+        out_shape=jax.ShapeDtypeStruct((length, width), FLOAT),
+        compiler_params=pltpu.CompilerParams(vmem_limit_bytes=VMEM_LIMIT),
+        cost_estimate=pl.CostEstimate(
+            flops=2 * length * width * weight.shape[1], bytes_accessed=16 * length * width, transcendentals=0
+        ),
+        name="tokens_grad",
+    )(*arrived, spare_grad, weight, tokens, gain, hidden_grad)
 
 
 def turn(values, cosine, sine):
@@ -436,9 +594,10 @@
 
 
 def project_kernel(turned, tiles, chained, block_ref, *refs):
-    x, weight, cosine, sine = refs[:4]
-    outs = refs[5 if chained else 4 :]
-    lin = matmul(x[...], weight[...], (1, 0))
+    x, gain, weight, cosine, sine = refs[:5]
+    outs = refs[6 if chained else 5 :]
+    outs[1][...] = (scaled_rows(x[...].astype(FLOAT))[0] * gain[...]).astype(HALF)
+    lin = matmul(outs[1][...], weight[...], (1, 0))
     for tile in range(weight.shape[1] // HEAD_DIM):
         part = lin[:, head_slice(tile)]
         if tile < turned or tile >= tiles:
@@ -446,19 +605,22 @@
         if tile < tiles:
             outs[0][0, :, head_slice(tile)] = part.astype(HALF)
         else:
-            outs[1][:, head_slice(tile - tiles)] = part.astype(HALF)
-
-
-def project(blocks, slot, x, weight, cosine, sine, turned, tiles, packed):
+            outs[2][:, head_slice(tile - tiles)] = part.astype(HALF)
+
+
+def project(blocks, slot, x, gain, weight, cosine, sine, turned, tiles, packed):
     length, width = x.shape
     count = cosine.shape[0]
-    extra = weight.shape[1] - tiles * HEAD_DIM if packed is None else 0
+    chained = packed is not None
+    extra = 0 if chained else weight.shape[1] - tiles * HEAD_DIM
     columns = tiles * HEAD_DIM + extra
-    chained = packed is not None
     table = pl.BlockSpec((1, length, HEAD_DIM), lambda i, b: (b[slot], 0, 0))
     packed_shape = (count, length, tiles * HEAD_DIM)
-    out_specs = [pl.BlockSpec((1,) + packed_shape[1:], lambda i, b: (b[slot], 0, 0))]
-    out_shape = [jax.ShapeDtypeStruct(packed_shape, HALF)]
+    out_specs = [
+        pl.BlockSpec((1,) + packed_shape[1:], lambda i, b: (b[slot], 0, 0)),
+        whole_block(x.shape),
+    ]
+    out_shape = [jax.ShapeDtypeStruct(packed_shape, HALF), jax.ShapeDtypeStruct(x.shape, HALF)]
     if extra:
         out_specs.append(whole_block((length, extra)))
         out_shape.append(jax.ShapeDtypeStruct((length, extra), HALF))
@@ -467,12 +629,12 @@
         grid_spec=pltpu.PrefetchScalarGridSpec(
             num_scalar_prefetch=1,
             grid=(1,),
-            in_specs=[whole_block(x.shape), whole_block((width, columns)), table, table]
+            in_specs=[whole_block(x.shape), whole_block(gain.shape), whole_block((width, columns)), table, table]
             + ([pl.BlockSpec(memory_space=pl.ANY)] if chained else []),
             out_specs=out_specs,
         ),
         out_shape=out_shape,
-        input_output_aliases={5: 0} if chained else {},
+        input_output_aliases={6: 0} if chained else {},
         compiler_params=pltpu.CompilerParams(vmem_limit_bytes=VMEM_LIMIT),
         cost_estimate=pl.CostEstimate(
             flops=2 * length * width * columns,
@@ -480,7 +642,7 @@
             transcendentals=0,
         ),
         name="project",
-    )(blocks, x, weight, cosine, sine, *([packed] if chained else []))
+    )(blocks, x, gain, weight, cosine, sine, *([packed] if chained else []))
 
 
 EXP_SCALE = HEAD_DIM**-0.5 * 1.4426950408889634
@@ -754,31 +916,9 @@
     order = jnp.asarray(ring_order(group), dtype=jnp.int32)
     ring_place = jnp.where(place % 2 == 0, place // 2, group - 1 - place // 2)
     slot_block = order[(ring_place + jnp.arange(group, dtype=jnp.int32)) % group]
-    blocks = jnp.arange(group, dtype=jnp.int32)
-    block_ring = jnp.where(blocks % 2 == 0, blocks // 2, group - 1 - blocks // 2)
-    block_slot = (block_ring - ring_place) % group
-
-    def by_slot(array):
-        return jnp.take(array, slot_block, axis=0)
-
-    def by_block(array):
-        return jnp.take(array, block_slot, axis=0)
-
-    inputs = tokens.astype(FLOAT)
-    inv_one = lax.rsqrt(jnp.mean(inputs * inputs, axis=1, keepdims=True) + EPS)
-    normed_one = inputs * inv_one
-    attn_in = (normed_one * attn_gain).astype(HALF)
-    expert_ids = jnp.arange(experts, dtype=jnp.int32)
-    picked = after(routes, attn_in)[:, :, None] == expert_ids[None, None, :]
-    token_gate = jnp.sum(jnp.where(picked, gates[:, :, None], 0.0), axis=1)
-    own_gates = lax.all_to_all(
-        token_gate.T.reshape(group, local_experts, length),
-        "narrow",
-        split_axis=0,
-        concat_axis=0,
-        tiled=True,
-    )
-    own_gates = by_slot(own_gates.transpose(0, 2, 1))
+    attn_gain_row = attn_gain.astype(FLOAT).reshape(1, width)
+    ffn_gain_row = ffn_gain.astype(FLOAT).reshape(1, width)
+    core = (lax.axis_index("wide") % 2).astype(jnp.int32).reshape(1)
 
     own_place = place.astype(jnp.int32).reshape(1)
     packed_weight = pack_heads(own_place, spare_heads, query_weight, key_weight, value_weight)
@@ -792,145 +932,138 @@
     sine = jnp.concatenate([-sine, sine], axis=1).reshape(group, length, HEAD_DIM)
 
     share = hidden_units // (copies * group)
-    taken = copies * share
-    padded = -(-taken // 128) * 128
-    per_expert = -(-(hidden_units + padded) // CHUNK) * CHUNK
+    per_expert = -(-(hidden_units + copies * share) // CHUNK) * CHUNK
     gap = per_expert - hidden_units
+    spacing = gap // copies
     column = jnp.arange(gap, dtype=jnp.int32)
     unit = jnp.where(
-        column < taken, ((column // share) * group + place) * share + column % share, -1
+        column % spacing < share,
+        ((column // spacing) * group + place) * share + column % spacing,
+        -1,
     )
     choice = (jnp.arange(hidden_units, dtype=jnp.int32)[:, None] == unit[None, :]).astype(HALF)
 
     heads = {}
+    attn_slots = [None] * group
+
+    def project_slot(slot, x):
+        result = project(
+            slot_block,
+            slot,
+            x,
+            attn_gain_row,
+            packed_weight,
+            cosine,
+            sine,
+            turned,
+            tiles,
+            heads.get("packed"),
+        )
+        heads["packed"], attn_slots[slot] = result[:2]
+        if slot == 0:
+            heads["spare"] = result[2]
 
     def project_slots(step, slots):
         for slot in (step, group - step) if step else (0,):
-            result = project(
-                slot_block,
-                slot,
-                slots[slot],
-                packed_weight,
-                cosine,
-                sine,
-                turned,
-                tiles,
-                heads.get("packed"),
+            project_slot(slot, slots[slot])
+        if step == 1:
+            expert_ids = jnp.arange(experts, dtype=jnp.int32)
+            picked = after(routes, slots[1])[:, :, None] == expert_ids[None, None, :]
+            token_gate = jnp.sum(jnp.where(picked, gates[:, :, None], 0.0), axis=1)
+            arrived = lax.all_to_all(
+                token_gate.T.reshape(group, local_experts, length),
+                "narrow",
+                split_axis=0,
+                concat_axis=0,
+                tiled=True,
             )
-            heads["packed"] = result[0]
-            if slot == 0:
-                heads["spare"] = result[1]
-        if step == 0:
-            heads["gates"] = own_gates
-        if step == 1:
-            heads["experts"] = pack_experts(
-                per_expert,
-                *after((choice, shared_gate, shared_up, shared_down, expert_gate, expert_up, expert_down), slots[1]),
-            )
-        return tuple(heads.values())
+            heads["gates"] = arrived.transpose(0, 2, 1)
+        return (heads["packed"],)
 
     half_ring = group // 2
-    attn_slots = ring_gather(attn_in, project_slots)
-    gate_weight, up_weight, down_weight = heads["experts"]
-    (packed_heads,) = project(
-        slot_block,
-        half_ring,
-        attn_slots[half_ring],
-        packed_weight,
-        cosine,
-        sine,
-        turned,
-        tiles,
-        heads["packed"],
-    )
-    spare_q = heads["spare"]
-    cot_slots = ring_gather(after(cotangent, attn_slots[half_ring]))
+    token_slots = ring_gather(tokens, project_slots)
+    cot_slots = ring_gather(after(cotangent, token_slots[half_ring]))
+    project_slot(half_ring, token_slots[half_ring])
+    packed_heads, spare_q, own_gates = heads["packed"], heads["spare"], heads["gates"]
     own_out, spare_out, level, spare_level = attention(own_place, packed_heads, spare_q)
     returned = lax.all_to_all(own_out, "narrow", split_axis=0, concat_axis=0, tiled=True)
-    attended = jnp.concatenate(
-        [returned.transpose(1, 0, 2).reshape(length, own_heads), spare_out], axis=1
-    )
-    hidden = inputs + matmul(attended, output_weight, (1, 0))
-    inv_two = lax.rsqrt(jnp.mean(hidden * hidden, axis=1, keepdims=True) + EPS)
-    normed_two = hidden * inv_two
-    ffn_in = (normed_two * ffn_gain).astype(HALF)
-
-    batches = [(0,)] + [(k, group - k) for k in range(1, half_ring)] + [(half_ring,)]
-    row_order = [slot for batch in batches if len(batch) == 2 for slot in batch] + [0, half_ring]
-    experts_state = {"kept": None}
+    gate_weight, up_weight, down_weight = pack_experts(
+        per_expert,
+        *after((choice, shared_gate, shared_up, shared_down, expert_gate, expert_up, expert_down), own_out),
+    )
+    hidden, attended, ffn_in = mix(returned, spare_out, output_weight, tokens, ffn_gain_row)
+
+    batches = [(0,), (1, group - 1), (2,), (half_ring, half_ring + 1), (half_ring - 1, half_ring + 2)]
+    row_order = [slot for batch in batches if len(batch) == 2 for slot in batch]
+    row_order += [slot for batch in batches if len(batch) == 1 for slot in batch]
+    rows_state = {"kept": None}
     out_parts, row_parts = [None] * group, [None] * group
 
-    def expert_batch(step, slots):
-        batch = batches[step]
+    def expert_batch(batch, slots):
         result = expert_rows(
             hidden_units,
+            batch,
             row_order.index(batch[0]) * length,
             seq_len,
-            experts_state["kept"],
+            rows_state["kept"],
+            slot_block,
             [slots[j] for j in batch],
             [cot_slots[j] for j in batch],
-            [own_gates[j] for j in batch],
+            own_gates,
             gate_weight,
             up_weight,
             down_weight,
         )
-        experts_state["kept"] = result[:3]
+        rows_state["kept"] = result[:3]
         for i, j in enumerate(batch):
             out_parts[j] = result[3 + i]
             row_parts[j] = result[3 + len(batch) + i]
         return tuple(result[3:])
 
-    ffn_slots = ring_gather(ffn_in, expert_batch)
-    expert_batch(half_ring, ffn_slots)
-    gated_inner, gate_grad, up_grad = experts_state["kept"]
-
-    core = (lax.axis_index("wide") % 2).astype(jnp.int32).reshape(1)
+    ffn_slots = ring_gather(
+        ffn_in, lambda step, slots: expert_batch(batches[step], slots) if step < 3 else ()
+    )
+    expert_batch(batches[3], ffn_slots)
+    row_sum, out_sum = RingSum(row_parts), RingSum(out_parts)
+    row_first = row_sum.hop()
+    out_sum.hop()
+    expert_batch(batches[4], ffn_slots)
+    gated_inner, gate_grad, up_grad = rows_state["kept"]
     ordered_cots = [cot_slots[j] for j in row_order]
     ordered_rows = [ffn_slots[j] for j in row_order]
-    weight_grads = {}
-
-    def expert_weights(step, arrived):
-        if step == 2:
-            weight_grads["down"] = out_grad(
-                hidden_units, local_experts, copies, core, ordered_cots, after(gated_inner, *arrived)
-            )
-            return tuple(weight_grads["down"])
-        if step == 1:
-            weight_grads["gate"] = in_grad(
-                hidden_units, local_experts, copies, core, ordered_rows, after(gate_grad, *arrived)
-            )
-            return tuple(weight_grads["gate"])
-        if step == 3:
-            weight_grads["up"] = in_grad(
-                hidden_units, local_experts, copies, core, ordered_rows, after(up_grad, *arrived)
-            )
-            return tuple(weight_grads["up"])
-        return ()
-
-    ffn_in_grad = ring_scatter(row_parts, expert_weights)
-    down_kept, down_sent, down_share = weight_grads["down"]
-    gate_kept, gate_sent, gate_share = weight_grads["gate"]
-    up_kept, up_sent, up_share = weight_grads["up"]
-    expert_down_grad = wide_finish(down_kept, down_sent)
-    expert_gate_grad = wide_finish(gate_kept, gate_sent)
-    expert_up_grad = wide_finish(up_kept, up_sent)
-    shared_down_grad = wide_scatter(down_share[:taken].reshape(copies, share, width)).astype(FLOAT)
-
-    hidden_grad = cotangent.astype(FLOAT) + norm_back(ffn_in_grad, normed_two, inv_two, ffn_gain)
-    branch_grad = hidden_grad.astype(HALF)
-    attended_grad = matmul(branch_grad, output_weight, (1, 1)).astype(HALF)
-    own_out_grad = lax.all_to_all(
-        attended_grad[:, :own_heads].reshape(length, group, HEAD_DIM).transpose(1, 0, 2),
-        "narrow",
-        split_axis=0,
-        concat_axis=0,
-        tiled=True,
-    )
-    late_parts = list(out_parts)
-    late_parts[half_ring], late_parts[half_ring + 1] = after(
-        (out_parts[half_ring], out_parts[half_ring + 1]), ffn_in_grad
-    )
-    mixed = (hidden + ring_scatter(late_parts)).astype(HALF)
+    row_sum.add()
+    row_second = row_sum.hop()
+    down_kept, down_sent = out_grad(
+        hidden_units, local_experts, copies, core, ordered_cots, after(gated_inner, *row_first)
+    )
+    down_got = wide_first(down_sent)
+    row_sum.add()
+    row_sum.hop(down_kept)
+    gate_kept, gate_sent, gate_share = in_grad(
+        hidden_units, local_experts, copies, core, ordered_rows, after(gate_grad, *row_second)
+    )
+    gate_got = wide_first(gate_sent)
+    row_sum.add()
+    row_last = row_sum.hop(gate_kept)
+
+    hidden_grad, branch_grad, out_grads, spare_out_grad, gain_terms = back(
+        row_sum.last(), hidden, cotangent, ffn_gain_row, output_weight, group
+    )
+    out_sum.add()
+    out_sum.hop(*row_last)
+    own_out_grad = lax.all_to_all(out_grads, "narrow", split_axis=0, concat_axis=0, tiled=True)
+    up_kept, up_sent, up_share = in_grad(
+        hidden_units, local_experts, copies, core, ordered_rows, after(up_grad, out_grads)
+    )
+    up_got = wide_first(up_sent)
+    down_terms = wide_rest(*after((down_kept, down_got), out_grads))
+    gate_terms = wide_rest(*after((gate_kept, gate_got), up_kept))
+    dense_kept, dense_sent = dense_wgrad(
+        core, copies, attended, branch_grad, gain_terms, gate_share, up_share
+    )
+    dense_got = wide_first(dense_sent)
+    out_sum.add()
+    out_sum.hop(own_out_grad)
     head_grad, spare_query_grad = attention_back(
         own_place,
         packed_heads,
@@ -940,20 +1073,46 @@
         level,
         spare_level,
         own_out_grad,
-        attended_grad[:, own_heads:],
+        spare_out_grad,
         cosine,
         sine,
     )
-    far = (half_ring, half_ring + 1)
-    near = tuple(j for j in range(group) if j not in far)
-    attn_part = dict(zip(far, attn_parts(slot_block, far, head_grad, packed_weight)))
-    attn_part.update(zip(near, attn_parts(slot_block, near, head_grad, packed_weight)))
-    attn_in_grad = ring_scatter([attn_part[j] for j in range(group)])
-    attn_in_grad = attn_in_grad + matmul(spare_query_grad, spare_query_weight, (1, 1))
-    tokens_grad = hidden_grad + norm_back(attn_in_grad, normed_one, inv_one, attn_gain)
-
-    def spread(grad):
-        return wide_scatter(grad.astype(HALF).reshape(copies, width // copies, grad.shape[1]))
+    attn_part = [None] * group
+
+    def attn_batch(slots, grad):
+        for j, part in zip(slots, attn_parts(slot_block, slots, grad, packed_weight)):
+            attn_part[j] = part
+
+    attn_batch((half_ring, half_ring + 1), head_grad)
+    attn_sum = RingSum(attn_part)
+    attn_first = attn_sum.hop()
+    attn_kept, attn_sent = attn_wgrad(
+        slot_block, core, copies, attn_slots, after(head_grad, *attn_part[half_ring : half_ring + 2]), spare_query_grad
+    )
+    attn_got = wide_first(attn_sent)
+    attn_batch((half_ring - 1, half_ring + 2), after(head_grad, attn_kept))
+    attn_sum.add()
+    attn_second = attn_sum.hop()
+    rest = tuple(j for j in range(group) if attn_part[j] is None)
+    attn_batch(rest, after(head_grad, *attn_first))
+    attn_terms = wide_rest(*after((attn_kept, attn_got), attn_part[rest[0]]))
+    dense_terms = wide_rest(*after((dense_kept, dense_got), head_grad))
+    up_terms = wide_rest(*after((up_kept, up_got), head_grad))
+    out_sum.add()
+    out_sum.hop(*attn_first)
+    attn_sum.add()
+    attn_third = attn_sum.hop(attn_part[rest[0]])
+    attn_sum.add()
+    attn_last = attn_sum.hop()
+    tokens_grad = input_grad(
+        attn_sum.last(), spare_query_grad, spare_query_weight, tokens, attn_gain_row, hidden_grad
+    )
+    mixed = (hidden + sum(part.astype(FLOAT) for part in out_sum.last())).astype(HALF)
+    down_total = wide_total(after(down_terms, *attn_first))
+    expert_down_grad = down_total[: -spacing].reshape(local_experts, hidden_units // copies, width)
+    shared_down_grad = down_total[-spacing:][:share]
+    expert_gate_grad = wide_total(after(gate_terms, *attn_second))
+    expert_up_grad = wide_total(after(up_terms, *attn_third))
 
     def exchange(part):
         return lax.all_to_all(
@@ -962,52 +1121,30 @@
             split_axis=0,
             concat_axis=0,
             tiled=True,
-        ).astype(FLOAT)
-
-    gain_terms = (ffn_in_grad * normed_two).astype(HALF)
-    gain_column = matmul(gain_terms, jnp.ones((length, 128), HALF), (0, 0))
-    out_wgrad = matmul(attended, branch_grad, (0, 0))
-    first = exchange(
-        jnp.concatenate(
-            [
-                spread(jnp.concatenate([out_wgrad, gain_column], axis=1)),
-                spread(
-                    jnp.concatenate(
-                        [
-                            gate_share[:, :padded],
-                            up_share[:, :padded],
-                        ],
-                        axis=1,
-                    )
-                ),
-            ],
-            axis=1,
         )
-    )
-    summed = jnp.sum(first[:, :, : width + 128], axis=0)
+
+    first = exchange(wide_total(after(dense_terms, *attn_second)).astype(HALF))
+    summed = jnp.sum(first[:, :, : width + 128].astype(FLOAT), axis=0)
     output_weight_grad = summed[:, :width]
     ffn_gain_grad = summed[:, width]
 
-    spot = jnp.arange(group * padded, dtype=jnp.int32)
-    spot_column = spot % padded
+    spot = jnp.arange(group * gap, dtype=jnp.int32)
+    spot_column = spot % gap
     spot_unit = jnp.where(
-        spot_column < taken,
-        ((spot_column // share) * group + spot // padded) * share + spot_column % share,
+        spot_column % spacing < share,
+        ((spot_column // spacing) * group + spot // gap) * share + spot_column % spacing,
         -1,
     )
     to_units = (spot_unit[:, None] == jnp.arange(hidden_units, dtype=jnp.int32)[None, :]).astype(HALF)
-    to_units = to_units.reshape(group, padded, hidden_units)
+    to_units = to_units.reshape(group, gap, hidden_units)
 
     def shared_columns(part):
-        return jnp.einsum("grc,gcu->ru", part.astype(HALF), to_units, preferred_element_type=FLOAT)
-
-    shared_gate_grad = shared_columns(first[:, :, width + 128 : width + 128 + padded])
-    shared_up_grad = shared_columns(first[:, :, width + 128 + padded :])
-
-    attn_kept, attn_sent = attn_wgrad(
-        slot_block, core, copies, attn_slots, head_grad, spare_query_grad
-    )
-    second = exchange(wide_finish(attn_kept, attn_sent).astype(HALF))
+        return jnp.einsum("grc,gcu->ru", part, to_units, preferred_element_type=FLOAT)
+
+    shared_gate_grad = shared_columns(first[:, :, width + 128 : width + 128 + gap])
+    shared_up_grad = shared_columns(first[:, :, width + 128 + gap :])
+
+    second = exchange(wide_total(attn_terms).astype(HALF)).astype(FLOAT)
     packed_sum = jnp.sum(second, axis=0)
     spare_width = spare_heads * HEAD_DIM
 

time: 621 us -> 569 us (0.916)
  waiting for transfers between devices: 162 us -> 98.3 us
  Pallas kernels: 257 us -> 313 us
  other arithmetic: 75.4 us -> 37.8 us
  matrix products: 13 us -> 4.74 us
    ppermute x35 -> x31, waiting for transfers between devices: 107 us -> 43.9 us  [the longest x12 21.5 us: hop(): self.forward = lax.ppermute(forward, 'narrow', ahead)]
    pallas_call x5 -> x18, Pallas kernels: 98.7 us -> 148 us  [the longest x5 103 us: expert_rows(): pl.pallas_call(functools.partial(rows_kernel, slots, units, chained), gri...]
    convert_element_type x31 -> x9, other arithmetic: 39 us -> 19 us  [the longest x5 10.5 us: wide_rest(): sum((half(term, 1 - mine).astype(FLOAT) for term in terms)).astype(HALF)]
    ppermute x12, waiting for transfers between devices: 21.9 us -> 41.1 us  [ring_gather(): forward = lax.ppermute(sent_ahead, 'narrow', ahead)]
    ppermute x9, waiting for transfers between devices: 13.7 us -> 1.66 us  [ring_gather(): backward = lax.ppermute(sent_back, 'narrow', back)]
    dot_general x7 -> x2, matrix products: 13 us -> 4.74 us  [shared_columns(): jnp.einsum('grc,gcu->ru', part, to_units, preferred_element_type=FLOAT)]
    all_to_all x2, waiting for transfers between devices: 19.4 us -> 11.7 us  [exchange(): lax.all_to_all(part.reshape(group, part.shape[0] // group, part.shape[1])...]
    add x5 -> x3, other arithmetic: 13.1 us -> 7.71 us  [wide_total(): return sum((term[0].astype(FLOAT) for term in terms))]
  transfers between devices with their start and end apart: 61 -> 57, of which waited for: 25 -> 20; matrix products, arithmetic and copies ran while one was open for 15% -> 10% of each run, Pallas kernels for 37% -> 52%
where the time goes in v4:
time: 569 us; the launch traced here: 559 us
  Pallas kernels  313 us (55%)
  waiting for transfers between devices  98.3 us (17%)
  starting transfers between devices  75.1 us (13%)
  other arithmetic  37.8 us (7%)
  local copies, waits for them, and re-layouts  28.4 us (5%)
    pallas_call x5, Pallas kernels, expert_rows(): pl.pallas_call(functools.partial(rows_kernel, slots, units, chained), gri...  103 us
    ppermute x12, waiting for transfers between devices, ring_gather(): forward = lax.ppermute(sent_ahead, 'narrow', ahead)  41.1 us
    pallas_call x2, Pallas kernels, in_grad(): pl.pallas_call(functools.partial(in_grad_kernel, len(slots), units), grid...  36.6 us
    pallas_call x8, Pallas kernels, project(): pl.pallas_call(functools.partial(project_kernel, turned, tiles, chained),...  35.4 us
    pallas_call x9, Pallas kernels, add_pairs(): pl.pallas_call(functools.partial(add_kernel, count), out_shape=[jax.Shape...  24.3 us
    ppermute x12, waiting for transfers between devices, hop(): self.forward = lax.ppermute(forward, 'narrow', ahead)  21.5 us
    pallas_call x3, Pallas kernels, attn_parts(): pl.pallas_call(functools.partial(part_kernel, slots), grid_spec=pltpu.Pre...  18.9 us
    pallas_call x1, Pallas kernels, out_grad(): pl.pallas_call(functools.partial(out_grad_kernel, len(slots), units), gri...  18.8 us
  transfers between devices with their start and end apart: 57, of which 20 were waited for; matrix products, arithmetic and copies ran while one was open for 10% of the time, Pallas kernels for 52%

profile of v4, /device:TPU:4, one launch (start us, length us, event | category | flops | bytes accessed | tf_op | source)
XLA Modules:
  0.0 559.3 jit_solution(2278693045047834745)
XLA Ops:
  73.2 9.9 %attention.1 = (bf16[8,256,128]{2,1,0:T(8,128)(2,1)}, bf16[256,256]{1,0:T(8,128)(2,1)}, f32[8,256,128]{2,1,0:T(8,128)}, f32[2,256,128]{2,1,0:T(8,128)}) custom-call(s32[1]{0:T(128)} %bitcast.place_ref, bf16[8,256,896]{2,1,0:T(8,128)(2,1)} %get-tuple-element.197.packed, bf16[256,256]{1,0:T(8,128)(2,1)} %get-tuple-element.198.spare_q), custom_call_target="tpu_custom_call" | custom-call | flops 3489660928 | bytes 7340032 | tf_op jit(solution)/shard_map/attention/pallas_call | solution.py:701
  83.1 6.1 %all-to-all-start = ((bf16[8,256,128]{2,1,0:T(8,128)(2,1)}), bf16[8,256,128]{2,1,0:T(8,128)(2,1)S(1)}, u32[]{:S(2)}, u32[]{:S(2)}) async-start(bf16[8,256,128]{2,1,0:T(8,128)(2,1)} %get-tuple-element.199.out), calls=%async_computation | async-start | bytes 1048576 | tf_op jit(solution)/shard_map/all_to_all | solution.py:989
  93.9 13.7 %pack_experts.1 = (bf16[1280,2048]{1,0:T(8,128)(2,1)}, bf16[1280,2048]{1,0:T(8,128)(2,1)}, bf16[2048,1280]{1,0:T(8,128)(2,1)}) custom-call(bf16[896,128]{1,0:T(8,128)(2,1)} %fusion.6.choice, bf16[1280,896]{1,0:T(8,128)(2,1)} %shared_gate, bf16[1280,896]{1,0:T(8,128)(2,1)} %shared_up, bf16[896,1280]{1,0:T(8,128)(2,1)} %shared_down, bf16[2,1280,896]{2,1,0:T(8,128)(2,1)} %gate, ...), custom_call_target="tpu_custom_call" | custom-call | bytes 31457280 | tf_op jit(solution)/shard_map/pack_experts/pallas_call | solution.py:259
  122.0 14.9 %expert_rows.5 = (bf16[2048,2048]{1,0:T(8,128)(2,1)}, bf16[2048,2048]{1,0:T(8,128)(2,1)}, bf16[2048,2048]{1,0:T(8,128)(2,1)}, bf16[256,1280]{1,0:T(8,128)(2,1)}, bf16[256,1280]{1,0:T(8,128)(2,1)}) custom-call(s32[8]{0:T(128)} %gather_fusion, bf16[256,1280]{1,0:T(8,128)(2,1)} %get-tuple-element.217.refs_0_.refs_6_, bf16[256,1280]{1,0:T(8,128)(2,1)} %cotangent.1, ...), custom_call_target="tpu_custom_call" | custom-call | flops 8053063680 | bytes 21495808 | tf_op jit(solution)/shard_map/expert_rows/pallas_call | solution.py:202
  139.0 7.3 %collective-permute-done.7.refs_1_ = bf16[256,1280]{1,0:T(8,128)(2,1)S(1)} collective-permute-done((bf16[256,1280]{1,0:T(8,128)(2,1)}, bf16[256,1280]{1,0:T(8,128)(2,1)S(1)}, u32[]{:S(2)}, u32[]{:S(2)}) %collective-permute-start.7) | collective-permute-done | bytes 655392 | tf_op jit(solution)/shard_map/ppermute | solution.py:44
  148.5 24.5 %expert_rows.6 = (bf16[2048,2048]{1,0:T(8,128)(2,1)}, bf16[2048,2048]{1,0:T(8,128)(2,1)}, bf16[2048,2048]{1,0:T(8,128)(2,1)}, bf16[256,1280]{1,0:T(8,128)(2,1)},...) custom-call(s32[8]{0:T(128)} %gather_fusion, ...), custom_call_target="tpu_custom_call", output_to_operand_aliasing={{0}: (9, {}), {1}: (10, {}), {2}: (11, {})} | custom-call | flops 16106127360 | bytes 27262976 | tf_op jit(solution)/shard_map/expert_rows/pallas_call | solution.py:202
  175.5 14.8 %expert_rows.7 = (bf16[2048,2048]{1,0:T(8,128)(2,1)}, bf16[2048,2048]{1,0:T(8,128)(2,1)}, bf16[2048,2048]{1,0:T(8,128)(2,1)}, bf16[256,1280]{1,0:T(8,128)(2,1)}, bf16[256,1280]{1,0:T(8,128)(2,1)}) custom-call(s32[8]{0:T(128)} %gather_fusion, bf16[256,1280]{1,0:T(8,128)(2,1)} %copy-done.25, ...), custom_call_target="tpu_custom_call", output_to_operand_aliasing={{0}: (7, {}), {1}: (8, {}), {2}: (9, {})} | custom-call | flops 8053063680 | bytes 21495808 | tf_op jit(solution)/shard_map/expert_rows/pallas_call | solution.py:202
  190.4 11.4 %collective-permute-done.13.refs_1_.refs_3_ = bf16[256,1280]{1,0:T(8,128)(2,1)S(1)} collective-permute-done((bf16[256,1280]{1,0:T(8,128)(2,1)S(1)}, bf16[256,1280]{1,0:T(8,128)(2,1)S(1)}, u32[]{:S(2)}, u32[]{:S(2)}) %collective-permute-start.13) | collective-permute-done | bytes 655392 | tf_op jit(solution)/shard_map/ppermute | solution.py:44
  202.2 10.7 %collective-permute-done.16.refs_0_.refs_2_ = bf16[256,1280]{1,0:T(8,128)(2,1)S(1)} collective-permute-done((bf16[256,1280]{1,0:T(8,128)(2,1)S(1)}, bf16[256,1280]{1,0:T(8,128)(2,1)S(1)}, u32[]{:S(2)}, u32[]{:S(2)}) %collective-permute-start.16) | collective-permute-done | bytes 655392 | tf_op jit(solution)/shard_map/ppermute | solution.py:44
  213.8 24.6 %expert_rows.8 = (bf16[2048,2048]{1,0:T(8,128)(2,1)}, bf16[2048,2048]{1,0:T(8,128)(2,1)}, bf16[2048,2048]{1,0:T(8,128)(2,1)}, bf16[256,1280]{1,0:T(8,128)(2,1)},...) custom-call(s32[8]{0:T(128)} %gather_fusion, ...), custom_call_target="tpu_custom_call", output_to_operand_aliasing={{0}: (9, {}), {1}: (10, {}), {2}: (11, {})} | custom-call | flops 16106127360 | bytes 27262976 | tf_op jit(solution)/shard_map/expert_rows/pallas_call | solution.py:202
  242.5 24.5 %expert_rows.9 = (bf16[2048,2048]{1,0:T(8,128)(2,1)}, bf16[2048,2048]{1,0:T(8,128)(2,1)}, bf16[2048,2048]{1,0:T(8,128)(2,1)}, bf16[256,1280]{1,0:T(8,128)(2,1)},...) custom-call(s32[8]{0:T(128)} %gather_fusion, ...), custom_call_target="tpu_custom_call", output_to_operand_aliasing={{0}: (9, {}), {1}: (10, {}), {2}: (11, {})} | custom-call | flops 16106127360 | bytes 27262976 | tf_op jit(solution)/shard_map/expert_rows/pallas_call | solution.py:202
  273.2 18.8 %expert_out_grad.1 = (bf16[2,480,1280]{2,1,0:T(8,128)(2,1)}, bf16[2,480,1280]{2,1,0:T(8,128)(2,1)}) custom-call(s32[1]{0:T(128)} %bitcast.4.core_ref, bf16[256,1280]{1,0:T(8,128)(2,1)} %copy-done.37, bf16[256,1280]{1,0:T(8,128)(2,1)} %collective-permute-done.12.refs_3_.refs_1_, bf16[256,1280]{1,0:T(8,128)(2,1)} %collective-permute-done.20.refs_2_, ...), custom_call_target="tpu_custom_call" | custom-call | flops 10737418240 | bytes 22151168 | tf_op jit(solution)/shard_map/expert_out_grad/pallas_call | solution.py:381
  297.1 18.3 %expert_in_grad.2 = (bf16[2,2,320,896]{3,2,1,0:T(8,128)(2,1)}, bf16[2,2,320,896]{3,2,1,0:T(8,128)(2,1)}, f32[1280,128]{1,0:T(8,128)}) custom-call(s32[1]{0:T(128)} %bitcast.4.core_ref, bf16[256,1280]{1,0:T(8,128)(2,1)} %copy-done.32, bf16[256,1280]{1,0:T(8,128)(2,1)} %copy-done.31, bf16[256,1280]{1,0:T(8,128)(2,1)} %copy-done.36, ...), custom_call_target="tpu_custom_call" | custom-call | flops 10737418240 | bytes 22151168 | tf_op jit(solution)/shard_map/expert_in_grad/pallas_call | solution.py:322
  323.8 10.8 %collective-permute-done.29.forward = bf16[256,1280]{1,0:T(8,128)(2,1)} collective-permute-done((bf16[256,1280]{1,0:T(8,128)(2,1)}, bf16[256,1280]{1,0:T(8,128)(2,1)}, u32[]{:S(2)}, u32[]{:S(2)}) %collective-permute-start.29) | collective-permute-done | bytes 655392 | tf_op jit(solution)/shard_map/ppermute | solution.py:65
  334.6 6.0 %back.1 = (f32[256,1280]{1,0:T(8,128)}, bf16[256,1280]{1,0:T(8,128)(2,1)}, bf16[8,256,128]{2,1,0:T(8,128)(2,1)}, bf16[256,256]{1,0:T(8,128)(2,1)}, bf16[256,1280]{1,0:T(8,128)(2,1)}) custom-call(bf16[256,1280]{1,0:T(8,128)(2,1)} %get-tuple-element.218.own, bf16[256,1280]{1,0:T(8,128)(2,1)} %collective-permute-done.29.forward, ...), custom_call_target="tpu_custom_call" | custom-call | flops 838860800 | bytes 11141120 | tf_op jit(solution)/shard_map/back/pallas_call | solution.py:462
  344.2 18.3 %expert_in_grad.3 = (bf16[2,2,320,896]{3,2,1,0:T(8,128)(2,1)}, bf16[2,2,320,896]{3,2,1,0:T(8,128)(2,1)}, f32[1280,128]{1,0:T(8,128)}) custom-call(s32[1]{0:T(128)} %bitcast.4.core_ref, bf16[256,1280]{1,0:T(8,128)(2,1)} %copy-done.32, bf16[256,1280]{1,0:T(8,128)(2,1)} %copy-done.31, bf16[256,1280]{1,0:T(8,128)(2,1)} %copy-done.36, ...), custom_call_target="tpu_custom_call" | custom-call | flops 10737418240 | bytes 22151168 | tf_op jit(solution)/shard_map/expert_in_grad/pallas_call | solution.py:322
  371.1 16.2 %attention_back.1 = (bf16[8,256,896]{2,1,0:T(8,128)(2,1)}, bf16[256,256]{1,0:T(8,128)(2,1)}) custom-call(s32[1]{0:T(128)} %bitcast.place_ref, bf16[8,256,896]{2,1,0:T(8,128)(2,1)} %get-tuple-element.197.packed, bf16[256,256]{1,0:T(8,128)(2,1)} %get-tuple-element.198.spare_q, bf16[8,256,128]{2,1,0:T(8,128)(2,1)} %get-tuple-element.199.out, ...), custom_call_target="tpu_custom_call" | custom-call | flops 8724152320 | bytes 14680064 | tf_op jit(solution)/shard_map/attention_back/pallas_call | solution.py:787
  404.3 6.9 %collective-permute-done.34.refs_0_ = bf16[256,1280]{1,0:T(8,128)(2,1)} collective-permute-done((bf16[256,1280]{1,0:T(8,128)(2,1)}, bf16[256,1280]{1,0:T(8,128)(2,1)}, u32[]{:S(2)}, u32[]{:S(2)}) %collective-permute-start.34) | collective-permute-done | bytes 655392 | tf_op jit(solution)/shard_map/ppermute | solution.py:65
  412.6 12.8 %attn_wgrad.1 = (bf16[2,320,1152]{2,1,0:T(8,128)(2,1)}, bf16[2,320,1152]{2,1,0:T(8,128)(2,1)}) custom-call(s32[8]{0:T(128)} %gather_fusion, s32[1]{0:T(128)} %bitcast.4.core_ref, bf16[256,1280]{1,0:T(8,128)(2,1)} %get-tuple-element.292.refs_0_.refs_8_, bf16[256,1280]{1,0:T(8,128)(2,1)} %get-tuple-element.293.refs_1_, ...), custom_call_target="tpu_custom_call" | custom-call | flops 6039797760 | bytes 8192000 | tf_op jit(solution)/shard_map/attn_wgrad/pallas_call | solution.py:862
  425.5 5.9 %attn_parts.5 = (bf16[256,1280]{1,0:T(8,128)(2,1)}, bf16[256,1280]{1,0:T(8,128)(2,1)}) custom-call(s32[8]{0:T(128)} %gather_fusion, bf16[8,256,896]{2,1,0:T(8,128)(2,1)} %get-tuple-element.302.grad.refs_9_, bf16[1280,1152]{1,0:T(8,128)(2,1)} %pack_heads.1.refs_2_.weight), custom_call_target="tpu_custom_call" | custom-call | flops 1174405120 | bytes 3604480 | tf_op jit(solution)/shard_map/attn_parts/pallas_call | solution.py:814
  444.2 7.2 %attn_parts.4 = (bf16[256,1280]{1,0:T(8,128)(2,1)}, bf16[256,1280]{1,0:T(8,128)(2,1)}, bf16[256,1280]{1,0:T(8,128)(2,1)}, bf16[256,1280]{1,0:T(8,128)(2,1)}) custom-call(s32[8]{0:T(128)} %gather_fusion, bf16[8,256,896]{2,1,0:T(8,128)(2,1)} %get-tuple-element.302.grad.refs_9_, bf16[1280,1152]{1,0:T(8,128)(2,1)} %pack_heads.1.refs_2_.weight), custom_call_target="tpu_custom_call" | custom-call | flops 2348810240 | bytes 4915200 | tf_op jit(solution)/shard_map/attn_parts/pallas_call | solution.py:814
  475.9 11.0 %collective-permute-done.43 = bf16[1,320,1152]{2,1,0:T(8,128)(2,1)} collective-permute-done((bf16[1,320,1152]{2,1,0:T(8,128)(2,1)S(1)}, bf16[1,320,1152]{2,1,0:T(8,128)(2,1)}, u32[]{:S(2)}, u32[]{:S(2)}) %collective-permute-start.43) | collective-permute-done | bytes 737312 | tf_op jit(solution)/shard_map/ppermute | solution.py:123
  516.8 7.0 %all-to-all-start.4 = ((bf16[8,40,1664]{2,1,0:T(8,128)(2,1)}), bf16[8,40,1664]{2,1,0:T(8,128)(2,1)}, u32[]{:S(2)}, u32[]{:S(2)}) async-start(bf16[8,40,1664]{2,1,0:T(8,128)(2,1)} %bitcast.37), calls=%async_computation.4 | async-start | bytes 2129920 | tf_op jit(solution)/shard_map/all_to_all | solution.py:1118
  544.2 7.5 %all-to-all-done.4 = bf16[8,40,1664]{2,1,0:T(8,128)(2,1)} async-done(((bf16[8,40,1664]{2,1,0:T(8,128)(2,1)}), bf16[8,40,1664]{2,1,0:T(8,128)(2,1)}, u32[]{:S(2)}, u32[]{:S(2)}) %all-to-all-start.4) | async-done | bytes 1064992 | tf_op jit(solution)/shard_map/all_to_all | solution.py:1118
  (256 shorter events, 249.0 us)
Async XLA Ops:
  54.1 29.0 %all-to-all-start.1 = ((f32[8,2,256]{2,1,0:T(2,128)}), f32[8,2,256]{2,1,0:T(2,128)S(1)}, u32[]{:S(2)}, u32[]{:S(2)}) async-start(f32[8,2,256]{2,1,0:T(2,128)} %reshape.386), calls=%async_computation.1 | async-start | bytes 32768 | tf_op jit(solution)/shard_map/all_to_all | solution.py:973
  83.1 31.4 %all-to-all-start = ((bf16[8,256,128]{2,1,0:T(8,128)(2,1)}), bf16[8,256,128]{2,1,0:T(8,128)(2,1)S(1)}, u32[]{:S(2)}, u32[]{:S(2)}) async-start(bf16[8,256,128]{2,1,0:T(8,128)(2,1)} %get-tuple-element.199.out), calls=%async_computation | async-start | bytes 1048576 | tf_op jit(solution)/shard_map/all_to_all | solution.py:989
  136.9 36.0 %collective-permute-start.18 = (bf16[256,1280]{1,0:T(8,128)(2,1)}, bf16[256,1280]{1,0:T(8,128)(2,1)}, u32[]{:S(2)}, u32[]{:S(2)}) collective-permute-start(bf16[256,1280]{1,0:T(8,128)(2,1)} %collective-permute-done.17.refs_3_.refs_5_), channel_id=1, source_target_pairs={{0,2},{2,4},{4,6},{6,7},{7,5},{5,3},{3,1},{1,0},{8,10},{10,12},{12... | collective-permute-start | bytes 1966088 | tf_op jit(solution)/shard_map/ppermute | solution.py:44
  137.5 35.4 %collective-permute-start.19 = (bf16[256,1280]{1,0:T(8,128)(2,1)S(1)}, bf16[256,1280]{1,0:T(8,128)(2,1)}, u32[]{:S(2)}, u32[]{:S(2)}) collective-permute-start(bf16[256,1280]{1,0:T(8,128)(2,1)S(1)} %collective-permute-done.15.refs_1_.refs_7_), channel_id=1, source_target_pairs={{2,0},{4,2},{6,4},{7,6},{5,7},{3,5},{1,3},{0,1},{10,8},{12,10},{14... | collective-permute-start | bytes 1966088 | tf_op jit(solution)/shard_map/ppermute | solution.py:46
  173.0 29.2 %collective-permute-start.20 = (bf16[256,1280]{1,0:T(8,128)(2,1)}, bf16[256,1280]{1,0:T(8,128)(2,1)}, u32[]{:S(2)}, u32[]{:S(2)}) collective-permute-start(bf16[256,1280]{1,0:T(8,128)(2,1)} %collective-permute-done.18.refs_3_), channel_id=1, source_target_pairs={{0,2},{2,4},{4,6},{6,7},{7,5},{5,3},{3,1},{1,0},{8,10},{10,12},{12... | collective-permute-start | bytes 1966088 | tf_op jit(solution)/shard_map/ppermute | solution.py:44
  238.4 28.6 %collective-permute-start.23 = (bf16[256,1280]{1,0:T(8,128)(2,1)}, bf16[256,1280]{1,0:T(8,128)(2,1)S(1)}, u32[]{:S(2)}, u32[]{:S(2)}) collective-permute-start(bf16[256,1280]{1,0:T(8,128)(2,1)} %get-tuple-element.259), channel_id=1, source_target_pairs={{0,2},{2,4},{4,6},{6,7},{7,5},{5,3},{3,1},{1,0},{8,10},{10,12},{12... | collective-permute-start | bytes 1966088 | tf_op jit(solution)/shard_map/ppermute | solution.py:65
  240.5 79.5 %collective-permute-start.21 = (bf16[256,1280]{1,0:T(8,128)(2,1)}, bf16[256,1280]{1,0:T(8,128)(2,1)S(1)}, u32[]{:S(2)}, u32[]{:S(2)}) collective-permute-start(bf16[256,1280]{1,0:T(8,128)(2,1)} %get-tuple-element.248), channel_id=1, source_target_pairs={{0,2},{2,4},{4,6},{6,7},{7,5},{5,3},{3,1},{1,0},{8,10},{10,12},{12... | collective-permute-start | bytes 1966088 | tf_op jit(solution)/shard_map/ppermute | solution.py:65
  240.8 79.3 %collective-permute-start.22 = (bf16[256,1280]{1,0:T(8,128)(2,1)}, bf16[256,1280]{1,0:T(8,128)(2,1)}, u32[]{:S(2)}, u32[]{:S(2)}) collective-permute-start(bf16[256,1280]{1,0:T(8,128)(2,1)} %get-tuple-element.249), channel_id=1, source_target_pairs={{2,0},{4,2},{6,4},{7,6},{5,7},{3,5},{1,3},{0,1},{10,8},{12,10},{14... | collective-permute-start | bytes 1966088 | tf_op jit(solution)/shard_map/ppermute | solution.py:67
  292.0 78.2 %collective-permute-start.46 = (bf16[2,480,1280]{2,1,0:T(8,128)(2,1)}, bf16[2,480,1280]{2,1,0:T(8,128)(2,1)S(1)}, u32[]{:S(2)}, u32[]{:S(2)}) collective-permute-start(bf16[2,480,1280]{2,1,0:T(8,128)(2,1)} %get-tuple-element.333), channel_id=1, source_target_pairs={{0,8},{8,0},{16,24},{24,16},{1,9},{9,1},{17,25},{25,17},{2,10},{10... | collective-permute-start | bytes 7372808 | tf_op jit(solution)/shard_map/ppermute | solution.py:106
  323.8 79.9 %collective-permute-start.48 = (bf16[2,2,320,896]{3,2,1,0:T(8,128)(2,1)}, bf16[2,2,320,896]{3,2,1,0:T(8,128)(2,1)}, u32[]{:S(2)}, u32[]{:S(2)}) collective-permute-start(bf16[2,2,320,896]{3,2,1,0:T(8,128)(2,1)} %get-tuple-element.339), channel_id=1, source_target_pairs={{0,8},{8,0},{16,24},{24,16},{1,9},{9,1},{17,25},{25,17},{2,10},{10... | collective-permute-start | bytes 6881288 | tf_op jit(solution)/shard_map/ppermute | solution.py:106
  340.5 29.8 %all-to-all-start.2 = ((bf16[8,256,128]{2,1,0:T(8,128)(2,1)}), bf16[8,256,128]{2,1,0:T(8,128)(2,1)S(1)}, u32[]{:S(2)}, u32[]{:S(2)}) async-start(bf16[8,256,128]{2,1,0:T(8,128)(2,1)} %get-tuple-element.280), calls=%async_computation.2 | async-start | bytes 1048576 | tf_op jit(solution)/shard_map/all_to_all | solution.py:1054
  367.9 88.0 %collective-permute-start.44 = (bf16[2,320,1664]{2,1,0:T(8,128)(2,1)}, bf16[2,320,1664]{2,1,0:T(8,128)(2,1)}, u32[]{:S(2)}, u32[]{:S(2)}) collective-permute-start(bf16[2,320,1664]{2,1,0:T(8,128)(2,1)} %get-tuple-element.327), channel_id=1, source_target_pairs={{0,8},{8,0},{16,24},{24,16},{1,9},{9,1},{17,25},{25,17},{2,10},{10... | collective-permute-start | bytes 6389768 | tf_op jit(solution)/shard_map/ppermute | solution.py:106
  367.9 30.0 %collective-permute-start.30 = (bf16[256,1280]{1,0:T(8,128)(2,1)}, bf16[256,1280]{1,0:T(8,128)(2,1)}, u32[]{:S(2)}, u32[]{:S(2)}) collective-permute-start(bf16[256,1280]{1,0:T(8,128)(2,1)} %get-tuple-element.276), channel_id=1, source_target_pairs={{0,2},{2,4},{4,6},{6,7},{7,5},{5,3},{3,1},{1,0},{8,10},{10,12},{12... | collective-permute-start | bytes 1966088 | tf_op jit(solution)/shard_map/ppermute | solution.py:65
  368.0 31.4 %collective-permute-start.31 = (bf16[256,1280]{1,0:T(8,128)(2,1)}, bf16[256,1280]{1,0:T(8,128)(2,1)}, u32[]{:S(2)}, u32[]{:S(2)}) collective-permute-start(bf16[256,1280]{1,0:T(8,128)(2,1)} %get-tuple-element.277), channel_id=1, source_target_pairs={{2,0},{4,2},{6,4},{7,6},{5,7},{3,5},{1,3},{0,1},{10,8},{12,10},{14... | collective-permute-start | bytes 1966088 | tf_op jit(solution)/shard_map/ppermute | solution.py:67
  397.8 53.5 %collective-permute-start.47 = (bf16[1,480,1280]{2,1,0:T(8,128)(2,1)}, bf16[1,480,1280]{2,1,0:T(8,128)(2,1)}, u32[]{:S(2)}, u32[]{:S(2)}) collective-permute-start(bf16[1,480,1280]{2,1,0:T(8,128)(2,1)} %add_convert_fusion), channel_id=1, source_target_pairs={{0,16},{8,24},{16,0},{24,8},{1,17},{9,25},{17,1},{25,9},{2,18},{10... | collective-permute-start | bytes 3686408 | tf_op jit(solution)/shard_map/ppermute | solution.py:123
  402.2 37.0 %collective-permute-start.35 = (bf16[256,1280]{1,0:T(8,128)(2,1)}, bf16[256,1280]{1,0:T(8,128)(2,1)}, u32[]{:S(2)}, u32[]{:S(2)}) collective-permute-start(bf16[256,1280]{1,0:T(8,128)(2,1)} %get-tuple-element.288), channel_id=1, source_target_pairs={{2,0},{4,2},{6,4},{7,6},{5,7},{3,5},{1,3},{0,1},{10,8},{12,10},{14... | collective-permute-start | bytes 1966088 | tf_op jit(solution)/shard_map/ppermute | solution.py:67
  403.7 32.2 %collective-permute-start.32 = (bf16[256,1280]{1,0:T(8,128)(2,1)}, bf16[256,1280]{1,0:T(8,128)(2,1)}, u32[]{:S(2)}, u32[]{:S(2)}) collective-permute-start(bf16[256,1280]{1,0:T(8,128)(2,1)} %get-tuple-element.281), channel_id=1, source_target_pairs={{0,2},{2,4},{4,6},{6,7},{7,5},{5,3},{3,1},{1,0},{8,10},{10,12},{12... | collective-permute-start | bytes 1966088 | tf_op jit(solution)/shard_map/ppermute | solution.py:65
  411.2 31.5 %collective-permute-start.33 = (bf16[256,1280]{1,0:T(8,128)(2,1)}, bf16[256,1280]{1,0:T(8,128)(2,1)}, u32[]{:S(2)}, u32[]{:S(2)}) collective-permute-start(bf16[256,1280]{1,0:T(8,128)(2,1)} %get-tuple-element.282), channel_id=1, source_target_pairs={{2,0},{4,2},{6,4},{7,6},{5,7},{3,5},{1,3},{0,1},{10,8},{12,10},{14... | collective-permute-start | bytes 1966088 | tf_op jit(solution)/shard_map/ppermute | solution.py:67
  439.2 58.9 %collective-permute-start.50 = (bf16[2,2,320,896]{3,2,1,0:T(8,128)(2,1)}, bf16[2,2,320,896]{3,2,1,0:T(8,128)(2,1)}, u32[]{:S(2)}, u32[]{:S(2)}) collective-permute-start(bf16[2,2,320,896]{3,2,1,0:T(8,128)(2,1)} %get-tuple-element.346), channel_id=1, source_target_pairs={{0,8},{8,0},{16,24},{24,16},{1,9},{9,1},{17,25},{25,17},{2,10},{10... | collective-permute-start | bytes 6881288 | tf_op jit(solution)/shard_map/ppermute | solution.py:106
  442.7 33.0 %collective-permute-start.49 = (bf16[1,2,320,896]{3,2,1,0:T(8,128)(2,1)}, bf16[1,2,320,896]{3,2,1,0:T(8,128)(2,1)}, u32[]{:S(2)}, u32[]{:S(2)}) collective-permute-start(bf16[1,2,320,896]{3,2,1,0:T(8,128)(2,1)} %add_convert_fusion.2), channel_id=1, source_target_pairs={{0,16},{8,24},{16,0},{24,8},{1,17},{9,25},{17,1},{25,9},{2,18},{10... | collective-permute-start | bytes 3440648 | tf_op jit(solution)/shard_map/ppermute | solution.py:123
  471.9 37.8 %collective-permute-start.45 = (bf16[1,320,1664]{2,1,0:T(8,128)(2,1)}, bf16[1,320,1664]{2,1,0:T(8,128)(2,1)}, u32[]{:S(2)}, u32[]{:S(2)}) collective-permute-start(bf16[1,320,1664]{2,1,0:T(8,128)(2,1)} %add_convert_fusion.4), channel_id=1, source_target_pairs={{0,16},{8,24},{16,0},{24,8},{1,17},{9,25},{17,1},{25,9},{2,18},{10... | collective-permute-start | bytes 3194888 | tf_op jit(solution)/shard_map/ppermute | solution.py:123
  500.7 32.6 %collective-permute-start.51 = (bf16[1,2,320,896]{3,2,1,0:T(8,128)(2,1)}, bf16[1,2,320,896]{3,2,1,0:T(8,128)(2,1)}, u32[]{:S(2)}, u32[]{:S(2)}) collective-permute-start(bf16[1,2,320,896]{3,2,1,0:T(8,128)(2,1)} %add_convert_fusion.1), channel_id=1, source_target_pairs={{0,16},{8,24},{16,0},{24,8},{1,17},{9,25},{17,1},{25,9},{2,18},{10... | collective-permute-start | bytes 3440648 | tf_op jit(solution)/shard_map/ppermute | solution.py:123
  506.0 30.3 %collective-permute-start.41 = (bf16[256,1280]{1,0:T(8,128)(2,1)}, bf16[256,1280]{1,0:T(8,128)(2,1)}, u32[]{:S(2)}, u32[]{:S(2)}) collective-permute-start(bf16[256,1280]{1,0:T(8,128)(2,1)} %add_pairs.17), channel_id=1, source_target_pairs={{0,2},{2,4},{4,6},{6,7},{7,5},{5,3},{3,1},{1,0},{8,10},{10,12},{12... | collective-permute-start | bytes 1966088 | tf_op jit(solution)/shard_map/ppermute | solution.py:65
  516.8 34.9 %all-to-all-start.4 = ((bf16[8,40,1664]{2,1,0:T(8,128)(2,1)}), bf16[8,40,1664]{2,1,0:T(8,128)(2,1)}, u32[]{:S(2)}, u32[]{:S(2)}) async-start(bf16[8,40,1664]{2,1,0:T(8,128)(2,1)} %bitcast.37), calls=%async_computation.4 | async-start | bytes 2129920 | tf_op jit(solution)/shard_map/all_to_all | solution.py:1118
  (72 other events, 1026.9 us)

commit v5 on v4

v5 whole, which is shorter than its diff:
```python
import functools

import jax
import jax.numpy as jnp
import numpy as np
from jax import lax
from jax.experimental import pallas as pl
from jax.experimental.pallas import tpu as pltpu
from jax.sharding import PartitionSpec as P

HEAD_DIM = 128
EPS = 1e-06
FLOAT = jnp.float32
HALF = jnp.bfloat16


def matmul(a, b, contract):
    return lax.dot_general(a, b, ((contract[:1], contract[1:]), ((), ())), preferred_element_type=FLOAT)


def ring_order(count):
    return list(range(0, count, 2)) + list(range(count - 1, 0, -2))


def ring_steps(count):
    order = ring_order(count)
    ahead = [(order[i], order[(i + 1) % count]) for i in range(count)]
    back = [(b, a) for a, b in ahead]
    return ahead, back


def after(value, *others):
    return lax.optimization_barrier((value, others))[0]


class RingGather:
    def __init__(self, block, mirrored=False):
        count = lax.axis_size("narrow")
        self.half = count // 2
        self.mirrored = mirrored
        self.step = 0
        self.slots = [block] + [None] * (count - 1)

    def hop(self, *others):
        count = len(self.slots)
        ahead, back = ring_steps(count)
        forward, backward = after((self.slots[-self.step], self.slots[self.step]), *others)
        self.step += 1
        arrived = []
        if self.step < self.half or not self.mirrored:
            arrived.append(lax.ppermute(forward, "narrow", ahead))
            self.slots[count - self.step] = arrived[-1]
        if self.step < self.half or self.mirrored:
            arrived.append(lax.ppermute(backward, "narrow", back))
            self.slots[self.step] = arrived[-1]
        return arrived


class RingSum:
    def __init__(self, parts, mirrored=False):
        self.mirrored = mirrored
        self.parts = parts
        self.half = len(parts) // 2
        self.step = 0
        self.forward, self.backward = self.part(self.half), self.part(self.half + 1)

    def part(self, offset):
        return self.parts[-offset if self.mirrored else offset]

    def hop(self, *others):
        ahead, back = ring_steps(len(self.parts))
        if self.mirrored:
            ahead, back = back, ahead
        self.step += 1
        if self.step == self.half:
            self.forward = lax.ppermute(after(self.forward, *others), "narrow", ahead)
            return [self.forward]
        forward, backward = after((self.forward, self.backward), *others)
        self.forward = lax.ppermute(forward, "narrow", ahead)
        self.backward = lax.ppermute(backward, "narrow", back)
        return [self.forward, self.backward]

    def add(self, *deps):
        return add_rings([self], *deps)

    def terms(self):
        arrived = [self.forward]
        own = [self.part(self.half - self.step)]
        if self.step < self.half - 1:
            arrived.append(self.backward)
            own.append(self.part(self.half + 1 + self.step))
        return arrived, own

    def last(self):
        return self.parts[0], self.forward, self.backward


def add_rings(rings, *deps):
    arrived, own = [], []
    for ring in rings:
        ring_arrived, ring_own = ring.terms()
        arrived += ring_arrived
        own += ring_own
    sums = launch_whole(
        functools.partial(add_kernel, len(own)),
        arrived + own,
        [(own[0].shape, HALF)] * len(own),
        "add_pairs",
        deps=deps,
    )
    left = list(sums)
    for ring in rings:
        ring.forward = left.pop(0)
        if ring.step < ring.half - 1:
            ring.backward = left.pop(0)
    return list(sums)


def add_kernel(count, *refs):
    for i in range(count):
        total = refs[i][...].astype(FLOAT) + refs[count + i][...].astype(FLOAT)
        refs[2 * count + i][...] = total.astype(HALF)


def wide_first(sent):
    count = lax.axis_size("wide")
    return lax.ppermute(sent, "wide", [(i, i ^ 1) for i in range(count)])


def wide_swap(sent, bit):
    count = lax.axis_size("wide")
    return lax.ppermute(sent, "wide", [(i, i ^ bit) for i in range(count)])


def sum_kernel(count, kind, place_ref, *refs):
    total = refs[0][...].astype(FLOAT)
    for ref in refs[1:count]:
        total += ref[...].reshape(total.shape).astype(FLOAT)
    refs[count][...] = total.reshape(refs[count].shape).astype(kind)


def sum_halves(halved, others, index, kind, *deps):
    rest = halved[0].shape[1:]
    pairs = halved[0].shape[0] // 2
    shape = (pairs,) + rest
    operands = [array.reshape((pairs, 2) + rest) for array in halved] + list(others)
    half_block = pl.BlockSpec((pairs, 1) + rest, lambda i, p: (0, p[0]) + (0,) * len(rest))
    return launch(
        functools.partial(sum_kernel, len(operands), kind),
        operands,
        [half_block] * len(halved) + [whole_block(shape)] * len(others),
        whole_block(shape),
        jax.ShapeDtypeStruct(shape, kind),
        "sum_halves",
        prefetch=[index],
        deps=deps,
        moved=sum(array.size for array in operands),
    )


def wide_rest(kept, got, *deps, sent=None):
    bit, others = 2, []
    halved = [kept, got]
    while True:
        mine = ((lax.axis_index("wide") // bit) % 2).astype(jnp.int32).reshape(1)
        if sent is None or bit > 2:
            sent = sum_halves(halved, others, 1 - mine, HALF, *deps)
        arrived = wide_swap(sent, bit)
        if 2 * bit == lax.axis_size("wide"):
            return sent, arrived, (halved, [arrived], mine)
        halved = [sum_halves(halved, [], mine, HALF), arrived]
        bit *= 2


def widen_out_kernel(rows, source, experts, shared):
    total = source[...].astype(FLOAT)
    for e in range(experts.shape[0]):
        experts[e] = total[e * rows : (e + 1) * rows]
    first = experts.shape[0] * rows
    shared[...] = total[first : first + shared.shape[0]]


def widen_out(source, experts, rows, share, *deps):
    width = source.shape[1]
    return launch_whole(
        functools.partial(widen_out_kernel, rows),
        [source],
        [((experts, rows, width), FLOAT), ((share, width), FLOAT)],
        "widen_out",
        deps=deps,
    )


def finish_dense_kernel(parts, to_units, out, gain, gate, up):
    group = parts.shape[0]
    width = out.shape[1]
    total = parts[0, :, : width + HEAD_DIM].astype(FLOAT)
    for g in range(1, group):
        total += parts[g, :, : width + HEAD_DIM].astype(FLOAT)
    out[...] = total[:, :width]
    gain[...] = total[:, width:]
    column = width + HEAD_DIM
    gap = to_units.shape[1]
    for share in (gate, up):
        share[...] = sum(
            matmul(parts[g, :, column : column + gap], to_units[g], (1, 0)) for g in range(group)
        )
        column += gap


def finish_dense(parts, to_units, width):
    rows, units = parts.shape[1], to_units.shape[2]
    shapes = [(rows, width), (rows, HEAD_DIM), (rows, units), (rows, units)]
    return launch_whole(
        finish_dense_kernel, [parts, to_units], [(shape, FLOAT) for shape in shapes], "finish_dense"
    )


def finish_attn_kernel(spare, parts, *refs):
    weights, grads, gain = refs[:3], refs[3:6], refs[6]
    group = parts.shape[0]
    total = 0.0
    tiles = ((0, 3 + 2 * spare), (1, 2), (2 + spare, 3 + spare))
    for weight, grad, (own, first) in zip(weights, grads, tiles):
        for g in range(group):
            grad[:, head_slice(g)] = parts[g, :, head_slice(own)].astype(FLOAT)
        columns = slice(first * HEAD_DIM, (first + spare) * HEAD_DIM)
        grad[:, group * HEAD_DIM :] = sum(
            parts[g, :, columns].astype(FLOAT) for g in range(group)
        )
        total += jnp.sum(grad[...] * weight[...].astype(FLOAT), axis=1, keepdims=True)
    gain[...] = jnp.broadcast_to(total, gain.shape)


def finish_attn(spare, parts, weights):
    rows, width = weights[0].shape
    shapes = [(rows, width)] * 3 + [(rows, HEAD_DIM)]
    return launch_whole(
        functools.partial(finish_attn_kernel, spare),
        [parts, *weights],
        [(shape, FLOAT) for shape in shapes],
        "finish_attn",
    )


def widen_kernel(source, target):
    target[...] = source[...].astype(FLOAT)


def widen(array, *deps):
    return launch_whole(widen_kernel, [array], [(array.shape, FLOAT)], "widen", deps=deps)[0]


VMEM_LIMIT = 60 * 2**20
CHUNK = 512


def whole_block(shape):
    return pl.BlockSpec(shape, lambda *_: (0,) * len(shape))


ANYWHERE = pl.BlockSpec(memory_space=pl.ANY)


def launch(
    kernel, operands, in_specs, out_specs, out_shape, name, prefetch=(), deps=(), through=(), grid=(1,), scratch=(), aliases=None, flops=0, moved=0
):
    inputs = len(prefetch) + len(operands)
    idle = len(deps) + len(through)
    aliases = dict(aliases or {})
    if through:
        out_specs, out_shape = list(out_specs), list(out_shape)
        for i, array in enumerate(through):
            aliases[inputs + len(deps) + i] = len(out_shape)
            out_specs.append(ANYWHERE)
            out_shape.append(jax.ShapeDtypeStruct(array.shape, array.dtype))

    def body(*refs):
        results = refs[inputs + idle : len(refs) - len(scratch)]
        own = results[: len(results) - len(through)]
        kernel(*refs[:inputs], *own, *refs[len(refs) - len(scratch) :])

    return pl.pallas_call(
        body,
        grid_spec=pltpu.PrefetchScalarGridSpec(
            num_scalar_prefetch=len(prefetch),
            grid=grid,
            in_specs=list(in_specs) + [ANYWHERE] * idle,
            out_specs=out_specs,
            scratch_shapes=list(scratch),
        ),
        out_shape=out_shape,
        input_output_aliases=aliases,
        compiler_params=pltpu.CompilerParams(vmem_limit_bytes=VMEM_LIMIT),
        cost_estimate=pl.CostEstimate(flops=int(flops), bytes_accessed=int(moved), transcendentals=0),
        name=name,
    )(*prefetch, *operands, *deps, *through)


def launch_whole(kernel, operands, shapes, name, **options):
    moved = sum(array.size * array.dtype.itemsize for array in operands)
    return launch(
        kernel,
        operands,
        [whole_block(array.shape) for array in operands],
        [whole_block(shape) for shape, _ in shapes],
        [jax.ShapeDtypeStruct(shape, kind) for shape, kind in shapes],
        name,
        moved=moved,
        **options,
    )


def rows_kernel(slots, units, chained, blocks_ref, *refs):
    count = len(slots)
    xs, cs, gates = refs[:count], refs[count : 2 * count], refs[2 * count]
    gate_w, up_w, down_w = refs[2 * count + 1 : 2 * count + 4]
    outs = refs[2 * count + 4 + (3 if chained else 0) :]
    inner, gate_g, up_g = outs[:3]
    ys, ds = outs[3 : 3 + count], outs[3 + count : 3 + 2 * count]
    y_sum, d_sum, x_rows, c_rows = outs[3 + 2 * count :]
    step = pl.program_id(0)
    length = xs[0].shape[0]
    chunk = gate_w.shape[1]
    per_expert = pl.num_programs(0) // gates.shape[2]

    @pl.when(step == 0)
    def _():
        for i in range(count):
            x_rows[i * length : (i + 1) * length] = xs[i][...]
            c_rows[i * length : (i + 1) * length] = cs[i][...]
        y_sum[...] = jnp.zeros_like(y_sum)
        d_sum[...] = jnp.zeros_like(d_sum)

    x, c = x_rows[...], c_rows[...]
    expert = step // per_expert
    column = (step % per_expert) * chunk + lax.broadcasted_iota(
        jnp.int32, (count * length, chunk), 1
    )
    picked = []
    for slot in slots:
        gate = gates[blocks_ref[slot]]
        own = gate[:, 0:1]
        for e in range(1, gate.shape[1]):
            own = jnp.where(expert == e, gate[:, e : e + 1], own)
        picked.append(own)
    scale = jnp.where(column < units, jnp.concatenate(picked, axis=0), 1.0)
    gate_pre = matmul(x, gate_w[...], (1, 0))
    up_pre = matmul(x, up_w[...], (1, 0))
    inner_grad = matmul(c, down_w[...], (1, 1)) * scale
    sigma = 0.5 * jnp.tanh(0.5 * gate_pre) + 0.5
    active = gate_pre * sigma
    inner[...] = (active * up_pre * scale).astype(HALF)
    gate_g[...] = (inner_grad * up_pre * (sigma + active * (1.0 - sigma))).astype(HALF)
    up_g[...] = (inner_grad * active).astype(HALF)
    y_sum[...] += matmul(inner[...], down_w[...], (1, 0))
    d_sum[...] += matmul(gate_g[...], gate_w[...], (1, 1)) + matmul(up_g[...], up_w[...], (1, 1))

    @pl.when(step == pl.num_programs(0) - 1)
    def _():
        for i in range(count):
            ys[i][...] = y_sum[i * length : (i + 1) * length].astype(HALF)
            ds[i][...] = d_sum[i * length : (i + 1) * length].astype(HALF)


def expert_rows(units, slots, place, total, kept, blocks, xs, cs, gates, gate_w, up_w, down_w, deps):
    count = len(xs)
    length, width = xs[0].shape
    padded = gate_w.shape[1]
    rows = count * length
    column_block = pl.BlockSpec((width, CHUNK), lambda f, b: (0, f))
    row_block = pl.BlockSpec((CHUNK, width), lambda f, b: (f, 0))
    kept_block = pl.BlockSpec((rows, CHUNK), lambda f, b: (place // rows, f))
    chained = kept is not None
    first_kept = 1 + 2 * count + 4
    return launch(
        functools.partial(rows_kernel, slots, units, chained),
        [*xs, *cs, gates, gate_w, up_w, down_w, *(kept if chained else ())],
        [whole_block(xs[0].shape)] * (2 * count)
        + [whole_block(gates.shape), column_block, column_block, row_block]
        + [ANYWHERE] * (3 if chained else 0),
        [kept_block] * 3 + [whole_block(xs[0].shape)] * (2 * count),
        [jax.ShapeDtypeStruct((total, padded), HALF)] * 3
        + [jax.ShapeDtypeStruct(xs[0].shape, HALF)] * (2 * count),
        "expert_rows",
        prefetch=[blocks],
        deps=deps,
        grid=(padded // CHUNK,),
        scratch=[pltpu.VMEM((rows, width), FLOAT)] * 2 + [pltpu.VMEM((rows, width), HALF)] * 2,
        aliases={first_kept + i: i for i in range(3)} if chained else {},
        flops=12 * rows * width * padded,
        moved=6 * width * padded + 6 * rows * padded + 8 * rows * width,
    )


def pack_in_kernel(units, choice, shared, weights, out, sems):
    experts = weights.shape[0]
    per_expert = out.shape[1] // experts
    copies = [
        pltpu.make_async_copy(weights.at[e], out.at[:, pl.ds(e * per_expert, units)], sems.at[e])
        for e in range(experts)
    ]
    start_all(copies)
    for e in range(experts):
        gap = slice(e * per_expert + units, (e + 1) * per_expert)
        if e == 0:
            out[:, gap] = matmul(shared[...], choice[...], (1, 0)).astype(HALF)
        else:
            out[:, gap] = jnp.zeros((out.shape[0], per_expert - units), HALF)
    wait_all(copies)


def pack_out_kernel(units, choice, shared, weights, out, sems):
    experts = weights.shape[0]
    per_expert = out.shape[0] // experts
    copies = [
        pltpu.make_async_copy(weights.at[e], out.at[pl.ds(e * per_expert, units)], sems.at[e])
        for e in range(experts)
    ]
    start_all(copies)
    for e in range(experts):
        gap = slice(e * per_expert + units, (e + 1) * per_expert)
        if e == 0:
            out[gap] = matmul(choice[...], shared[...], (0, 0)).astype(HALF)
        else:
            out[gap] = jnp.zeros((per_expert - units, out.shape[1]), HALF)
    wait_all(copies)


def pack_experts(kernel, units, shape, choice, shared, weights, *deps):
    return launch(
        functools.partial(kernel, units),
        [choice, shared, weights],
        [whole_block(choice.shape), whole_block(shared.shape), ANYWHERE],
        whole_block(shape),
        jax.ShapeDtypeStruct(shape, HALF),
        "pack_experts",
        deps=deps,
        scratch=[pltpu.SemaphoreType.DMA((weights.shape[0],))],
        moved=4 * shape[0] * shape[1],
    )


def fetch_rows(slots, rows, sems):
    length = slots[0].shape[0]
    copies = [
        pltpu.make_async_copy(slot, rows.at[pl.ds(i * length, length)], sems.at[i])
        for i, slot in enumerate(slots)
    ]
    for copy in copies:
        copy.start()
    for copy in copies:
        copy.wait()


def in_grad_kernel(count, units, split, *refs):
    core_ref, slots, grad = refs[0], refs[1 : 1 + count], refs[1 + count]
    outs, (share, rows, total, sems) = refs[2 + count : -4], refs[-4:]
    step = pl.program_id(0)
    chunk = grad.shape[1]
    per_expert = -(-units // chunk)

    @pl.when(step == 0)
    def _():
        fetch_rows(slots, rows, sems)

    total[...] = matmul(rows[...], grad[...], (0, 0))
    size = outs[0].shape[2]

    def copy_rows(columns):
        own = slice(0, columns.stop - columns.start)
        if not split:
            for i in range(outs[0].shape[0]):
                outs[0][i, 0, :, columns] = total[i * size : (i + 1) * size, own].astype(HALF)
            return
        for j in range(outs[0].shape[0]):
            for target, parity in zip(outs, (core_ref[0], 1 - core_ref[0])):
                start = pl.multiple_of((2 * j + parity) * size, 8)
                target[j, 0, :, columns] = total[pl.ds(start, size), own].astype(HALF)

    for part in range(per_expert):

        @pl.when(step % per_expert == part)
        def _():
            copy_rows(slice(part * chunk, min((part + 1) * chunk, units)))

    @pl.when(step == per_expert - 1)
    def _():
        share[...] = total[:, units - (per_expert - 1) * chunk :]


def in_grad(units, experts, copies, core, split, slots, grad, *deps):
    length, width = slots[0].shape
    total, padded = grad.shape
    per_expert = padded // experts // CHUNK
    share = padded // experts - units
    parts = 2 if split else 1
    shape = (copies // parts, experts, width // copies, units)
    block = pl.BlockSpec((shape[0], 1) + shape[2:], lambda f, c: (0, f // per_expert, 0, 0))
    return launch(
        functools.partial(in_grad_kernel, len(slots), units, split),
        [*slots, grad],
        [ANYWHERE] * len(slots) + [pl.BlockSpec((total, CHUNK), lambda f, c: (0, f))],
        [block] * parts + [whole_block((width, share))],
        [jax.ShapeDtypeStruct(shape, HALF)] * parts + [jax.ShapeDtypeStruct((width, share), FLOAT)],
        "expert_in_grad",
        prefetch=[core],
        deps=deps,
        grid=(padded // CHUNK,),
        scratch=[
            pltpu.VMEM((total, width), HALF),
            pltpu.VMEM((width, CHUNK), FLOAT),
            pltpu.SemaphoreType.DMA((len(slots),)),
        ],
        flops=2 * total * width * padded,
        moved=2 * (total + width) * (padded + width),
    )


def out_grad_kernel(count, units, *refs):
    slots, inner = refs[:count], refs[count]
    out, rows, total, sems = refs[count + 1 :]
    step = pl.program_id(0)
    chunk = inner.shape[1]
    per_expert = total.shape[0] // chunk
    experts = pl.num_programs(0) // per_expert
    copies = out.shape[0]

    @pl.when(step == 0)
    def _():
        fetch_rows(slots, rows, sems)

    part = step % per_expert
    total[pl.ds(pl.multiple_of(part * chunk, chunk), chunk)] = matmul(inner[...], rows[...], (0, 0))

    def split(first, size, row):
        for i in range(copies):
            out[i, row : row + size] = total[first + i * size : first + (i + 1) * size].astype(HALF)

    for e in range(experts):

        @pl.when(step == (e + 1) * per_expert - 1)
        def _():
            split(0, units // copies, e * (units // copies))
            if e == 0:
                split(units, (total.shape[0] - units) // copies, experts * (units // copies))


def out_grad(units, experts, copies, slots, inner, *deps):
    length, width = slots[0].shape
    total, padded = inner.shape
    share = padded // experts - units
    shape = (copies, (experts * units + share) // copies, width)
    return launch(
        functools.partial(out_grad_kernel, len(slots), units),
        [*slots, inner],
        [ANYWHERE] * len(slots) + [pl.BlockSpec((total, CHUNK), lambda f: (0, f))],
        whole_block(shape),
        jax.ShapeDtypeStruct(shape, HALF),
        "expert_out_grad",
        deps=deps,
        grid=(padded // CHUNK,),
        scratch=[
            pltpu.VMEM((total, width), HALF),
            pltpu.VMEM((padded // experts, width), FLOAT),
            pltpu.SemaphoreType.DMA((len(slots),)),
        ],
        flops=2 * total * width * padded,
        moved=2 * (total + width) * (padded + width),
    )


def scaled_rows(values):
    scale = lax.rsqrt(jnp.mean(values * values, axis=1, keepdims=True) + EPS)
    return values * scale, scale


def mix_kernel(returned, spare_out, weight, tokens, gain, hidden, attended, ffn_in):
    for head in range(returned.shape[0]):
        attended[:, head_slice(head)] = returned[head]
    attended[:, returned.shape[0] * HEAD_DIM :] = spare_out[...]
    hidden[...] = tokens[...].astype(FLOAT) + matmul(attended[...], weight[...], (1, 0))
    ffn_in[...] = (scaled_rows(hidden[...])[0] * gain[...]).astype(HALF)


def mix(returned, spare_out, weight, tokens, gain, *deps):
    return launch_whole(
        mix_kernel,
        [returned, spare_out, weight, tokens, gain],
        [(tokens.shape, FLOAT), (tokens.shape, HALF), (tokens.shape, HALF)],
        "mix",
        deps=deps,
        flops=2 * tokens.shape[0] * tokens.shape[1] ** 2,
    )


def norm_grad(grad_out, normed, scale, gain):
    scaled = grad_out * gain
    return scale * (scaled - normed * jnp.mean(scaled * normed, axis=1, keepdims=True))


def back_kernel(
    own, forward, backward, hidden, cotangent, gain, weight, hidden_grad, branch, out_grad, spare_grad, terms
):
    ffn_in_grad = own[...].astype(FLOAT) + forward[...].astype(FLOAT) + backward[...].astype(FLOAT)
    normed, scale = scaled_rows(hidden[...])
    terms[...] = (ffn_in_grad * normed).astype(HALF)
    hidden_grad[...] = cotangent[...].astype(FLOAT) + norm_grad(ffn_in_grad, normed, scale, gain[...])
    branch[...] = hidden_grad[...].astype(HALF)
    attended_grad = matmul(branch[...], weight[...], (1, 1)).astype(HALF)
    for head in range(out_grad.shape[0]):
        out_grad[head] = attended_grad[:, head_slice(head)]
    spare_grad[...] = attended_grad[:, out_grad.shape[0] * HEAD_DIM :]


def back(arrived, hidden, cotangent, gain, weight, heads, *deps):
    length, width = hidden.shape
    shapes = [
        ((length, width), FLOAT),
        ((length, width), HALF),
        ((heads, length, HEAD_DIM), HALF),
        ((length, width - heads * HEAD_DIM), HALF),
        ((length, width), HALF),
    ]
    return launch_whole(
        back_kernel,
        [*arrived, hidden, cotangent, gain, weight],
        shapes,
        "back",
        deps=deps,
        flops=2 * length * width**2,
    )


def dense_wgrad(attended, branch, terms, gate_share, up_share, out):
    width = attended.shape[1]
    ones = jnp.ones((terms.shape[0], HEAD_DIM), HALF)
    out[:, :width] = matmul(attended[...], branch[...], (0, 0)).astype(HALF)
    out[:, width : width + HEAD_DIM] = matmul(terms[...], ones, (0, 0)).astype(HALF)
    column = width + HEAD_DIM
    for share in (gate_share, up_share):
        out[:, column : column + share.shape[1]] = share[...].astype(HALF)
        column += share.shape[1]


def tokens_grad_kernel(own, forward, backward, spare_grad, weight, tokens, gain, hidden_grad, out):
    attn_in_grad = (
        own[...].astype(FLOAT)
        + forward[...].astype(FLOAT)
        + backward[...].astype(FLOAT)
        + matmul(spare_grad[...], weight[...], (1, 1))
    )
    normed, scale = scaled_rows(tokens[...].astype(FLOAT))
    out[...] = hidden_grad[...] + norm_grad(attn_in_grad, normed, scale, gain[...])


def input_grad(arrived, spare_grad, weight, tokens, gain, hidden_grad, *deps):
    length, width = tokens.shape
    return launch_whole(
        tokens_grad_kernel,
        [*arrived, spare_grad, weight, tokens, gain, hidden_grad],
        [((length, width), FLOAT)],
        "tokens_grad",
        deps=deps,
        flops=2 * length * width * weight.shape[1],
    )[0]


def turn(values, cosine, sine):
    return values * cosine + pltpu.roll(values, HEAD_DIM // 2, 1) * sine


def head_slice(index):
    return slice(index * HEAD_DIM, (index + 1) * HEAD_DIM)


def start_all(copies):
    for copy in copies:
        copy.start()


def wait_all(copies):
    for copy in copies:
        copy.wait()


def pack_heads_kernel(spare, place_ref, query, key, value, out, sems):
    width = query.shape[1]
    own = pl.ds(pl.multiple_of(place_ref[0] * HEAD_DIM, HEAD_DIM), HEAD_DIM)
    rest = pl.ds(width - spare * HEAD_DIM, spare * HEAD_DIM)
    pieces = [
        (query, own, 1),
        (key, own, 1),
        (key, rest, spare),
        (value, own, 1),
        (value, rest, spare),
        (query, rest, spare),
    ]
    copies, tile = [], 0
    for i, (source, columns, tiles) in enumerate(pieces):
        target = out.at[:, pl.ds(tile * HEAD_DIM, tiles * HEAD_DIM)]
        copies.append(pltpu.make_async_copy(source.at[:, columns], target, sems.at[i]))
        tile += tiles
    start_all(copies)
    wait_all(copies)


def pack_heads(place, spare, query, key, value):
    width = query.shape[0]
    columns = (3 + 3 * spare) * HEAD_DIM
    return launch(
        functools.partial(pack_heads_kernel, spare),
        [query, key, value],
        [ANYWHERE] * 3,
        whole_block((width, columns)),
        jax.ShapeDtypeStruct((width, columns), HALF),
        "pack_heads",
        prefetch=[place],
        scratch=[pltpu.SemaphoreType.DMA((6,))],
        moved=4 * width * columns,
    )


def project_kernel(count, turned, tiles, chained, block_ref, *refs):
    xs, (gain, weight) = refs[:count], refs[count : count + 2]
    tables = refs[count + 2 : 3 * count + 2]
    outs = refs[3 * count + (3 if chained else 2) :]
    packed, normed = outs[0], outs[1 : 1 + count]
    step = pl.program_id(0)
    for i in range(count):

        @pl.when(step == i)
        def _():
            cosine, sine = tables[2 * i][0], tables[2 * i + 1][0]
            normed[i][...] = (scaled_rows(xs[i][...].astype(FLOAT))[0] * gain[...]).astype(HALF)
            lin = matmul(normed[i][...], weight[...], (1, 0))
            for tile in range(weight.shape[1] // HEAD_DIM):
                part = lin[:, head_slice(tile)]
                if tile < turned or tile >= tiles:
                    part = turn(part, cosine, sine)
                if tile < tiles:
                    packed[0, :, head_slice(tile)] = part.astype(HALF)
                else:
                    outs[1 + count][:, head_slice(tile - tiles)] = part.astype(HALF)


def project(blocks, slots, xs, gain, weight, cosine, sine, turned, tiles, packed, deps):
    count = len(slots)
    length, width = xs[0].shape
    chained = packed is not None
    extra = 0 if chained else weight.shape[1] - tiles * HEAD_DIM
    columns = tiles * HEAD_DIM + extra
    packed_shape = cosine.shape[:2] + (tiles * HEAD_DIM,)

    def place(i, b):
        block = b[slots[0]]
        for step in range(1, count):
            block = jnp.where(i == step, b[slots[step]], block)
        return block, 0, 0

    def table(slot):
        return pl.BlockSpec((1, length, HEAD_DIM), lambda i, b: (b[slot], 0, 0))

    out_specs = [pl.BlockSpec((1,) + packed_shape[1:], place)] + [whole_block(xs[0].shape)] * count
    out_shape = [jax.ShapeDtypeStruct(packed_shape, HALF)]
    out_shape += [jax.ShapeDtypeStruct(xs[0].shape, HALF)] * count
    if extra:
        out_specs.append(whole_block((length, extra)))
        out_shape.append(jax.ShapeDtypeStruct((length, extra), HALF))
    return launch(
        functools.partial(project_kernel, count, turned, tiles, chained),
        [*xs, gain, weight] + [cosine, sine] * count + ([packed] if chained else []),
        [whole_block(x.shape) for x in xs]
        + [whole_block(gain.shape), whole_block((width, columns))]
        + [spec for slot in slots for spec in (table(slot), table(slot))]
        + ([ANYWHERE] if chained else []),
        out_specs,
        out_shape,
        "project",
        prefetch=[blocks],
        deps=deps,
        grid=(count,),
        aliases={3 * count + 3: 0} if chained else {},
        flops=2 * count * length * width * columns,
        moved=2 * (count * length * (width + columns) + width * columns),
    )


EXP_SCALE = HEAD_DIM**-0.5 * 1.4426950408889634


def masked_scores(query, keys, first):
    scores = matmul(query, keys, (1, 1)) * EXP_SCALE
    row = lax.broadcasted_iota(jnp.int32, scores.shape, 0)
    column = lax.broadcasted_iota(jnp.int32, scores.shape, 1)
    return jnp.where(column <= row + first, scores, -1e30)


def attend(query, keys, values, first):
    scores = masked_scores(query, keys, first)
    peak = jnp.max(scores, axis=1, keepdims=True)
    shifted = jnp.exp2(scores - peak)
    total = jnp.sum(shifted, axis=1, keepdims=True)
    out = matmul(shifted.astype(HALF), values, (1, 0)) / total
    level = jnp.broadcast_to(peak + jnp.log2(total), (query.shape[0], HEAD_DIM))
    return out.astype(HALF), level


def packed_rows(packed, columns, blocks):
    return packed[:blocks, :, columns].reshape(blocks * packed.shape[1], HEAD_DIM)


def attention_kernel(spare, packed, out, level):
    for block in range(packed.shape[0]):
        out[block], level[block] = attend(
            packed[block, :, head_slice(0)],
            packed_rows(packed, head_slice(1), block + 1),
            packed_rows(packed, head_slice(2 + spare), block + 1),
            block * packed.shape[1],
        )


def attention(spare, packed, *deps):
    count, length, columns = packed.shape
    area = count * (count + 1) // 2 * length * length
    shape = (count, length, HEAD_DIM)
    return launch_whole(
        functools.partial(attention_kernel, spare),
        [packed],
        [(shape, HALF), (shape, FLOAT)],
        "attention",
        deps=deps,
        flops=8 * area * HEAD_DIM,
    )


def spare_attention_kernel(spare, place_ref, packed, queries, out, level):
    count, length = packed.shape[:2]
    for head in range(spare):
        out[:, head_slice(head)], level[head] = attend(
            queries[:, head_slice(head)],
            packed_rows(packed, head_slice(2 + head), count),
            packed_rows(packed, head_slice(3 + spare + head), count),
            place_ref[0] * length,
        )


def spare_attention(place, packed, queries, *deps):
    count, length, columns = packed.shape
    spare = queries.shape[1] // HEAD_DIM
    area = spare * count * length * length
    level_shape = (spare, length, HEAD_DIM)
    return launch_whole(
        functools.partial(spare_attention_kernel, spare),
        [packed, queries],
        [(queries.shape, HALF), (level_shape, FLOAT)],
        "spare_attention",
        prefetch=[place],
        deps=deps,
        flops=8 * area * HEAD_DIM,
    )


def attend_back(query, keys, values, first, level, out, out_grad):
    scores = masked_scores(query, keys, first)
    probs = jnp.exp2(scores - level[:, :1])
    prob_grad = matmul(out_grad, values, (1, 1))
    shared = jnp.sum(out_grad.astype(FLOAT) * out.astype(FLOAT), axis=1, keepdims=True)
    score_grad = (probs * (prob_grad - shared)).astype(HALF)
    value_grad = matmul(probs.astype(HALF), out_grad, (0, 0))
    query_grad = matmul(score_grad, keys, (1, 0)) * HEAD_DIM**-0.5
    key_grad = matmul(score_grad, query, (0, 0)) * HEAD_DIM**-0.5
    return query_grad, key_grad, value_grad


def attention_back_kernel(
    spare, blocks_ref, packed, out, level, out_grad, cosine, sine, spare_back, weight, grad, *rest
):
    parts, (key_sum, value_sum) = rest[:-2], rest[-2:]
    count, length = packed.shape[:2]
    key_sum[...] = jnp.zeros_like(key_sum)
    value_sum[...] = jnp.zeros_like(value_sum)
    for block in range(count):
        query_grad, key_grad, value_grad = attend_back(
            packed[block, :, head_slice(0)],
            packed_rows(packed, head_slice(1), block + 1),
            packed_rows(packed, head_slice(2 + spare), block + 1),
            block * length,
            level[block],
            out[block],
            out_grad[block],
        )
        grad[block, :, head_slice(0)] = turn(query_grad, cosine[block], -sine[block]).astype(HALF)
        seen = (block + 1) * length
        key_sum[:seen] += key_grad
        value_sum[:seen] += value_grad
    for block in range(count):
        rows = slice(block * length, (block + 1) * length)
        grad[block, :, head_slice(1)] = turn(key_sum[rows], cosine[block], -sine[block]).astype(HALF)
        grad[block, :, head_slice(2 + spare)] = value_sum[rows].astype(HALF)
        for head in range(spare):
            grad[block, :, head_slice(2 + head)] = spare_back[block, :, head_slice(head)]
            grad[block, :, head_slice(3 + spare + head)] = spare_back[block, :, head_slice(spare + head)]
    for slot in range(count):
        parts[slot][...] = matmul(grad[blocks_ref[slot]], weight[...], (1, 1)).astype(HALF)


def attention_back(blocks, packed, out, level, out_grad, cosine, sine, spare_back, weight, through, *deps):
    count, length, columns = packed.shape
    width = weight.shape[0]
    spare = spare_back.shape[2] // (2 * HEAD_DIM)
    area = count * (count + 1) // 2 * length * length
    operands = (packed, out, level, out_grad, cosine, sine, spare_back)
    shapes = [packed.shape] + [(length, width)] * count
    return launch(
        functools.partial(attention_back_kernel, spare),
        [*operands, weight],
        [whole_block(array.shape) for array in operands] + [whole_block((width, columns))],
        [whole_block(shape) for shape in shapes],
        [jax.ShapeDtypeStruct(shape, HALF) for shape in shapes],
        "attention_back",
        prefetch=[blocks],
        deps=deps,
        through=through,
        scratch=[pltpu.VMEM((count * length, HEAD_DIM), FLOAT)] * 2,
        flops=20 * area * HEAD_DIM + 2 * count * length * width * columns,
        moved=8 * count * length * columns + 2 * (count * length + columns) * width,
    )


def spare_back_kernel(spare, place_ref, other_ref, packed, queries, out, level, out_grad, cosine, sine, *refs):
    dense, halves, (grad, query_out, dense_out, half_sum) = refs[:5], refs[5:7], refs[7:]
    half_sum[...] = (
        (halves[0][...].astype(FLOAT) + halves[1][...].astype(FLOAT)).reshape(half_sum.shape).astype(HALF)
    )
    count, length = packed.shape[:2]
    place = place_ref[0]
    dense_wgrad(*dense, dense_out)
    for head in range(spare):
        query_grad, key_grad, value_grad = attend_back(
            queries[:, head_slice(head)],
            packed_rows(packed, head_slice(2 + head), count),
            packed_rows(packed, head_slice(3 + spare + head), count),
            place * length,
            level[head],
            out[:, head_slice(head)],
            out_grad[:, head_slice(head)],
        )
        query_out[:, head_slice(head)] = turn(query_grad, cosine[place], -sine[place]).astype(HALF)
        for block in range(count):
            rows = slice(block * length, (block + 1) * length)
            grad[block, :, head_slice(head)] = turn(
                key_grad[rows], cosine[block], -sine[block]
            ).astype(HALF)
            grad[block, :, head_slice(spare + head)] = value_grad[rows].astype(HALF)


def spare_attention_back(place, packed, queries, out, level, out_grad, cosine, sine, dense, halves, other):
    count, length, columns = packed.shape
    spare = queries.shape[1] // HEAD_DIM
    area = spare * count * length * length
    operands = (packed, queries, out, level, out_grad, cosine, sine, *dense)
    width = dense[0].shape[1]
    dense_columns = width + HEAD_DIM + dense[3].shape[1] + dense[4].shape[1]
    shapes = [(count, length, 2 * spare * HEAD_DIM), queries.shape, (width, dense_columns)]
    rest = halves[0].shape[1:]
    pairs = halves[0].shape[0] // 2
    half_block = pl.BlockSpec((pairs, 1) + rest, lambda i, p, o: (0, o[0]) + (0,) * len(rest))
    shapes.append((pairs,) + rest)
    return launch(
        functools.partial(spare_back_kernel, spare),
        [*operands, *(array.reshape((pairs, 2) + rest) for array in halves)],
        [whole_block(array.shape) for array in operands] + [half_block] * 2,
        [whole_block(shape) for shape in shapes],
        [jax.ShapeDtypeStruct(shape, HALF) for shape in shapes],
        "spare_back",
        prefetch=[place, other],
        flops=20 * area * HEAD_DIM,
    )


def attn_wgrad_kernel(count, blocks_ref, core_ref, *refs):
    slots, own, grad, spare_grad = refs[:count], refs[count], refs[count + 1], refs[count + 2]
    kept, sent, rows, total, sems = refs[count + 3 :]
    length = own.shape[0]
    copies = [
        pltpu.make_async_copy(
            slot, rows.at[pl.ds(pl.multiple_of(blocks_ref[i] * length, length), length)], sems.at[i]
        )
        for i, slot in enumerate(slots)
    ]
    for copy in copies:
        copy.start()
    columns = grad.shape[2]
    total[:, columns:] = matmul(own[...], spare_grad[...], (0, 0))
    for copy in copies:
        copy.wait()
    total[:, :columns] = matmul(rows[...], grad[...].reshape(count * length, columns), (0, 0))
    size = kept.shape[1]
    for j in range(kept.shape[0]):
        for target, parity in ((kept, core_ref[0]), (sent, 1 - core_ref[0])):
            start = pl.multiple_of((2 * j + parity) * size, 8)
            target[j] = total[pl.ds(start, size)].astype(HALF)


def attn_wgrad(blocks, core, copies, slots, grad, spare_grad, *deps):
    length, width = slots[0].shape
    count, _, columns = grad.shape
    wide = columns + spare_grad.shape[1]
    part = (copies // 2, width // copies, wide)
    return launch(
        functools.partial(attn_wgrad_kernel, count),
        [*slots, slots[0], grad, spare_grad],
        [ANYWHERE] * count
        + [whole_block(slots[0].shape), whole_block(grad.shape), whole_block(spare_grad.shape)],
        [whole_block(part)] * 2,
        [jax.ShapeDtypeStruct(part, HALF)] * 2,
        "attn_wgrad",
        prefetch=[blocks, core],
        deps=deps,
        scratch=[
            pltpu.VMEM((count * length, width), HALF),
            pltpu.VMEM((width, wide), FLOAT),
            pltpu.SemaphoreType.DMA((count,)),
        ],
        flops=2 * count * length * width * wide,
        moved=2 * (count * length + wide) * width,
    )


def on_device(
    tokens,
    routes,
    gates,
    attn_gain,
    query_weight,
    key_weight,
    value_weight,
    output_weight,
    ffn_gain,
    shared_gate,
    shared_up,
    shared_down,
    expert_gate,
    expert_up,
    expert_down,
    cotangent,
):
    length, width = tokens.shape
    hidden_units = expert_gate.shape[2]
    local_experts = expert_gate.shape[0]
    group = lax.axis_size("narrow")
    copies = lax.axis_size("wide")
    place = lax.axis_index("narrow")
    experts = group * local_experts
    seq_len = length * group
    own_heads = group * HEAD_DIM
    spare_heads = width // HEAD_DIM - group

    ring_place = jnp.where(place % 2 == 0, place // 2, group - 1 - place // 2)
    ring_slot = (ring_place + jnp.arange(group, dtype=jnp.int32)) % group
    slot_block = jnp.where(ring_slot < group // 2, 2 * ring_slot, 2 * (group - ring_slot) - 1)
    attn_gain_row = attn_gain.astype(FLOAT).reshape(1, width)
    ffn_gain_row = ffn_gain.astype(FLOAT).reshape(1, width)
    core = (lax.axis_index("wide") % 2).astype(jnp.int32).reshape(1)

    own_place = place.astype(jnp.int32).reshape(1)
    packed_weight = pack_heads(own_place, spare_heads, query_weight, key_weight, value_weight)
    spare_query_weight = query_weight[:, own_heads:]
    turned, tiles = 2 + spare_heads, 3 + 2 * spare_heads
    half = HEAD_DIM // 2
    angles = np.arange(seq_len)[:, None] * 10000.0 ** (-2.0 * np.arange(half) / HEAD_DIM)[None, :]
    turns = np.stack([np.cos(angles), -np.sin(angles), np.sin(angles)]).astype(np.float32)
    cosine = jnp.asarray(np.concatenate([turns[0], turns[0]], axis=1).reshape(group, length, HEAD_DIM))
    sine = jnp.asarray(np.concatenate([turns[1], turns[2]], axis=1).reshape(group, length, HEAD_DIM))

    share = hidden_units // (copies * group)
    per_expert = -(-(hidden_units + copies * share) // CHUNK) * CHUNK
    gap = per_expert - hidden_units
    spacing = gap // copies
    column = jnp.arange(gap, dtype=jnp.int32)
    unit = jnp.where(
        column % spacing < share,
        ((column // spacing) * group + place) * share + column % spacing,
        -1,
    )
    choice = (jnp.arange(hidden_units, dtype=jnp.int32)[:, None] == unit[None, :]).astype(HALF)

    heads = {"packed": None}
    attn_slots = [None] * group

    def project_slots(*slots, deps=()):
        result = project(
            slot_block,
            slots,
            [token_ring.slots[j] for j in slots],
            attn_gain_row,
            packed_weight,
            cosine,
            sine,
            turned,
            tiles,
            heads["packed"],
            deps,
        )
        heads["packed"] = result[0]
        for i, j in enumerate(slots):
            attn_slots[j] = result[1 + i]
        return result

    half_ring = group // 2
    token_ring = RingGather(tokens)
    token_ring.hop()
    spare_q = project_slots(0)[2]
    padded = local_experts * per_expert
    token_ring.hop(spare_q)
    expert_ids = jnp.arange(experts, dtype=jnp.int32)
    picked = routes[:, :, None] == expert_ids[None, None, :]
    token_gate = jnp.sum(jnp.where(picked, gates[:, :, None], 0.0), axis=1)
    own_gates = lax.all_to_all(
        token_gate.T.reshape(group, local_experts, length),
        "narrow",
        split_axis=0,
        concat_axis=0,
        tiled=True,
    )
    project_slots(1, group - 1)
    gate_weight = pack_experts(
        pack_in_kernel, hidden_units, (width, padded), choice, shared_gate, expert_gate, heads["packed"]
    )
    token_ring.hop(gate_weight)
    project_slots(2, group - 2)
    up_weight = pack_experts(
        pack_in_kernel, hidden_units, (width, padded), choice, shared_up, expert_up, heads["packed"]
    )
    last_hop = token_ring.hop(up_weight)
    project_slots(half_ring - 1, half_ring + 1)
    cot_ring = RingGather(cotangent, mirrored=True)
    cot_ring.hop(*last_hop)
    project_slots(half_ring)
    packed_heads = heads["packed"]
    own_out, level = attention(spare_heads, packed_heads)
    cot_ring.hop(packed_heads)
    returned = lax.all_to_all(own_out, "narrow", split_axis=0, concat_axis=0, tiled=True)
    spare_out, spare_level = spare_attention(own_place, packed_heads, spare_q, own_out)
    down_weight = pack_experts(
        pack_out_kernel, hidden_units, (padded, width), choice, shared_down, expert_down, spare_out, own_gates
    )
    own_gates = own_gates.transpose(0, 2, 1)
    cot_ring.hop(own_out)
    hidden, attended, ffn_in = mix(
        returned, spare_out, output_weight, tokens, ffn_gain_row
    )

    pairs = [(half_ring, half_ring + 1), (2, group - 2)]
    singles = [0, 1, group - 1, half_ring - 1]
    row_order = [slot for pair in pairs for slot in pair] + singles
    rows_state = {"kept": None}
    out_parts, row_parts = [None] * group, [None] * group

    def expert_batch(*batch, deps=()):
        result = expert_rows(
            hidden_units,
            batch,
            row_order.index(batch[0]) * length,
            seq_len,
            rows_state["kept"],
            slot_block,
            [ffn_ring.slots[j] for j in batch],
            [cot_ring.slots[j] for j in batch],
            own_gates,
            gate_weight,
            up_weight,
            down_weight,
            deps,
        )
        rows_state["kept"] = result[:3]
        for i, j in enumerate(batch):
            out_parts[j] = result[3 + i]
            row_parts[j] = result[3 + len(batch) + i]
        return tuple(result[3:])

    ffn_ring = RingGather(ffn_in)
    ffn_ring.hop()
    row_done = expert_batch(0)
    ffn_ring.hop(*row_done)
    cot_ring.hop(*row_done)
    ffn_ring.hop(*expert_batch(1))
    ffn_ring.hop(*expert_batch(group - 1))
    expert_batch(half_ring - 1)
    expert_batch(*pairs[0])
    row_sum, out_sum = RingSum(row_parts), RingSum(out_parts, mirrored=True)
    row_sum.hop()
    out_sum.hop()
    expert_batch(*pairs[1])
    gated_inner, gate_grad, up_grad = rows_state["kept"]
    ordered_cots = [cot_ring.slots[j] for j in row_order]
    ordered_rows = [ffn_ring.slots[j] for j in row_order]

    def over_wide(parts):
        return lax.psum_scatter(parts, "wide", scatter_dimension=0, tiled=False)

    row_added = add_rings([row_sum, out_sum])
    row_sum.hop()
    out_sum.hop()
    down_grad = out_grad(
        hidden_units, local_experts, copies, ordered_cots, gated_inner, *row_added
    )
    row_added = add_rings([row_sum, out_sum])
    down_total = over_wide(after(down_grad, *row_added))
    row_sum.hop(down_grad)
    out_sum.hop(down_grad)
    gate_wgrad, gate_share = in_grad(
        hidden_units, local_experts, copies, core, False, ordered_rows, gate_grad, *row_added
    )
    row_added = add_rings([row_sum, out_sum])
    gate_total = over_wide(after(gate_wgrad, *row_added))
    row_last = row_sum.hop(gate_wgrad)
    out_last = out_sum.hop(gate_wgrad)
    up_kept, up_sent, up_share = in_grad(
        hidden_units, local_experts, copies, core, True, ordered_rows, up_grad, *row_added
    )

    hidden_grad, branch_grad, out_grads, spare_out_grad, gain_terms = back(
        row_sum.last(), after(hidden, up_kept), cotangent, ffn_gain_row, output_weight, group, out_last[0], out_sum.backward
    )
    up_got = wide_first(after(up_sent, out_grads))
    own_out_grad = lax.all_to_all(out_grads, "narrow", split_axis=0, concat_axis=0, tiled=True)
    other = (1 - (lax.axis_index("wide") // 2) % 2).astype(jnp.int32).reshape(1)
    spare_back, spare_query_grad, dense_grad, up_sent_half = spare_attention_back(
        own_place,
        packed_heads,
        spare_q,
        spare_out,
        spare_level,
        spare_out_grad,
        cosine,
        sine,
        (attended, branch_grad, gain_terms, gate_share, up_share),
        (up_kept, up_got),
        other,
    )
    _, up_cross, up_terms = wide_rest(up_kept, up_got, sent=up_sent_half)

    head_grad, *attn_part, dense_grad = attention_back(
        slot_block, packed_heads, own_out, level, own_out_grad, cosine, sine, spare_back, packed_weight, [dense_grad]
    )
    dense_total = over_wide(dense_grad.reshape(copies, width // copies, dense_grad.shape[1]))

    def exchange(part):
        return lax.all_to_all(
            part.reshape(group, part.shape[0] // group, part.shape[1]),
            "narrow",
            split_axis=0,
            concat_axis=0,
            tiled=True,
        )

    spot = jnp.arange(group * gap, dtype=jnp.int32)
    spot_column = spot % gap
    spot_unit = jnp.where(
        spot_column % spacing < share,
        ((spot_column // spacing) * group + spot // gap) * share + spot_column % spacing,
        -1,
    )
    to_units = (spot_unit[:, None] == jnp.arange(hidden_units, dtype=jnp.int32)[None, :]).astype(HALF)
    to_units = to_units.reshape(group, gap, hidden_units)

    attn_sum = RingSum(attn_part)
    attn_sum.hop()
    attn_kept, attn_sent = attn_wgrad(
        slot_block, core, copies, attn_slots, after(head_grad, *attn_part), spare_query_grad
    )
    attn_added = attn_sum.add()
    attn_got = wide_first(after(attn_sent, *attn_added))
    attn_sum.hop()
    attn_sent_half, attn_cross, attn_terms = wide_rest(attn_kept, attn_got, *attn_added)
    attn_added = attn_sum.add(attn_sent_half)
    attn_sum.hop()
    expert_down_grad, shared_down_grad = widen_out(
        down_total, local_experts, hidden_units // copies, share, *attn_added
    )
    gate_total = widen(gate_total, *attn_added)
    attn_added = attn_sum.add(attn_cross, expert_down_grad, gate_total)
    attn_last = attn_sum.hop()
    up_total = sum_halves(*up_terms, FLOAT, attn_last[0])[0]
    first = exchange(after(dense_total, *attn_added))
    output_weight_grad, ffn_gain_columns, shared_gate_grad, shared_up_grad = finish_dense(
        first, to_units, width
    )
    second = exchange(
        sum_halves(
            *attn_terms, HALF, attn_last[0], attn_sum.backward, up_cross, output_weight_grad
        )[0]
    )
    tokens_grad = input_grad(
        attn_sum.last(), spare_query_grad, spare_query_weight, tokens, attn_gain_row, hidden_grad
    )
    mixed = (hidden + sum(part.astype(FLOAT) for part in out_sum.last())).astype(HALF)
    expert_gate_grad, expert_up_grad = gate_total, up_total

    ffn_gain_grad = ffn_gain_columns[:, 0]
    own_rows = width // (copies * group)
    first_row = (lax.axis_index("wide") * group + place) * own_rows

    def own_part(array):
        return lax.dynamic_slice_in_dim(array, first_row, own_rows, axis=0)

    query_weight_grad, key_weight_grad, value_weight_grad, attn_gain_columns = finish_attn(
        spare_heads, second, [own_part(query_weight), own_part(key_weight), own_part(value_weight)]
    )
    attn_gain_grad = attn_gain_columns[:, 0] / own_part(attn_gain).astype(FLOAT)
    return (
        mixed,
        tokens_grad,
        attn_gain_grad,
        query_weight_grad,
        key_weight_grad,
        value_weight_grad,
        output_weight_grad,
        ffn_gain_grad,
        shared_gate_grad,
        shared_up_grad,
        shared_down_grad,
        expert_gate_grad,
        expert_up_grad,
        expert_down_grad,
    )


def solution(mesh):
    rows = P(("wide", "narrow"), None)
    vector = P(("wide", "narrow"))
    held = P("narrow", None, None)
    in_specs = (rows, rows, rows) + (P(),) * 9 + (held, held, held, rows)
    out_specs = (rows, rows, vector) + (rows,) * 4 + (vector,) + (rows,) * 3 + (P("narrow", "wide", None),) * 3
    return jax.shard_map(
        on_device, mesh=mesh, in_specs=in_specs, out_specs=out_specs, check_vma=False
    )
```

time: 569 us -> 552 us (0.970)
  other arithmetic: 37.8 us -> 6.44 us
  waiting for transfers between devices: 98.3 us -> 83.3 us
  Pallas kernels: 313 us -> 327 us
  between operations: 1.42 us -> 14.6 us
    ppermute x26, waiting for transfers between devices: 61.4 us -> 30.4 us  [the longest x11 18.6 us: hop(): arrived.append(lax.ppermute(forward, 'narrow', ahead))]
    convert_element_type x8 -> x1, other arithmetic: 16.2 us -> 1.6 us  [on_device(): (spot_unit[:, None] == jnp.arange(hidden_units, dtype=jnp.int32)[None, :]...]
    pallas_call x37 -> x39, Pallas kernels: 313 us -> 327 us  [launch(): pl.pallas_call(body, grid_spec=pltpu.PrefetchScalarGridSpec(num_scalar_pr...]
    all_to_all x2, waiting for transfers between devices: 11.7 us -> 24 us  [exchange(): lax.all_to_all(part.reshape(group, part.shape[0] // group, part.shape[1])...]
    unnamed x79 -> x126, local copies, waits for them, and re-layouts: 9.5 us -> 21.8 us
    add x3 -> x0, other arithmetic: 7.71 us -> none  [wide_total(): return sum((term[0].astype(FLOAT) for term in terms))]
    squeeze x8 -> x0, local copies, waits for them, and re-layouts: 7.69 us -> none  [half(): return lax.dynamic_index_in_dim(pairs, index, axis=1, keepdims=False)]
    ppermute x9, starting transfers between devices: 15.3 us -> 8.12 us  [hop(): self.backward = lax.ppermute(backward, 'narrow', back)]
  transfers between devices with their start and end apart: 57 -> 54, of which waited for: 20 -> 25; matrix products, arithmetic and copies ran while one was open for 10% -> 3% of each run, Pallas kernels for 52% -> 53%
where the time goes in v5:
time: 552 us; the launch traced here: 544 us
  Pallas kernels  327 us (59%)
  waiting for transfers between devices  83.3 us (15%)
  starting transfers between devices  80.4 us (15%)
  local copies, waits for them, and re-layouts  32.3 us (6%)
  between operations  14.6 us (3%)
  other arithmetic  6.44 us (1%)
    pallas_call x39, Pallas kernels, launch(): pl.pallas_call(body, grid_spec=pltpu.PrefetchScalarGridSpec(num_scalar_pr...  327 us
    ppermute x9, waiting for transfers between devices, hop(): self.forward = lax.ppermute(forward, 'narrow', ahead)  24.9 us
    all_to_all x2, waiting for transfers between devices, exchange(): lax.all_to_all(part.reshape(group, part.shape[0] // group, part.shape[1])...  24 us
    unnamed x126, local copies, waits for them, and re-layouts  21.8 us
    ppermute x11, waiting for transfers between devices, hop(): arrived.append(lax.ppermute(forward, 'narrow', ahead))  18.6 us
    all_to_all x2, starting transfers between devices, exchange(): lax.all_to_all(part.reshape(group, part.shape[0] // group, part.shape[1])...  15.4 us
    ppermute x10, starting transfers between devices, hop(): arrived.append(lax.ppermute(backward, 'narrow', back))  12.8 us
    ppermute x11, starting transfers between devices, hop(): arrived.append(lax.ppermute(forward, 'narrow', ahead))  12.3 us
  transfers between devices with their start and end apart: 54, of which 25 were waited for; matrix products, arithmetic and copies ran while one was open for 3% of the time, Pallas kernels for 53%

profile of v5, /device:TPU:4, one launch (start us, length us, event | category | flops | bytes accessed | tf_op | source)
XLA Modules:
  0.0 543.6 jit_solution(10700646525320517256)
XLA Ops:
  26.8 6.2 %project.6 = (bf16[8,256,896]{2,1,0:T(8,128)(2,1)}, bf16[256,1280]{1,0:T(8,128)(2,1)}, bf16[256,1280]{1,0:T(8,128)(2,1)}) custom-call(s32[8]{0:T(128)} %compare_select_fusion.3.refs_0_, bf16[256,1280]{1,0:T(8,128)(2,1)} %copy-done.16, bf16[256,1280]{1,0:T(8,128)(2,1)} %copy-done.15, ...), custom_call_target="tpu_custom_call", output_to_operand_aliasing={{0}: (9, {})} | custom-call | flops 1174405120 | bytes 4521984 | tf_op jit(solution)/shard_map/project/pallas_call | solution.py:283
  33.0 6.5 %pack_experts.3.refs_4_.refs_6_ = bf16[1280,2048]{1,0:T(8,128)(2,1)} custom-call(bf16[896,128]{1,0:T(8,128)(2,1)} %fusion.1.refs_0_, bf16[1280,896]{1,0:T(8,128)(2,1)} %refs_1_.7, bf16[2,1280,896]{2,1,0:T(8,128)(2,1)} %refs_2_.7, bf16[8,256,896]{2,1,0:T(8,128)(2,1)} %get-tuple-element.173.refs_3_.refs_9_), custom_call_target="tpu_custom_call" | custom-call | bytes 10485760 | tf_op jit(solution)/shard_map/pack_experts/pallas_call | solution.py:283
  42.8 6.1 %project.7 = (bf16[8,256,896]{2,1,0:T(8,128)(2,1)}, bf16[256,1280]{1,0:T(8,128)(2,1)}, bf16[256,1280]{1,0:T(8,128)(2,1)}) custom-call(s32[8]{0:T(128)} %compare_select_fusion.3.refs_0_, bf16[256,1280]{1,0:T(8,128)(2,1)} %copy-done.21, bf16[256,1280]{1,0:T(8,128)(2,1)} %copy-done.20, ...), custom_call_target="tpu_custom_call", output_to_operand_aliasing={{0}: (9, {})} | custom-call | flops 1174405120 | bytes 4521984 | tf_op jit(solution)/shard_map/project/pallas_call | solution.py:283
  48.9 6.5 %pack_experts.4.refs_5_.refs_7_ = bf16[1280,2048]{1,0:T(8,128)(2,1)} custom-call(bf16[896,128]{1,0:T(8,128)(2,1)} %fusion.1.refs_0_, bf16[1280,896]{1,0:T(8,128)(2,1)} %refs_1_.8, bf16[2,1280,896]{2,1,0:T(8,128)(2,1)} %refs_2_.8, bf16[8,256,896]{2,1,0:T(8,128)(2,1)} %get-tuple-element.176.refs_3_.refs_9_), custom_call_target="tpu_custom_call" | custom-call | bytes 10485760 | tf_op jit(solution)/shard_map/pack_experts/pallas_call | solution.py:283
  63.3 6.1 %project.8 = (bf16[8,256,896]{2,1,0:T(8,128)(2,1)}, bf16[256,1280]{1,0:T(8,128)(2,1)}, bf16[256,1280]{1,0:T(8,128)(2,1)}) custom-call(s32[8]{0:T(128)} %compare_select_fusion.3.refs_0_, bf16[256,1280]{1,0:T(8,128)(2,1)} %copy-done.22, bf16[256,1280]{1,0:T(8,128)(2,1)} %copy-done.19, ...), custom_call_target="tpu_custom_call", output_to_operand_aliasing={{0}: (9, {})} | custom-call | flops 1174405120 | bytes 4521984 | tf_op jit(solution)/shard_map/project/pallas_call | solution.py:283
  74.7 8.0 %attention.1 = (bf16[8,256,128]{2,1,0:T(8,128)(2,1)}, f32[8,256,128]{2,1,0:T(8,128)}) custom-call(bf16[8,256,896]{2,1,0:T(8,128)(2,1)} %get-tuple-element.179.refs_0_.refs_1_.refs_2_), custom_call_target="tpu_custom_call" | custom-call | flops 2415919104 | bytes 3670016 | tf_op jit(solution)/shard_map/attention/pallas_call | solution.py:283
  97.6 6.4 %pack_experts.5.refs_6_.refs_8_ = bf16[2048,1280]{1,0:T(8,128)(2,1)} custom-call(bf16[896,128]{1,0:T(8,128)(2,1)} %fusion.1.refs_0_, bf16[896,1280]{1,0:T(8,128)(2,1)} %refs_1_.9, bf16[2,896,1280]{2,1,0:T(8,128)(2,1)} %refs_2_.10, bf16[256,256]{1,0:T(8,128)(2,1)} %get-tuple-element.181.refs_1_.refs_3_.refs_4_, f32[8,2,256]{2,1,0:T(2,128)} %copy-done.46), custom_call_target="tpu_custom_call" | custom-call | bytes 10485760 | tf_op jit(solution)/shard_map/pack_experts/pallas_call | solution.py:283
  121.4 14.9 %expert_rows.6 = (bf16[2048,2048]{1,0:T(8,128)(2,1)}, bf16[2048,2048]{1,0:T(8,128)(2,1)}, bf16[2048,2048]{1,0:T(8,128)(2,1)}, bf16[256,1280]{1,0:T(8,128)(2,1)}, bf16[256,1280]{1,0:T(8,128)(2,1)}) custom-call(s32[8]{0:T(128)} %compare_select_fusion.3.refs_0_, bf16[256,1280]{1,0:T(8,128)(2,1)} %get-tuple-element.186.refs_1_.refs_5_, ...), custom_call_target="tpu_custom_call" | custom-call | flops 8053063680 | bytes 21495808 | tf_op jit(solution)/shard_map/expert_rows/pallas_call | solution.py:283
  146.1 14.8 %expert_rows.7 = (bf16[2048,2048]{1,0:T(8,128)(2,1)}, bf16[2048,2048]{1,0:T(8,128)(2,1)}, bf16[2048,2048]{1,0:T(8,128)(2,1)}, bf16[256,1280]{1,0:T(8,128)(2,1)}, bf16[256,1280]{1,0:T(8,128)(2,1)}) custom-call(s32[8]{0:T(128)} %compare_select_fusion.3.refs_0_, ...), custom_call_target="tpu_custom_call", output_to_operand_aliasing={{0}: (7, {}), {1}: (8, {}), {2}: (9, {})} | custom-call | flops 8053063680 | bytes 21495808 | tf_op jit(solution)/shard_map/expert_rows/pallas_call | solution.py:283
  160.9 7.6 %collective-permute-done.9.refs_2_.refs_4_ = bf16[256,1280]{1,0:T(8,128)(2,1)S(1)} collective-permute-done((bf16[256,1280]{1,0:T(8,128)(2,1)S(1)}, bf16[256,1280]{1,0:T(8,128)(2,1)S(1)}, u32[]{:S(2)}, u32[]{:S(2)}) %collective-permute-start.9) | collective-permute-done | bytes 655392 | tf_op jit(solution)/shard_map/ppermute | solution.py:51
  171.0 14.8 %expert_rows.8 = (bf16[2048,2048]{1,0:T(8,128)(2,1)}, bf16[2048,2048]{1,0:T(8,128)(2,1)}, bf16[2048,2048]{1,0:T(8,128)(2,1)}, bf16[256,1280]{1,0:T(8,128)(2,1)}, bf16[256,1280]{1,0:T(8,128)(2,1)}) custom-call(s32[8]{0:T(128)} %compare_select_fusion.3.refs_0_, ...), custom_call_target="tpu_custom_call", output_to_operand_aliasing={{0}: (7, {}), {1}: (8, {}), {2}: (9, {})} | custom-call | flops 8053063680 | bytes 21495808 | tf_op jit(solution)/shard_map/expert_rows/pallas_call | solution.py:283
  188.6 14.8 %expert_rows.9 = (bf16[2048,2048]{1,0:T(8,128)(2,1)}, bf16[2048,2048]{1,0:T(8,128)(2,1)}, bf16[2048,2048]{1,0:T(8,128)(2,1)}, bf16[256,1280]{1,0:T(8,128)(2,1)}, bf16[256,1280]{1,0:T(8,128)(2,1)}) custom-call(s32[8]{0:T(128)} %compare_select_fusion.3.refs_0_, ...), custom_call_target="tpu_custom_call", output_to_operand_aliasing={{0}: (7, {}), {1}: (8, {}), {2}: (9, {})} | custom-call | flops 8053063680 | bytes 21495808 | tf_op jit(solution)/shard_map/expert_rows/pallas_call | solution.py:283
  204.2 24.7 %expert_rows.10 = (bf16[2048,2048]{1,0:T(8,128)(2,1)}, bf16[2048,2048]{1,0:T(8,128)(2,1)}, bf16[2048,2048]{1,0:T(8,128)(2,1)}, bf16[256,1280]{1,0:T(8,128)(2,1)}...) custom-call(s32[8]{0:T(128)} %compare_select_fusion.3.refs_0_, ...), custom_call_target="tpu_custom_call", output_to_operand_aliasing={{0}: (9, {}), {1}: (10, {}), {2}: (11, {})} | custom-call | flops 16106127360 | bytes 27262976 | tf_op jit(solution)/shard_map/expert_rows/pallas_call | solution.py:283
  233.0 24.5 %expert_rows.11 = (bf16[2048,2048]{1,0:T(8,128)(2,1)}, bf16[2048,2048]{1,0:T(8,128)(2,1)}, bf16[2048,2048]{1,0:T(8,128)(2,1)}, bf16[256,1280]{1,0:T(8,128)(2,1)}...) custom-call(s32[8]{0:T(128)} %compare_select_fusion.3.refs_0_, ...), custom_call_target="tpu_custom_call", output_to_operand_aliasing={{0}: (9, {}), {1}: (10, {}), {2}: (11, {})} | custom-call | flops 16106127360 | bytes 27262976 | tf_op jit(solution)/shard_map/expert_rows/pallas_call | solution.py:283
  267.4 18.8 %expert_out_grad.1 = bf16[4,480,1280]{2,1,0:T(8,128)(2,1)} custom-call(bf16[256,1280]{1,0:T(8,128)(2,1)} %collective-permute-done.20.refs_3_.refs_0_, bf16[256,1280]{1,0:T(8,128)(2,1)} %collective-permute-done.18.refs_4_.refs_1_, bf16[256,1280]{1,0:T(8,128)(2,1)} %copy-done.55, bf16[256,1280]{1,0:T(8,128)(2,1)} %collective-permute-done.16.refs_4_.refs_3_, ...), custom_call_target="tpu_custom_call" | custom-call | flops 10737418240 | bytes 22151168 | tf_op jit(solution)/shard_map/expert_out_grad/pallas_call | solution.py:283
  298.2 19.1 %expert_in_grad.2 = (bf16[4,2,320,896]{3,2,1,0:T(8,128)(2,1)}, f32[1280,128]{1,0:T(8,128)}) custom-call(s32[1]{0:T(128)} %bitcast.3.refs_0_.refs_1_, bf16[256,1280]{1,0:T(8,128)(2,1)} %copy-done.54, bf16[256,1280]{1,0:T(8,128)(2,1)} %copy-done.53, bf16[256,1280]{1,0:T(8,128)(2,1)} %copy-done.52, bf16[256,1280]{1,0:T(8,128)(2,1)} %copy-done.51, ...), custom_call_target="tpu_custom_call" | custom-call | flops 10737418240 | bytes 22151168 | tf_op jit(solution)/shard_map/expert_in_grad/pallas_call | solution.py:283
  326.1 18.3 %expert_in_grad.3 = (bf16[2,2,320,896]{3,2,1,0:T(8,128)(2,1)}, bf16[2,2,320,896]{3,2,1,0:T(8,128)(2,1)}, f32[1280,128]{1,0:T(8,128)}) custom-call(s32[1]{0:T(128)} %bitcast.3.refs_0_.refs_1_, bf16[256,1280]{1,0:T(8,128)(2,1)} %copy-done.54, bf16[256,1280]{1,0:T(8,128)(2,1)} %copy-done.53, bf16[256,1280]{1,0:T(8,128)(2,1)} %copy-done.52, ...), custom_call_target="tpu_custom_call" | custom-call | flops 10737418240 | bytes 22151168 | tf_op jit(solution)/shard_map/expert_in_grad/pallas_call | solution.py:283
  360.9 12.3 %spare_back.1 = (bf16[8,256,512]{2,1,0:T(8,128)(2,1)}, bf16[256,256]{1,0:T(8,128)(2,1)}, bf16[1280,1664]{1,0:T(8,128)(2,1)}, bf16[1,2,320,896]{3,2,1,0:T(8,128)(2,1)}) custom-call(s32[1]{0:T(128)} %bitcast.refs_0_, s32[1]{0:T(128)} %bitcast.4.refs_1_, bf16[8,256,896]{2,1,0:T(8,128)(2,1)} %get-tuple-element.179.refs_0_.refs_1_.refs_2_, ...), custom_call_target="tpu_custom_call" | custom-call | flops 2684354560 | tf_op jit(solution)/shard_map/spare_back/pallas_call | solution.py:283
  374.0 19.5 %attention_back.1 = (bf16[8,256,896]{2,1,0:T(8,128)(2,1)}, bf16[256,1280]{1,0:T(8,128)(2,1)}, bf16[256,1280]{1,0:T(8,128)(2,1)}, bf16[256,1280]{1,0:T(8,128)(2,1...) custom-call(s32[8]{0:T(128)} %compare_select_fusion.3.refs_0_, ...), custom_call_target="tpu_custom_call", output_to_operand_aliasing={{9}: (9, {})} | custom-call | flops 10737418240 | bytes 22216704 | tf_op jit(solution)/shard_map/attention_back/pallas_call | solution.py:283
  396.7 12.8 %attn_wgrad.1 = (bf16[2,320,1152]{2,1,0:T(8,128)(2,1)}, bf16[2,320,1152]{2,1,0:T(8,128)(2,1)}) custom-call(s32[8]{0:T(128)} %compare_select_fusion.3.refs_0_, s32[1]{0:T(128)} %bitcast.3.refs_0_.refs_1_, bf16[256,1280]{1,0:T(8,128)(2,1)} %get-tuple-element.283.refs_2_.refs_10_, bf16[256,1280]{1,0:T(8,128)(2,1)} %get-tuple-element.284.refs_3_, ...), custom_call_target="tpu_custom_call" | custom-call | flops 6039797760 | bytes 8192000 | tf_op jit(solution)/shard_map/attn_wgrad/pallas_call | solution.py:283
  424.6 9.1 %collective-permute-done.38.refs_0_ = bf16[256,1280]{1,0:T(8,128)(2,1)S(1)} collective-permute-done((bf16[256,1280]{1,0:T(8,128)(2,1)}, bf16[256,1280]{1,0:T(8,128)(2,1)S(1)}, u32[]{:S(2)}, u32[]{:S(2)}) %collective-permute-start.38) | collective-permute-done | bytes 655392 | tf_op jit(solution)/shard_map/ppermute | solution.py:79
  445.0 10.0 %collective-permute-done.41.refs_0_ = bf16[256,1280]{1,0:T(8,128)(2,1)S(1)} collective-permute-done((bf16[256,1280]{1,0:T(8,128)(2,1)}, bf16[256,1280]{1,0:T(8,128)(2,1)S(1)}, u32[]{:S(2)}, u32[]{:S(2)}) %collective-permute-start.41) | collective-permute-done | bytes 655392 | tf_op jit(solution)/shard_map/ppermute | solution.py:79
  471.6 21.3 %all-to-all-done.3.refs_0_ = bf16[8,40,1664]{2,1,0:T(8,128)(2,1)S(1)} async-done(((bf16[8,40,1664]{2,1,0:T(8,128)(2,1)}), bf16[8,40,1664]{2,1,0:T(8,128)(2,1)S(1)}, u32[]{:S(2)}, u32[]{:S(2)}) %all-to-all-start.3) | async-done | bytes 1064992 | tf_op jit(solution)/shard_map/all_to_all | solution.py:1251
  502.8 10.3 %all-to-all-start.4 = ((bf16[8,40,1152]{2,1,0:T(8,128)(2,1)}), bf16[8,40,1152]{2,1,0:T(8,128)(2,1)S(1)}, u32[]{:S(2)}, u32[]{:S(2)}) async-start(bf16[8,40,1152]{2,1,0:T(8,128)(2,1)} %bitcast.32), calls=%async_computation.7 | async-start | bytes 1474560 | tf_op jit(solution)/shard_map/all_to_all | solution.py:1251
  (269 shorter events, 215.6 us)
Async XLA Ops:
  58.3 24.3 %all-to-all-start.1 = ((f32[8,2,256]{2,1,0:T(2,128)}), f32[8,2,256]{2,1,0:T(2,128)S(1)}, u32[]{:S(2)}, u32[]{:S(2)}) async-start(f32[8,2,256]{2,1,0:T(2,128)} %reshape.173), calls=%async_computation.1 | async-start | bytes 32768 | tf_op jit(solution)/shard_map/all_to_all | solution.py:1120
  82.6 31.1 %all-to-all-start = ((bf16[8,256,128]{2,1,0:T(8,128)(2,1)}), bf16[8,256,128]{2,1,0:T(8,128)(2,1)S(1)}, u32[]{:S(2)}, u32[]{:S(2)}) async-start(bf16[8,256,128]{2,1,0:T(8,128)(2,1)} %get-tuple-element.180.refs_3_.refs_2_), calls=%async_computation | async-start | bytes 1048576 | tf_op jit(solution)/shard_map/all_to_all | solution.py:1144
  88.7 350.6 %reduce-scatter.4.cloned.1.call-start = ((), (), s32[]{:S(2)}) async-start(), calls=%async_computation.8 | async-start | bytes 6144000 | tf_op jit(solution)/shard_map/reduce_scatter | solution.py:1201
  109.5 26.8 %collective-permute-start.16 = (bf16[256,1280]{1,0:T(8,128)(2,1)S(1)}, bf16[256,1280]{1,0:T(8,128)(2,1)}, u32[]{:S(2)}, u32[]{:S(2)}) collective-permute-start(bf16[256,1280]{1,0:T(8,128)(2,1)S(1)} %collective-permute-done.14.refs_2_.refs_6_), channel_id=1, source_target_pairs={{0,2},{2,4},{4,6},{6,7},{7,5},{5,3},{3,1},{1,0},{8,10},{10,12},{12... | collective-permute-start | bytes 1966088 | tf_op jit(solution)/shard_map/ppermute | solution.py:51
  110.0 26.2 %collective-permute-start.17 = (bf16[256,1280]{1,0:T(8,128)(2,1)S(1)}, bf16[256,1280]{1,0:T(8,128)(2,1)S(1)}, u32[]{:S(2)}, u32[]{:S(2)}) collective-permute-start(bf16[256,1280]{1,0:T(8,128)(2,1)S(1)} %collective-permute-done.11.refs_2_.refs_5_), channel_id=1, source_target_pairs={{2,0},{4,2},{6,4},{7,6},{5,7},{3,5},{1,3},{0,1},{10,8},{12,10},{14... | collective-permute-start | bytes 1966088 | tf_op jit(solution)/shard_map/ppermute | solution.py:54
  119.2 24.2 %collective-permute-start.7 = (bf16[256,1280]{1,0:T(8,128)(2,1)}, bf16[256,1280]{1,0:T(8,128)(2,1)S(1)}, u32[]{:S(2)}, u32[]{:S(2)}) collective-permute-start(bf16[256,1280]{1,0:T(8,128)(2,1)} %get-tuple-element.186.refs_1_.refs_5_), channel_id=1, source_target_pairs={{0,2},{2,4},{4,6},{6,7},{7,5},{5,3},{3,1},{1,0},{8,10},{10,12},{12... | collective-permute-start | bytes 1966088 | tf_op jit(solution)/shard_map/ppermute | solution.py:51
  119.8 24.2 %collective-permute-start.8 = (bf16[256,1280]{1,0:T(8,128)(2,1)}, bf16[256,1280]{1,0:T(8,128)(2,1)S(1)}, u32[]{:S(2)}, u32[]{:S(2)}) collective-permute-start(bf16[256,1280]{1,0:T(8,128)(2,1)} %get-tuple-element.186.refs_1_.refs_5_), channel_id=1, source_target_pairs={{2,0},{4,2},{6,4},{7,6},{5,7},{3,5},{1,3},{0,1},{10,8},{12,10},{14... | collective-permute-start | bytes 1966088 | tf_op jit(solution)/shard_map/ppermute | solution.py:54
  137.1 48.8 %collective-permute-start.18 = (bf16[256,1280]{1,0:T(8,128)(2,1)}, bf16[256,1280]{1,0:T(8,128)(2,1)}, u32[]{:S(2)}, u32[]{:S(2)}) collective-permute-start(bf16[256,1280]{1,0:T(8,128)(2,1)} %collective-permute-done.16.refs_4_.refs_3_), channel_id=1, source_target_pairs={{0,2},{2,4},{4,6},{6,7},{7,5},{5,3},{3,1},{1,0},{8,10},{10,12},{12... | collective-permute-start | bytes 1966088 | tf_op jit(solution)/shard_map/ppermute | solution.py:51
  137.8 48.1 %collective-permute-start.19 = (bf16[256,1280]{1,0:T(8,128)(2,1)}, bf16[256,1280]{1,0:T(8,128)(2,1)S(1)}, u32[]{:S(2)}, u32[]{:S(2)}) collective-permute-start(bf16[256,1280]{1,0:T(8,128)(2,1)} %copy-done.55), channel_id=1, source_target_pairs={{2,0},{4,2},{6,4},{7,6},{5,7},{3,5},{1,3},{0,1},{10,8},{12,10},{14... | collective-permute-start | bytes 1966088 | tf_op jit(solution)/shard_map/ppermute | solution.py:54
  144.0 24.4 %collective-permute-start.9 = (bf16[256,1280]{1,0:T(8,128)(2,1)S(1)}, bf16[256,1280]{1,0:T(8,128)(2,1)S(1)}, u32[]{:S(2)}, u32[]{:S(2)}) collective-permute-start(bf16[256,1280]{1,0:T(8,128)(2,1)S(1)} %collective-permute-done.7.refs_1_.refs_7_), channel_id=1, source_target_pairs={{0,2},{2,4},{4,6},{6,7},{7,5},{5,3},{3,1},{1,0},{8,10},{10,12},{12... | collective-permute-start | bytes 1966088 | tf_op jit(solution)/shard_map/ppermute | solution.py:51
  228.9 28.6 %collective-permute-start.21 = (bf16[256,1280]{1,0:T(8,128)(2,1)}, bf16[256,1280]{1,0:T(8,128)(2,1)S(1)}, u32[]{:S(2)}, u32[]{:S(2)}) collective-permute-start(bf16[256,1280]{1,0:T(8,128)(2,1)} %get-tuple-element.218), channel_id=1, source_target_pairs={{0,2},{2,4},{4,6},{6,7},{7,5},{5,3},{3,1},{1,0},{8,10},{10,12},{12... | collective-permute-start | bytes 1966088 | tf_op jit(solution)/shard_map/ppermute | solution.py:79
  230.9 26.7 %collective-permute-start.22 = (bf16[256,1280]{1,0:T(8,128)(2,1)}, bf16[256,1280]{1,0:T(8,128)(2,1)S(1)}, u32[]{:S(2)}, u32[]{:S(2)}) collective-permute-start(bf16[256,1280]{1,0:T(8,128)(2,1)} %get-tuple-element.219), channel_id=1, source_target_pairs={{2,0},{4,2},{6,4},{7,6},{5,7},{3,5},{1,3},{0,1},{10,8},{12,10},{14... | collective-permute-start | bytes 1966088 | tf_op jit(solution)/shard_map/ppermute | solution.py:80
  231.0 26.6 %collective-permute-start.23 = (bf16[256,1280]{1,0:T(8,128)(2,1)}, bf16[256,1280]{1,0:T(8,128)(2,1)S(1)}, u32[]{:S(2)}, u32[]{:S(2)}) collective-permute-start(bf16[256,1280]{1,0:T(8,128)(2,1)} %get-tuple-element.222), channel_id=1, source_target_pairs={{2,0},{4,2},{6,4},{7,6},{5,7},{3,5},{1,3},{0,1},{10,8},{12,10},{14... | collective-permute-start | bytes 1966088 | tf_op jit(solution)/shard_map/ppermute | solution.py:79
  232.7 24.9 %collective-permute-start.24 = (bf16[256,1280]{1,0:T(8,128)(2,1)S(1)}, bf16[256,1280]{1,0:T(8,128)(2,1)S(1)}, u32[]{:S(2)}, u32[]{:S(2)}) collective-permute-start(bf16[256,1280]{1,0:T(8,128)(2,1)S(1)} %copy-done.58), channel_id=1, source_target_pairs={{0,2},{2,4},{4,6},{6,7},{7,5},{5,3},{3,1},{1,0},{8,10},{10,12},{12... | collective-permute-start | bytes 1966088 | tf_op jit(solution)/shard_map/ppermute | solution.py:80
  263.2 23.0 %collective-permute-start.25 = (bf16[256,1280]{1,0:T(8,128)(2,1)}, bf16[256,1280]{1,0:T(8,128)(2,1)S(1)}, u32[]{:S(2)}, u32[]{:S(2)}) collective-permute-start(bf16[256,1280]{1,0:T(8,128)(2,1)} %get-tuple-element.233.refs_9_), channel_id=1, source_target_pairs={{0,2},{2,4},{4,6},{6,7},{7,5},{5,3},{3,1},{1,0},{8,10},{10,12},{12... | collective-permute-start | bytes 1966088 | tf_op jit(solution)/shard_map/ppermute | solution.py:79
  265.3 24.4 %collective-permute-start.27 = (bf16[256,1280]{1,0:T(8,128)(2,1)}, bf16[256,1280]{1,0:T(8,128)(2,1)S(1)}, u32[]{:S(2)}, u32[]{:S(2)}) collective-permute-start(bf16[256,1280]{1,0:T(8,128)(2,1)} %get-tuple-element.237.refs_11_), channel_id=1, source_target_pairs={{2,0},{4,2},{6,4},{7,6},{5,7},{3,5},{1,3},{0,1},{10,8},{12,10},{14... | collective-permute-start | bytes 1966088 | tf_op jit(solution)/shard_map/ppermute | solution.py:79
  295.1 147.1 %reduce-scatter.6.cloned.1.call-start = ((), (), s32[]{:S(2)}) async-start(), calls=%async_computation.9 | async-start | bytes 5734400 | tf_op jit(solution)/shard_map/reduce_scatter | solution.py:1201
  357.4 104.2 %reduce-scatter.8.cloned.1.call-start = ((), (), s32[]{:S(2)}) async-start(), calls=%async_computation.10 | async-start | bytes 5324800 | tf_op jit(solution)/shard_map/reduce_scatter | solution.py:1201
  423.3 35.1 %collective-permute-start.42 = (bf16[1,320,1152]{2,1,0:T(8,128)(2,1)}, bf16[1,320,1152]{2,1,0:T(8,128)(2,1)S(1)}, u32[]{:S(2)}, u32[]{:S(2)}) collective-permute-start(bf16[1,320,1152]{2,1,0:T(8,128)(2,1)} %sum_halves.3.refs_4_), channel_id=1, source_target_pairs={{0,16},{8,24},{16,0},{24,8},{1,17},{9,25},{17,1},{25,9},{2,18},{10... | collective-permute-start | bytes 2211848 | tf_op jit(solution)/shard_map/ppermute | solution.py:132
  461.6 31.2 %all-to-all-start.3 = ((bf16[8,40,1664]{2,1,0:T(8,128)(2,1)}), bf16[8,40,1664]{2,1,0:T(8,128)(2,1)S(1)}, u32[]{:S(2)}, u32[]{:S(2)}) async-start(bf16[8,40,1664]{2,1,0:T(8,128)(2,1)} %bitcast.36), calls=%async_computation.6 | async-start | bytes 2129920 | tf_op jit(solution)/shard_map/all_to_all | solution.py:1251
  466.7 30.4 %collective-permute-start.45 = (bf16[1,2,320,896]{3,2,1,0:T(8,128)(2,1)}, bf16[1,2,320,896]{3,2,1,0:T(8,128)(2,1)S(1)}, u32[]{:S(2)}, u32[]{:S(2)}) collective-permute-start(bf16[1,2,320,896]{3,2,1,0:T(8,128)(2,1)} %get-tuple-element.308), channel_id=1, source_target_pairs={{0,16},{8,24},{16,0},{24,8},{1,17},{9,25},{17,1},{25,9},{2,18},{10... | collective-permute-start | bytes 3440648 | tf_op jit(solution)/shard_map/ppermute | solution.py:132
  467.8 29.6 %collective-permute-start.44 = (bf16[256,1280]{1,0:T(8,128)(2,1)S(1)}, bf16[256,1280]{1,0:T(8,128)(2,1)}, u32[]{:S(2)}, u32[]{:S(2)}) collective-permute-start(bf16[256,1280]{1,0:T(8,128)(2,1)S(1)} %copy-done.12), channel_id=1, source_target_pairs={{2,0},{4,2},{6,4},{7,6},{5,7},{3,5},{1,3},{0,1},{10,8},{12,10},{14... | collective-permute-start | bytes 1966088 | tf_op jit(solution)/shard_map/ppermute | solution.py:80
  469.4 29.9 %collective-permute-start.43 = (bf16[256,1280]{1,0:T(8,128)(2,1)}, bf16[256,1280]{1,0:T(8,128)(2,1)S(1)}, u32[]{:S(2)}, u32[]{:S(2)}) collective-permute-start(bf16[256,1280]{1,0:T(8,128)(2,1)} %add_pairs.11), channel_id=1, source_target_pairs={{0,2},{2,4},{4,6},{6,7},{7,5},{5,3},{3,1},{1,0},{8,10},{10,12},{12... | collective-permute-start | bytes 1966088 | tf_op jit(solution)/shard_map/ppermute | solution.py:76
  502.8 29.0 %all-to-all-start.4 = ((bf16[8,40,1152]{2,1,0:T(8,128)(2,1)}), bf16[8,40,1152]{2,1,0:T(8,128)(2,1)S(1)}, u32[]{:S(2)}, u32[]{:S(2)}) async-start(bf16[8,40,1152]{2,1,0:T(8,128)(2,1)} %bitcast.32), calls=%async_computation.7 | async-start | bytes 1474560 | tf_op jit(solution)/shard_map/all_to_all | solution.py:1251
  (93 other events, 881.4 us)
Sparse Core Ops, SparseCore 0:
  295.2 49.0 reduce-scatter.3
  347.1 49.7 reduce-scatter.5
  399.4 60.7 reduce-scatter.7

commit v6 on v5

--- a/solution.py
+++ b/solution.py
@@ -199,7 +199,7 @@
         total += parts[g, :, : width + HEAD_DIM].astype(FLOAT)
     out[...] = total[:, :width]
     gain[...] = total[:, width:]
-    column = width + HEAD_DIM
+    column = width
     gap = to_units.shape[1]
     for share in (gate, up):
         share[...] = sum(
@@ -632,15 +632,14 @@
     )
 
 
-def dense_wgrad(attended, branch, terms, gate_share, up_share, out):
+def dense_wgrad(share, attended, branch, terms, gate_share, up_share, out):
     width = attended.shape[1]
-    ones = jnp.ones((terms.shape[0], HEAD_DIM), HALF)
+    gap = gate_share.shape[1]
     out[:, :width] = matmul(attended[...], branch[...], (0, 0)).astype(HALF)
-    out[:, width : width + HEAD_DIM] = matmul(terms[...], ones, (0, 0)).astype(HALF)
-    column = width + HEAD_DIM
-    for share in (gate_share, up_share):
-        out[:, column : column + share.shape[1]] = share[...].astype(HALF)
-        column += share.shape[1]
+    gain = matmul(terms[...], jnp.ones((terms.shape[0], gap), HALF), (0, 0))
+    column = lax.broadcasted_iota(jnp.int32, gain.shape, 1)
+    out[:, width : width + gap] = jnp.where(column == share, gain, gate_share[...]).astype(HALF)
+    out[:, width + gap :] = up_share[...].astype(HALF)
 
 
 def tokens_grad_kernel(own, forward, backward, spare_grad, weight, tokens, gain, hidden_grad, out):
@@ -928,14 +927,14 @@
     )
 
 
-def spare_back_kernel(spare, place_ref, other_ref, packed, queries, out, level, out_grad, cosine, sine, *refs):
+def spare_back_kernel(spare, share, place_ref, other_ref, packed, queries, out, level, out_grad, cosine, sine, *refs):
     dense, halves, (grad, query_out, dense_out, half_sum) = refs[:5], refs[5:7], refs[7:]
     half_sum[...] = (
         (halves[0][...].astype(FLOAT) + halves[1][...].astype(FLOAT)).reshape(half_sum.shape).astype(HALF)
     )
     count, length = packed.shape[:2]
     place = place_ref[0]
-    dense_wgrad(*dense, dense_out)
+    dense_wgrad(share, *dense, dense_out)
     for head in range(spare):
         query_grad, key_grad, value_grad = attend_back(
             queries[:, head_slice(head)],
@@ -955,20 +954,20 @@
             grad[block, :, head_slice(spare + head)] = value_grad[rows].astype(HALF)
 
 
-def spare_attention_back(place, packed, queries, out, level, out_grad, cosine, sine, dense, halves, other):
+def spare_attention_back(place, packed, queries, out, level, out_grad, cosine, sine, dense, share, halves, other):
     count, length, columns = packed.shape
     spare = queries.shape[1] // HEAD_DIM
     area = spare * count * length * length
     operands = (packed, queries, out, level, out_grad, cosine, sine, *dense)
     width = dense[0].shape[1]
-    dense_columns = width + HEAD_DIM + dense[3].shape[1] + dense[4].shape[1]
+    dense_columns = width + dense[3].shape[1] + dense[4].shape[1]
     shapes = [(count, length, 2 * spare * HEAD_DIM), queries.shape, (width, dense_columns)]
     rest = halves[0].shape[1:]
     pairs = halves[0].shape[0] // 2
     half_block = pl.BlockSpec((pairs, 1) + rest, lambda i, p, o: (0, o[0]) + (0,) * len(rest))
     shapes.append((pairs,) + rest)
     return launch(
-        functools.partial(spare_back_kernel, spare),
+        functools.partial(spare_back_kernel, spare, share),
         [*operands, *(array.reshape((pairs, 2) + rest) for array in halves)],
         [whole_block(array.shape) for array in operands] + [half_block] * 2,
         [whole_block(shape) for shape in shapes],
@@ -1237,6 +1236,7 @@
         cosine,
         sine,
         (attended, branch_grad, gain_terms, gate_share, up_share),
+        share,
         (up_kept, up_got),
         other,
     )
@@ -1290,7 +1290,7 @@
     )
     second = exchange(
         sum_halves(
-            *attn_terms, HALF, attn_last[0], attn_sum.backward, up_cross, output_weight_grad
+            *attn_terms, HALF, attn_last[0], attn_sum.backward, up_cross, first
         )[0]
     )
     tokens_grad = input_grad(
@@ -1299,7 +1299,7 @@
     mixed = (hidden + sum(part.astype(FLOAT) for part in out_sum.last())).astype(HALF)
     expert_gate_grad, expert_up_grad = gate_total, up_total
 
-    ffn_gain_grad = ffn_gain_columns[:, 0]
+    ffn_gain_grad = ffn_gain_columns[:, share]
     own_rows = width // (copies * group)
     first_row = (lax.axis_index("wide") * group + place) * own_rows
 

time: 552 us -> 551 us (level)
    all_to_all x2, waiting for transfers between devices: 24 us -> 0.01 us  [exchange(): lax.all_to_all(part.reshape(group, part.shape[0] // group, part.shape[1])...]
    ppermute x2, waiting for transfers between devices: 3.36 us -> 24.2 us  [wide_swap(): return lax.ppermute(sent, 'wide', [(i, i ^ bit) for i in range(count)])]
    unnamed x126 -> x122, local copies, waits for them, and re-layouts: 21.8 us -> 20.9 us
  transfers between devices with their start and end apart: 54 -> 54, of which waited for: 25 -> 23; matrix products, arithmetic and copies ran while one was open for 3% -> 3% of each run, Pallas kernels for 53% -> 53%
where the time goes in v6:
time: 551 us; the launch traced here: 543 us
  Pallas kernels  326 us (59%)
  waiting for transfers between devices  83.3 us (15%)
  starting transfers between devices  81.3 us (15%)
  local copies, waits for them, and re-layouts  32.3 us (6%)
  between operations  14.6 us (3%)
    pallas_call x39, Pallas kernels, launch(): pl.pallas_call(body, grid_spec=pltpu.PrefetchScalarGridSpec(num_scalar_pr...  326 us
    ppermute x2, waiting for transfers between devices, wide_swap(): return lax.ppermute(sent, 'wide', [(i, i ^ bit) for i in range(count)])  24.2 us
    ppermute x9, waiting for transfers between devices, hop(): self.forward = lax.ppermute(forward, 'narrow', ahead)  24.1 us
    unnamed x122, local copies, waits for them, and re-layouts  20.9 us
    ppermute x11, waiting for transfers between devices, hop(): arrived.append(lax.ppermute(forward, 'narrow', ahead))  20.2 us
    all_to_all x2, starting transfers between devices, exchange(): lax.all_to_all(part.reshape(group, part.shape[0] // group, part.shape[1])...  16.1 us
    ppermute x10, starting transfers between devices, hop(): arrived.append(lax.ppermute(backward, 'narrow', back))  13.8 us
    ppermute x11, starting transfers between devices, hop(): arrived.append(lax.ppermute(forward, 'narrow', ahead))  11.3 us
  transfers between devices with their start and end apart: 54, of which 23 were waited for; matrix products, arithmetic and copies ran while one was open for 3% of the time, Pallas kernels for 53%

profile of v6, /device:TPU:4, one launch (start us, length us, event | category | flops | bytes accessed | tf_op | source)
XLA Modules:
  0.0 543.0 jit_solution(15136648405334413169)
XLA Ops:
  26.8 6.1 %project.6 = (bf16[8,256,896]{2,1,0:T(8,128)(2,1)}, bf16[256,1280]{1,0:T(8,128)(2,1)}, bf16[256,1280]{1,0:T(8,128)(2,1)}) custom-call(s32[8]{0:T(128)} %compare_select_fusion.3.refs_0_, bf16[256,1280]{1,0:T(8,128)(2,1)} %copy-done.16, bf16[256,1280]{1,0:T(8,128)(2,1)} %copy-done.15, ...), custom_call_target="tpu_custom_call", output_to_operand_aliasing={{0}: (9, {})} | custom-call | flops 1174405120 | bytes 4521984 | tf_op jit(solution)/shard_map/project/pallas_call | solution.py:283
  33.0 6.5 %pack_experts.3.refs_4_.refs_6_ = bf16[1280,2048]{1,0:T(8,128)(2,1)} custom-call(bf16[896,128]{1,0:T(8,128)(2,1)} %fusion.1.refs_0_, bf16[1280,896]{1,0:T(8,128)(2,1)} %refs_1_.7, bf16[2,1280,896]{2,1,0:T(8,128)(2,1)} %refs_2_.7, bf16[8,256,896]{2,1,0:T(8,128)(2,1)} %get-tuple-element.173.refs_3_.refs_9_), custom_call_target="tpu_custom_call" | custom-call | bytes 10485760 | tf_op jit(solution)/shard_map/pack_experts/pallas_call | solution.py:283
  42.8 6.1 %project.7 = (bf16[8,256,896]{2,1,0:T(8,128)(2,1)}, bf16[256,1280]{1,0:T(8,128)(2,1)}, bf16[256,1280]{1,0:T(8,128)(2,1)}) custom-call(s32[8]{0:T(128)} %compare_select_fusion.3.refs_0_, bf16[256,1280]{1,0:T(8,128)(2,1)} %copy-done.21, bf16[256,1280]{1,0:T(8,128)(2,1)} %copy-done.20, ...), custom_call_target="tpu_custom_call", output_to_operand_aliasing={{0}: (9, {})} | custom-call | flops 1174405120 | bytes 4521984 | tf_op jit(solution)/shard_map/project/pallas_call | solution.py:283
  48.9 6.6 %pack_experts.4.refs_5_.refs_7_ = bf16[1280,2048]{1,0:T(8,128)(2,1)} custom-call(bf16[896,128]{1,0:T(8,128)(2,1)} %fusion.1.refs_0_, bf16[1280,896]{1,0:T(8,128)(2,1)} %refs_1_.8, bf16[2,1280,896]{2,1,0:T(8,128)(2,1)} %refs_2_.8, bf16[8,256,896]{2,1,0:T(8,128)(2,1)} %get-tuple-element.176.refs_3_.refs_9_), custom_call_target="tpu_custom_call" | custom-call | bytes 10485760 | tf_op jit(solution)/shard_map/pack_experts/pallas_call | solution.py:283
  63.3 6.1 %project.8 = (bf16[8,256,896]{2,1,0:T(8,128)(2,1)}, bf16[256,1280]{1,0:T(8,128)(2,1)}, bf16[256,1280]{1,0:T(8,128)(2,1)}) custom-call(s32[8]{0:T(128)} %compare_select_fusion.3.refs_0_, bf16[256,1280]{1,0:T(8,128)(2,1)} %copy-done.22, bf16[256,1280]{1,0:T(8,128)(2,1)} %copy-done.19, ...), custom_call_target="tpu_custom_call", output_to_operand_aliasing={{0}: (9, {})} | custom-call | flops 1174405120 | bytes 4521984 | tf_op jit(solution)/shard_map/project/pallas_call | solution.py:283
  74.7 7.9 %attention.1 = (bf16[8,256,128]{2,1,0:T(8,128)(2,1)}, f32[8,256,128]{2,1,0:T(8,128)}) custom-call(bf16[8,256,896]{2,1,0:T(8,128)(2,1)} %get-tuple-element.179.refs_0_.refs_1_.refs_2_), custom_call_target="tpu_custom_call" | custom-call | flops 2415919104 | bytes 3670016 | tf_op jit(solution)/shard_map/attention/pallas_call | solution.py:283
  97.6 6.4 %pack_experts.5.refs_6_.refs_8_ = bf16[2048,1280]{1,0:T(8,128)(2,1)} custom-call(bf16[896,128]{1,0:T(8,128)(2,1)} %fusion.1.refs_0_, bf16[896,1280]{1,0:T(8,128)(2,1)} %refs_1_.9, bf16[2,896,1280]{2,1,0:T(8,128)(2,1)} %refs_2_.10, bf16[256,256]{1,0:T(8,128)(2,1)} %get-tuple-element.181.refs_1_.refs_3_.refs_4_, f32[8,2,256]{2,1,0:T(2,128)} %copy-done.46), custom_call_target="tpu_custom_call" | custom-call | bytes 10485760 | tf_op jit(solution)/shard_map/pack_experts/pallas_call | solution.py:283
  121.6 14.8 %expert_rows.6 = (bf16[2048,2048]{1,0:T(8,128)(2,1)}, bf16[2048,2048]{1,0:T(8,128)(2,1)}, bf16[2048,2048]{1,0:T(8,128)(2,1)}, bf16[256,1280]{1,0:T(8,128)(2,1)}, bf16[256,1280]{1,0:T(8,128)(2,1)}) custom-call(s32[8]{0:T(128)} %compare_select_fusion.3.refs_0_, bf16[256,1280]{1,0:T(8,128)(2,1)} %get-tuple-element.186.refs_1_.refs_5_, ...), custom_call_target="tpu_custom_call" | custom-call | flops 8053063680 | bytes 21495808 | tf_op jit(solution)/shard_map/expert_rows/pallas_call | solution.py:283
  146.1 14.8 %expert_rows.7 = (bf16[2048,2048]{1,0:T(8,128)(2,1)}, bf16[2048,2048]{1,0:T(8,128)(2,1)}, bf16[2048,2048]{1,0:T(8,128)(2,1)}, bf16[256,1280]{1,0:T(8,128)(2,1)}, bf16[256,1280]{1,0:T(8,128)(2,1)}) custom-call(s32[8]{0:T(128)} %compare_select_fusion.3.refs_0_, ...), custom_call_target="tpu_custom_call", output_to_operand_aliasing={{0}: (7, {}), {1}: (8, {}), {2}: (9, {})} | custom-call | flops 8053063680 | bytes 21495808 | tf_op jit(solution)/shard_map/expert_rows/pallas_call | solution.py:283
  160.9 8.1 %collective-permute-done.9.refs_2_.refs_4_ = bf16[256,1280]{1,0:T(8,128)(2,1)S(1)} collective-permute-done((bf16[256,1280]{1,0:T(8,128)(2,1)S(1)}, bf16[256,1280]{1,0:T(8,128)(2,1)S(1)}, u32[]{:S(2)}, u32[]{:S(2)}) %collective-permute-start.9) | collective-permute-done | bytes 655392 | tf_op jit(solution)/shard_map/ppermute | solution.py:51
  171.2 14.8 %expert_rows.8 = (bf16[2048,2048]{1,0:T(8,128)(2,1)}, bf16[2048,2048]{1,0:T(8,128)(2,1)}, bf16[2048,2048]{1,0:T(8,128)(2,1)}, bf16[256,1280]{1,0:T(8,128)(2,1)}, bf16[256,1280]{1,0:T(8,128)(2,1)}) custom-call(s32[8]{0:T(128)} %compare_select_fusion.3.refs_0_, ...), custom_call_target="tpu_custom_call", output_to_operand_aliasing={{0}: (7, {}), {1}: (8, {}), {2}: (9, {})} | custom-call | flops 8053063680 | bytes 21495808 | tf_op jit(solution)/shard_map/expert_rows/pallas_call | solution.py:283
  189.0 14.8 %expert_rows.9 = (bf16[2048,2048]{1,0:T(8,128)(2,1)}, bf16[2048,2048]{1,0:T(8,128)(2,1)}, bf16[2048,2048]{1,0:T(8,128)(2,1)}, bf16[256,1280]{1,0:T(8,128)(2,1)}, bf16[256,1280]{1,0:T(8,128)(2,1)}) custom-call(s32[8]{0:T(128)} %compare_select_fusion.3.refs_0_, ...), custom_call_target="tpu_custom_call", output_to_operand_aliasing={{0}: (7, {}), {1}: (8, {}), {2}: (9, {})} | custom-call | flops 8053063680 | bytes 21495808 | tf_op jit(solution)/shard_map/expert_rows/pallas_call | solution.py:283
  204.6 24.7 %expert_rows.10 = (bf16[2048,2048]{1,0:T(8,128)(2,1)}, bf16[2048,2048]{1,0:T(8,128)(2,1)}, bf16[2048,2048]{1,0:T(8,128)(2,1)}, bf16[256,1280]{1,0:T(8,128)(2,1)}...) custom-call(s32[8]{0:T(128)} %compare_select_fusion.3.refs_0_, ...), custom_call_target="tpu_custom_call", output_to_operand_aliasing={{0}: (9, {}), {1}: (10, {}), {2}: (11, {})} | custom-call | flops 16106127360 | bytes 27262976 | tf_op jit(solution)/shard_map/expert_rows/pallas_call | solution.py:283
  233.4 24.5 %expert_rows.11 = (bf16[2048,2048]{1,0:T(8,128)(2,1)}, bf16[2048,2048]{1,0:T(8,128)(2,1)}, bf16[2048,2048]{1,0:T(8,128)(2,1)}, bf16[256,1280]{1,0:T(8,128)(2,1)}...) custom-call(s32[8]{0:T(128)} %compare_select_fusion.3.refs_0_, ...), custom_call_target="tpu_custom_call", output_to_operand_aliasing={{0}: (9, {}), {1}: (10, {}), {2}: (11, {})} | custom-call | flops 16106127360 | bytes 27262976 | tf_op jit(solution)/shard_map/expert_rows/pallas_call | solution.py:283
  267.7 18.8 %expert_out_grad.1 = bf16[4,480,1280]{2,1,0:T(8,128)(2,1)} custom-call(bf16[256,1280]{1,0:T(8,128)(2,1)} %collective-permute-done.20.refs_3_.refs_0_, bf16[256,1280]{1,0:T(8,128)(2,1)} %collective-permute-done.18.refs_4_.refs_1_, bf16[256,1280]{1,0:T(8,128)(2,1)} %collective-permute-done.17.refs_3_.refs_2_, ...), custom_call_target="tpu_custom_call" | custom-call | flops 10737418240 | bytes 22151168 | tf_op jit(solution)/shard_map/expert_out_grad/pallas_call | solution.py:283
  297.9 19.1 %expert_in_grad.2 = (bf16[4,2,320,896]{3,2,1,0:T(8,128)(2,1)}, f32[1280,128]{1,0:T(8,128)}) custom-call(s32[1]{0:T(128)} %bitcast.3.refs_0_.refs_1_, bf16[256,1280]{1,0:T(8,128)(2,1)} %copy-done.53, bf16[256,1280]{1,0:T(8,128)(2,1)} %copy-done.52, bf16[256,1280]{1,0:T(8,128)(2,1)} %copy-done.51, bf16[256,1280]{1,0:T(8,128)(2,1)} %copy-done.50, ...), custom_call_target="tpu_custom_call" | custom-call | flops 10737418240 | bytes 22151168 | tf_op jit(solution)/shard_map/expert_in_grad/pallas_call | solution.py:283
  325.8 18.3 %expert_in_grad.3 = (bf16[2,2,320,896]{3,2,1,0:T(8,128)(2,1)}, bf16[2,2,320,896]{3,2,1,0:T(8,128)(2,1)}, f32[1280,128]{1,0:T(8,128)}) custom-call(s32[1]{0:T(128)} %bitcast.3.refs_0_.refs_1_, bf16[256,1280]{1,0:T(8,128)(2,1)} %copy-done.53, bf16[256,1280]{1,0:T(8,128)(2,1)} %copy-done.52, bf16[256,1280]{1,0:T(8,128)(2,1)} %copy-done.51, ...), custom_call_target="tpu_custom_call" | custom-call | flops 10737418240 | bytes 22151168 | tf_op jit(solution)/shard_map/expert_in_grad/pallas_call | solution.py:283
  361.1 12.1 %spare_back.1 = (bf16[8,256,512]{2,1,0:T(8,128)(2,1)}, bf16[256,256]{1,0:T(8,128)(2,1)}, bf16[1280,1536]{1,0:T(8,128)(2,1)}, bf16[1,2,320,896]{3,2,1,0:T(8,128)(2,1)}) custom-call(s32[1]{0:T(128)} %bitcast.refs_0_, s32[1]{0:T(128)} %bitcast.4.refs_1_, bf16[8,256,896]{2,1,0:T(8,128)(2,1)} %get-tuple-element.179.refs_0_.refs_1_.refs_2_, ...), custom_call_target="tpu_custom_call" | custom-call | flops 2684354560 | tf_op jit(solution)/shard_map/spare_back/pallas_call | solution.py:283
  374.0 19.5 %attention_back.1 = (bf16[8,256,896]{2,1,0:T(8,128)(2,1)}, bf16[256,1280]{1,0:T(8,128)(2,1)}, bf16[256,1280]{1,0:T(8,128)(2,1)}, bf16[256,1280]{1,0:T(8,128)(2,1...) custom-call(s32[8]{0:T(128)} %compare_select_fusion.3.refs_0_, ...), custom_call_target="tpu_custom_call", output_to_operand_aliasing={{9}: (9, {})} | custom-call | flops 10737418240 | bytes 22216704 | tf_op jit(solution)/shard_map/attention_back/pallas_call | solution.py:283
  396.7 12.8 %attn_wgrad.1 = (bf16[2,320,1152]{2,1,0:T(8,128)(2,1)}, bf16[2,320,1152]{2,1,0:T(8,128)(2,1)}) custom-call(s32[8]{0:T(128)} %compare_select_fusion.3.refs_0_, s32[1]{0:T(128)} %bitcast.3.refs_0_.refs_1_, bf16[256,1280]{1,0:T(8,128)(2,1)} %get-tuple-element.283.refs_2_.refs_10_, bf16[256,1280]{1,0:T(8,128)(2,1)} %get-tuple-element.284.refs_3_, ...), custom_call_target="tpu_custom_call" | custom-call | flops 6039797760 | bytes 8192000 | tf_op jit(solution)/shard_map/attn_wgrad/pallas_call | solution.py:283
  424.6 9.0 %collective-permute-done.38.refs_0_ = bf16[256,1280]{1,0:T(8,128)(2,1)S(1)} collective-permute-done((bf16[256,1280]{1,0:T(8,128)(2,1)}, bf16[256,1280]{1,0:T(8,128)(2,1)S(1)}, u32[]{:S(2)}, u32[]{:S(2)}) %collective-permute-start.38) | collective-permute-done | bytes 655392 | tf_op jit(solution)/shard_map/ppermute | solution.py:79
  444.9 9.9 %collective-permute-done.41.refs_0_ = bf16[256,1280]{1,0:T(8,128)(2,1)S(1)} collective-permute-done((bf16[256,1280]{1,0:T(8,128)(2,1)}, bf16[256,1280]{1,0:T(8,128)(2,1)S(1)}, u32[]{:S(2)}, u32[]{:S(2)}) %collective-permute-start.41) | collective-permute-done | bytes 655392 | tf_op jit(solution)/shard_map/ppermute | solution.py:79
  470.3 22.2 %collective-permute-done.45.refs_6_.refs_3_ = bf16[1,2,320,896]{3,2,1,0:T(8,128)(2,1)S(1)} collective-permute-done((bf16[1,2,320,896]{3,2,1,0:T(8,128)(2,1)}, bf16[1,2,320,896]{3,2,1,0:T(8,128)(2,1)S(1)}, u32[]{:S(2)}, u32[]{:S(2)}) %collective-permute-start.45) | collective-permute-done | bytes 1146912 | tf_op jit(solution)/shard_map/ppermute | solution.py:132
  502.0 10.0 %all-to-all-start.4 = ((bf16[8,40,1152]{2,1,0:T(8,128)(2,1)}), bf16[8,40,1152]{2,1,0:T(8,128)(2,1)S(1)}, u32[]{:S(2)}, u32[]{:S(2)}) async-start(bf16[8,40,1152]{2,1,0:T(8,128)(2,1)} %bitcast.32), calls=%async_computation.7 | async-start | bytes 1474560 | tf_op jit(solution)/shard_map/all_to_all | solution.py:1251
  (265 shorter events, 214.3 us)
Async XLA Ops:
  58.3 24.3 %all-to-all-start.1 = ((f32[8,2,256]{2,1,0:T(2,128)}), f32[8,2,256]{2,1,0:T(2,128)S(1)}, u32[]{:S(2)}, u32[]{:S(2)}) async-start(f32[8,2,256]{2,1,0:T(2,128)} %reshape.173), calls=%async_computation.1 | async-start | bytes 32768 | tf_op jit(solution)/shard_map/all_to_all | solution.py:1119
  82.6 31.3 %all-to-all-start = ((bf16[8,256,128]{2,1,0:T(8,128)(2,1)}), bf16[8,256,128]{2,1,0:T(8,128)(2,1)S(1)}, u32[]{:S(2)}, u32[]{:S(2)}) async-start(bf16[8,256,128]{2,1,0:T(8,128)(2,1)} %get-tuple-element.180.refs_3_.refs_2_), calls=%async_computation | async-start | bytes 1048576 | tf_op jit(solution)/shard_map/all_to_all | solution.py:1143
  88.7 350.6 %reduce-scatter.4.cloned.1.call-start = ((), (), s32[]{:S(2)}) async-start(), calls=%async_computation.8 | async-start | bytes 6144000 | tf_op jit(solution)/shard_map/reduce_scatter | solution.py:1200
  109.6 26.8 %collective-permute-start.16 = (bf16[256,1280]{1,0:T(8,128)(2,1)}, bf16[256,1280]{1,0:T(8,128)(2,1)}, u32[]{:S(2)}, u32[]{:S(2)}) collective-permute-start(bf16[256,1280]{1,0:T(8,128)(2,1)} %collective-permute-done.14.refs_2_.refs_6_), channel_id=1, source_target_pairs={{0,2},{2,4},{4,6},{6,7},{7,5},{5,3},{3,1},{1,0},{8,10},{10,12},{12... | collective-permute-start | bytes 1966088 | tf_op jit(solution)/shard_map/ppermute | solution.py:51
  110.0 26.4 %collective-permute-start.17 = (bf16[256,1280]{1,0:T(8,128)(2,1)S(1)}, bf16[256,1280]{1,0:T(8,128)(2,1)}, u32[]{:S(2)}, u32[]{:S(2)}) collective-permute-start(bf16[256,1280]{1,0:T(8,128)(2,1)S(1)} %collective-permute-done.11.refs_2_.refs_5_), channel_id=1, source_target_pairs={{2,0},{4,2},{6,4},{7,6},{5,7},{3,5},{1,3},{0,1},{10,8},{12,10},{14... | collective-permute-start | bytes 1966088 | tf_op jit(solution)/shard_map/ppermute | solution.py:54
  119.3 24.4 %collective-permute-start.7 = (bf16[256,1280]{1,0:T(8,128)(2,1)}, bf16[256,1280]{1,0:T(8,128)(2,1)S(1)}, u32[]{:S(2)}, u32[]{:S(2)}) collective-permute-start(bf16[256,1280]{1,0:T(8,128)(2,1)} %get-tuple-element.186.refs_1_.refs_5_), channel_id=1, source_target_pairs={{0,2},{2,4},{4,6},{6,7},{7,5},{5,3},{3,1},{1,0},{8,10},{10,12},{12... | collective-permute-start | bytes 1966088 | tf_op jit(solution)/shard_map/ppermute | solution.py:51
  119.9 24.2 %collective-permute-start.8 = (bf16[256,1280]{1,0:T(8,128)(2,1)}, bf16[256,1280]{1,0:T(8,128)(2,1)S(1)}, u32[]{:S(2)}, u32[]{:S(2)}) collective-permute-start(bf16[256,1280]{1,0:T(8,128)(2,1)} %get-tuple-element.186.refs_1_.refs_5_), channel_id=1, source_target_pairs={{2,0},{4,2},{6,4},{7,6},{5,7},{3,5},{1,3},{0,1},{10,8},{12,10},{14... | collective-permute-start | bytes 1966088 | tf_op jit(solution)/shard_map/ppermute | solution.py:54
  136.4 49.6 %collective-permute-start.18 = (bf16[256,1280]{1,0:T(8,128)(2,1)}, bf16[256,1280]{1,0:T(8,128)(2,1)}, u32[]{:S(2)}, u32[]{:S(2)}) collective-permute-start(bf16[256,1280]{1,0:T(8,128)(2,1)} %collective-permute-done.16.refs_4_.refs_3_), channel_id=1, source_target_pairs={{0,2},{2,4},{4,6},{6,7},{7,5},{5,3},{3,1},{1,0},{8,10},{10,12},{12... | collective-permute-start | bytes 1966088 | tf_op jit(solution)/shard_map/ppermute | solution.py:51
  137.0 49.0 %collective-permute-start.19 = (bf16[256,1280]{1,0:T(8,128)(2,1)}, bf16[256,1280]{1,0:T(8,128)(2,1)S(1)}, u32[]{:S(2)}, u32[]{:S(2)}) collective-permute-start(bf16[256,1280]{1,0:T(8,128)(2,1)} %collective-permute-done.17.refs_3_.refs_2_), channel_id=1, source_target_pairs={{2,0},{4,2},{6,4},{7,6},{5,7},{3,5},{1,3},{0,1},{10,8},{12,10},{14... | collective-permute-start | bytes 1966088 | tf_op jit(solution)/shard_map/ppermute | solution.py:54
  144.1 25.0 %collective-permute-start.9 = (bf16[256,1280]{1,0:T(8,128)(2,1)S(1)}, bf16[256,1280]{1,0:T(8,128)(2,1)S(1)}, u32[]{:S(2)}, u32[]{:S(2)}) collective-permute-start(bf16[256,1280]{1,0:T(8,128)(2,1)S(1)} %collective-permute-done.7.refs_1_.refs_7_), channel_id=1, source_target_pairs={{0,2},{2,4},{4,6},{6,7},{7,5},{5,3},{3,1},{1,0},{8,10},{10,12},{12... | collective-permute-start | bytes 1966088 | tf_op jit(solution)/shard_map/ppermute | solution.py:51
  229.3 28.6 %collective-permute-start.21 = (bf16[256,1280]{1,0:T(8,128)(2,1)}, bf16[256,1280]{1,0:T(8,128)(2,1)S(1)}, u32[]{:S(2)}, u32[]{:S(2)}) collective-permute-start(bf16[256,1280]{1,0:T(8,128)(2,1)} %get-tuple-element.218), channel_id=1, source_target_pairs={{0,2},{2,4},{4,6},{6,7},{7,5},{5,3},{3,1},{1,0},{8,10},{10,12},{12... | collective-permute-start | bytes 1966088 | tf_op jit(solution)/shard_map/ppermute | solution.py:79
  230.7 27.3 %collective-permute-start.22 = (bf16[256,1280]{1,0:T(8,128)(2,1)}, bf16[256,1280]{1,0:T(8,128)(2,1)S(1)}, u32[]{:S(2)}, u32[]{:S(2)}) collective-permute-start(bf16[256,1280]{1,0:T(8,128)(2,1)} %get-tuple-element.219), channel_id=1, source_target_pairs={{2,0},{4,2},{6,4},{7,6},{5,7},{3,5},{1,3},{0,1},{10,8},{12,10},{14... | collective-permute-start | bytes 1966088 | tf_op jit(solution)/shard_map/ppermute | solution.py:80
  231.4 26.6 %collective-permute-start.23 = (bf16[256,1280]{1,0:T(8,128)(2,1)}, bf16[256,1280]{1,0:T(8,128)(2,1)S(1)}, u32[]{:S(2)}, u32[]{:S(2)}) collective-permute-start(bf16[256,1280]{1,0:T(8,128)(2,1)} %get-tuple-element.222), channel_id=1, source_target_pairs={{2,0},{4,2},{6,4},{7,6},{5,7},{3,5},{1,3},{0,1},{10,8},{12,10},{14... | collective-permute-start | bytes 1966088 | tf_op jit(solution)/shard_map/ppermute | solution.py:79
  233.0 25.0 %collective-permute-start.24 = (bf16[256,1280]{1,0:T(8,128)(2,1)S(1)}, bf16[256,1280]{1,0:T(8,128)(2,1)S(1)}, u32[]{:S(2)}, u32[]{:S(2)}) collective-permute-start(bf16[256,1280]{1,0:T(8,128)(2,1)S(1)} %copy-done.56), channel_id=1, source_target_pairs={{0,2},{2,4},{4,6},{6,7},{7,5},{5,3},{3,1},{1,0},{8,10},{10,12},{12... | collective-permute-start | bytes 1966088 | tf_op jit(solution)/shard_map/ppermute | solution.py:80
  263.5 23.0 %collective-permute-start.25 = (bf16[256,1280]{1,0:T(8,128)(2,1)}, bf16[256,1280]{1,0:T(8,128)(2,1)S(1)}, u32[]{:S(2)}, u32[]{:S(2)}) collective-permute-start(bf16[256,1280]{1,0:T(8,128)(2,1)} %get-tuple-element.233.refs_9_), channel_id=1, source_target_pairs={{0,2},{2,4},{4,6},{6,7},{7,5},{5,3},{3,1},{1,0},{8,10},{10,12},{12... | collective-permute-start | bytes 1966088 | tf_op jit(solution)/shard_map/ppermute | solution.py:79
  265.7 23.9 %collective-permute-start.27 = (bf16[256,1280]{1,0:T(8,128)(2,1)}, bf16[256,1280]{1,0:T(8,128)(2,1)S(1)}, u32[]{:S(2)}, u32[]{:S(2)}) collective-permute-start(bf16[256,1280]{1,0:T(8,128)(2,1)} %get-tuple-element.237.refs_11_), channel_id=1, source_target_pairs={{2,0},{4,2},{6,4},{7,6},{5,7},{3,5},{1,3},{0,1},{10,8},{12,10},{14... | collective-permute-start | bytes 1966088 | tf_op jit(solution)/shard_map/ppermute | solution.py:79
  294.8 147.3 %reduce-scatter.6.cloned.1.call-start = ((), (), s32[]{:S(2)}) async-start(), calls=%async_computation.9 | async-start | bytes 5734400 | tf_op jit(solution)/shard_map/reduce_scatter | solution.py:1200
  357.6 102.3 %reduce-scatter.8.cloned.1.call-start = ((), (), s32[]{:S(2)}) async-start(), calls=%async_computation.10 | async-start | bytes 4915200 | tf_op jit(solution)/shard_map/reduce_scatter | solution.py:1200
  423.2 33.6 %collective-permute-start.42 = (bf16[1,320,1152]{2,1,0:T(8,128)(2,1)}, bf16[1,320,1152]{2,1,0:T(8,128)(2,1)S(1)}, u32[]{:S(2)}, u32[]{:S(2)}) collective-permute-start(bf16[1,320,1152]{2,1,0:T(8,128)(2,1)} %sum_halves.3.refs_4_), channel_id=1, source_target_pairs={{0,16},{8,24},{16,0},{24,8},{1,17},{9,25},{17,1},{25,9},{2,18},{10... | collective-permute-start | bytes 2211848 | tf_op jit(solution)/shard_map/ppermute | solution.py:132
  459.9 37.6 %all-to-all-start.3 = ((bf16[8,40,1536]{2,1,0:T(8,128)(2,1)}), bf16[8,40,1536]{2,1,0:T(8,128)(2,1)S(1)}, u32[]{:S(2)}, u32[]{:S(2)}) async-start(bf16[8,40,1536]{2,1,0:T(8,128)(2,1)} %bitcast.36), calls=%async_computation.6 | async-start | bytes 1966080 | tf_op jit(solution)/shard_map/all_to_all | solution.py:1251
  466.0 26.5 %collective-permute-start.45 = (bf16[1,2,320,896]{3,2,1,0:T(8,128)(2,1)}, bf16[1,2,320,896]{3,2,1,0:T(8,128)(2,1)S(1)}, u32[]{:S(2)}, u32[]{:S(2)}) collective-permute-start(bf16[1,2,320,896]{3,2,1,0:T(8,128)(2,1)} %get-tuple-element.308), channel_id=1, source_target_pairs={{0,16},{8,24},{16,0},{24,8},{1,17},{9,25},{17,1},{25,9},{2,18},{10... | collective-permute-start | bytes 3440648 | tf_op jit(solution)/shard_map/ppermute | solution.py:132
  466.6 29.2 %collective-permute-start.44 = (bf16[256,1280]{1,0:T(8,128)(2,1)}, bf16[256,1280]{1,0:T(8,128)(2,1)S(1)}, u32[]{:S(2)}, u32[]{:S(2)}) collective-permute-start(bf16[256,1280]{1,0:T(8,128)(2,1)} %get-tuple-element.306), channel_id=1, source_target_pairs={{2,0},{4,2},{6,4},{7,6},{5,7},{3,5},{1,3},{0,1},{10,8},{12,10},{14... | collective-permute-start | bytes 1966088 | tf_op jit(solution)/shard_map/ppermute | solution.py:80
  468.0 29.5 %collective-permute-start.43 = (bf16[256,1280]{1,0:T(8,128)(2,1)}, bf16[256,1280]{1,0:T(8,128)(2,1)S(1)}, u32[]{:S(2)}, u32[]{:S(2)}) collective-permute-start(bf16[256,1280]{1,0:T(8,128)(2,1)} %add_pairs.11), channel_id=1, source_target_pairs={{0,2},{2,4},{4,6},{6,7},{7,5},{5,3},{3,1},{1,0},{8,10},{10,12},{12... | collective-permute-start | bytes 1966088 | tf_op jit(solution)/shard_map/ppermute | solution.py:76
  502.0 29.2 %all-to-all-start.4 = ((bf16[8,40,1152]{2,1,0:T(8,128)(2,1)}), bf16[8,40,1152]{2,1,0:T(8,128)(2,1)S(1)}, u32[]{:S(2)}, u32[]{:S(2)}) async-start(bf16[8,40,1152]{2,1,0:T(8,128)(2,1)} %bitcast.32), calls=%async_computation.7 | async-start | bytes 1474560 | tf_op jit(solution)/shard_map/all_to_all | solution.py:1251
  (91 other events, 849.0 us)
Sparse Core Ops, SparseCore 0:
  294.9 49.4 reduce-scatter.3
  347.2 49.6 reduce-scatter.5
  399.4 57.6 reduce-scatter.7
